TPU v7x, 256 devices: a whole 4x4x8 slice. The times are simulated.
256 devices in a mesh: seq: 64 (over x, z_hi, y), batch: 4 (over z_lo, core).
Axes of the slice: x: 4, y: 4, z: 8 (z_hi: 4, z_lo: 2; z = z_hi * 2 + z_lo), core: 2. Of those that a mesh axis runs over, the one named last changes fastest.
Arguments:
- sequence: bfloat16 [32768, 512], P(('batch', 'seq')), parts along dimension 0, may hold values from -6 to 6
- upstream: bfloat16 [32768, 512], P(('batch', 'seq')), parts along dimension 0, may hold values from -6 to 6
- norm_gain: float32 [512], replicated, may hold values from 0.1 to 1.9
- in_proj: bfloat16 [512, 2304], replicated, may hold values from -0.25 to 0.25
- step_proj: bfloat16 [512, 16], replicated, may hold values from -0.25 to 0.25
- conv_weight: float32 [4, 1280], replicated, may hold values from -3 to 3
- conv_bias: float32 [1280], replicated, may hold values from -3 to 3
- step_bias: float32 [16], replicated, may hold values from -5.5 to -3.5
- decay_log: float32 [16], replicated
- skip_gain: float32 [16], replicated, may hold values from 0.5 to 2
- out_proj: bfloat16 [1024, 512], replicated, may hold values from -0.1875 to 0.1875
Outputs:
- layer_out: bfloat16 [32768, 512], P(('batch', 'seq')), parts along dimension 0
- grad_input: bfloat16 [32768, 512], P(('batch', 'seq')), parts along dimension 0
- grad_in_proj: float32 [2048, 2304], P(('batch', 'seq')), parts along dimension 0
- grad_out_proj: float32 [4096, 512], P(('batch', 'seq')), parts along dimension 0
There are 4 independent parts, one for each index of `batch`. A program takes and returns all parts, laid end to end along the dimension named above; an argument that names none is the same for every part. Nothing has to cross between parts.
All inputs are finite; a program needn't handle non-finite values.
Results may differ from a plain program's by a relative error of at most 0.015.
Values may be sent and summed in bfloat16 or wider, within the bound.
No kernel may reach another device: no remote copies, remote signals or barrier semaphores. Data moves between devices by JAX's collectives and lax.ppermute only.
A program may use at most 192 MiB of HBM per device.

v0:
```python
import jax
import jax.numpy as jnp
from jax import lax
from jax.sharding import PartitionSpec as P

epsilon = 1e-06


def padded(block, sides, width):
    for axis, dim in sides:
        count = lax.axis_size(axis)
        forward = [(i, i + 1) for i in range(count - 1)]
        backward = [(target, source) for source, target in forward]
        low = lax.ppermute(
            lax.slice_in_dim(block, block.shape[dim] - width, None, axis=dim), axis, forward
        )
        high = lax.ppermute(lax.slice_in_dim(block, 0, width, axis=dim), axis, backward)
        block = jnp.concatenate([low, block, high], axis=dim)
    return block


def prefix(x, axis, join, neutral, backward):
    count = lax.axis_size(axis)
    place = lax.axis_index(axis)
    ahead = count - 1 - place if backward else place
    gathered = jax.tree.map(
        lambda a, kind: lax.all_gather(a.astype(kind), axis), x, (jnp.bfloat16, jnp.bfloat16)
    )
    state = jax.tree.map(lambda a, e: jnp.zeros_like(a) + jnp.asarray(e, a.dtype), x, neutral)

    def prefix_one(turn, state):
        source = count - 1 - turn if backward else turn
        return join(
            state,
            jax.tree.map(
                lambda a, own: lax.dynamic_index_in_dim(a, source, 0, False).astype(own.dtype),
                gathered,
                x,
            ),
        )

    return lax.fori_loop(0, ahead, prefix_one, state)


def entering(x, axis, join, neutral, backward):
    count = lax.axis_size(axis)
    place = lax.axis_index(axis)
    ahead = count - 1 - place if backward else place
    gathered = jax.tree.map(
        lambda a, kind: lax.all_gather(a.astype(kind), axis),
        x,
        jax.tree.map(lambda a: jnp.bfloat16 if a.dtype == jnp.float32 else a.dtype, x),
    )
    state = jax.tree.map(lambda a, e: jnp.zeros_like(a) + jnp.asarray(e, a.dtype), x, neutral)

    def entering_one(turn, state):
        source = count - 1 - turn if backward else turn
        return join(
            state,
            jax.tree.map(
                lambda a, own: lax.dynamic_index_in_dim(a, source, 0, False).astype(own.dtype),
                gathered,
                x,
            ),
        )

    return lax.fori_loop(0, ahead, entering_one, state)


def normed(vector, norm_gain):
    scale = lax.rsqrt(jnp.mean(vector * vector, axis=-1, keepdims=True) + epsilon)
    return vector * scale * norm_gain


def contract_rows(left, right):
    return lax.dot_general(
        left, right, (((0,), (0,)), ((), ())), preferred_element_type=jnp.float32
    )


def contract_cols(left, right):
    return lax.dot_general(
        left, right, (((1,), (1,)), ((), ())), preferred_element_type=jnp.float32
    )


def prepare(extended, step_raw, conv_weight, conv_bias, step_bias, decay_log, inner_width):
    count_rows = step_raw.shape[0]
    convolved = conv_bias
    for tap in range(conv_weight.shape[0]):
        convolved = convolved + extended[tap : tap + count_rows] * conv_weight[tap]
    activated = jax.nn.silu(convolved)
    heads = step_raw.shape[1]
    state_dim = (activated.shape[1] - inner_width) // 2
    inputs_ssd = activated[:, :inner_width].reshape(count_rows, heads, inner_width // heads)
    b_matrix = activated[:, inner_width : inner_width + state_dim]
    c_matrix = activated[:, inner_width + state_dim :]
    step_size = jax.nn.softplus(step_raw + step_bias)
    log_decay = -jnp.exp(decay_log) * step_size
    cumul = jnp.cumsum(log_decay, axis=0)
    driven = inputs_ssd * step_size[:, :, None]
    totals = cumul[-1]
    weight_end = jnp.exp(totals[None, :] - cumul)
    local_state = jnp.einsum(
        "th,thp,tn->hpn", weight_end, driven, b_matrix, precision=lax.Precision.HIGHEST
    )
    return ((inputs_ssd, b_matrix, c_matrix, cumul, driven), local_state, totals)


def finish(inner_vals, gate_rows, carried, skip_gain):
    inputs_ssd, b_matrix, c_matrix, cumul, driven = inner_vals
    count_rows = inputs_ssd.shape[0]
    scores = jnp.dot(c_matrix, b_matrix.T, precision=lax.Precision.HIGHEST)
    places = jnp.arange(count_rows)
    lower_mask = (places[:, None] >= places[None, :])[None, :, :]
    differ = cumul.T[:, :, None] - cumul.T[:, None, :]
    decays = jnp.where(lower_mask, jnp.exp(jnp.where(lower_mask, differ, 0.0)), 0.0)
    intra = jnp.einsum("hts,ts,shp->thp", decays, scores, driven, precision=lax.Precision.HIGHEST)
    carry_in = jnp.einsum(
        "th,tn,hpn->thp", jnp.exp(cumul), c_matrix, carried, precision=lax.Precision.HIGHEST
    )
    mixed_heads = intra + carry_in + skip_gain[None, :, None] * inputs_ssd
    return (mixed_heads.reshape(count_rows, -1) * jax.nn.silu(gate_rows)).astype(jnp.bfloat16)


def link_pair(earlier, later):
    return (earlier[0] + later[0], jnp.exp(later[0])[:, None, None] * earlier[1] + later[1])


def frontend(frame_in, norm_gain, in_proj, step_proj, inner_width):
    normal_rows, pullback = jax.vjp(lambda vector: normed(vector, norm_gain), frame_in)
    normal_bf = normal_rows.astype(jnp.bfloat16)
    projected = jnp.dot(normal_bf, in_proj, preferred_element_type=jnp.float32)
    step_raw = jnp.dot(normal_bf, step_proj, preferred_element_type=jnp.float32)
    xbc_rows = lax.optimization_barrier(projected[:, inner_width:].astype(jnp.bfloat16))
    return (normal_bf, pullback, projected[:, :inner_width], xbc_rows, step_raw)


def backend(pullback, d_gate, d_xbc, d_step, in_proj, step_proj):
    d_proj = jnp.concatenate([d_gate, d_xbc], axis=1).astype(jnp.bfloat16)
    d_normed = contract_cols(d_proj, in_proj) + contract_cols(
        d_step.astype(jnp.bfloat16), step_proj
    )
    (d_frame,) = pullback(d_normed)
    return (d_frame, d_proj)


def shards(
    sequence,
    upstream,
    norm_gain,
    in_proj,
    step_proj,
    conv_weight,
    conv_bias,
    step_bias,
    decay_log,
    skip_gain,
    out_proj,
):
    inner_width = out_proj.shape[0]
    count_rows = sequence.shape[0]
    margin = conv_weight.shape[0] - 1
    forward_in = sequence.astype(jnp.float32)
    mirror_in = forward_in[::-1, ::-1]
    upstream_rev = upstream[::-1, ::-1]
    normal_f, pullback_f, gate_f, xbc_f, raw_f = frontend(
        forward_in, norm_gain, in_proj, step_proj, inner_width
    )
    normal_r, pullback_r, gate_r, xbc_r, raw_r = frontend(
        mirror_in, norm_gain, in_proj, step_proj, inner_width
    )
    packed = jnp.concatenate([xbc_r[count_rows - margin :], xbc_f[count_rows - margin :]], axis=0)
    widened = padded(packed, (("seq", 0),), margin)
    lead_f = widened[:margin]
    lead_r = widened[3 * margin :]
    extended_f = jnp.concatenate([lead_f, xbc_f], axis=0).astype(jnp.float32)
    extended_r = jnp.concatenate([lead_r, xbc_r], axis=0).astype(jnp.float32)

    def local_core(extended, raw_rows):
        return prepare(
            extended, raw_rows, conv_weight, conv_bias, step_bias, decay_log, inner_width
        )

    def local_post(inner_vals, gate_rows, carried):
        return finish(inner_vals, gate_rows, carried, skip_gain)

    pre_f, pre_back_f = jax.vjp(local_core, extended_f, raw_f)
    inner_f, local_f, totals_f = pre_f
    empty = (jnp.zeros_like(totals_f), jnp.zeros_like(local_f))
    carried_f = prefix((totals_f, local_f), "seq", link_pair, empty, False)[1]
    gated_f, post_back_f = jax.vjp(local_post, inner_f, gate_f, carried_f)
    d_gated_f = contract_cols(upstream, out_proj).astype(jnp.bfloat16)
    d_inner_f, d_gate_f, d_carried_f = post_back_f(d_gated_f)
    pre_r, pre_back_r = jax.vjp(local_core, extended_r, raw_r)
    inner_r, local_r, totals_r = pre_r
    carried_r = prefix((totals_r, local_r), "seq", link_pair, empty, True)[1]
    reach_f = entering((totals_f, d_carried_f), "seq", link_pair, empty, True)[1]
    gated_r, post_back_r = jax.vjp(local_post, inner_r, gate_r, carried_r)
    d_gated_r = contract_cols(upstream_rev, out_proj).astype(jnp.bfloat16)
    d_inner_r, d_gate_r, d_carried_r = post_back_r(d_gated_r)
    reach_r = entering((totals_r, d_carried_r), "seq", link_pair, empty, False)[1]
    d_totals_f = jnp.exp(totals_f) * jnp.sum(carried_f * reach_f, axis=(1, 2))
    d_totals_r = jnp.exp(totals_r) * jnp.sum(carried_r * reach_r, axis=(1, 2))
    d_ext_f, d_raw_f = pre_back_f((d_inner_f, reach_f, d_totals_f))
    d_ext_r, d_raw_r = pre_back_r((d_inner_r, reach_r, d_totals_r))
    packed_grad = jnp.concatenate([d_ext_f[:margin], d_ext_r[:margin]], axis=0)
    returned = padded(packed_grad, (("seq", 0),), margin)
    d_xbc_f = jnp.concatenate(
        [d_ext_f[margin:count_rows], d_ext_f[count_rows:] + returned[3 * margin :]], axis=0
    )
    d_xbc_r = jnp.concatenate(
        [d_ext_r[margin:count_rows], d_ext_r[count_rows:] + returned[:margin]], axis=0
    )
    d_frame_f, d_proj_f = backend(pullback_f, d_gate_f, d_xbc_f, d_raw_f, in_proj, step_proj)
    d_frame_r, d_proj_r = backend(pullback_r, d_gate_r, d_xbc_r, d_raw_r, in_proj, step_proj)
    branch_f = jnp.dot(gated_f, out_proj, preferred_element_type=jnp.float32)
    branch_r = jnp.dot(gated_r, out_proj, preferred_element_type=jnp.float32)
    layer_out = (branch_f + branch_r[::-1, ::-1]).astype(jnp.bfloat16)
    grad_input = (d_frame_f + d_frame_r[::-1, ::-1]).astype(jnp.bfloat16)
    stacked_normal = jnp.concatenate([normal_f, normal_r], axis=0)
    stacked_proj = jnp.concatenate([d_proj_f, d_proj_r], axis=0)
    stacked_gated = jnp.concatenate([gated_f, gated_r], axis=0)
    stacked_up = jnp.concatenate([upstream, upstream_rev], axis=0)
    grad_in_proj = lax.psum_scatter(
        contract_rows(stacked_normal, stacked_proj), "seq", scatter_dimension=0, tiled=True
    )
    grad_out_proj = lax.psum_scatter(
        contract_rows(stacked_gated, stacked_up), "seq", scatter_dimension=0, tiled=True
    )
    return (layer_out, grad_input, grad_in_proj, grad_out_proj)


def solution(mesh):
    return jax.shard_map(
        shards,
        mesh=mesh,
        in_specs=(
            P(("batch", "seq"), None),
            P(("batch", "seq"), None),
            P(),
            P(),
            P(),
            P(),
            P(),
            P(),
            P(),
            P(),
            P(),
        ),
        out_specs=(
            P(("batch", "seq"), None),
            P(("batch", "seq"), None),
            P(("batch", "seq"), None),
            P(("batch", "seq"), None),
        ),
        check_vma=False,
    )
```

profile of v0, /device:TPU:6, one launch (start us, length us, event | category | flops | bytes accessed | tf_op | source)
XLA Modules:
  0.0 1461.8 jit_solution(4390449467375026554)
XLA Ops:
  12.1 3.5 collective-permute-start
  17.2 9.4 collective-permute-start.1
  31.8 2.2 convolution_convert_fusion.5
  40.1 2.3 convolution_convert_fusion.4
  43.3 172.1 %all-gather.4 = bf16[64,1,16]{2,1,0:T(2,128)(2,1)S(1)} all-gather(bf16[1,1,16]{2,1,0:T(2,128)(2,1)S(1)} %bitcast.268), channel_id=1, replica_groups=mesh['seq'=64,'batch'=4] {'seq'}, dimensions={0}, use_global_device_ids=true | all-gather | bytes 2080 | tf_op jit(solution)/shard_map/all_gather | solution.py:27
  217.9 87.4 %while.52 = (s32[]{:T(128)}, f32[16,64,128]{2,1,0:T(8,128)S(1)}, s32[]{:T(128)}, bf16[64,16]{1,0:T(8,128)(2,1)}, bf16[64,16,64,128]{3,2,1,0:T(8,128)(2,1)}, /*index=5*/s32[]{:T(128)}, s32[]{:T(128)}, s32[]{:T(128)}) while((s32[]{:T(128)}, f32[16,64,128]{2,1,0:T(8,128)S(1)}, s32[]{:T(128)}, bf16[64,16]{1,0:T(8,128)(2,1)}, ...), condition=%wide.region_3.5_spmd, body=%wide.region_2.4_spmd.sunk | while | flops 393237 | bytes 1311015 | solution.py:42
  306.9 4.1 fusion.5
  312.2 2.9 fusion.69
  316.4 2.2 convolution_convert_fusion.2
  318.7 2.9 rev.14
  322.4 187.5 %all-gather.5 = bf16[64,1,16]{2,1,0:T(2,128)(2,1)S(1)} all-gather(bf16[1,1,16]{2,1,0:T(2,128)(2,1)S(1)} %bitcast.269), channel_id=1, replica_groups=mesh['seq'=64,'batch'=4] {'seq'}, dimensions={0}, use_global_device_ids=true | all-gather | bytes 2080 | tf_op jit(solution)/shard_map/all_gather | solution.py:27
  511.8 17.6 %while.53 = (s32[]{:T(128)}, f32[16,64,128]{2,1,0:T(8,128)S(1)}, s32[]{:T(128)}, bf16[64,16]{1,0:T(8,128)(2,1)S(1)}, bf16[64,16,64,128]{3,2,1,0:T(8,128)(2,1)}, ...) while((s32[]{:T(128)}, f32[16,64,128]{2,1,0:T(8,128)S(1)}, s32[]{:T(128)}, bf16[64,16]{1,0:T(8,128)(2,1)S(1)}, ...), condition=%wide.region_7.9_spmd, body=%wide.region_6.8_spmd.sunk | while | flops 393238 | bytes 1311035 | solution.py:42
  532.2 4.4 fusion.3
  538.7 3.0 fusion.72
  541.7 2.1 copy.168
  543.8 2.3 convolution_convert_fusion
  546.3 2.7 convolution_bitcast_fusion.11
  549.0 2.7 convolution_bitcast_fusion.9
  551.7 2.7 fusion.73
  554.3 3.0 convolution_bitcast_fusion
  558.3 4.1 multiply_reduce_fusion.1
  565.6 41.2 %while.54 = (s32[]{:T(128)}, f32[16,64,128]{2,1,0:T(8,128)}, s32[]{:T(128)}, bf16[64,16]{1,0:T(8,128)(2,1)}, bf16[64,16,64,128]{3,2,1,0:T(8,128)(2,1)}, /*index=5*/s32[]{:T(128)}, s32[]{:T(128)}, s32[]{:T(128)}, s32[]{:T(128)}) while((s32[]{:T(128)}, f32[16,64,128]{2,1,0:T(8,128)}, s32[]{:T(128)}, bf16[64,16]{1,0:T(8,128)(2,1)}, ...), condition=%wide.region_9.11_spmd, body=%wide.region_8.10_spmd.sunk | while | flops 393238 | bytes 1311035 | solution.py:67
  608.5 4.3 multiply_reduce_fusion.4
  612.8 187.9 %all-gather.17.cloned.1.call-done = bf16[1024,64,128]{2,1,0:T(8,128)(2,1)} async-done(((bf16[16,64,128]{2,1,0:T(8,128)(2,1)}), bf16[1024,64,128]{2,1,0:T(8,128)(2,1)}) %all-gather.17.cloned.1.call-update) | async-done | bytes 16777232 | tf_op jit(solution)/shard_map/all_gather | solution.py:50
  801.6 131.3 %while.55 = (s32[]{:T(128)}, f32[16,64,128]{2,1,0:T(8,128)}, s32[]{:T(128)}, bf16[64,16]{1,0:T(8,128)(2,1)}, bf16[64,16,64,128]{3,2,1,0:T(8,128)(2,1)}, /*index=5*/s32[]{:T(128)}, s32[]{:T(128)}, s32[]{:T(128)}) while((s32[]{:T(128)}, f32[16,64,128]{2,1,0:T(8,128)}, s32[]{:T(128)}, bf16[64,16]{1,0:T(8,128)(2,1)}, ...), condition=%wide.region_18.20_spmd, body=%wide.region_17.19_spmd.sunk | while | flops 393237 | bytes 1311015 | solution.py:67
  802.3 2.1 convert_add_fusion.11
  807.7 2.1 convert_add_fusion.11
  810.5 2.1 convert_add_fusion.11
  816.0 2.1 convert_add_fusion.11
  818.7 2.1 convert_add_fusion.11
  824.2 2.1 convert_add_fusion.11
  826.9 2.1 convert_add_fusion.11
  829.6 2.1 convert_add_fusion.11
  832.4 2.1 convert_add_fusion.11
  835.1 2.1 convert_add_fusion.11
  837.8 2.1 convert_add_fusion.11
  840.5 2.1 convert_add_fusion.11
  846.0 2.1 convert_add_fusion.11
  848.8 2.1 convert_add_fusion.11
  851.5 2.1 convert_add_fusion.11
  859.7 2.1 convert_add_fusion.11
  870.7 2.1 convert_add_fusion.11
  878.9 2.1 convert_add_fusion.11
  881.6 2.1 convert_add_fusion.11
  889.8 2.1 convert_add_fusion.11
  892.5 2.1 convert_add_fusion.11
  900.7 2.1 convert_add_fusion.11
  903.4 2.1 convert_add_fusion.11
  911.6 2.1 convert_add_fusion.11
  914.4 2.1 convert_add_fusion.11
  922.6 2.1 convert_add_fusion.11
  925.3 2.1 convert_add_fusion.11
  934.5 4.3 multiply_reduce_fusion.2
  940.9 2.1 copy.170
  943.0 2.4 convolution_bitcast_fusion.10
  945.4 2.2 convolution_bitcast_fusion.8
  951.1 20.5 %collective-permute-start.2 = (f32[3,1280]{1,0:T(4,128)S(1)}, f32[3,1280]{1,0:T(4,128)S(1)}, u32[]{:S(2)}, u32[]{:S(2)}) collective-permute-start(f32[3,1280]{1,0:T(4,128)S(1)} %pad_add_fusion.3), channel_id=1, source_target_pairs={{4,0},{8,4},{12,8},{16,12},{20,16},{24,20},{28,24},{32,28},{36,32}... | collective-permute-start | bytes 46088 | tf_op jit(solution)/shard_map/ppermute | solution.py:17
  972.2 2.1 collective-permute-start.3
  974.5 8.5 collective-permute-done.3
  983.1 3.0 fusion.8
  986.1 2.3 fusion.219
  988.4 3.2 rev.13
  1013.0 151.2 %reduce-scatter.5.cloned.1.call-done = f32[16,512]{1,0:T(8,128)} async-done(((f32[1024,512]{1,0:T(8,128)}), f32[16,512]{1,0:T(8,128)}) %reduce-scatter.5.cloned.1.call-update) | async-done | bytes 32784 | tf_op jit(solution)/shard_map/reduce_scatter | solution.py:228
  1164.2 290.5 %reduce-scatter.3.cloned.1.call-done = f32[8,2304]{1,0:T(8,128)} async-done(((f32[512,2304]{1,0:T(8,128)}), f32[8,2304]{1,0:T(8,128)}) %reduce-scatter.3.cloned.1.call-update) | async-done | bytes 73744 | tf_op jit(solution)/shard_map/reduce_scatter | solution.py:225
  (517 shorter events, 287.3 us)
Async XLA Ops:
  7.2 4.3 copy-start
  7.2 210.7 %all-gather.11.cloned.1.call-start = ((), (), s32[]{:S(2)}) async-start(), calls=%async_computation.4 | async-start | bytes 17039360 | tf_op jit(solution)/shard_map/all_gather | solution.py:27
  11.4 4.7 copy-start.25
  11.4 15.2 %copy-start.23 = (bf16[128,512]{1,0:T(8,128)(2,1)}, bf16[128,512]{1,0:T(8,128)(2,1)S(1)}, u32[]{:S(2)}) copy-start(bf16[128,512]{1,0:T(8,128)(2,1)S(1)} %get-tuple-element.445) | copy-start | bytes 393220
  11.9 14.6 copy-start.84
  11.9 14.6 %copy-start.54 = (bf16[512,16]{0,1:T(8,128)(2,1)S(1)}, bf16[512,16]{0,1:T(8,128)(2,1)}, u32[]{:S(2)}) copy-start(bf16[512,16]{0,1:T(8,128)(2,1)} %param.24) | copy-start | bytes 49156
  12.0 14.6 %copy-start.85 = (f32[16]{0:T(128)S(1)}, f32[16]{0:T(128)}, u32[]{:S(2)}) copy-start(f32[16]{0:T(128)} %param.27) | copy-start | bytes 196
  12.1 16.5 %collective-permute-start = (bf16[3,1280]{1,0:T(4,128)(2,1)S(1)}, bf16[3,1280]{1,0:T(4,128)(2,1)S(1)}, u32[]{:S(2)}, u32[]{:S(2)}) collective-permute-start(bf16[3,1280]{1,0:T(4,128)(2,1)S(1)} %slice.137), channel_id=1, source_target_pairs={{0,4},{4,8},{8,12},{12,16},{16,20},{20,24},{24,28},{28,32},{32,36}... | collective-permute-start | bytes 23048 | tf_op jit(solution)/shard_map/ppermute | solution.py:14
  15.6 12.9 copy-start.61
  17.1 11.7 copy-start.68
  17.2 11.5 collective-permute-start.1
  26.6 7.5 copy-start.81
  27.4 4.5 copy-start.56
  31.8 275.0 %copy-start.6 = (f32[128,1024]{0,1:T(8,128)}, f32[128,1024]{0,1:T(8,128)S(1)}, u32[]{:S(2)}) copy-start(f32[128,1024]{0,1:T(8,128)S(1)} %copy.142) | copy-start | bytes 1572868
  34.1 477.6 %all-gather.13.cloned.1.call-start = ((), (), s32[]{:S(2)}) async-start(), calls=%async_computation.5 | async-start | bytes 17039360 | tf_op jit(solution)/shard_map/all_gather | solution.py:27
  40.1 177.8 %copy-start.2 = (f32[128,1024]{0,1:T(8,128)}, f32[128,1024]{0,1:T(8,128)S(1)}, u32[]{:S(2)}) copy-start(f32[128,1024]{0,1:T(8,128)S(1)} %copy.152) | copy-start | bytes 1572868
  42.4 522.3 %all-gather.15.cloned.1.call-start = ((), (), s32[]{:S(2)}) async-start(), calls=%async_computation.6 | async-start | bytes 17039360 | tf_op jit(solution)/shard_map/all_gather | solution.py:50
  217.8 89.0 %copy-start.32 = (f32[128,128]{1,0:T(8,128)}, f32[128,128]{1,0:T(8,128)S(1)}, u32[]{:S(2)}) copy-start(f32[128,128]{1,0:T(8,128)S(1)} %fusion.167) | copy-start | bytes 196612
  306.8 4.1 copy-start.16
  312.2 4.2 copy-start.45
  316.4 195.3 %copy-start.3 = (f32[128,1024]{0,1:T(8,128)}, f32[128,1024]{0,1:T(8,128)S(1)}, u32[]{:S(2)}) copy-start(f32[128,1024]{0,1:T(8,128)S(1)} %copy.160) | copy-start | bytes 1572868
  318.6 482.1 %all-gather.17.cloned.1.call-start = ((), (), s32[]{:S(2)}) async-start(), calls=%async_computation.7 | async-start | bytes 17039360 | tf_op jit(solution)/shard_map/all_gather | solution.py:50
  530.0 8.7 copy-start.28
  541.7 9.9 copy-start.27
  546.2 618.0 %reduce-scatter.5.cloned.1.call-start = ((), (), s32[]{:S(2)}) async-start(), calls=%async_computation.3 | async-start | bytes 2129920 | tf_op jit(solution)/shard_map/reduce_scatter | solution.py:228
  546.2 5.4 copy-start.21
  546.3 5.4 copy-start.22
  557.4 5.1 copy-start.35
  557.4 6.2 copy-start.36
  564.7 890.1 %reduce-scatter.3.cloned.1.call-start = ((), (), s32[]{:S(2)}) async-start(), calls=%async_computation.2 | async-start | bytes 4792320 | tf_op jit(solution)/shard_map/reduce_scatter | solution.py:225
  942.9 5.8 copy-start.38
  942.9 7.0 copy-start.12
  942.9 7.0 copy-start.13
  942.9 7.0 copy-start.14
  942.9 7.0 copy-start.15
  942.9 7.0 copy-start.53
  951.1 23.4 %collective-permute-start.2 = (f32[3,1280]{1,0:T(4,128)S(1)}, f32[3,1280]{1,0:T(4,128)S(1)}, u32[]{:S(2)}, u32[]{:S(2)}) collective-permute-start(f32[3,1280]{1,0:T(4,128)S(1)} %pad_add_fusion.3), channel_id=1, source_target_pairs={{4,0},{8,4},{12,8},{16,12},{20,16},{24,20},{28,24},{32,28},{36,32}... | collective-permute-start | bytes 46088 | tf_op jit(solution)/shard_map/ppermute | solution.py:17
  972.2 10.8 copy-start.29
  972.2 10.8 collective-permute-start.3
  974.4 8.7 copy-start.31
  974.4 8.7 copy-start.24
  974.4 8.7 copy-start.26
  974.4 8.7 copy-start.86
  974.4 8.7 copy-start.87
  974.5 11.6 copy-start.65
  988.4 9.1 copy-start.33
  988.4 9.1 copy-start.34
  991.6 6.0 copy-start.10
  991.6 6.0 copy-start.20
  991.6 6.0 copy-start.42
  991.6 6.0 copy-start.43
  991.6 6.0 copy-start.44
  993.6 6.0 copy-start.1
  999.6 5.8 copy-start.41
  999.6 5.8 copy-start.57
  999.6 5.9 copy-start.58
  999.6 5.9 copy-start.59
  999.6 5.9 copy-start.60
  1002.1 6.8 copy-start.5
  1002.1 6.8 copy-start.55
  1002.1 6.8 copy-start.62
  1002.1 6.8 copy-start.70
  1002.1 6.8 copy-start.72
  1002.1 6.8 copy-start.82
  (34 other events, 72.6 us)
Sparse Core Ops, SparseCore 0:
  34.2 154.9 all-gather.10
  192.5 167.2 all-gather.12
  363.2 168.4 all-gather.14
  546.3 254.3 all-gather.16
  803.6 360.5 reduce-scatter.4
  1170.3 284.4 reduce-scatter.2
where the time goes:
time: 1480 us; the launch traced here: 1460 us
  waiting for transfers between devices  638 us (43%)
  blocking collectives  360 us (24%)
  other arithmetic  296 us (20%)
  matrix products  80.7 us (5%)
  starting transfers between devices  35.7 us (2%)
  local copies, waits for them, and re-layouts  32.8 us (2%)
  between operations  15.8 us (1%)
    all_gather x2, blocking collectives, prefix(): lax.all_gather(a.astype(kind), axis)  360 us
    reduce_scatter x1, waiting for transfers between devices, shards(): lax.psum_scatter(contract_rows(stacked_normal, stacked_proj), 'seq', scat...  291 us
    add x126, other arithmetic, link_pair(): jnp.exp(later[0])[:, None, None] * earlier[1] + later[1]  199 us
    all_gather x2, waiting for transfers between devices, entering(): lax.all_gather(a.astype(kind), axis)  188 us
    reduce_scatter x1, waiting for transfers between devices, shards(): lax.psum_scatter(contract_rows(stacked_gated, stacked_up), 'seq', scatter...  151 us
    exp x126, other arithmetic, link_pair(): jnp.exp(later[0])[:, None, None] * earlier[1] + later[1]  75.8 us
    ppermute x2, starting transfers between devices, padded(): lax.ppermute(lax.slice_in_dim(block, 0, width, axis=dim), axis, backward)  29.9 us
  transfers between devices with their start and end apart: 10, of which 4 were waited for; matrix products, arithmetic and copies ran while one was open for 27% of the time, Pallas kernels for 0%

commit v1 on v0

v1 whole, which is shorter than its diff:
```python
import functools

import jax
import jax.numpy as jnp
from jax import lax
from jax.experimental import pallas as pl
from jax.experimental.pallas import tpu as pltpu
from jax.sharding import PartitionSpec as P

epsilon = 1e-06
SIDE = 4
COUNT = SIDE**3
f32 = jnp.float32
bf16 = jnp.bfloat16
INTERPRET = False


def call(body, outs, args, scratch=(), scalars=0, flops=10**9, vmem=40 * 2**20):
    specs = [pl.BlockSpec(memory_space=pltpu.SMEM)] * scalars
    specs += [pl.BlockSpec(memory_space=pltpu.VMEM)] * (len(args) - scalars)
    moved = sum(a.size * a.dtype.itemsize for a in args)
    return pl.pallas_call(
        body,
        out_shape=[jax.ShapeDtypeStruct(shape, kind) for shape, kind in outs],
        in_specs=specs,
        out_specs=[pl.BlockSpec(memory_space=pltpu.VMEM)] * len(outs),
        scratch_shapes=list(scratch),
        compiler_params=pltpu.CompilerParams(vmem_limit_bytes=vmem),
        cost_estimate=pl.CostEstimate(flops=flops, bytes_accessed=moved, transcendentals=0),
        interpret=INTERPRET,
    )(*args)


def mm(left, right):
    return lax.dot_general(left, right, (((1,), (0,)), ((), ())), preferred_element_type=f32)


def mm_cols(left, right):
    return lax.dot_general(left, right, (((1,), (1,)), ((), ())), preferred_element_type=f32)


def mm_rows(left, right):
    return lax.dot_general(left, right, (((0,), (0,)), ((), ())), preferred_element_type=f32)


def iota(shape, dim):
    return lax.broadcasted_iota(jnp.int32, shape, dim)


def ones_where(mask):
    return jnp.where(mask, 1.0, 0.0).astype(bf16)


def anti(size):
    return ones_where(iota((size, size), 0) + iota((size, size), 1) == size - 1)


def pieces_of(value, count):
    found = []
    for _ in range(count):
        piece = value.astype(bf16)
        found.append(piece)
        value = value - piece.astype(f32)
    return found


def mirror_exact(block):
    turned = mm(block, anti(block.shape[1])).astype(bf16)
    return mm(anti(block.shape[0]), turned).astype(bf16)


def mirror_wide(block):
    high, low = pieces_of(block, 2)
    return mirror_exact(high).astype(f32) + mirror_exact(low).astype(f32)


def head_mask(heads, width):
    lanes = heads * width
    return ones_where(iota((heads, lanes), 0) == iota((heads, lanes), 1) // width)


def expand(value, mask):
    found = pieces_of(value, 3)
    return mm(jnp.concatenate(found, axis=1), jnp.concatenate([mask] * 3, axis=0))


def fold(value, mask):
    total = None
    for piece in pieces_of(value, 3):
        part = mm_cols(piece, mask)
        total = part if total is None else total + part
    return total


def triangle(size, low):
    rows, cols = iota((size, size), 0), iota((size, size), 1)
    return rows >= cols if low else rows <= cols


def tri_sum(mask, value):
    total = None
    for piece in pieces_of(value, 3):
        part = mm(ones_where(mask), piece)
        total = part if total is None else total + part
    return total


def tri_sum_turned(mask, value):
    total = None
    for piece in pieces_of(value, 3):
        part = mm_rows(piece, ones_where(mask))
        total = part if total is None else total + part
    return total


def softplus(value):
    return jnp.maximum(value, 0.0) + jnp.log1p(jnp.exp(-jnp.abs(value)))


def sigmoid(value):
    return 1.0 / (1.0 + jnp.exp(-value))


def norm_rows(block, gain):
    wide = block.astype(f32)
    scale = lax.rsqrt(jnp.mean(wide * wide, axis=-1, keepdims=True) + epsilon)
    return (wide * scale * gain).astype(bf16)


def pre_kernel(
    seq, up, low, high, gain, in_proj, step_proj, conv_w, conv_b, step_bias, decay_log, out_proj,
    payload, both, normal, cot, gate, conv, d_gated, raw, step, cumul, cumul_t,
    ext,
):
    rows = seq.shape[0]
    inner = out_proj.shape[0]
    heads = step_bias.shape[1]
    state = (conv_w.shape[1] - inner) // 2
    taps = conv_w.shape[0]
    both[:rows, :] = seq[...]
    both[rows:, :] = mirror_exact(seq[...])
    cot[:rows, :] = up[...]
    cot[rows:, :] = mirror_exact(up[...])
    halo = jnp.concatenate([low[...], mirror_exact(high[...])], axis=0)
    normal[...] = norm_rows(both[...], gain[...])
    normal_halo = norm_rows(halo, gain[...])
    gate[...] = mm(normal[...], in_proj[:, :inner])
    xbc = mm(normal[...], in_proj[:, inner:]).astype(bf16).astype(f32)
    xbc_halo = mm(normal_halo, in_proj[:, inner:]).astype(bf16).astype(f32)
    raw[...] = mm(normal[...], step_proj[...])
    d_gated[...] = mm_cols(cot[...], out_proj[...]).astype(bf16)
    margin = low.shape[0]
    mask = head_mask(heads, inner // heads)
    ends = []
    for frame in range(2):
        at = slice(frame * rows, (frame + 1) * rows)
        ext[:8, :] = xbc_halo[(frame + 1) * margin - 8 : (frame + 1) * margin, :]
        ext[8:, :] = xbc[at, :]
        found = conv_b[...]
        for tap in range(taps):
            start = 9 - taps + tap
            found = found + ext[start : start + rows, :] * conv_w[tap : tap + 1, :]
        conv[at, :] = found
        act = found * sigmoid(found)
        size = softplus(raw[at, :] + step_bias[...])
        decay = -jnp.exp(decay_log[...]) * size
        upto = tri_sum(triangle(rows, True), decay)
        step[at, :] = size
        cumul[at, :] = upto
        cumul_t[frame * heads : (frame + 1) * heads, :] = tri_sum_turned(triangle(rows, False), decay)
        end = upto[rows - 1 : rows, :]
        ends.append(end)
        spread = expand(jnp.concatenate([size * jnp.exp(end - upto), jnp.exp(upto)], axis=0), mask)
        driven = (act[:, :inner] * spread[:rows]).astype(bf16)
        local = mm_rows(driven, act[:, inner : inner + state].astype(bf16))
        wide = gate[at, :]
        d_mixed = d_gated[at, :].astype(f32) * (wide * sigmoid(wide))
        back = mm_rows((d_mixed * spread[rows:]).astype(bf16), act[:, inner + state :].astype(bf16))
        for place, block in ((frame, local), (2 + frame, back)):
            payload[:, 16 * place : 16 * place + 16, :] = block.reshape(COUNT, 16, state).astype(bf16)
    chunk_head = iota((COUNT, heads), 0) // (COUNT // heads)
    chosen = chunk_head == iota((COUNT, heads), 1)
    lanes = iota((COUNT, state), 1)
    packed = jnp.zeros((COUNT, state), f32)
    for frame in range(2):
        column = jnp.sum(jnp.where(chosen, ends[frame], 0.0), axis=1, keepdims=True)
        for nth, piece in enumerate(pieces_of(column, 3)):
            packed = jnp.where(lanes == 3 * frame + nth, piece.astype(f32), packed)
    tail = jnp.broadcast_to(packed.reshape(COUNT, 1, state), (COUNT, 8, state))
    payload[:, 64:, :] = tail.astype(bf16)


def scan_kernel(got, out, wide, done):
    count, rows, state = got.shape
    wide[...] = got[...].astype(f32).reshape(count * rows, state)
    tails = wide[pl.ds(64, count, stride=rows), :]
    above = iota((count, count), 0)
    beside = iota((count, count), 1)
    after = ones_where(above > beside)
    weights = []
    for frame in range(2):
        at = 3 * frame
        column = (tails[:, at + 2 : at + 3] + tails[:, at + 1 : at + 2]) + tails[:, at : at + 1]
        column = jnp.maximum(column, -110.0)
        line = jnp.sum(jnp.where(above == beside, column, 0.0), axis=0, keepdims=True)
        between = None
        for piece in pieces_of(jnp.where(beside < above, line, 0.0), 3):
            part = mm(piece, after)
            between = part if between is None else between + part
        found = jnp.where(above > beside, jnp.exp(between), 0.0)
        weights.append(pieces_of(found, 2))
    for place, (frame, turned) in enumerate(((0, False), (1, True), (0, True), (1, False))):
        pair = weights[frame]
        block = jnp.concatenate(
            [wide[pl.ds(16 * place + row, count, stride=rows), :] for row in range(16)], axis=1
        ).astype(bf16)
        if turned:
            mixed = mm_rows(jnp.concatenate(pair, axis=1), block)
        else:
            mixed = mm(jnp.concatenate(pair, axis=0), block)
        mixed = mixed[:count] + mixed[count:]
        for row in range(16):
            done[pl.ds(16 * place + row, count, stride=64), :] = mixed[:, state * row : state * (row + 1)]
    out[...] = done[...].reshape(count, 64, state).astype(bf16)


def intra_kernel(conv, gate, d_gated, step, cumul, cumul_t, mixed, d_driven, d_bc, d_cumul):
    rows = conv.shape[0] // 2
    inner = gate.shape[1]
    heads = step.shape[1]
    state = (conv.shape[1] - inner) // 2
    mask = head_mask(heads, inner // heads)
    lower = triangle(rows, True)
    first = iota((rows, 2 * inner // heads), 1) < inner // heads
    wide_pair = 2 * inner // heads
    for frame in range(2):
        at = slice(frame * rows, (frame + 1) * rows)
        found = conv[at, :]
        act = found * sigmoid(found)
        bmat = act[:, inner : inner + state].astype(bf16)
        cmat = act[:, inner + state :].astype(bf16)
        driven = act[:, :inner] * expand(step[at, :], mask)
        wide = gate[at, :]
        d_mixed = d_gated[at, :].astype(f32) * (wide * sigmoid(wide))
        scores = mm_cols(cmat, bmat)
        upto, line = cumul[at, :], cumul_t[frame * heads : (frame + 1) * heads, :]
        d_scores = jnp.zeros((rows, rows), f32)
        sums = []
        for pair in range(heads // 2):
            lanes = slice(pair * wide_pair, (pair + 1) * wide_pair)
            decays = []
            for head in (2 * pair, 2 * pair + 1):
                differ = upto[:, head : head + 1] - line[head : head + 1, :]
                decays.append(jnp.exp(jnp.where(lower, differ, -1e30)))
            weights = [(decay * scores).astype(bf16) for decay in decays]
            drive, d_mix = driven[:, lanes], d_mixed[:, lanes]
            drive_bf, d_mix_bf = drive.astype(bf16), d_mix.astype(bf16)
            drive_two = jnp.concatenate(
                [jnp.where(first, drive, 0.0), jnp.where(first, 0.0, drive)], axis=0
            ).astype(bf16)
            d_mix_two = jnp.concatenate(
                [jnp.where(first, d_mix, 0.0), jnp.where(first, 0.0, d_mix)], axis=0
            ).astype(bf16)
            mix = mm(jnp.concatenate(weights, axis=1), drive_two)
            d_weights = mm_cols(d_mix_two, drive_bf)
            d_drive = mm_rows(jnp.concatenate(weights, axis=0), d_mix_two)
            d_scores = d_scores + decays[0] * d_weights[:rows] + decays[1] * d_weights[rows:]
            mixed[at, lanes] = mix
            d_driven[at, lanes] = d_drive
            sums.append(d_mix_bf.astype(f32) * mix - drive_bf.astype(f32) * d_drive)
        d_scores = d_scores.astype(bf16)
        d_bc[at, :state] = mm_rows(d_scores, cmat)
        d_bc[at, state:] = mm(d_scores, bmat)
        d_cumul[at, :] = fold(jnp.concatenate(sums, axis=1), mask)


def post_kernel(
    got, conv, gate, d_gated, raw, step, cumul, mixed, d_driven, d_bc, d_cumul, step_bias, decay_log, skip_gain,
    gated, d_gate, d_conv, d_step,
):
    rows = conv.shape[0] // 2
    inner = gate.shape[1]
    heads = step.shape[1]
    state = (conv.shape[1] - inner) // 2
    mask = head_mask(heads, inner // heads)
    skip = expand(jnp.broadcast_to(skip_gain[...], (8, heads)), mask)[:1]
    for frame in range(2):
        at = slice(frame * rows, (frame + 1) * rows)
        found = conv[at, :]
        share = sigmoid(found)
        act = found * share
        inputs = act[:, :inner]
        bmat = act[:, inner : inner + state].astype(bf16)
        cmat = act[:, inner + state :].astype(bf16)
        upto = cumul[at, :]
        end = upto[rows - 1 : rows, :]
        spread = expand(jnp.concatenate([step[at, :], jnp.exp(upto), jnp.exp(end - upto)], axis=0), mask)
        sizes, grown, left = spread[:rows], spread[rows : 2 * rows], spread[2 * rows :]
        carried = got[:, 16 * frame : 16 * frame + 16, :].reshape(inner, state)
        reach = got[:, 32 + 16 * frame : 48 + 16 * frame, :].reshape(inner, state)
        inter = grown * mm_cols(cmat, carried)
        whole = mixed[at, :] + inter + skip * inputs
        wide = gate[at, :]
        opened = sigmoid(wide)
        silu = wide * opened
        gated[at, :] = (whole * silu).astype(bf16)
        d_out = d_gated[at, :].astype(f32)
        d_gate[at, :] = (d_out * whole * (opened * (1.0 + wide * (1.0 - opened)))).astype(bf16)
        d_mixed = d_out * silu
        d_cmat = d_bc[at, state:] + mm((d_mixed * grown).astype(bf16), carried)
        answer = left * mm_cols(bmat, reach)
        driven = inputs * sizes
        d_drive = d_driven[at, :] + answer
        d_bmat = d_bc[at, :state] + mm((left * driven).astype(bf16), reach)
        products = carried.astype(f32) * reach.astype(f32)
        met = None
        for piece in pieces_of(products, 3):
            part = mm_cols(jnp.ones((8, state), bf16), piece)
            met = part if met is None else met + part
        folded = fold(jnp.concatenate([driven * answer, d_mixed * inter, d_drive * inputs, met], axis=0), mask)
        held, entered, by_size = folded[:rows], folded[rows : 2 * rows], folded[2 * rows : 3 * rows]
        d_end = jnp.exp(end) * folded[3 * rows : 3 * rows + 1] + jnp.sum(held, axis=0, keepdims=True)
        d_decay = tri_sum(triangle(rows, False), d_cumul[at, :] + entered - held) + d_end
        d_size = by_size - jnp.exp(decay_log[...]) * d_decay
        d_step[at, :] = (d_size * sigmoid(raw[at, :] + step_bias[...])).astype(bf16)
        d_act = jnp.concatenate([skip * d_mixed + d_drive * sizes, d_bmat, d_cmat], axis=1)
        d_conv[at, :] = d_act * (share * (1.0 + found * (1.0 - share)))


def out_term_kernel(place, gated, cot, normal, d_gate, *refs):
    by_x, by_y, whole, parted = refs[:4], refs[4:8], refs[8], refs[9]
    columns = cot.shape[1]
    whole[...] = mm_rows(gated[...], cot[...])
    parted[...] = mm_rows(normal[...], d_gate[...]).reshape(parted.shape)
    chunk = whole.shape[0] // SIDE
    for step in range(SIDE):
        to_x = lax.rem(place[0] + step, SIDE)
        to_y = lax.rem(place[2] + step, SIDE)
        block = whole[pl.ds(pl.multiple_of(to_x * chunk, chunk), chunk), :].reshape(-1, 2, 8, columns)
        block = jnp.concatenate(
            [block[:, 0].reshape(-1, columns), block[:, 1].reshape(-1, columns)], axis=1
        )
        by_x[step][...] = block.astype(by_x[step].dtype)
        by_y[step][...] = parted[:, to_y].reshape(by_y[step].shape).astype(by_y[step].dtype)


def in_term_kernel(place, d_conv, ahead, behind, conv_w, normal, *refs):
    d_xbc, by_x, by_y, ext, whole, parted = refs[0], refs[1:5], refs[5:9], refs[9], refs[10], refs[11]
    rows = d_conv.shape[0] // 2
    taps = conv_w.shape[0]
    for frame, halo in enumerate((ahead, behind)):
        at = slice(frame * rows, (frame + 1) * rows)
        ext[:rows, :] = d_conv[at, :]
        ext[rows:, :] = halo[...]
        total = None
        for tap in range(taps):
            start = taps - 1 - tap
            part = ext[start : start + rows, :] * conv_w[tap : tap + 1, :]
            total = part if total is None else total + part
        d_xbc[at, :] = total.astype(bf16)
    half = whole.shape[1]
    whole[...] = mm_rows(normal[...], d_xbc[:, :half])
    parted[...] = mm_rows(normal[...], d_xbc[:, half:]).reshape(parted.shape)
    chunk = whole.shape[0] // SIDE
    for step in range(SIDE):
        to_x = lax.rem(place[0] + step, SIDE)
        to_y = lax.rem(place[2] + step, SIDE)
        block = whole[pl.ds(pl.multiple_of(to_x * chunk, chunk), chunk), :]
        by_x[step][...] = block.astype(by_x[step].dtype)
        by_y[step][...] = parted[:, to_y].reshape(by_y[step].shape).astype(by_y[step].dtype)


def result_kernel(both, gain, gated, out_proj, d_gate, d_xbc, d_step, in_proj, step_proj, layer, grad):
    rows = both.shape[0] // 2
    inner = out_proj.shape[0]
    branch = mm(gated[...], out_proj[...])
    layer[...] = (branch[:rows] + mirror_wide(branch[rows:])).astype(bf16)
    d_normal = mm_cols(d_gate[...], in_proj[:, :inner]) + mm_cols(d_xbc[...], in_proj[:, inner:])
    d_normal = d_normal + mm_cols(d_step[...], step_proj[...])
    wide = both[...].astype(f32)
    scale = lax.rsqrt(jnp.mean(wide * wide, axis=-1, keepdims=True) + epsilon)
    d_scaled = d_normal * gain[...]
    along = jnp.mean(d_scaled * wide, axis=-1, keepdims=True)
    d_wide = scale * d_scaled - wide * (scale * scale * scale * along)
    grad[...] = (d_wide[:rows] + mirror_wide(d_wide[rows:])).astype(bf16)


def total_of(refs):
    total = refs[0][...]
    for ref in refs[1:]:
        total = total + ref[...].astype(f32)
    return total


def first_sum_kernel(place, *refs):
    out_x, in_x, gate_y, in_y = refs[:4], refs[4:8], refs[8:12], refs[12:16]
    by_y, by_x, parted, whole = refs[16:20], refs[20:24], refs[24], refs[25]
    parted[...] = jnp.concatenate([total_of(out_x), total_of(in_x)], axis=1).reshape(parted.shape)
    whole[...] = jnp.concatenate([total_of(gate_y), total_of(in_y)], axis=1)
    chunk = whole.shape[0] // SIDE
    for step in range(SIDE):
        to_x = lax.rem(place[0] + step, SIDE)
        to_y = lax.rem(place[2] + step, SIDE)
        by_y[step][...] = parted[:, to_y].reshape(by_y[step].shape).astype(by_y[step].dtype)
        block = whole[pl.ds(pl.multiple_of(to_x * chunk, chunk), chunk), :]
        by_x[step][...] = block.astype(by_x[step].dtype)


def second_sum_kernel(place, *refs):
    first, second, by_z, keep = refs[:4], refs[4:8], refs[8:12], refs[12]
    keep[:, 0] = total_of(first).reshape(SIDE, 8, -1)
    keep[:, 1] = total_of(second).reshape(SIDE, 8, -1)
    for step in range(SIDE):
        to_z = lax.rem(place[1] + step, SIDE)
        by_z[step][...] = keep[to_z].reshape(by_z[step].shape).astype(by_z[step].dtype)


def last_sum_kernel(*refs):
    parts, grad_in, grad_out = refs[:4], refs[4], refs[5]
    total = total_of(parts)
    columns = grad_out.shape[1]
    grad_out[:8, :] = total[:8, :columns]
    grad_out[8:, :] = total[:8, columns : 2 * columns]
    grad_in[...] = jnp.concatenate([total[8:, : 2 * columns], total[:8, 2 * columns :], total[8:, 2 * columns :]], axis=1)


def axis_pairs(stride, step):
    pairs = []
    for source in range(COUNT):
        digit = source // stride % SIDE
        pairs.append((source, source + ((digit + step) % SIDE - digit) * stride))
    return pairs


def exchange(parts, stride):
    return [parts[0]] + [
        lax.ppermute(parts[step], "seq", axis_pairs(stride, step)) for step in range(1, SIDE)
    ]


def slots(rows, columns):
    return [((rows, columns), f32)] + [((rows, columns), bf16)] * (SIDE - 1)


def shards(
    sequence,
    upstream,
    norm_gain,
    in_proj,
    step_proj,
    conv_weight,
    conv_bias,
    step_bias,
    decay_log,
    skip_gain,
    out_proj,
):
    rows, width = sequence.shape
    inner = out_proj.shape[0]
    heads = step_bias.shape[0]
    state = inner // heads * 2
    channels = conv_weight.shape[1]
    both_rows = 2 * rows
    stride_x, stride_z, stride_y = SIDE * SIDE, SIDE, 1
    index = lax.axis_index("seq")
    place = jnp.stack([index // stride_x, index // stride_z % SIDE, index % SIDE]).astype(jnp.int32)
    upward = [(i, i + 1) for i in range(COUNT - 1)]
    downward = [(i + 1, i) for i in range(COUNT - 1)]
    low = lax.ppermute(sequence[rows - 16 :], "seq", upward)
    high = lax.ppermute(sequence[:16], "seq", downward)
    gain, bias, decay = norm_gain[None], step_bias[None], decay_log[None]
    payload, both, normal, cot, gate, conv, d_gated, raw, step, cumul, cumul_t = call(
        pre_kernel,
        [
            ((COUNT, 72, state), bf16),
            ((both_rows, width), bf16),
            ((both_rows, width), bf16),
            ((both_rows, width), bf16),
            ((both_rows, inner), f32),
            ((both_rows, channels), f32),
            ((both_rows, inner), bf16),
            ((both_rows, heads), f32),
            ((both_rows, heads), f32),
            ((both_rows, heads), f32),
            ((2 * heads, rows), f32),
        ],
        (
            sequence, upstream, low, high, gain, in_proj, step_proj,
            conv_weight, conv_bias[None], bias, decay, out_proj,
        ),
        [pltpu.VMEM((rows + 8, channels), f32)],
    )
    got = lax.all_to_all(payload, "seq", 0, 0)
    mixed, d_driven, d_bc, d_cumul = call(
        intra_kernel,
        [
            ((both_rows, inner), f32),
            ((both_rows, inner), f32),
            ((both_rows, 2 * state), f32),
            ((both_rows, heads), f32),
        ],
        (conv, gate, d_gated, step, cumul, cumul_t),
        flops=8 * 10**9,
    )
    (scanned,) = call(
        scan_kernel,
        [((COUNT, 64, state), bf16)],
        (got,),
        [pltpu.VMEM((COUNT * 72, state), f32), pltpu.VMEM((COUNT * 64, state), f32)],
    )
    states = lax.all_to_all(scanned, "seq", 0, 0)
    gated, d_gate, d_conv, d_step = call(
        post_kernel,
        [
            ((both_rows, inner), bf16),
            ((both_rows, inner), bf16),
            ((both_rows, channels), f32),
            ((both_rows, heads), bf16),
        ],
        (
            states, conv, gate, d_gated, raw, step, cumul, mixed, d_driven, d_bc, d_cumul,
            bias, decay, skip_gain[None],
        ),
    )
    ahead = lax.ppermute(d_conv[:8], "seq", downward)
    behind = lax.ppermute(d_conv[rows : rows + 8], "seq", upward)
    eighth = 8 * COUNT // SIDE
    half = (channels) // 2
    terms = call(
        out_term_kernel,
        slots(eighth, inner) + slots(eighth, inner),
        (place, gated, cot, normal, d_gate),
        [pltpu.VMEM((inner, width), f32), pltpu.VMEM((COUNT // SIDE, SIDE, 8, inner), f32)],
        scalars=1,
        flops=4 * 10**9,
    )
    out_x = exchange(terms[:4], stride_x)
    gate_y = exchange(terms[4:], stride_y)
    d_xbc, *terms = call(
        in_term_kernel,
        [((both_rows, channels), bf16)] + slots(eighth, half) + slots(eighth, half),
        (place, d_conv, ahead, behind, conv_weight, normal),
        [
            pltpu.VMEM((rows + 8, channels), f32),
            pltpu.VMEM((width, half), f32),
            pltpu.VMEM((COUNT // SIDE, SIDE, 8, half), f32),
        ],
        scalars=1,
    )
    in_x = exchange(terms[:4], stride_x)
    in_y = exchange(terms[4:], stride_y)
    layer_out, grad_input = call(
        result_kernel,
        [((rows, width), bf16), ((rows, width), bf16)],
        (both, gain, gated, out_proj, d_gate, d_xbc, d_step, in_proj, step_proj),
        flops=8 * 10**9,
    )
    joined = inner + half
    parts = call(
        first_sum_kernel,
        slots(eighth // SIDE, joined) + slots(eighth // SIDE, joined),
        (place, *out_x, *in_x, *gate_y, *in_y),
        [pltpu.VMEM((SIDE, SIDE, 8, joined), f32), pltpu.VMEM((eighth, joined), f32)],
        scalars=1,
    )
    first = exchange(parts[:4], stride_y)
    second = exchange(parts[4:], stride_x)
    parts = call(
        second_sum_kernel,
        slots(16, joined),
        (place, *first, *second),
        [pltpu.VMEM((SIDE, 2, 8, joined), f32)],
        scalars=1,
    )
    last = exchange(parts, stride_z)
    grad_in_proj, grad_out_proj = call(
        last_sum_kernel,
        [((8, inner + channels), f32), ((16, width), f32)],
        tuple(last),
    )
    return (layer_out, grad_input, grad_in_proj, grad_out_proj)


def solution(mesh):
    rows = P(("batch", "seq"), None)
    return jax.shard_map(
        shards,
        mesh=mesh,
        in_specs=(rows, rows) + (P(),) * 9,
        out_specs=(rows,) * 4,
        check_vma=False,
    )
```

time: 1480 us -> 200 us (0.14); the launches traced: 1460 us -> 197 us
  waiting for transfers between devices: 638 us -> 54.9 us
  blocking collectives: 360 us -> 41.8 us
  other arithmetic: 296 us -> 0.08 us
  matrix products: 80.7 us -> 0 us
  Pallas kernels: 0 us -> 24.9 us
  between operations: 15.8 us -> 0.98 us
    reduce_scatter x2 -> x0, waiting for transfers between devices: 442 us -> none  [the longest x1 291 us: shards(): lax.psum_scatter(contract_rows(stacked_normal, stacked_proj), 'seq', scat...]
    all_gather x2 -> x0, blocking collectives: 360 us -> none  [prefix(): lax.all_gather(a.astype(kind), axis)]
    add x126 -> x0, other arithmetic: 199 us -> none  [link_pair(): jnp.exp(later[0])[:, None, None] * earlier[1] + later[1]]
    all_gather x4 -> x0, waiting for transfers between devices: 188 us -> none  [the longest x2 188 us: entering(): lax.all_gather(a.astype(kind), axis)]
    dot_general x38 -> x0, matrix products: 80.7 us -> none  [the longest x6 24.2 us: finish(): jnp.einsum('hts,ts,shp->thp', decays, scores, driven, precision=lax.Preci...]
    exp x128 -> x0, other arithmetic: 77.1 us -> none  [the longest x126 75.8 us: link_pair(): jnp.exp(later[0])[:, None, None] * earlier[1] + later[1]]
    all_to_all x0 -> x1, blocking collectives: none -> 41.8 us  [shards(): got = lax.all_to_all(payload, 'seq', 0, 0)]
    ppermute x4 -> x25, waiting for transfers between devices: 8.51 us -> 41.5 us  [the longest x21 31.8 us: exchange(): lax.ppermute(parts[step], 'seq', axis_pairs(stride, step))]
  transfers between devices with their start and end apart: 10 -> 26, of which waited for: 4 -> 17; matrix products, arithmetic and copies ran while one was open for 27% -> 1% of each run, Pallas kernels for 0% -> 4%
where the time goes in v1:
time: 200 us; the launch traced here: 197 us
  waiting for transfers between devices  54.9 us (27%)
  starting transfers between devices  49 us (24%)
  blocking collectives  41.8 us (21%)
  local copies, waits for them, and re-layouts  25.3 us (13%)
  Pallas kernels  24.9 us (12%)
    all_to_all x1, blocking collectives, shards(): got = lax.all_to_all(payload, 'seq', 0, 0)  41.8 us
    ppermute x21, waiting for transfers between devices, exchange(): lax.ppermute(parts[step], 'seq', axis_pairs(stride, step))  31.8 us
    pallas_call x10, Pallas kernels, call(): pl.pallas_call(body, out_shape=[jax.ShapeDtypeStruct(shape, kind) for sha...  24.9 us
    unnamed x85, local copies, waits for them, and re-layouts  23.8 us
    ppermute x21, starting transfers between devices, exchange(): lax.ppermute(parts[step], 'seq', axis_pairs(stride, step))  20.4 us
    all_to_all x1, waiting for transfers between devices, shards(): states = lax.all_to_all(scanned, 'seq', 0, 0)  13.4 us
    ppermute x1, waiting for transfers between devices, shards(): behind = lax.ppermute(d_conv[rows:rows + 8], 'seq', upward)  9.74 us
    ppermute x1, starting transfers between devices, shards(): high = lax.ppermute(sequence[:16], 'seq', downward)  9.36 us
  transfers between devices with their start and end apart: 26, of which 17 were waited for; matrix products, arithmetic and copies ran while one was open for 1% of the time, Pallas kernels for 4%

profile of v1, /device:TPU:6, one launch (start us, length us, event | category | flops | bytes accessed | tf_op | source)
XLA Modules:
  0.0 197.0 jit_solution(5894539547512220106)
XLA Ops:
  0.6 0.7 fusion.1
  1.4 3.5 %collective-permute-start = (bf16[16,512]{1,0:T(8,128)(2,1)S(1)}, bf16[16,512]{1,0:T(8,128)(2,1)S(1)}, u32[]{:S(2)}, u32[]{:S(2)}) collective-permute-start(bf16[16,512]{1,0:T(8,128)(2,1)S(1)} %get-tuple-element.111), channel_id=1, source_target_pairs={{0,4},{4,8},{8,12},{12,16},{16,20},{20,24},{24,28},{28,32},{32,36}... | collective-permute-start | bytes 49160 | tf_op jit(solution)/shard_map/ppermute | solution.py:469
  4.9 9.4 %collective-permute-start.1 = (bf16[16,512]{1,0:T(8,128)(2,1)S(1)}, bf16[16,512]{1,0:T(8,128)(2,1)S(1)}, u32[]{:S(2)}, u32[]{:S(2)}) collective-permute-start(bf16[16,512]{1,0:T(8,128)(2,1)S(1)} %get-tuple-element.110), channel_id=1, source_target_pairs={{4,0},{8,4},{12,8},{16,12},{20,16},{24,20},{28,24},{32,28},{36,32}... | collective-permute-start | bytes 49160 | tf_op jit(solution)/shard_map/ppermute | solution.py:470
  14.2 0.8 copy.15.step_proj
  15.1 0.7 broadcast_in_dim.16.conv_b
  15.8 1.7 copy-done
  17.4 1.2 copy-done.2
  18.7 0.9 copy-done.13
  19.6 0.9 copy-done.14
  20.5 0.7 copy-done.25
  21.2 0.7 copy-done.27
  23.2 3.7 %shard_map.138 = (bf16[64,72,128]{2,1,0:T(8,128)(2,1)S(1)}, bf16[256,512]{1,0:T(8,128)(2,1)S(1)}, bf16[256,512]{1,0:T(8,128)(2,1)S(1)}, bf16[256,512]{1,0:T(8,12...) custom-call(bf16[128,512]{1,0:T(8,128)(2,1)S(1)} %copy-done.13, ...), custom_call_target="tpu_custom_call" | custom-call | flops 1000000000 | bytes 3746944 | tf_op jit(solution)/shard_map/pallas_call | solution.py:22
  27.6 41.8 %all_to_all.10.got = bf16[64,72,128]{2,1,0:T(8,128)(2,1)S(1)} all-to-all(bf16[64,72,128]{2,1,0:T(8,128)(2,1)S(1)} %get-tuple-element.57), channel_id=1, replica_groups=mesh['seq'=64,'batch'=4] {'seq'}, dimensions={0} | all-to-all | bytes 2359296 | tf_op jit(solution)/shard_map/all_to_all | solution.py:493
  69.4 3.3 %shard_map.139 = bf16[64,64,128]{2,1,0:T(8,128)(2,1)} custom-call(bf16[64,72,128]{2,1,0:T(8,128)(2,1)S(1)} %all_to_all.10.got), custom_call_target="tpu_custom_call" | custom-call | flops 1000000000 | bytes 1179648 | tf_op jit(solution)/shard_map/pallas_call | solution.py:22
  72.7 8.3 %all-to-all-start.1 = ((bf16[64,64,128]{2,1,0:T(8,128)(2,1)}), bf16[64,64,128]{2,1,0:T(8,128)(2,1)S(1)}, u32[]{:S(2)}, u32[]{:S(2)}) async-start(bf16[64,64,128]{2,1,0:T(8,128)(2,1)} %shard_map.139), calls=%async_computation.1 | async-start | bytes 2097152 | tf_op jit(solution)/shard_map/all_to_all | solution.py:511
  81.1 1.0 copy-done.9
  82.1 0.9 copy-done.18
  83.0 0.9 copy-done.21
  83.9 0.7 copy-done.41
  84.6 2.7 %shard_map.140 = (f32[256,1024]{1,0:T(8,128)S(1)}, f32[256,1024]{1,0:T(8,128)S(1)}, f32[256,256]{1,0:T(8,128)S(1)}, f32[256,16]{1,0:T(8,128)S(1)}) custom-call(f32[256,1280]{1,0:T(8,128)S(1)} %get-tuple-element.58.conv, f32[256,1024]{1,0:T(8,128)S(1)} %get-tuple-element.59.gate, bf16[256,1024]{1,0:T(8,128)(2,1)S(1)} %copy-done.9, f32[256,16]{1,0:T(8,128)S(1)} %copy-done.18, ...), custom_call_target="tpu_custom_call" | custom-call | flops 8000000000 | bytes 2932736 | tf_op jit(solution)/shard_map/pallas_call | solution.py:22
  87.4 1.0 copy-done.4
  88.3 1.0 copy-done.6
  89.3 0.7 copy-done.11
  90.7 13.4 %all-to-all-done.1.got = bf16[64,64,128]{2,1,0:T(8,128)(2,1)S(1)} async-done(((bf16[64,64,128]{2,1,0:T(8,128)(2,1)}), bf16[64,64,128]{2,1,0:T(8,128)(2,1)S(1)}, u32[]{:S(2)}, u32[]{:S(2)}) %all-to-all-start.1) | async-done | bytes 1048608 | tf_op jit(solution)/shard_map/all_to_all | solution.py:511
  104.1 1.2 copy-done.5
  105.3 1.2 copy-done.7
  106.5 1.0 copy-done.10
  107.6 0.9 copy-done.12
  108.5 0.9 copy-done.16
  109.4 0.9 copy-done.19
  110.3 0.9 copy-done.22
  111.2 0.9 copy-done.24
  112.1 5.8 %shard_map.141 = (bf16[256,1024]{1,0:T(8,128)(2,1)S(1)}, bf16[256,1024]{1,0:T(8,128)(2,1)S(1)}, f32[256,1280]{1,0:T(8,128)S(1)}, bf16[256,16]{1,0:T(8,128)(2,1)S(1)}) custom-call(bf16[64,64,128]{2,1,0:T(8,128)(2,1)S(1)} %all-to-all-done.1.got, f32[256,1280]{1,0:T(8,128)S(1)} %get-tuple-element.58.conv, f32[256,1024]{1,0:T(8,128)S(1)} %get-tuple-element.59.gate, ...), custom_call_target="tpu_custom_call" | custom-call | flops 1000000000 | bytes 6357184 | tf_op jit(solution)/shard_map/pallas_call | solution.py:22
  117.9 5.5 %collective-permute-start.2 = (f32[8,1280]{1,0:T(8,128)S(1)}, f32[8,1280]{1,0:T(8,128)S(1)}, u32[]{:S(2)}, u32[]{:S(2)}) collective-permute-start(f32[8,1280]{1,0:T(8,128)S(1)} %get-tuple-element.109), channel_id=1, source_target_pairs={{4,0},{8,4},{12,8},{16,12},{20,16},{24,20},{28,24},{32,28},{36,32}... | collective-permute-start | bytes 122888 | tf_op jit(solution)/shard_map/ppermute | solution.py:525
  123.5 1.9 collective-permute-start.3
  125.5 9.7 %collective-permute-done.3.behind = f32[8,1280]{1,0:T(8,128)S(1)} collective-permute-done((f32[8,1280]{1,0:T(8,128)S(1)}, f32[8,1280]{1,0:T(8,128)S(1)}, u32[]{:S(2)}, u32[]{:S(2)}) %collective-permute-start.3) | collective-permute-done | bytes 40992 | tf_op jit(solution)/shard_map/ppermute | solution.py:526
  135.2 2.1 %shard_map.142 = (bf16[256,1280]{1,0:T(8,128)(2,1)S(1)}, f32[128,640]{1,0:T(8,128)S(1)}, bf16[128,640]{1,0:T(8,128)(2,1)S(1)}, bf16[128,640]{1,0:T(8,128)(2,1)S(...) custom-call(s32[3]{0:T(128)S(1)} %pad_add_fusion.place, ...), custom_call_target="tpu_custom_call" | custom-call | flops 1000000000 | bytes 1675276 | tf_op jit(solution)/shard_map/pallas_call | solution.py:22
  137.5 1.7 shard_map.144
  139.2 4.3 %collective-permute-start.10 = (bf16[128,1024]{1,0:T(8,128)(2,1)S(1)}, bf16[128,1024]{1,0:T(8,128)(2,1)S(1)}, u32[]{:S(2)}, u32[]{:S(2)}) collective-permute-start(bf16[128,1024]{1,0:T(8,128)(2,1)S(1)} %get-tuple-element.87), channel_id=1, source_target_pairs={{0,4},{4,8},{8,12},{12,0},{16,20},{20,24},{24,28},{28,16},{32,36},... | collective-permute-start | bytes 786440 | tf_op jit(solution)/shard_map/ppermute | solution.py:437
  143.5 4.9 %collective-permute-done.13.refs_13_ = bf16[128,640]{1,0:T(8,128)(2,1)S(1)} collective-permute-done((bf16[128,640]{1,0:T(8,128)(2,1)S(1)}, bf16[128,640]{1,0:T(8,128)(2,1)S(1)}, u32[]{:S(2)}, u32[]{:S(2)}) %collective-permute-start.13) | collective-permute-done | bytes 163872 | tf_op jit(solution)/shard_map/ppermute | solution.py:437
  148.4 1.7 collective-permute-start.8
  151.3 2.6 %collective-permute-start.12 = (bf16[128,1024]{1,0:T(8,128)(2,1)S(1)}, bf16[128,1024]{1,0:T(8,128)(2,1)S(1)}, u32[]{:S(2)}, u32[]{:S(2)}) collective-permute-start(bf16[128,1024]{1,0:T(8,128)(2,1)S(1)} %get-tuple-element.89), channel_id=1, source_target_pairs={{0,12},{4,0},{8,4},{12,8},{16,28},{20,16},{24,20},{28,24},{32,44},... | collective-permute-start | bytes 786440 | tf_op jit(solution)/shard_map/ppermute | solution.py:437
  153.9 3.1 %collective-permute-done.8.refs_6_ = bf16[128,640]{1,0:T(8,128)(2,1)S(1)} collective-permute-done((bf16[128,640]{1,0:T(8,128)(2,1)S(1)}, bf16[128,640]{1,0:T(8,128)(2,1)S(1)}, u32[]{:S(2)}, u32[]{:S(2)}) %collective-permute-start.8) | collective-permute-done | bytes 163872 | tf_op jit(solution)/shard_map/ppermute | solution.py:437
  157.0 1.9 collective-permute-done.9.refs_7_
  158.9 1.3 collective-permute-start.5
  160.4 1.3 collective-permute-done.12.refs_11_
  161.6 1.8 collective-permute-done.4.refs_1_
  163.4 3.5 %collective-permute-done.5.refs_2_ = bf16[128,1024]{1,0:T(8,128)(2,1)S(1)} collective-permute-done((bf16[128,1024]{1,0:T(8,128)(2,1)S(1)}, bf16[128,1024]{1,0:T(8,128)(2,1)S(1)}, u32[]{:S(2)}, u32[]{:S(2)}) %collective-permute-start.5) | collective-permute-done | bytes 262176 | tf_op jit(solution)/shard_map/ppermute | solution.py:437
  166.9 4.8 %collective-permute-done.6.refs_3_ = bf16[128,1024]{1,0:T(8,128)(2,1)S(1)} collective-permute-done((bf16[128,1024]{1,0:T(8,128)(2,1)S(1)}, bf16[128,1024]{1,0:T(8,128)(2,1)S(1)}, u32[]{:S(2)}, u32[]{:S(2)}) %collective-permute-start.6) | collective-permute-done | bytes 262176 | tf_op jit(solution)/shard_map/ppermute | solution.py:437
  171.7 1.2 shard_map.145
  173.0 1.8 collective-permute-start.17
  174.8 2.3 %collective-permute-start.18 = (bf16[32,1664]{1,0:T(8,128)(2,1)S(1)}, bf16[32,1664]{1,0:T(8,128)(2,1)S(1)}, u32[]{:S(2)}, u32[]{:S(2)}) collective-permute-start(bf16[32,1664]{1,0:T(8,128)(2,1)S(1)} %get-tuple-element.97), channel_id=1, source_target_pairs={{0,12},{4,0},{8,4},{12,8},{16,28},{20,16},{24,20},{28,24},{32,44},... | collective-permute-start | bytes 319496 | tf_op jit(solution)/shard_map/ppermute | solution.py:437
  177.5 0.7 collective-permute-start.20
  178.2 1.8 collective-permute-done.16.refs_1_
  180.0 0.9 collective-permute-done.18.refs_3_
  180.9 0.8 collective-permute-done.19.refs_5_
  181.7 2.0 %collective-permute-done.20.refs_6_ = bf16[32,1664]{1,0:T(8,128)(2,1)S(1)} collective-permute-done((bf16[32,1664]{1,0:T(8,128)(2,1)S(1)}, bf16[32,1664]{1,0:T(8,128)(2,1)S(1)}, u32[]{:S(2)}, u32[]{:S(2)}) %collective-permute-start.20) | collective-permute-done | bytes 106528 | tf_op jit(solution)/shard_map/ppermute | solution.py:437
  183.7 2.2 %collective-permute-done.21.refs_7_ = bf16[32,1664]{1,0:T(8,128)(2,1)S(1)} collective-permute-done((bf16[32,1664]{1,0:T(8,128)(2,1)S(1)}, bf16[32,1664]{1,0:T(8,128)(2,1)S(1)}, u32[]{:S(2)}, u32[]{:S(2)}) %collective-permute-start.21) | collective-permute-done | bytes 106528 | tf_op jit(solution)/shard_map/ppermute | solution.py:437
  186.0 0.7 shard_map.146
  187.4 3.5 %collective-permute-start.24 = (bf16[16,1664]{1,0:T(8,128)(2,1)S(1)}, bf16[16,1664]{1,0:T(8,128)(2,1)S(1)}, u32[]{:S(2)}, u32[]{:S(2)}) collective-permute-start(bf16[16,1664]{1,0:T(8,128)(2,1)S(1)} %get-tuple-element.105), channel_id=1, source_target_pairs={{0,48},{4,52},{8,56},{12,60},{16,0},{20,4},{24,8},{28,12},{32,16},... | collective-permute-start | bytes 159752 | tf_op jit(solution)/shard_map/ppermute | solution.py:437
  190.9 3.1 %shard_map.143 = (bf16[128,512]{1,0:T(8,128)(2,1)}, bf16[128,512]{1,0:T(8,128)(2,1)}) custom-call(bf16[256,512]{1,0:T(8,128)(2,1)S(1)} %copy-done.35, f32[1,512]{1,0:T(1,128)S(1)} %bitcast.8, bf16[256,1024]{1,0:T(8,128)(2,1)S(1)} %get-tuple-element.69.gated, bf16[1024,512]{1,0:T(8,128)(2,1)S(1)} %copy-done.3, ...), custom_call_target="tpu_custom_call" | custom-call | flops 8000000000 | bytes 5400576 | tf_op jit(solution)/shard_map/pallas_call | solution.py:22
  194.0 0.8 collective-permute-done.23.refs_2_
  194.9 1.5 collective-permute-done.24.refs_3_
  196.3 0.7 shard_map.147
  (88 shorter events, 5.6 us)
Async XLA Ops:
  1.4 14.4 %collective-permute-start = (bf16[16,512]{1,0:T(8,128)(2,1)S(1)}, bf16[16,512]{1,0:T(8,128)(2,1)S(1)}, u32[]{:S(2)}, u32[]{:S(2)}) collective-permute-start(bf16[16,512]{1,0:T(8,128)(2,1)S(1)} %get-tuple-element.111), channel_id=1, source_target_pairs={{0,4},{4,8},{8,12},{12,16},{16,20},{20,24},{24,28},{28,32},{32,36}... | collective-permute-start | bytes 49160 | tf_op jit(solution)/shard_map/ppermute | solution.py:469
  4.9 10.9 %collective-permute-start.1 = (bf16[16,512]{1,0:T(8,128)(2,1)S(1)}, bf16[16,512]{1,0:T(8,128)(2,1)S(1)}, u32[]{:S(2)}, u32[]{:S(2)}) collective-permute-start(bf16[16,512]{1,0:T(8,128)(2,1)S(1)} %get-tuple-element.110), channel_id=1, source_target_pairs={{4,0},{8,4},{12,8},{16,12},{20,16},{24,20},{28,24},{32,28},{36,32}... | collective-permute-start | bytes 49160 | tf_op jit(solution)/shard_map/ppermute | solution.py:470
  15.8 1.7 copy-start
  17.4 1.2 copy-start.2
  18.7 0.9 copy-start.13
  19.6 0.9 copy-start.14
  20.5 0.7 copy-start.25
  21.2 0.7 copy-start.27
  27.5 41.9 %copy-start.8 = (bf16[256,1024]{1,0:T(8,128)(2,1)}, bf16[256,1024]{1,0:T(8,128)(2,1)S(1)}, u32[]{:S(2)}) copy-start(bf16[256,1024]{1,0:T(8,128)(2,1)S(1)} %get-tuple-element.60.d_gated) | copy-start | bytes 1572868
  27.5 41.9 %copy-start.15 = (f32[256,16]{1,0:T(8,128)}, f32[256,16]{1,0:T(8,128)S(1)}, u32[]{:S(2)}) copy-start(f32[256,16]{1,0:T(8,128)S(1)} %get-tuple-element.61.raw) | copy-start | bytes 49156
  27.5 41.9 %copy-start.17 = (f32[256,16]{1,0:T(8,128)}, f32[256,16]{1,0:T(8,128)S(1)}, u32[]{:S(2)}) copy-start(f32[256,16]{1,0:T(8,128)S(1)} %get-tuple-element.62.step) | copy-start | bytes 49156
  27.5 41.9 %copy-start.20 = (f32[256,16]{1,0:T(8,128)}, f32[256,16]{1,0:T(8,128)S(1)}, u32[]{:S(2)}) copy-start(f32[256,16]{1,0:T(8,128)S(1)} %get-tuple-element.63.cumul) | copy-start | bytes 49156
  27.5 41.9 %copy-start.34 = (bf16[256,512]{1,0:T(8,128)(2,1)}, bf16[256,512]{1,0:T(8,128)(2,1)S(1)}, u32[]{:S(2)}) copy-start(bf16[256,512]{1,0:T(8,128)(2,1)S(1)} %get-tuple-element.56.both) | copy-start | bytes 786436
  27.5 41.9 %copy-start.36 = (bf16[256,512]{1,0:T(8,128)(2,1)}, bf16[256,512]{1,0:T(8,128)(2,1)S(1)}, u32[]{:S(2)}) copy-start(bf16[256,512]{1,0:T(8,128)(2,1)S(1)} %get-tuple-element.72.normal) | copy-start | bytes 786436
  27.5 41.9 %copy-start.38 = (bf16[256,512]{1,0:T(8,128)(2,1)}, bf16[256,512]{1,0:T(8,128)(2,1)S(1)}, u32[]{:S(2)}) copy-start(bf16[256,512]{1,0:T(8,128)(2,1)S(1)} %get-tuple-element.77.cot) | copy-start | bytes 786436
  72.7 31.4 %all-to-all-start.1 = ((bf16[64,64,128]{2,1,0:T(8,128)(2,1)}), bf16[64,64,128]{2,1,0:T(8,128)(2,1)S(1)}, u32[]{:S(2)}, u32[]{:S(2)}) async-start(bf16[64,64,128]{2,1,0:T(8,128)(2,1)} %shard_map.139), calls=%async_computation.1 | async-start | bytes 2097152 | tf_op jit(solution)/shard_map/all_to_all | solution.py:511
  81.1 1.0 copy-start.9
  82.1 0.9 copy-start.18
  83.0 0.9 copy-start.21
  83.9 0.7 copy-start.41
  84.6 19.4 %copy-start.30 = (f32[16]{0:T(128)S(1)}, f32[16]{0:T(128)}, u32[]{:S(2)}) copy-start(f32[16]{0:T(128)} %param.18) | copy-start | bytes 196
  84.6 19.4 %copy-start.32 = (f32[16]{0:T(128)S(1)}, f32[16]{0:T(128)}, u32[]{:S(2)}) copy-start(f32[16]{0:T(128)} %param.19) | copy-start | bytes 196
  84.6 19.4 %copy-start.33 = (f32[16]{0:T(128)S(1)}, f32[16]{0:T(128)}, u32[]{:S(2)}) copy-start(f32[16]{0:T(128)} %param.20) | copy-start | bytes 196
  87.4 1.0 copy-start.4
  88.3 1.0 copy-start.6
  89.3 0.7 copy-start.11
  104.1 1.2 copy-start.5
  105.3 1.2 copy-start.7
  106.5 1.0 copy-start.10
  107.6 0.9 copy-start.12
  108.5 0.9 copy-start.16
  109.4 0.9 copy-start.19
  110.3 0.9 copy-start.22
  111.2 0.9 copy-start.24
  112.1 23.1 %copy-start.26 = (f32[4,1280]{1,0:T(4,128)S(1)}, f32[4,1280]{1,0:T(4,128)}, u32[]{:S(2)}) copy-start(f32[4,1280]{1,0:T(4,128)} %conv_w.3) | copy-start | bytes 61444
  112.1 23.1 %copy-start.37 = (bf16[256,512]{1,0:T(8,128)(2,1)S(1)}, bf16[256,512]{1,0:T(8,128)(2,1)}, u32[]{:S(2)}) copy-start(bf16[256,512]{1,0:T(8,128)(2,1)} %copy-done.36) | copy-start | bytes 786436
  117.9 7.5 %collective-permute-start.2 = (f32[8,1280]{1,0:T(8,128)S(1)}, f32[8,1280]{1,0:T(8,128)S(1)}, u32[]{:S(2)}, u32[]{:S(2)}) collective-permute-start(f32[8,1280]{1,0:T(8,128)S(1)} %get-tuple-element.109), channel_id=1, source_target_pairs={{4,0},{8,4},{12,8},{16,12},{20,16},{24,20},{28,24},{32,28},{36,32}... | collective-permute-start | bytes 122888 | tf_op jit(solution)/shard_map/ppermute | solution.py:525
  123.5 11.8 %collective-permute-start.3 = (f32[8,1280]{1,0:T(8,128)S(1)}, f32[8,1280]{1,0:T(8,128)S(1)}, u32[]{:S(2)}, u32[]{:S(2)}) collective-permute-start(f32[8,1280]{1,0:T(8,128)S(1)} %get-tuple-element.108), channel_id=1, source_target_pairs={{0,4},{4,8},{8,12},{12,16},{16,20},{20,24},{24,28},{28,32},{32,36}... | collective-permute-start | bytes 122888 | tf_op jit(solution)/shard_map/ppermute | solution.py:526
  135.2 2.3 %copy-start.39 = (bf16[256,512]{1,0:T(8,128)(2,1)S(1)}, bf16[256,512]{1,0:T(8,128)(2,1)}, u32[]{:S(2)}) copy-start(bf16[256,512]{1,0:T(8,128)(2,1)} %copy-done.38) | copy-start | bytes 786436
  137.3 11.0 %collective-permute-start.13 = (bf16[128,640]{1,0:T(8,128)(2,1)S(1)}, bf16[128,640]{1,0:T(8,128)(2,1)S(1)}, u32[]{:S(2)}, u32[]{:S(2)}) collective-permute-start(bf16[128,640]{1,0:T(8,128)(2,1)S(1)} %get-tuple-element.91), channel_id=1, source_target_pairs={{0,4},{4,8},{8,12},{12,0},{16,20},{20,24},{24,28},{28,16},{32,36},... | collective-permute-start | bytes 491528 | tf_op jit(solution)/shard_map/ppermute | solution.py:437
  137.4 12.7 %collective-permute-start.14 = (bf16[128,640]{1,0:T(8,128)(2,1)S(1)}, bf16[128,640]{1,0:T(8,128)(2,1)S(1)}, u32[]{:S(2)}, u32[]{:S(2)}) collective-permute-start(bf16[128,640]{1,0:T(8,128)(2,1)S(1)} %get-tuple-element.92), channel_id=1, source_target_pairs={{0,8},{4,12},{8,0},{12,4},{16,24},{20,28},{24,16},{28,20},{32,40},... | collective-permute-start | bytes 491528 | tf_op jit(solution)/shard_map/ppermute | solution.py:437
  139.2 20.9 %collective-permute-start.10 = (bf16[128,1024]{1,0:T(8,128)(2,1)S(1)}, bf16[128,1024]{1,0:T(8,128)(2,1)S(1)}, u32[]{:S(2)}, u32[]{:S(2)}) collective-permute-start(bf16[128,1024]{1,0:T(8,128)(2,1)S(1)} %get-tuple-element.87), channel_id=1, source_target_pairs={{0,4},{4,8},{8,12},{12,0},{16,20},{20,24},{24,28},{28,16},{32,36},... | collective-permute-start | bytes 786440 | tf_op jit(solution)/shard_map/ppermute | solution.py:437
  143.5 7.1 %collective-permute-start.15 = (bf16[128,640]{1,0:T(8,128)(2,1)S(1)}, bf16[128,640]{1,0:T(8,128)(2,1)S(1)}, u32[]{:S(2)}, u32[]{:S(2)}) collective-permute-start(bf16[128,640]{1,0:T(8,128)(2,1)S(1)} %get-tuple-element.93), channel_id=1, source_target_pairs={{0,12},{4,0},{8,4},{12,8},{16,28},{20,16},{24,20},{28,24},{32,44},... | collective-permute-start | bytes 491528 | tf_op jit(solution)/shard_map/ppermute | solution.py:437
  143.5 7.8 %collective-permute-start.7 = (bf16[128,640]{1,0:T(8,128)(2,1)S(1)}, bf16[128,640]{1,0:T(8,128)(2,1)S(1)}, u32[]{:S(2)}, u32[]{:S(2)}) collective-permute-start(bf16[128,640]{1,0:T(8,128)(2,1)S(1)} %get-tuple-element.83), channel_id=1, source_target_pairs={{0,64},{4,68},{8,72},{12,76},{16,80},{20,84},{24,88},{28,92},{32,9... | collective-permute-start | bytes 491528 | tf_op jit(solution)/shard_map/ppermute | solution.py:437
  148.4 8.6 %collective-permute-start.8 = (bf16[128,640]{1,0:T(8,128)(2,1)S(1)}, bf16[128,640]{1,0:T(8,128)(2,1)S(1)}, u32[]{:S(2)}, u32[]{:S(2)}) collective-permute-start(bf16[128,640]{1,0:T(8,128)(2,1)S(1)} %get-tuple-element.84), channel_id=1, source_target_pairs={{0,128},{4,132},{8,136},{12,140},{16,144},{20,148},{24,152},{28,15... | collective-permute-start | bytes 491528 | tf_op jit(solution)/shard_map/ppermute | solution.py:437
  150.1 8.8 %collective-permute-start.9 = (bf16[128,640]{1,0:T(8,128)(2,1)S(1)}, bf16[128,640]{1,0:T(8,128)(2,1)S(1)}, u32[]{:S(2)}, u32[]{:S(2)}) collective-permute-start(bf16[128,640]{1,0:T(8,128)(2,1)S(1)} %get-tuple-element.85), channel_id=1, source_target_pairs={{0,192},{4,196},{8,200},{12,204},{16,208},{20,212},{24,216},{28,22... | collective-permute-start | bytes 491528 | tf_op jit(solution)/shard_map/ppermute | solution.py:437
  150.6 9.7 %collective-permute-start.11 = (bf16[128,1024]{1,0:T(8,128)(2,1)S(1)}, bf16[128,1024]{1,0:T(8,128)(2,1)S(1)}, u32[]{:S(2)}, u32[]{:S(2)}) collective-permute-start(bf16[128,1024]{1,0:T(8,128)(2,1)S(1)} %get-tuple-element.88), channel_id=1, source_target_pairs={{0,8},{4,12},{8,0},{12,4},{16,24},{20,28},{24,16},{28,20},{32,40},... | collective-permute-start | bytes 786440 | tf_op jit(solution)/shard_map/ppermute | solution.py:437
  151.3 10.4 %collective-permute-start.12 = (bf16[128,1024]{1,0:T(8,128)(2,1)S(1)}, bf16[128,1024]{1,0:T(8,128)(2,1)S(1)}, u32[]{:S(2)}, u32[]{:S(2)}) collective-permute-start(bf16[128,1024]{1,0:T(8,128)(2,1)S(1)} %get-tuple-element.89), channel_id=1, source_target_pairs={{0,12},{4,0},{8,4},{12,8},{16,28},{20,16},{24,20},{28,24},{32,44},... | collective-permute-start | bytes 786440 | tf_op jit(solution)/shard_map/ppermute | solution.py:437
  157.0 6.4 %collective-permute-start.4 = (bf16[128,1024]{1,0:T(8,128)(2,1)S(1)}, bf16[128,1024]{1,0:T(8,128)(2,1)S(1)}, u32[]{:S(2)}, u32[]{:S(2)}) collective-permute-start(bf16[128,1024]{1,0:T(8,128)(2,1)S(1)} %get-tuple-element.79), channel_id=1, source_target_pairs={{0,64},{4,68},{8,72},{12,76},{16,80},{20,84},{24,88},{28,92},{32,9... | collective-permute-start | bytes 786440 | tf_op jit(solution)/shard_map/ppermute | solution.py:437
  158.9 8.0 %collective-permute-start.5 = (bf16[128,1024]{1,0:T(8,128)(2,1)S(1)}, bf16[128,1024]{1,0:T(8,128)(2,1)S(1)}, u32[]{:S(2)}, u32[]{:S(2)}) collective-permute-start(bf16[128,1024]{1,0:T(8,128)(2,1)S(1)} %get-tuple-element.80), channel_id=1, source_target_pairs={{0,128},{4,132},{8,136},{12,140},{16,144},{20,148},{24,152},{28,15... | collective-permute-start | bytes 786440 | tf_op jit(solution)/shard_map/ppermute | solution.py:437
  160.2 11.6 %collective-permute-start.6 = (bf16[128,1024]{1,0:T(8,128)(2,1)S(1)}, bf16[128,1024]{1,0:T(8,128)(2,1)S(1)}, u32[]{:S(2)}, u32[]{:S(2)}) collective-permute-start(bf16[128,1024]{1,0:T(8,128)(2,1)S(1)} %get-tuple-element.81), channel_id=1, source_target_pairs={{0,192},{4,196},{8,200},{12,204},{16,208},{20,212},{24,216},{28,22... | collective-permute-start | bytes 786440 | tf_op jit(solution)/shard_map/ppermute | solution.py:437
  172.9 7.1 %collective-permute-start.16 = (bf16[32,1664]{1,0:T(8,128)(2,1)S(1)}, bf16[32,1664]{1,0:T(8,128)(2,1)S(1)}, u32[]{:S(2)}, u32[]{:S(2)}) collective-permute-start(bf16[32,1664]{1,0:T(8,128)(2,1)S(1)} %get-tuple-element.95), channel_id=1, source_target_pairs={{0,4},{4,8},{8,12},{12,0},{16,20},{20,24},{24,28},{28,16},{32,36},... | collective-permute-start | bytes 319496 | tf_op jit(solution)/shard_map/ppermute | solution.py:437
  173.0 7.0 %collective-permute-start.17 = (bf16[32,1664]{1,0:T(8,128)(2,1)S(1)}, bf16[32,1664]{1,0:T(8,128)(2,1)S(1)}, u32[]{:S(2)}, u32[]{:S(2)}) collective-permute-start(bf16[32,1664]{1,0:T(8,128)(2,1)S(1)} %get-tuple-element.96), channel_id=1, source_target_pairs={{0,8},{4,12},{8,0},{12,4},{16,24},{20,28},{24,16},{28,20},{32,40},... | collective-permute-start | bytes 319496 | tf_op jit(solution)/shard_map/ppermute | solution.py:437
  174.8 6.1 %collective-permute-start.18 = (bf16[32,1664]{1,0:T(8,128)(2,1)S(1)}, bf16[32,1664]{1,0:T(8,128)(2,1)S(1)}, u32[]{:S(2)}, u32[]{:S(2)}) collective-permute-start(bf16[32,1664]{1,0:T(8,128)(2,1)S(1)} %get-tuple-element.97), channel_id=1, source_target_pairs={{0,12},{4,0},{8,4},{12,8},{16,28},{20,16},{24,20},{28,24},{32,44},... | collective-permute-start | bytes 319496 | tf_op jit(solution)/shard_map/ppermute | solution.py:437
  177.0 4.7 %collective-permute-start.19 = (bf16[32,1664]{1,0:T(8,128)(2,1)S(1)}, bf16[32,1664]{1,0:T(8,128)(2,1)S(1)}, u32[]{:S(2)}, u32[]{:S(2)}) collective-permute-start(bf16[32,1664]{1,0:T(8,128)(2,1)S(1)} %get-tuple-element.99), channel_id=1, source_target_pairs={{0,64},{4,68},{8,72},{12,76},{16,80},{20,84},{24,88},{28,92},{32,9... | collective-permute-start | bytes 319496 | tf_op jit(solution)/shard_map/ppermute | solution.py:437
  177.5 6.2 %collective-permute-start.20 = (bf16[32,1664]{1,0:T(8,128)(2,1)S(1)}, bf16[32,1664]{1,0:T(8,128)(2,1)S(1)}, u32[]{:S(2)}, u32[]{:S(2)}) collective-permute-start(bf16[32,1664]{1,0:T(8,128)(2,1)S(1)} %get-tuple-element.100), channel_id=1, source_target_pairs={{0,128},{4,132},{8,136},{12,140},{16,144},{20,148},{24,152},{28,15... | collective-permute-start | bytes 319496 | tf_op jit(solution)/shard_map/ppermute | solution.py:437
  180.0 5.9 %collective-permute-start.21 = (bf16[32,1664]{1,0:T(8,128)(2,1)S(1)}, bf16[32,1664]{1,0:T(8,128)(2,1)S(1)}, u32[]{:S(2)}, u32[]{:S(2)}) collective-permute-start(bf16[32,1664]{1,0:T(8,128)(2,1)S(1)} %get-tuple-element.101), channel_id=1, source_target_pairs={{0,192},{4,196},{8,200},{12,204},{16,208},{20,212},{24,216},{28,22... | collective-permute-start | bytes 319496 | tf_op jit(solution)/shard_map/ppermute | solution.py:437
  185.9 4.9 %copy-start.1 = (bf16[512,2304]{1,0:T(8,128)(2,1)S(1)}, bf16[512,2304]{1,0:T(8,128)(2,1)}, u32[]{:S(2)}) copy-start(bf16[512,2304]{1,0:T(8,128)(2,1)} %in_proj.3) | copy-start | bytes 7077892
  186.0 4.9 %copy-start.3 = (bf16[1024,512]{1,0:T(8,128)(2,1)S(1)}, bf16[1024,512]{1,0:T(8,128)(2,1)}, u32[]{:S(2)}) copy-start(bf16[1024,512]{1,0:T(8,128)(2,1)} %out_proj.3) | copy-start | bytes 3145732
  186.0 4.9 %copy-start.28 = (f32[512]{0:T(512)S(1)}, f32[512]{0:T(512)}, u32[]{:S(2)}) copy-start(f32[512]{0:T(512)} %param.13) | copy-start | bytes 6148
  186.0 4.9 %copy-start.35 = (bf16[256,512]{1,0:T(8,128)(2,1)S(1)}, bf16[256,512]{1,0:T(8,128)(2,1)}, u32[]{:S(2)}) copy-start(bf16[256,512]{1,0:T(8,128)(2,1)} %copy-done.34) | copy-start | bytes 786436
  186.6 7.4 %collective-permute-start.22 = (bf16[16,1664]{1,0:T(8,128)(2,1)S(1)}, bf16[16,1664]{1,0:T(8,128)(2,1)S(1)}, u32[]{:S(2)}, u32[]{:S(2)}) collective-permute-start(bf16[16,1664]{1,0:T(8,128)(2,1)S(1)} %get-tuple-element.103), channel_id=1, source_target_pairs={{0,16},{4,20},{8,24},{12,28},{16,32},{20,36},{24,40},{28,44},{32,4... | collective-permute-start | bytes 159752 | tf_op jit(solution)/shard_map/ppermute | solution.py:437
  186.7 8.1 %collective-permute-start.23 = (bf16[16,1664]{1,0:T(8,128)(2,1)S(1)}, bf16[16,1664]{1,0:T(8,128)(2,1)S(1)}, u32[]{:S(2)}, u32[]{:S(2)}) collective-permute-start(bf16[16,1664]{1,0:T(8,128)(2,1)S(1)} %get-tuple-element.104), channel_id=1, source_target_pairs={{0,32},{4,36},{8,40},{12,44},{16,48},{20,52},{24,56},{28,60},{32,0... | collective-permute-start | bytes 159752 | tf_op jit(solution)/shard_map/ppermute | solution.py:437
  187.4 9.0 %collective-permute-start.24 = (bf16[16,1664]{1,0:T(8,128)(2,1)S(1)}, bf16[16,1664]{1,0:T(8,128)(2,1)S(1)}, u32[]{:S(2)}, u32[]{:S(2)}) collective-permute-start(bf16[16,1664]{1,0:T(8,128)(2,1)S(1)} %get-tuple-element.105), channel_id=1, source_target_pairs={{0,48},{4,52},{8,56},{12,60},{16,0},{20,4},{24,8},{28,12},{32,16},... | collective-permute-start | bytes 159752 | tf_op jit(solution)/shard_map/ppermute | solution.py:437
  (4 other events, 2.6 us)

commit v2 on v1

v2 whole, which is shorter than its diff:
```python
import functools

import jax
import jax.numpy as jnp
from jax import lax
from jax.experimental import pallas as pl
from jax.experimental.pallas import tpu as pltpu
from jax.sharding import PartitionSpec as P

epsilon = 1e-06
SIDE = 4
COUNT = SIDE**3
f32 = jnp.float32
bf16 = jnp.bfloat16
INTERPRET = False


def call(body, outs, args, scratch=(), scalars=0, flops=10**9, vmem=58 * 2**20):
    specs = [pl.BlockSpec(memory_space=pltpu.SMEM)] * scalars
    specs += [pl.BlockSpec(memory_space=pltpu.VMEM)] * (len(args) - scalars)
    moved = sum(a.size * a.dtype.itemsize for a in args)
    return pl.pallas_call(
        body,
        out_shape=[jax.ShapeDtypeStruct(shape, kind) for shape, kind in outs],
        in_specs=specs,
        out_specs=[pl.BlockSpec(memory_space=pltpu.VMEM)] * len(outs),
        scratch_shapes=list(scratch),
        compiler_params=pltpu.CompilerParams(vmem_limit_bytes=vmem),
        cost_estimate=pl.CostEstimate(flops=flops, bytes_accessed=moved, transcendentals=0),
        interpret=INTERPRET,
    )(*args)


def mm(left, right):
    return lax.dot_general(left, right, (((1,), (0,)), ((), ())), preferred_element_type=f32)


def mm_cols(left, right):
    return lax.dot_general(left, right, (((1,), (1,)), ((), ())), preferred_element_type=f32)


def mm_rows(left, right):
    return lax.dot_general(left, right, (((0,), (0,)), ((), ())), preferred_element_type=f32)


def iota(shape, dim):
    return lax.broadcasted_iota(jnp.int32, shape, dim)


def ones_where(mask):
    return jnp.where(mask, 1.0, 0.0).astype(bf16)


def anti(size):
    return ones_where(iota((size, size), 0) + iota((size, size), 1) == size - 1)


def pieces_of(value, count):
    found = []
    for _ in range(count):
        piece = value.astype(bf16)
        found.append(piece)
        value = value - piece.astype(f32)
    return found


def mirror_exact(block):
    turned = mm(block, anti(block.shape[1])).astype(bf16)
    return mm(anti(block.shape[0]), turned).astype(bf16)


def mirror_wide(block):
    high, low = pieces_of(block, 2)
    return mirror_exact(high).astype(f32) + mirror_exact(low).astype(f32)


def head_mask(heads, width):
    lanes = heads * width
    return ones_where(iota((heads, lanes), 0) == iota((heads, lanes), 1) // width)


def expand(value, mask):
    found = pieces_of(value, 3)
    return mm(jnp.concatenate(found, axis=1), jnp.concatenate([mask] * 3, axis=0))


def fold(value, mask):
    total = None
    for piece in pieces_of(value, 2):
        part = mm_cols(piece, mask)
        total = part if total is None else total + part
    return total


def triangle(size, low):
    rows, cols = iota((size, size), 0), iota((size, size), 1)
    return rows >= cols if low else rows <= cols


def tri_sum(mask, value):
    total = None
    for piece in pieces_of(value, 3):
        part = mm(ones_where(mask), piece)
        total = part if total is None else total + part
    return total


def tri_sum_turned(mask, value):
    total = None
    for piece in pieces_of(value, 3):
        part = mm_rows(piece, ones_where(mask))
        total = part if total is None else total + part
    return total


def softplus(value):
    return jnp.maximum(value, 0.0) + jnp.log1p(jnp.exp(-jnp.abs(value)))


def sigmoid(value):
    return 1.0 / (1.0 + jnp.exp(-value))


def norm_rows(block, gain):
    wide = block.astype(f32)
    scale = lax.rsqrt(jnp.mean(wide * wide, axis=-1, keepdims=True) + epsilon)
    return (wide * scale * gain.reshape(1, -1)).astype(bf16)


def pre_kernel(
    seq, up, low, high, gain, in_proj, step_proj, conv_w, conv_b, step_bias, decay_log, out_proj,
    payload, both, normal, normal_halo, cot, gate, conv, d_gated, raw, step, cumul, cumul_t,
    ext,
):
    rows = seq.shape[0]
    inner = out_proj.shape[0]
    heads = step_bias.shape[0]
    state = (conv_w.shape[1] - inner) // 2
    taps = conv_w.shape[0]
    both[:rows, :] = seq[...]
    both[rows:, :] = mirror_exact(seq[...])
    cot[:rows, :] = up[...]
    cot[rows:, :] = mirror_exact(up[...])
    halo = jnp.concatenate([low[...], mirror_exact(high[...])], axis=0)
    normal[...] = norm_rows(both[...], gain[...])
    normal_halo[...] = norm_rows(halo, gain[...])
    gate[...] = mm(normal[...], in_proj[:, :inner])
    xbc = mm(normal[...], in_proj[:, inner:]).astype(bf16).astype(f32)
    xbc_halo = mm(normal_halo[...], in_proj[:, inner:]).astype(bf16).astype(f32)
    raw[...] = mm_cols(normal[...], step_proj[...])
    d_gated[...] = mm_cols(cot[...], out_proj[...]).astype(bf16)
    margin = low.shape[0]
    mask = head_mask(heads, inner // heads)
    ends = []
    for frame in range(2):
        at = slice(frame * rows, (frame + 1) * rows)
        ext[:8, :] = xbc_halo[(frame + 1) * margin - 8 : (frame + 1) * margin, :]
        ext[8:, :] = xbc[at, :]
        found = conv_b[...].reshape(1, -1)
        for tap in range(taps):
            start = 9 - taps + tap
            found = found + ext[start : start + rows, :] * conv_w[tap : tap + 1, :]
        conv[at, :] = found
        act = found * sigmoid(found)
        size = softplus(raw[at, :] + step_bias[...].reshape(1, -1))
        decay = -jnp.exp(decay_log[...].reshape(1, -1)) * size
        upto = tri_sum(triangle(rows, True), decay)
        step[at, :] = size
        cumul[at, :] = upto
        cumul_t[frame * heads : (frame + 1) * heads, :] = tri_sum_turned(triangle(rows, False), decay)
        end = upto[rows - 1 : rows, :]
        ends.append(end)
        spread = expand(jnp.concatenate([size * jnp.exp(end - upto), jnp.exp(upto)], axis=0), mask)
        driven = (act[:, :inner] * spread[:rows]).astype(bf16)
        local = mm_rows(driven, act[:, inner : inner + state].astype(bf16))
        wide = gate[at, :]
        d_mixed = d_gated[at, :].astype(f32) * (wide * sigmoid(wide))
        back = mm_rows((d_mixed * spread[rows:]).astype(bf16), act[:, inner + state :].astype(bf16))
        part = inner // SIDE
        for place, block in ((frame, local), (2 + frame, back)):
            block = block.astype(bf16).reshape(SIDE, part, state)
            payload[:, place * part : (place + 1) * part, :] = block
    packed = pack_totals(ends, heads, state)
    for to in range(SIDE):
        shifted = ones_where(iota((16, heads), 1) == iota((16, heads), 0) + to * (heads // SIDE))
        payload[to, inner:, :] = mm(shifted, packed).astype(bf16)


def pack_totals(ends, heads, state):
    chosen = iota((heads, heads), 0) == iota((heads, heads), 1)
    lanes = iota((heads, state), 1)
    packed = jnp.zeros((heads, state), f32)
    for frame in range(2):
        column = jnp.sum(jnp.where(chosen, ends[frame], 0.0), axis=1, keepdims=True)
        packed = pack_column(packed, column, lanes, frame)
    return packed.astype(bf16)


def pack_column(packed, column, lanes, frame):
    for nth, piece in enumerate(pieces_of(column, 3)):
        packed = jnp.where(lanes == 3 * frame + nth, piece.astype(f32), packed)
    return packed


def unpack_column(packed, frame):
    at = 3 * frame
    return (packed[:, at + 2 : at + 3] + packed[:, at + 1 : at + 2]) + packed[:, at : at + 1]


SCANS = ((0, False), (1, True), (0, True), (1, False))


def chain(got, totals, place, state, visit):
    frame, turned = SCANS[place]
    part = state.shape[0]
    size = part // SIDE
    order = range(SIDE - 1, -1, -1) if turned else range(SIDE)
    for at in order:
        visit(at, state)
        grown = jnp.exp(totals[at][frame])
        factors = [
            jnp.broadcast_to(grown[head : head + 1, :], (size, 1)) for head in range(part // size)
        ]
        state = jnp.concatenate(factors, axis=0) * state
        state = state + got[at, place * part : (place + 1) * part, :].astype(f32)
    return state


def tails_of(got, inner):
    found = []
    for at in range(SIDE):
        tail = got[at, inner:, :].astype(f32)
        found.append([unpack_column(tail, frame) for frame in range(2)])
    return found


def group_kernel(got, out):
    state = got.shape[2]
    inner = got.shape[1] - 16
    part = inner // SIDE
    totals = tails_of(got, inner)
    for place in range(4):
        block = chain(got, totals, place, jnp.zeros((part, state), f32), lambda at, value: None)
        out[:, 16 * place : 16 * place + 16, :] = block.reshape(16, 16, state).astype(bf16)
    lanes = iota((16, state), 1)
    packed = jnp.zeros((16, state), f32)
    for frame in range(2):
        column = jnp.maximum(totals[0][frame], -110.0)
        for at in range(1, SIDE):
            column = column + jnp.maximum(totals[at][frame], -110.0)
        packed = pack_column(packed, column, lanes, frame)
    chosen = ones_where(iota((16, 16), 1) == iota((16, 16), 0) // SIDE)
    packed = mm(chosen, packed.astype(bf16))
    out[:, 64:, :] = jnp.broadcast_to(packed.reshape(16, 1, state), (16, 8, state)).astype(bf16)


def spread_kernel(got, entering, out):
    state = got.shape[2]
    inner = got.shape[1] - 16
    part = inner // SIDE
    totals = tails_of(got, inner)
    for place in range(4):

        def visit(at, value, place=place):
            out[at, place * part : (place + 1) * part, :] = value.astype(bf16)

        block = entering[:, 16 * place : 16 * place + 16, :].astype(f32).reshape(part, state)
        chain(got, totals, place, block, visit)


def scan_kernel(got, out, wide, done):
    count, rows, state = got.shape
    wide[...] = got[...].astype(f32).reshape(count * rows, state)
    tails = wide[pl.ds(64, count, stride=rows), :]
    above = iota((count, count), 0)
    beside = iota((count, count), 1)
    after = ones_where(above > beside)
    weights = []
    for frame in range(2):
        column = jnp.maximum(unpack_column(tails, frame), -110.0)
        line = jnp.sum(jnp.where(above == beside, column, 0.0), axis=0, keepdims=True)
        between = None
        for piece in pieces_of(jnp.where(beside < above, line, 0.0), 3):
            part = mm(piece, after)
            between = part if between is None else between + part
        found = jnp.where(above > beside, jnp.exp(between), 0.0)
        weights.append(pieces_of(found, 2))
    for place, (frame, turned) in enumerate(SCANS):
        pair = weights[frame]
        block = jnp.concatenate(
            [wide[pl.ds(16 * place + row, count, stride=rows), :] for row in range(16)], axis=1
        ).astype(bf16)
        if turned:
            mixed = mm_rows(jnp.concatenate(pair, axis=1), block)
        else:
            mixed = mm(jnp.concatenate(pair, axis=0), block)
        mixed = mixed[:count] + mixed[count:]
        for row in range(16):
            done[pl.ds(16 * place + row, count, stride=64), :] = mixed[:, state * row : state * (row + 1)]
    out[...] = done[...].reshape(count, 64, state).astype(bf16)


def intra_kernel(conv, gate, d_gated, step, cumul, cumul_t, mixed, d_driven, d_bc, d_cumul):
    rows = conv.shape[0] // 2
    inner = gate.shape[1]
    heads = step.shape[1]
    state = (conv.shape[1] - inner) // 2
    mask = head_mask(heads, inner // heads)
    lower = triangle(rows, True)
    first = iota((rows, 2 * inner // heads), 1) < inner // heads
    wide_pair = 2 * inner // heads
    for frame in range(2):
        at = slice(frame * rows, (frame + 1) * rows)
        found = conv[at, :]
        act = found * sigmoid(found)
        bmat = act[:, inner : inner + state].astype(bf16)
        cmat = act[:, inner + state :].astype(bf16)
        driven = act[:, :inner] * expand(step[at, :], mask)
        wide = gate[at, :]
        d_mixed = d_gated[at, :].astype(f32) * (wide * sigmoid(wide))
        scores = mm_cols(cmat, bmat)
        upto, line = cumul[at, :], cumul_t[frame * heads : (frame + 1) * heads, :]
        d_scores = jnp.zeros((rows, rows), f32)
        sums = []
        for pair in range(heads // 2):
            lanes = slice(pair * wide_pair, (pair + 1) * wide_pair)
            decays = []
            for head in (2 * pair, 2 * pair + 1):
                differ = upto[:, head : head + 1] - line[head : head + 1, :]
                decays.append(jnp.exp(jnp.where(lower, differ, -1e30)))
            weights = [(decay * scores).astype(bf16) for decay in decays]
            drive, d_mix = driven[:, lanes], d_mixed[:, lanes]
            drive_bf, d_mix_bf = drive.astype(bf16), d_mix.astype(bf16)
            drive_two = jnp.concatenate(
                [jnp.where(first, drive, 0.0), jnp.where(first, 0.0, drive)], axis=0
            ).astype(bf16)
            d_mix_two = jnp.concatenate(
                [jnp.where(first, d_mix, 0.0), jnp.where(first, 0.0, d_mix)], axis=0
            ).astype(bf16)
            mix = mm(jnp.concatenate(weights, axis=1), drive_two)
            d_weights = mm_cols(d_mix_two, drive_bf)
            d_drive = mm_rows(jnp.concatenate(weights, axis=0), d_mix_two)
            d_scores = d_scores + decays[0] * d_weights[:rows] + decays[1] * d_weights[rows:]
            mixed[at, lanes] = mix
            d_driven[at, lanes] = d_drive
            sums.append(d_mix_bf.astype(f32) * mix - drive_bf.astype(f32) * d_drive)
        d_scores = d_scores.astype(bf16)
        d_bc[at, :state] = mm_rows(d_scores, cmat)
        d_bc[at, state:] = mm(d_scores, bmat)
        d_cumul[at, :] = fold(jnp.concatenate(sums, axis=1), mask)


def post_kernel(
    place, got, conv, gate, d_gated, raw, step, cumul, mixed, d_driven, d_bc, d_cumul, step_bias, decay_log, skip_gain,
    conv_w, cot, normal, normal_halo,
    gated, d_gate, d_xbc, d_edge, d_ahead, d_step, *refs,
):
    by_x, by_y, ext, d_conv_out, whole, parted = refs[:4], refs[4:8], refs[8], refs[9], refs[10], refs[11]
    rows = conv.shape[0] // 2
    inner = gate.shape[1]
    heads = step.shape[1]
    state = (conv.shape[1] - inner) // 2
    mask = head_mask(heads, inner // heads)
    skip = expand(jnp.broadcast_to(skip_gain[...].reshape(1, -1), (8, heads)), mask)[:1]
    for frame in range(2):
        at = slice(frame * rows, (frame + 1) * rows)
        found = conv[at, :]
        share = sigmoid(found)
        act = found * share
        inputs = act[:, :inner]
        bmat = act[:, inner : inner + state].astype(bf16)
        cmat = act[:, inner + state :].astype(bf16)
        upto = cumul[at, :]
        end = upto[rows - 1 : rows, :]
        spread = expand(jnp.concatenate([step[at, :], jnp.exp(upto), jnp.exp(end - upto)], axis=0), mask)
        sizes, grown, left = spread[:rows], spread[rows : 2 * rows], spread[2 * rows :]
        part = inner // SIDE
        carried = got[:, frame * part : (frame + 1) * part, :].reshape(inner, state)
        reach = got[:, (2 + frame) * part : (3 + frame) * part, :].reshape(inner, state)
        inter = grown * mm_cols(cmat, carried)
        full = mixed[at, :] + inter + skip * inputs
        wide = gate[at, :]
        opened = sigmoid(wide)
        silu = wide * opened
        gated[at, :] = (full * silu).astype(bf16)
        d_out = d_gated[at, :].astype(f32)
        d_gate[at, :] = (d_out * full * (opened * (1.0 + wide * (1.0 - opened)))).astype(bf16)
        d_mixed = d_out * silu
        d_cmat = d_bc[at, state:] + mm((d_mixed * grown).astype(bf16), carried)
        answer = left * mm_cols(bmat, reach)
        driven = inputs * sizes
        d_drive = d_driven[at, :] + answer
        d_bmat = d_bc[at, :state] + mm((left * driven).astype(bf16), reach)
        products = carried.astype(f32) * reach.astype(f32)
        met = jnp.sum(products.reshape(heads, inner // heads, state), axis=1)
        met = jnp.sum(met, axis=1, keepdims=True)
        met = jnp.sum(jnp.where(iota((heads, heads), 0) == iota((heads, heads), 1), met, 0.0), axis=0, keepdims=True)
        folded = fold(jnp.concatenate([driven * answer, d_mixed * inter, d_drive * inputs], axis=0), mask)
        held, entered, by_size = folded[:rows], folded[rows : 2 * rows], folded[2 * rows :]
        d_end = jnp.exp(end) * met + jnp.sum(held, axis=0, keepdims=True)
        d_decay = tri_sum(triangle(rows, False), d_cumul[at, :] + entered - held) + d_end
        d_size = by_size - jnp.exp(decay_log[...].reshape(1, -1)) * d_decay
        d_step[at, :] = (d_size * sigmoid(raw[at, :] + step_bias[...].reshape(1, -1))).astype(bf16)
        d_act = jnp.concatenate([skip * d_mixed + d_drive * sizes, d_bmat, d_cmat], axis=1)
        margin = normal_halo.shape[0] // 2
        ext[:margin, :] = jnp.zeros((margin, ext.shape[1]), f32)
        ext[margin : margin + rows, :] = d_act * (share * (1.0 + found * (1.0 - share)))
        ext[margin + rows :, :] = jnp.zeros((8, ext.shape[1]), f32)
        taps = conv_w.shape[0]
        total = None
        for tap in range(taps):
            start = taps - 1 - tap
            part = ext[start : start + margin + rows, :] * conv_w[tap : tap + 1, :]
            total = part if total is None else total + part
        d_xbc[at, :] = total[margin:].astype(bf16)
        d_conv_out[frame * margin : (frame + 1) * margin, :] = total[:margin].astype(bf16)
        d_ahead[8 * frame : 8 * frame + 8, :] = total[margin - 8 : margin]
        d_edge[8 * frame : 8 * frame + 8, :] = total[margin + rows - 8 :]
    columns = cot.shape[1]
    half = d_xbc.shape[1] // 2
    out_term = mm_rows(gated[...], cot[...]).reshape(COUNT, 2, 8, columns)
    gate_term = mm_rows(normal[...], d_gate[...]).reshape(COUNT // SIDE, SIDE, 8, inner)
    in_term = mm_rows(normal[...], d_xbc[...]) + mm_rows(normal_halo[...], d_conv_out[...])
    whole[:, :columns] = out_term[:, 0].reshape(-1, columns)
    whole[:, columns : 2 * columns] = out_term[:, 1].reshape(-1, columns)
    whole[:, 2 * columns :] = in_term[:, :half]
    parted[:, :, :, :inner] = gate_term
    parted[:, :, :, inner:] = in_term[:, half:].reshape(COUNT // SIDE, SIDE, 8, half)
    send_x(place, whole, by_x)
    send_y(place, parted, by_y)


def send_x(place, whole, slots):
    chunk = whole.shape[0] // SIDE
    for step in range(SIDE):
        to = lax.rem(place[0] + step, SIDE)
        block = whole[pl.ds(pl.multiple_of(to * chunk, chunk), chunk), :]
        slots[step][...] = block.astype(slots[step].dtype)


def send_y(place, parted, slots):
    for step in range(SIDE):
        block = parted[:, lax.rem(place[2] + step, SIDE)]
        slots[step][...] = block.reshape(slots[step].shape).astype(slots[step].dtype)


def result_kernel(
    both, gain, gated, out_proj, d_gate, d_xbc, d_edge, ahead, behind, d_step, in_proj, step_proj,
    layer, grad, d_whole,
):
    rows = both.shape[0] // 2
    inner = out_proj.shape[0]
    branch = mm(gated[...], out_proj[...])
    layer[...] = (branch[:rows] + mirror_wide(branch[rows:])).astype(bf16)
    d_whole[...] = d_xbc[...]
    for frame, halo in enumerate((ahead, behind)):
        edge = d_edge[8 * frame : 8 * frame + 8, :] + halo[...]
        keep = d_xbc[(frame + 1) * rows - 16 : (frame + 1) * rows, :].astype(f32)
        edge = jnp.concatenate([keep[:8], edge], axis=0)
        d_whole[(frame + 1) * rows - 16 : (frame + 1) * rows, :] = edge.astype(bf16)
    d_normal = mm_cols(d_gate[...], in_proj[:, :inner]) + mm_cols(d_whole[...], in_proj[:, inner:])
    d_normal = d_normal + mm(d_step[...], step_proj[...])
    wide = both[...].astype(f32)
    scale = lax.rsqrt(jnp.mean(wide * wide, axis=-1, keepdims=True) + epsilon)
    d_scaled = d_normal * gain[...].reshape(1, -1)
    along = jnp.mean(d_scaled * wide, axis=-1, keepdims=True)
    d_wide = scale * d_scaled - wide * (scale * scale * scale * along)
    grad[...] = (d_wide[:rows] + mirror_wide(d_wide[rows:])).astype(bf16)


def total_of(refs):
    total = refs[0][...].astype(f32)
    for ref in refs[1:]:
        total = total + ref[...].astype(f32)
    return total


def first_sum_kernel(place, *refs):
    from_x, from_y, by_y, by_x, parted, whole = refs[:4], refs[4:8], refs[9:13], refs[13:17], refs[17], refs[18]
    parted[...] = total_of(from_x).reshape(parted.shape)
    whole[...] = total_of(from_y)
    send_y(place, parted, by_y)
    send_x(place, whole, by_x)


def second_sum_kernel(place, *refs):
    first, second, by_z, keep = refs[:4], refs[4:8], refs[8:12], refs[12]
    keep[:, 0] = total_of(first).reshape(SIDE, 8, -1)
    keep[:, 1] = total_of(second).reshape(SIDE, 8, -1)
    for step in range(SIDE):
        to = lax.rem(place[1] + step, SIDE)
        by_z[step][...] = keep[to].reshape(by_z[step].shape).astype(by_z[step].dtype)


def last_sum_kernel(*refs):
    grad_in, grad_out = refs[4:]
    total = total_of(refs[:4])
    columns = grad_out.shape[1]
    grad_out[:8, :] = total[:8, :columns]
    grad_out[8:, :] = total[:8, columns : 2 * columns]
    grad_in[...] = jnp.concatenate([total[8:, : 2 * columns], total[:8, 2 * columns :], total[8:, 2 * columns :]], axis=1)


def axis_pairs(stride, step):
    pairs = []
    for source in range(COUNT):
        digit = source // stride % SIDE
        pairs.append((source, source + ((digit + step) % SIDE - digit) * stride))
    return pairs


def exchange(parts, stride):
    return [parts[0]] + [lax.ppermute(parts[step], "seq", axis_pairs(stride, step)) for step in range(1, SIDE)]


def transpose_over(parts, groups):
    return lax.all_to_all(parts, "seq", 0, 0, axis_index_groups=groups)


def slots(rows, columns, kind):
    return [((rows, columns), kind)] + [((rows, columns), bf16)] * (SIDE - 1)


def shards(
    sequence,
    upstream,
    norm_gain,
    in_proj,
    step_proj,
    conv_weight,
    conv_bias,
    step_bias,
    decay_log,
    skip_gain,
    out_proj,
):
    rows, width = sequence.shape
    inner = out_proj.shape[0]
    heads = step_bias.shape[0]
    state = inner // heads * 2
    channels = conv_weight.shape[1]
    both_rows = 2 * rows
    stride_x, stride_z, stride_y = SIDE * SIDE, SIDE, 1
    index = lax.axis_index("seq")
    place = jnp.stack([index // stride_x, index // stride_z % SIDE, index % SIDE]).astype(jnp.int32)
    beside = [[SIDE * base + digit for digit in range(SIDE)] for base in range(COUNT // SIDE)]
    across = [[base + SIDE * digit for digit in range(COUNT // SIDE)] for base in range(SIDE)]
    upward = [(i, i + 1) for i in range(COUNT - 1)]
    downward = [(i + 1, i) for i in range(COUNT - 1)]
    low = lax.ppermute(sequence[rows - 16 :], "seq", upward)
    high = lax.ppermute(sequence[:16], "seq", downward)
    step_turned = step_proj.T
    payload, both, normal, normal_halo, cot, gate, conv, d_gated, raw, step, cumul, cumul_t = call(
        pre_kernel,
        [
            ((SIDE, inner + 16, state), bf16),
            ((both_rows, width), bf16),
            ((both_rows, width), bf16),
            ((32, width), bf16),
            ((both_rows, width), bf16),
            ((both_rows, inner), f32),
            ((both_rows, channels), f32),
            ((both_rows, inner), bf16),
            ((both_rows, heads), f32),
            ((both_rows, heads), f32),
            ((both_rows, heads), f32),
            ((2 * heads, rows), f32),
        ],
        (
            sequence, upstream, low, high, norm_gain, in_proj, step_turned,
            conv_weight, conv_bias, step_bias, decay_log, out_proj,
        ),
        [pltpu.VMEM((rows + 8, channels), f32)],
    )
    got = transpose_over(payload, beside)
    (summary,) = call(group_kernel, [((COUNT // SIDE, 72, state), bf16)], (got,), vmem=16 * 2**20)
    summaries = transpose_over(summary, across)
    mixed, d_driven, d_bc, d_cumul = call(
        intra_kernel,
        [
            ((both_rows, inner), f32),
            ((both_rows, inner), f32),
            ((both_rows, 2 * state), f32),
            ((both_rows, heads), f32),
        ],
        (conv, gate, d_gated, step, cumul, cumul_t),
        flops=8 * 10**9,
    )
    groups = COUNT // SIDE
    (scanned,) = call(
        scan_kernel,
        [((groups, 64, state), bf16)],
        (summaries,),
        [pltpu.VMEM((groups * 72, state), f32), pltpu.VMEM((groups * 64, state), f32)],
        vmem=16 * 2**20,
    )
    entering = transpose_over(scanned, across)
    (spread,) = call(spread_kernel, [((SIDE, inner, state), bf16)], (got, entering), vmem=16 * 2**20)
    states = transpose_over(spread, beside)
    eighth = 8 * COUNT // SIDE
    joined = inner + channels // 2
    gated, d_gate, d_xbc, d_edge, d_ahead, d_step, *parts = call(
        post_kernel,
        [
            ((both_rows, inner), bf16),
            ((both_rows, inner), bf16),
            ((both_rows, channels), bf16),
            ((16, channels), f32),
            ((16, channels), f32),
            ((both_rows, heads), bf16),
        ]
        + slots(eighth, joined, bf16) * 2,
        (
            place, states, conv, gate, d_gated, raw, step, cumul, mixed, d_driven, d_bc, d_cumul,
            step_bias, decay_log, skip_gain, conv_weight, cot, normal, normal_halo,
        ),
        [
            pltpu.VMEM((rows + 24, channels), f32),
            pltpu.VMEM((32, channels), bf16),
            pltpu.VMEM((8 * COUNT, joined), f32),
            pltpu.VMEM((COUNT // SIDE, SIDE, 8, joined), f32),
        ],
        scalars=1,
    )
    from_x = exchange(parts[:4], stride_x)
    from_y = exchange(parts[4:], stride_y)
    ahead = lax.ppermute(d_ahead[:8], "seq", downward)
    behind = lax.ppermute(d_ahead[8:], "seq", upward)
    layer_out, grad_input = call(
        result_kernel,
        [((rows, width), bf16), ((rows, width), bf16)],
        (
            both, norm_gain, gated, out_proj, d_gate, d_xbc, d_edge, ahead, behind, d_step,
            in_proj, step_turned,
        ),
        [pltpu.VMEM((both_rows, channels), bf16)],
        flops=8 * 10**9,
    )
    parts = call(
        first_sum_kernel,
        slots(eighth // SIDE, joined, f32) * 2,
        (place, *from_x, *from_y, layer_out),
        [pltpu.VMEM((SIDE, SIDE, 8, joined), f32), pltpu.VMEM((eighth, joined), f32)],
        scalars=1,
        vmem=16 * 2**20,
    )
    first = exchange(parts[:4], stride_y)
    second = exchange(parts[4:], stride_x)
    parts = call(
        second_sum_kernel,
        slots(16, joined, f32),
        (place, *first, *second),
        [pltpu.VMEM((SIDE, 2, 8, joined), f32)],
        scalars=1,
        vmem=16 * 2**20,
    )
    last = exchange(parts, stride_z)
    grad_in_proj, grad_out_proj = call(
        last_sum_kernel,
        [((8, inner + channels), f32), ((16, width), f32)],
        tuple(last),
        vmem=16 * 2**20,
    )
    return (layer_out, grad_input, grad_in_proj, grad_out_proj)


def solution(mesh):
    rows = P(("batch", "seq"), None)
    return jax.shard_map(
        shards,
        mesh=mesh,
        in_specs=(rows, rows) + (P(),) * 9,
        out_specs=(rows,) * 4,
        check_vma=False,
    )
```

time: 200 us -> 173 us (0.86)
  local copies, waits for them, and re-layouts: 25.3 us -> 4.06 us
  waiting for transfers between devices: 54.9 us -> 42.9 us
  Pallas kernels: 24.9 us -> 36.4 us
  blocking collectives: 41.8 us -> 31.9 us
  starting transfers between devices: 49 us -> 55.2 us
    unnamed x85 -> x18, local copies, waits for them, and re-layouts: 23.8 us -> 2.52 us
    ppermute x21 -> x15, waiting for transfers between devices: 31.8 us -> 18.3 us  [exchange(): lax.ppermute(parts[step], 'seq', axis_pairs(stride, step))]
    pallas_call x10, Pallas kernels: 24.9 us -> 36.4 us  [call(): pl.pallas_call(body, out_shape=[jax.ShapeDtypeStruct(shape, kind) for sha...]
    all_to_all x1 -> x2, blocking collectives: 41.8 us -> 31.9 us  [transpose_over(): return lax.all_to_all(parts, 'seq', 0, 0, axis_index_groups=groups)]
    ppermute x1, waiting for transfers between devices: 0.01 us -> 8.8 us  [shards(): low = lax.ppermute(sequence[rows - 16:], 'seq', upward)]
    ppermute x2, waiting for transfers between devices: 9.74 us -> 1.36 us  [the longest x1 1.06 us: shards(): ahead = lax.ppermute(d_ahead[:8], 'seq', downward)]
    ppermute x2, starting transfers between devices: 7.43 us -> 10.9 us  [the longest x1 8.47 us: shards(): ahead = lax.ppermute(d_ahead[:8], 'seq', downward)]
    ppermute x21 -> x15, starting transfers between devices: 20.4 us -> 22 us  [exchange(): lax.ppermute(parts[step], 'seq', axis_pairs(stride, step))]
  transfers between devices with their start and end apart: 26 -> 21, of which waited for: 17 -> 15; matrix products, arithmetic and copies ran while one was open for 1% -> 1% of each run, Pallas kernels for 4% -> 7%
where the time goes in v2:
time: 173 us; the launch traced here: 172 us
  starting transfers between devices  55.2 us (32%)
  waiting for transfers between devices  42.9 us (25%)
  Pallas kernels  36.4 us (21%)
  blocking collectives  31.9 us (18%)
  local copies, waits for them, and re-layouts  4.06 us (2%)
    pallas_call x10, Pallas kernels, call(): pl.pallas_call(body, out_shape=[jax.ShapeDtypeStruct(shape, kind) for sha...  36.4 us
    all_to_all x2, blocking collectives, transpose_over(): return lax.all_to_all(parts, 'seq', 0, 0, axis_index_groups=groups)  31.9 us
    ppermute x15, starting transfers between devices, exchange(): lax.ppermute(parts[step], 'seq', axis_pairs(stride, step))  22 us
    ppermute x15, waiting for transfers between devices, exchange(): lax.ppermute(parts[step], 'seq', axis_pairs(stride, step))  18.3 us
    all_to_all x2, waiting for transfers between devices, transpose_over(): return lax.all_to_all(parts, 'seq', 0, 0, axis_index_groups=groups)  14.4 us
    ppermute x1, starting transfers between devices, shards(): high = lax.ppermute(sequence[:16], 'seq', downward)  10.9 us
    all_to_all x2, starting transfers between devices, transpose_over(): return lax.all_to_all(parts, 'seq', 0, 0, axis_index_groups=groups)  9.47 us
    ppermute x1, waiting for transfers between devices, shards(): low = lax.ppermute(sequence[rows - 16:], 'seq', upward)  8.8 us
  transfers between devices with their start and end apart: 21, of which 15 were waited for; matrix products, arithmetic and copies ran while one was open for 1% of the time, Pallas kernels for 7%

profile of v2, /device:TPU:6, one launch (start us, length us, event | category | flops | bytes accessed | tf_op | source)
XLA Modules:
  0.0 171.8 jit_solution(5993631284632471433)
XLA Ops:
  0.6 0.7 fusion
  1.4 10.9 %collective-permute-start.1 = (bf16[16,512]{1,0:T(8,128)(2,1)S(1)}, bf16[16,512]{1,0:T(8,128)(2,1)S(1)}, u32[]{:S(2)}, u32[]{:S(2)}) collective-permute-start(bf16[16,512]{1,0:T(8,128)(2,1)S(1)} %get-tuple-element.96), channel_id=1, source_target_pairs={{4,0},{8,4},{12,8},{16,12},{20,16},{24,20},{28,24},{32,28},{36,32}... | collective-permute-start | bytes 49160 | tf_op jit(solution)/shard_map/ppermute | solution.py:551
  12.3 1.9 %collective-permute-start = (bf16[16,512]{1,0:T(8,128)(2,1)S(1)}, bf16[16,512]{1,0:T(8,128)(2,1)S(1)}, u32[]{:S(2)}, u32[]{:S(2)}) collective-permute-start(bf16[16,512]{1,0:T(8,128)(2,1)S(1)} %get-tuple-element.97), channel_id=1, source_target_pairs={{0,4},{4,8},{8,12},{12,16},{16,20},{20,24},{24,28},{28,32},{32,36}... | collective-permute-start | bytes 49160 | tf_op jit(solution)/shard_map/ppermute | solution.py:550
  14.2 0.0 collective-permute-done.1.high
  14.2 0.0 copy-start.5
  14.2 8.8 %collective-permute-done.low = bf16[16,512]{1,0:T(8,128)(2,1)S(1)} collective-permute-done((bf16[16,512]{1,0:T(8,128)(2,1)S(1)}, bf16[16,512]{1,0:T(8,128)(2,1)S(1)}, u32[]{:S(2)}, u32[]{:S(2)}) %collective-permute-start) | collective-permute-done | bytes 16416 | tf_op jit(solution)/shard_map/ppermute | solution.py:550
  23.0 0.0 copy-done.5
  23.0 0.6 copy-done.6
  23.6 7.0 %shard_map.138 = (bf16[4,1040,128]{2,1,0:T(8,128)(2,1)}, bf16[256,512]{1,0:T(8,128)(2,1)}, bf16[256,512]{1,0:T(8,128)(2,1)}, bf16[32,512]{1,0:T(8,128)(2,1)}, bf...) custom-call(bf16[128,512]{1,0:T(8,128)(2,1)} %seq.1, ...), custom_call_target="tpu_custom_call" | custom-call | flops 1000000000 | bytes 3746944 | tf_op jit(solution)/shard_map/pallas_call | solution.py:22
  30.6 17.6 %all_to_all.20.got = bf16[4,1040,128]{2,1,0:T(8,128)(2,1)S(1)} all-to-all(bf16[4,1040,128]{2,1,0:T(8,128)(2,1)} %get-tuple-element.51), channel_id=1, replica_groups={{0,4,8,12},{16,20,24,28},{32,36,40,44},{48,52,56,60},{64,68,72,76},{80,..., dimensions={0} | all-to-all | bytes 2129920 | tf_op jit(solution)/shard_map/all_to_all | solution.py:517
  48.3 0.4 shard_map.139
  48.6 14.2 %all_to_all.21.got = bf16[16,72,128]{2,1,0:T(8,128)(2,1)S(1)} all-to-all(bf16[16,72,128]{2,1,0:T(8,128)(2,1)S(1)} %shard_map.139), channel_id=1, replica_groups={{0,16,32,48,64,80,96,112,128,144,160,176,192,208,224,240},{4,20,36,52,6..., dimensions={0} | all-to-all | bytes 589824 | tf_op jit(solution)/shard_map/all_to_all | solution.py:517
  62.9 1.6 shard_map.140
  64.5 5.8 %all-to-all-start.2 = ((bf16[16,64,128]{2,1,0:T(8,128)(2,1)}), bf16[16,64,128]{2,1,0:T(8,128)(2,1)S(1)}, u32[]{:S(2)}, u32[]{:S(2)}) async-start(bf16[16,64,128]{2,1,0:T(8,128)(2,1)} %shard_map.140), calls=%async_computation.2 | async-start | bytes 524288 | tf_op jit(solution)/shard_map/all_to_all | solution.py:517
  70.2 9.8 %all-to-all-done.2.entering = bf16[16,64,128]{2,1,0:T(8,128)(2,1)S(1)} async-done(((bf16[16,64,128]{2,1,0:T(8,128)(2,1)}), bf16[16,64,128]{2,1,0:T(8,128)(2,1)S(1)}, u32[]{:S(2)}, u32[]{:S(2)}) %all-to-all-start.2) | async-done | bytes 262176 | tf_op jit(solution)/shard_map/all_to_all | solution.py:517
  80.0 1.3 shard_map.141
  81.4 3.7 %all-to-all-start.3 = ((bf16[4,1024,128]{2,1,0:T(8,128)(2,1)}), bf16[4,1024,128]{2,1,0:T(8,128)(2,1)S(1)}, u32[]{:S(2)}, u32[]{:S(2)}) async-start(bf16[4,1024,128]{2,1,0:T(8,128)(2,1)} %shard_map.141), calls=%async_computation.3 | async-start | bytes 2097152 | tf_op jit(solution)/shard_map/all_to_all | solution.py:517
  85.1 0.6 pad_add_fusion.place
  85.7 5.4 %shard_map.142 = (f32[256,1024]{1,0:T(8,128)}, f32[256,1024]{1,0:T(8,128)}, f32[256,256]{1,0:T(8,128)}, f32[256,16]{1,0:T(8,128)}) custom-call(f32[256,1280]{1,0:T(8,128)} %get-tuple-element.52.conv, f32[256,1024]{1,0:T(8,128)} %get-tuple-element.53.gate, bf16[256,1024]{1,0:T(8,128)(2,1)} %get-tuple-element.54.d_gated, f32[256,16]{1,0:T(8,128)} %get-tuple-element.56.step, ...), custom_call_target="tpu_custom_call" | custom-call | flops 8000000000 | bytes 2932736 | tf_op jit(solution)/shard_map/pallas_call | solution.py:22
  91.1 4.7 %all-to-all-done.3.got = bf16[4,1024,128]{2,1,0:T(8,128)(2,1)S(1)} async-done(((bf16[4,1024,128]{2,1,0:T(8,128)(2,1)}), bf16[4,1024,128]{2,1,0:T(8,128)(2,1)S(1)}, u32[]{:S(2)}, u32[]{:S(2)}) %all-to-all-start.3) | async-done | bytes 1048608 | tf_op jit(solution)/shard_map/all_to_all | solution.py:517
  95.7 1.0 copy-done.4
  96.7 12.2 %shard_map.143 = (bf16[256,1024]{1,0:T(8,128)(2,1)}, bf16[256,1024]{1,0:T(8,128)(2,1)}, bf16[256,1280]{1,0:T(8,128)(2,1)}, f32[16,1280]{1,0:T(8,128)}, f32[16,12...) custom-call(s32[3]{0:T(128)} %pad_add_fusion.place, ...), custom_call_target="tpu_custom_call" | custom-call | flops 1000000000 | bytes 6934732 | tf_op jit(solution)/shard_map/pallas_call | solution.py:22
  108.9 2.5 %collective-permute-start.4 = (bf16[128,1664]{1,0:T(8,128)(2,1)}, bf16[128,1664]{1,0:T(8,128)(2,1)S(1)}, u32[]{:S(2)}, u32[]{:S(2)}) collective-permute-start(bf16[128,1664]{1,0:T(8,128)(2,1)} %get-tuple-element.75), channel_id=1, source_target_pairs={{0,64},{4,68},{8,72},{12,76},{16,80},{20,84},{24,88},{28,92},{32,9... | collective-permute-start | bytes 1277960 | tf_op jit(solution)/shard_map/ppermute | solution.py:513
  111.4 0.8 fusion.1
  112.2 2.5 %collective-permute-start.3 = (f32[8,1280]{1,0:T(8,128)S(1)}, f32[8,1280]{1,0:T(8,128)S(1)}, u32[]{:S(2)}, u32[]{:S(2)}) collective-permute-start(f32[8,1280]{1,0:T(8,128)S(1)} %get-tuple-element.98), channel_id=1, source_target_pairs={{0,4},{4,8},{8,12},{12,16},{16,20},{20,24},{24,28},{28,32},{32,36}... | collective-permute-start | bytes 122888 | tf_op jit(solution)/shard_map/ppermute | solution.py:628
  114.7 8.5 %collective-permute-start.2 = (f32[8,1280]{1,0:T(8,128)S(1)}, f32[8,1280]{1,0:T(8,128)S(1)}, u32[]{:S(2)}, u32[]{:S(2)}) collective-permute-start(f32[8,1280]{1,0:T(8,128)S(1)} %get-tuple-element.99), channel_id=1, source_target_pairs={{4,0},{8,4},{12,8},{16,12},{20,16},{24,20},{28,24},{32,28},{36,32}... | collective-permute-start | bytes 122888 | tf_op jit(solution)/shard_map/ppermute | solution.py:627
  123.2 0.3 collective-permute-start.5
  123.4 0.0 collective-permute-start.6
  123.4 0.3 collective-permute-done.3.behind
  123.7 0.0 collective-permute-start.7
  123.7 1.1 collective-permute-done.2.ahead
  124.8 0.0 collective-permute-start.8
  124.8 0.0 collective-permute-done.4.refs_1_
  124.8 2.3 %collective-permute-start.9 = (bf16[128,1664]{1,0:T(8,128)(2,1)}, bf16[128,1664]{1,0:T(8,128)(2,1)S(1)}, u32[]{:S(2)}, u32[]{:S(2)}) collective-permute-start(bf16[128,1664]{1,0:T(8,128)(2,1)} %get-tuple-element.81), channel_id=1, source_target_pairs={{0,12},{4,0},{8,4},{12,8},{16,28},{20,16},{24,20},{28,24},{32,44},... | collective-permute-start | bytes 1277960 | tf_op jit(solution)/shard_map/ppermute | solution.py:513
  127.1 0.0 copy-done.7
  127.1 5.9 %shard_map.144 = (bf16[128,512]{1,0:T(8,128)(2,1)}, bf16[128,512]{1,0:T(8,128)(2,1)}) custom-call(bf16[256,512]{1,0:T(8,128)(2,1)} %get-tuple-element.50.both, f32[512]{0:T(512)} %gain.3, bf16[256,1024]{1,0:T(8,128)(2,1)} %get-tuple-element.66.gated, bf16[1024,512]{1,0:T(8,128)(2,1)} %out_proj.3, bf16[256,1024]{1,0:T(8,128)(2,1)} %get-tuple-element.67.d_gate, ...), custom_call_target="tpu_custom_call" | custom-call | flops 8000000000 | bytes 5564416 | tf_op jit(solution)/shard_map/pallas_call | solution.py:22
  133.0 1.4 collective-permute-done.5.refs_2_
  134.3 4.2 %collective-permute-done.6.refs_3_ = bf16[128,1664]{1,0:T(8,128)(2,1)S(1)} collective-permute-done((bf16[128,1664]{1,0:T(8,128)(2,1)}, bf16[128,1664]{1,0:T(8,128)(2,1)S(1)}, u32[]{:S(2)}, u32[]{:S(2)}) %collective-permute-start.6) | collective-permute-done | bytes 426016 | tf_op jit(solution)/shard_map/ppermute | solution.py:513
  138.6 0.5 collective-permute-done.7.refs_5_
  139.1 0.0 collective-permute-done.8.refs_6_
  139.1 0.7 collective-permute-done.9.refs_7_
  139.8 0.0 copy-start.3
  139.8 0.9 copy-done.3
  140.7 1.3 shard_map.145
  142.0 0.3 collective-permute-start.10
  142.3 3.7 %collective-permute-start.11 = (bf16[32,1664]{1,0:T(8,128)(2,1)S(1)}, bf16[32,1664]{1,0:T(8,128)(2,1)S(1)}, u32[]{:S(2)}, u32[]{:S(2)}) collective-permute-start(bf16[32,1664]{1,0:T(8,128)(2,1)S(1)} %get-tuple-element.84), channel_id=1, source_target_pairs={{0,8},{4,12},{8,0},{12,4},{16,24},{20,28},{24,16},{28,20},{32,40},... | collective-permute-start | bytes 319496 | tf_op jit(solution)/shard_map/ppermute | solution.py:513
  146.0 0.0 collective-permute-start.12
  146.0 2.4 %collective-permute-start.13 = (bf16[32,1664]{1,0:T(8,128)(2,1)S(1)}, bf16[32,1664]{1,0:T(8,128)(2,1)S(1)}, u32[]{:S(2)}, u32[]{:S(2)}) collective-permute-start(bf16[32,1664]{1,0:T(8,128)(2,1)S(1)} %get-tuple-element.87), channel_id=1, source_target_pairs={{0,64},{4,68},{8,72},{12,76},{16,80},{20,84},{24,88},{28,92},{32,9... | collective-permute-start | bytes 319496 | tf_op jit(solution)/shard_map/ppermute | solution.py:513
  148.4 4.2 %collective-permute-start.14 = (bf16[32,1664]{1,0:T(8,128)(2,1)S(1)}, bf16[32,1664]{1,0:T(8,128)(2,1)S(1)}, u32[]{:S(2)}, u32[]{:S(2)}) collective-permute-start(bf16[32,1664]{1,0:T(8,128)(2,1)S(1)} %get-tuple-element.88), channel_id=1, source_target_pairs={{0,128},{4,132},{8,136},{12,140},{16,144},{20,148},{24,152},{28,15... | collective-permute-start | bytes 319496 | tf_op jit(solution)/shard_map/ppermute | solution.py:513
  152.6 0.0 collective-permute-done.10.refs_1_
  152.6 0.0 collective-permute-start.15
  152.6 0.0 collective-permute-done.11.refs_2_
  152.6 0.0 collective-permute-done.12.refs_3_
  152.6 0.6 collective-permute-done.13.refs_5_
  153.2 2.1 %collective-permute-done.14.refs_6_ = bf16[32,1664]{1,0:T(8,128)(2,1)S(1)} collective-permute-done((bf16[32,1664]{1,0:T(8,128)(2,1)S(1)}, bf16[32,1664]{1,0:T(8,128)(2,1)S(1)}, u32[]{:S(2)}, u32[]{:S(2)}) %collective-permute-start.14) | collective-permute-done | bytes 106528 | tf_op jit(solution)/shard_map/ppermute | solution.py:513
  155.3 3.2 %collective-permute-done.15.refs_7_ = bf16[32,1664]{1,0:T(8,128)(2,1)S(1)} collective-permute-done((bf16[32,1664]{1,0:T(8,128)(2,1)S(1)}, bf16[32,1664]{1,0:T(8,128)(2,1)S(1)}, u32[]{:S(2)}, u32[]{:S(2)}) %collective-permute-start.15) | collective-permute-done | bytes 106528 | tf_op jit(solution)/shard_map/ppermute | solution.py:513
  158.5 0.7 shard_map.146
  159.2 0.1 collective-permute-start.16
  159.3 6.3 %collective-permute-start.17 = (bf16[16,1664]{1,0:T(8,128)(2,1)S(1)}, bf16[16,1664]{1,0:T(8,128)(2,1)S(1)}, u32[]{:S(2)}, u32[]{:S(2)}) collective-permute-start(bf16[16,1664]{1,0:T(8,128)(2,1)S(1)} %get-tuple-element.92), channel_id=1, source_target_pairs={{0,32},{4,36},{8,40},{12,44},{16,48},{20,52},{24,56},{28,60},{32,0... | collective-permute-start | bytes 159752 | tf_op jit(solution)/shard_map/ppermute | solution.py:513
  165.6 0.0 collective-permute-start.18
  165.6 0.1 collective-permute-done.16.refs_1_
  165.6 2.7 %collective-permute-done.17.refs_2_ = bf16[16,1664]{1,0:T(8,128)(2,1)S(1)} collective-permute-done((bf16[16,1664]{1,0:T(8,128)(2,1)S(1)}, bf16[16,1664]{1,0:T(8,128)(2,1)S(1)}, u32[]{:S(2)}, u32[]{:S(2)}) %collective-permute-start.17) | collective-permute-done | bytes 53280 | tf_op jit(solution)/shard_map/ppermute | solution.py:513
  168.3 2.8 %collective-permute-done.18.refs_3_ = bf16[16,1664]{1,0:T(8,128)(2,1)S(1)} collective-permute-done((bf16[16,1664]{1,0:T(8,128)(2,1)S(1)}, bf16[16,1664]{1,0:T(8,128)(2,1)S(1)}, u32[]{:S(2)}, u32[]{:S(2)}) %collective-permute-start.18) | collective-permute-done | bytes 53280 | tf_op jit(solution)/shard_map/ppermute | solution.py:513
  171.1 0.7 shard_map.147
  (11 shorter events, 0.0 us)
Async XLA Ops:
  1.4 12.9 %collective-permute-start.1 = (bf16[16,512]{1,0:T(8,128)(2,1)S(1)}, bf16[16,512]{1,0:T(8,128)(2,1)S(1)}, u32[]{:S(2)}, u32[]{:S(2)}) collective-permute-start(bf16[16,512]{1,0:T(8,128)(2,1)S(1)} %get-tuple-element.96), channel_id=1, source_target_pairs={{4,0},{8,4},{12,8},{16,12},{20,16},{24,20},{28,24},{32,28},{36,32}... | collective-permute-start | bytes 49160 | tf_op jit(solution)/shard_map/ppermute | solution.py:551
  12.3 10.8 %collective-permute-start = (bf16[16,512]{1,0:T(8,128)(2,1)S(1)}, bf16[16,512]{1,0:T(8,128)(2,1)S(1)}, u32[]{:S(2)}, u32[]{:S(2)}) collective-permute-start(bf16[16,512]{1,0:T(8,128)(2,1)S(1)} %get-tuple-element.97), channel_id=1, source_target_pairs={{0,4},{4,8},{8,12},{12,16},{16,20},{20,24},{24,28},{28,32},{32,36}... | collective-permute-start | bytes 49160 | tf_op jit(solution)/shard_map/ppermute | solution.py:550
  14.2 8.8 %copy-start.5 = (bf16[16,512]{1,0:T(8,128)(2,1)}, bf16[16,512]{1,0:T(8,128)(2,1)S(1)}, u32[]{:S(2)}) copy-start(bf16[16,512]{1,0:T(8,128)(2,1)S(1)} %collective-permute-done.1.high) | copy-start | bytes 49156
  23.0 0.6 copy-start.6
  64.5 15.5 %all-to-all-start.2 = ((bf16[16,64,128]{2,1,0:T(8,128)(2,1)}), bf16[16,64,128]{2,1,0:T(8,128)(2,1)S(1)}, u32[]{:S(2)}, u32[]{:S(2)}) async-start(bf16[16,64,128]{2,1,0:T(8,128)(2,1)} %shard_map.140), calls=%async_computation.2 | async-start | bytes 524288 | tf_op jit(solution)/shard_map/all_to_all | solution.py:517
  81.4 14.4 %all-to-all-start.3 = ((bf16[4,1024,128]{2,1,0:T(8,128)(2,1)}), bf16[4,1024,128]{2,1,0:T(8,128)(2,1)S(1)}, u32[]{:S(2)}, u32[]{:S(2)}) async-start(bf16[4,1024,128]{2,1,0:T(8,128)(2,1)} %shard_map.141), calls=%async_computation.3 | async-start | bytes 2097152 | tf_op jit(solution)/shard_map/all_to_all | solution.py:517
  95.7 1.0 copy-start.4
  108.9 15.9 %collective-permute-start.4 = (bf16[128,1664]{1,0:T(8,128)(2,1)}, bf16[128,1664]{1,0:T(8,128)(2,1)S(1)}, u32[]{:S(2)}, u32[]{:S(2)}) collective-permute-start(bf16[128,1664]{1,0:T(8,128)(2,1)} %get-tuple-element.75), channel_id=1, source_target_pairs={{0,64},{4,68},{8,72},{12,76},{16,80},{20,84},{24,88},{28,92},{32,9... | collective-permute-start | bytes 1277960 | tf_op jit(solution)/shard_map/ppermute | solution.py:513
  112.2 11.5 %collective-permute-start.3 = (f32[8,1280]{1,0:T(8,128)S(1)}, f32[8,1280]{1,0:T(8,128)S(1)}, u32[]{:S(2)}, u32[]{:S(2)}) collective-permute-start(f32[8,1280]{1,0:T(8,128)S(1)} %get-tuple-element.98), channel_id=1, source_target_pairs={{0,4},{4,8},{8,12},{12,16},{16,20},{20,24},{24,28},{28,32},{32,36}... | collective-permute-start | bytes 122888 | tf_op jit(solution)/shard_map/ppermute | solution.py:628
  114.7 10.1 %collective-permute-start.2 = (f32[8,1280]{1,0:T(8,128)S(1)}, f32[8,1280]{1,0:T(8,128)S(1)}, u32[]{:S(2)}, u32[]{:S(2)}) collective-permute-start(f32[8,1280]{1,0:T(8,128)S(1)} %get-tuple-element.99), channel_id=1, source_target_pairs={{4,0},{8,4},{12,8},{16,12},{20,16},{24,20},{28,24},{32,28},{36,32}... | collective-permute-start | bytes 122888 | tf_op jit(solution)/shard_map/ppermute | solution.py:627
  123.2 11.2 %collective-permute-start.5 = (bf16[128,1664]{1,0:T(8,128)(2,1)}, bf16[128,1664]{1,0:T(8,128)(2,1)S(1)}, u32[]{:S(2)}, u32[]{:S(2)}) collective-permute-start(bf16[128,1664]{1,0:T(8,128)(2,1)} %get-tuple-element.76), channel_id=1, source_target_pairs={{0,128},{4,132},{8,136},{12,140},{16,144},{20,148},{24,152},{28,15... | collective-permute-start | bytes 1277960 | tf_op jit(solution)/shard_map/ppermute | solution.py:513
  123.4 15.1 %collective-permute-start.6 = (bf16[128,1664]{1,0:T(8,128)(2,1)}, bf16[128,1664]{1,0:T(8,128)(2,1)S(1)}, u32[]{:S(2)}, u32[]{:S(2)}) collective-permute-start(bf16[128,1664]{1,0:T(8,128)(2,1)} %get-tuple-element.77), channel_id=1, source_target_pairs={{0,192},{4,196},{8,200},{12,204},{16,208},{20,212},{24,216},{28,22... | collective-permute-start | bytes 1277960 | tf_op jit(solution)/shard_map/ppermute | solution.py:513
  123.7 3.3 %copy-start.7 = (f32[8,1280]{1,0:T(8,128)}, f32[8,1280]{1,0:T(8,128)S(1)}, u32[]{:S(2)}) copy-start(f32[8,1280]{1,0:T(8,128)S(1)} %collective-permute-done.3.behind) | copy-start | bytes 122884
  123.7 15.4 %collective-permute-start.7 = (bf16[128,1664]{1,0:T(8,128)(2,1)}, bf16[128,1664]{1,0:T(8,128)(2,1)S(1)}, u32[]{:S(2)}, u32[]{:S(2)}) collective-permute-start(bf16[128,1664]{1,0:T(8,128)(2,1)} %get-tuple-element.79), channel_id=1, source_target_pairs={{0,4},{4,8},{8,12},{12,0},{16,20},{20,24},{24,28},{28,16},{32,36},... | collective-permute-start | bytes 1277960 | tf_op jit(solution)/shard_map/ppermute | solution.py:513
  124.8 2.3 %copy-start.8 = (f32[8,1280]{1,0:T(8,128)}, f32[8,1280]{1,0:T(8,128)S(1)}, u32[]{:S(2)}) copy-start(f32[8,1280]{1,0:T(8,128)S(1)} %collective-permute-done.2.ahead) | copy-start | bytes 122884
  124.8 14.3 %collective-permute-start.8 = (bf16[128,1664]{1,0:T(8,128)(2,1)}, bf16[128,1664]{1,0:T(8,128)(2,1)S(1)}, u32[]{:S(2)}, u32[]{:S(2)}) collective-permute-start(bf16[128,1664]{1,0:T(8,128)(2,1)} %get-tuple-element.80), channel_id=1, source_target_pairs={{0,8},{4,12},{8,0},{12,4},{16,24},{20,28},{24,16},{28,20},{32,40},... | collective-permute-start | bytes 1277960 | tf_op jit(solution)/shard_map/ppermute | solution.py:513
  124.8 15.0 %collective-permute-start.9 = (bf16[128,1664]{1,0:T(8,128)(2,1)}, bf16[128,1664]{1,0:T(8,128)(2,1)S(1)}, u32[]{:S(2)}, u32[]{:S(2)}) collective-permute-start(bf16[128,1664]{1,0:T(8,128)(2,1)} %get-tuple-element.81), channel_id=1, source_target_pairs={{0,12},{4,0},{8,4},{12,8},{16,28},{20,16},{24,20},{28,24},{32,44},... | collective-permute-start | bytes 1277960 | tf_op jit(solution)/shard_map/ppermute | solution.py:513
  127.1 12.7 %copy-start = (s32[3]{0:T(128)S(1)}, s32[3]{0:T(128)}, u32[]{:S(2)}) copy-start(s32[3]{0:T(128)} %pad_add_fusion.place) | copy-start | bytes 40
  127.1 12.7 %copy-start.1 = (bf16[128,1664]{1,0:T(8,128)(2,1)S(1)}, bf16[128,1664]{1,0:T(8,128)(2,1)}, u32[]{:S(2)}) copy-start(bf16[128,1664]{1,0:T(8,128)(2,1)} %get-tuple-element.74.refs_0_) | copy-start | bytes 1277956
  127.1 12.7 %copy-start.2 = (bf16[128,1664]{1,0:T(8,128)(2,1)S(1)}, bf16[128,1664]{1,0:T(8,128)(2,1)}, u32[]{:S(2)}) copy-start(bf16[128,1664]{1,0:T(8,128)(2,1)} %get-tuple-element.78.refs_4_) | copy-start | bytes 1277956
  139.8 0.9 copy-start.3
  142.0 10.6 %collective-permute-start.10 = (bf16[32,1664]{1,0:T(8,128)(2,1)S(1)}, bf16[32,1664]{1,0:T(8,128)(2,1)S(1)}, u32[]{:S(2)}, u32[]{:S(2)}) collective-permute-start(bf16[32,1664]{1,0:T(8,128)(2,1)S(1)} %get-tuple-element.83), channel_id=1, source_target_pairs={{0,4},{4,8},{8,12},{12,0},{16,20},{20,24},{24,28},{28,16},{32,36},... | collective-permute-start | bytes 319496 | tf_op jit(solution)/shard_map/ppermute | solution.py:513
  142.3 10.3 %collective-permute-start.11 = (bf16[32,1664]{1,0:T(8,128)(2,1)S(1)}, bf16[32,1664]{1,0:T(8,128)(2,1)S(1)}, u32[]{:S(2)}, u32[]{:S(2)}) collective-permute-start(bf16[32,1664]{1,0:T(8,128)(2,1)S(1)} %get-tuple-element.84), channel_id=1, source_target_pairs={{0,8},{4,12},{8,0},{12,4},{16,24},{20,28},{24,16},{28,20},{32,40},... | collective-permute-start | bytes 319496 | tf_op jit(solution)/shard_map/ppermute | solution.py:513
  146.0 6.7 %collective-permute-start.12 = (bf16[32,1664]{1,0:T(8,128)(2,1)S(1)}, bf16[32,1664]{1,0:T(8,128)(2,1)S(1)}, u32[]{:S(2)}, u32[]{:S(2)}) collective-permute-start(bf16[32,1664]{1,0:T(8,128)(2,1)S(1)} %get-tuple-element.85), channel_id=1, source_target_pairs={{0,12},{4,0},{8,4},{12,8},{16,28},{20,16},{24,20},{28,24},{32,44},... | collective-permute-start | bytes 319496 | tf_op jit(solution)/shard_map/ppermute | solution.py:513
  146.0 7.3 %collective-permute-start.13 = (bf16[32,1664]{1,0:T(8,128)(2,1)S(1)}, bf16[32,1664]{1,0:T(8,128)(2,1)S(1)}, u32[]{:S(2)}, u32[]{:S(2)}) collective-permute-start(bf16[32,1664]{1,0:T(8,128)(2,1)S(1)} %get-tuple-element.87), channel_id=1, source_target_pairs={{0,64},{4,68},{8,72},{12,76},{16,80},{20,84},{24,88},{28,92},{32,9... | collective-permute-start | bytes 319496 | tf_op jit(solution)/shard_map/ppermute | solution.py:513
  148.4 6.9 %collective-permute-start.14 = (bf16[32,1664]{1,0:T(8,128)(2,1)S(1)}, bf16[32,1664]{1,0:T(8,128)(2,1)S(1)}, u32[]{:S(2)}, u32[]{:S(2)}) collective-permute-start(bf16[32,1664]{1,0:T(8,128)(2,1)S(1)} %get-tuple-element.88), channel_id=1, source_target_pairs={{0,128},{4,132},{8,136},{12,140},{16,144},{20,148},{24,152},{28,15... | collective-permute-start | bytes 319496 | tf_op jit(solution)/shard_map/ppermute | solution.py:513
  152.6 5.9 %collective-permute-start.15 = (bf16[32,1664]{1,0:T(8,128)(2,1)S(1)}, bf16[32,1664]{1,0:T(8,128)(2,1)S(1)}, u32[]{:S(2)}, u32[]{:S(2)}) collective-permute-start(bf16[32,1664]{1,0:T(8,128)(2,1)S(1)} %get-tuple-element.89), channel_id=1, source_target_pairs={{0,192},{4,196},{8,200},{12,204},{16,208},{20,212},{24,216},{28,22... | collective-permute-start | bytes 319496 | tf_op jit(solution)/shard_map/ppermute | solution.py:513
  159.2 6.4 %collective-permute-start.16 = (bf16[16,1664]{1,0:T(8,128)(2,1)S(1)}, bf16[16,1664]{1,0:T(8,128)(2,1)S(1)}, u32[]{:S(2)}, u32[]{:S(2)}) collective-permute-start(bf16[16,1664]{1,0:T(8,128)(2,1)S(1)} %get-tuple-element.91), channel_id=1, source_target_pairs={{0,16},{4,20},{8,24},{12,28},{16,32},{20,36},{24,40},{28,44},{32,4... | collective-permute-start | bytes 159752 | tf_op jit(solution)/shard_map/ppermute | solution.py:513
  159.3 9.0 %collective-permute-start.17 = (bf16[16,1664]{1,0:T(8,128)(2,1)S(1)}, bf16[16,1664]{1,0:T(8,128)(2,1)S(1)}, u32[]{:S(2)}, u32[]{:S(2)}) collective-permute-start(bf16[16,1664]{1,0:T(8,128)(2,1)S(1)} %get-tuple-element.92), channel_id=1, source_target_pairs={{0,32},{4,36},{8,40},{12,44},{16,48},{20,52},{24,56},{28,60},{32,0... | collective-permute-start | bytes 159752 | tf_op jit(solution)/shard_map/ppermute | solution.py:513
  165.6 5.6 %collective-permute-start.18 = (bf16[16,1664]{1,0:T(8,128)(2,1)S(1)}, bf16[16,1664]{1,0:T(8,128)(2,1)S(1)}, u32[]{:S(2)}, u32[]{:S(2)}) collective-permute-start(bf16[16,1664]{1,0:T(8,128)(2,1)S(1)} %get-tuple-element.93), channel_id=1, source_target_pairs={{0,48},{4,52},{8,56},{12,60},{16,0},{20,4},{24,8},{28,12},{32,16},... | collective-permute-start | bytes 159752 | tf_op jit(solution)/shard_map/ppermute | solution.py:513

commit v3 on v2

--- a/solution.py
+++ b/solution.py
@@ -15,12 +15,18 @@
 INTERPRET = False
 
 
-def call(body, outs, args, scratch=(), scalars=0, flops=10**9, vmem=58 * 2**20):
+def call(body, outs, args, scratch=(), scalars=0, unused=0, flops=10**9, vmem=58 * 2**20):
+    after = len(args) - unused
     specs = [pl.BlockSpec(memory_space=pltpu.SMEM)] * scalars
-    specs += [pl.BlockSpec(memory_space=pltpu.VMEM)] * (len(args) - scalars)
-    moved = sum(a.size * a.dtype.itemsize for a in args)
+    specs += [pl.BlockSpec(memory_space=pltpu.VMEM)] * (after - scalars)
+    specs += [pl.BlockSpec(memory_space=pl.ANY)] * unused
+    moved = sum(a.size * a.dtype.itemsize for a in args[:after])
+
+    def used(*refs):
+        body(*refs[:after], *refs[len(args) :])
+
     return pl.pallas_call(
-        body,
+        used,
         out_shape=[jax.ShapeDtypeStruct(shape, kind) for shape, kind in outs],
         in_specs=specs,
         out_specs=[pl.BlockSpec(memory_space=pltpu.VMEM)] * len(outs),
@@ -444,28 +450,37 @@
         slots[step][...] = block.reshape(slots[step].shape).astype(slots[step].dtype)
 
 
-def result_kernel(
-    both, gain, gated, out_proj, d_gate, d_xbc, d_edge, ahead, behind, d_step, in_proj, step_proj,
-    layer, grad, d_whole,
-):
+def result_kernel(both, gated, out_proj, d_gate, d_xbc, d_step, in_proj, step_proj, layer, d_normal):
     rows = both.shape[0] // 2
     inner = out_proj.shape[0]
     branch = mm(gated[...], out_proj[...])
     layer[...] = (branch[:rows] + mirror_wide(branch[rows:])).astype(bf16)
-    d_whole[...] = d_xbc[...]
-    for frame, halo in enumerate((ahead, behind)):
-        edge = d_edge[8 * frame : 8 * frame + 8, :] + halo[...]
-        keep = d_xbc[(frame + 1) * rows - 16 : (frame + 1) * rows, :].astype(f32)
-        edge = jnp.concatenate([keep[:8], edge], axis=0)
-        d_whole[(frame + 1) * rows - 16 : (frame + 1) * rows, :] = edge.astype(bf16)
-    d_normal = mm_cols(d_gate[...], in_proj[:, :inner]) + mm_cols(d_whole[...], in_proj[:, inner:])
-    d_normal = d_normal + mm(d_step[...], step_proj[...])
+    found = mm_cols(d_gate[...], in_proj[:, :inner]) + mm(d_step[...], step_proj[...])
+    keep = iota((d_xbc.shape[0], 1), 0) % rows < rows - 8
+    edgeless = jnp.where(keep, d_xbc[...].astype(f32), 0.0).astype(bf16)
+    d_normal[...] = found + mm_cols(edgeless, in_proj[:, inner:])
+
+
+def input_kernel(both, gain, d_normal, d_edge, ahead, behind, in_proj, grad, d_whole):
+    rows = both.shape[0] // 2
+    inner = in_proj.shape[1] - d_edge.shape[1]
+    edge = (d_edge[...] + jnp.concatenate([ahead[...], behind[...]], axis=0)).astype(bf16)
+    added = mm_cols(edge, in_proj[:, inner:])
+    d_whole[...] = d_normal[...]
+    for frame in range(2):
+        last = slice((frame + 1) * rows - 8, (frame + 1) * rows)
+        d_whole[last, :] = d_whole[last, :] + added[8 * frame : 8 * frame + 8]
     wide = both[...].astype(f32)
     scale = lax.rsqrt(jnp.mean(wide * wide, axis=-1, keepdims=True) + epsilon)
-    d_scaled = d_normal * gain[...].reshape(1, -1)
+    d_scaled = d_whole[...] * gain[...].reshape(1, -1)
     along = jnp.mean(d_scaled * wide, axis=-1, keepdims=True)
     d_wide = scale * d_scaled - wide * (scale * scale * scale * along)
     grad[...] = (d_wide[:rows] + mirror_wide(d_wide[rows:])).astype(bf16)
+
+
+def edge_kernel(d_ahead, ahead, behind):
+    ahead[...] = d_ahead[:8, :]
+    behind[...] = d_ahead[8:, :]
 
 
 def total_of(refs):
@@ -476,25 +491,25 @@
 
 
 def first_sum_kernel(place, *refs):
-    from_x, from_y, by_y, by_x, parted, whole = refs[:4], refs[4:8], refs[9:13], refs[13:17], refs[17], refs[18]
+    from_x, from_y, by_y, by_x, parted, whole = refs[:4], refs[4:8], refs[8:12], refs[12:16], refs[16], refs[17]
     parted[...] = total_of(from_x).reshape(parted.shape)
     whole[...] = total_of(from_y)
     send_y(place, parted, by_y)
     send_x(place, whole, by_x)
 
 
-def second_sum_kernel(place, *refs):
-    first, second, by_z, keep = refs[:4], refs[4:8], refs[8:12], refs[12]
-    keep[:, 0] = total_of(first).reshape(SIDE, 8, -1)
-    keep[:, 1] = total_of(second).reshape(SIDE, 8, -1)
-    for step in range(SIDE):
-        to = lax.rem(place[1] + step, SIDE)
-        by_z[step][...] = keep[to].reshape(by_z[step].shape).astype(by_z[step].dtype)
-
-
-def last_sum_kernel(*refs):
-    grad_in, grad_out = refs[4:]
-    total = total_of(refs[:4])
+def second_sum_kernel(*refs):
+    first, second, by_z = refs[:4], refs[4:8], refs[8]
+    first = total_of(first).reshape(SIDE, 8, -1)
+    second = total_of(second).reshape(SIDE, 8, -1)
+    for to in range(SIDE):
+        by_z[to] = jnp.concatenate([first[to], second[to]], axis=0).astype(bf16)
+
+
+def last_sum_kernel(parts, grad_in, grad_out):
+    total = parts[0].astype(f32)
+    for step in range(1, SIDE):
+        total = total + parts[step].astype(f32)
     columns = grad_out.shape[1]
     grad_out[:8, :] = total[:8, :columns]
     grad_out[8:, :] = total[:8, columns : 2 * columns]
@@ -543,6 +558,7 @@
     stride_x, stride_z, stride_y = SIDE * SIDE, SIDE, 1
     index = lax.axis_index("seq")
     place = jnp.stack([index // stride_x, index // stride_z % SIDE, index % SIDE]).astype(jnp.int32)
+    aligned = [[base + SIDE * digit for digit in range(SIDE)] for base in range(COUNT) if base // SIDE % SIDE == 0]
     beside = [[SIDE * base + digit for digit in range(SIDE)] for base in range(COUNT // SIDE)]
     across = [[base + SIDE * digit for digit in range(COUNT // SIDE)] for base in range(SIDE)]
     upward = [(i, i + 1) for i in range(COUNT - 1)]
@@ -624,41 +640,51 @@
     )
     from_x = exchange(parts[:4], stride_x)
     from_y = exchange(parts[4:], stride_y)
-    ahead = lax.ppermute(d_ahead[:8], "seq", downward)
-    behind = lax.ppermute(d_ahead[8:], "seq", upward)
-    layer_out, grad_input = call(
+    ahead, behind = call(
+        edge_kernel,
+        [((8, channels), f32)] * 2,
+        (d_ahead, from_y[1]),
+        unused=1,
+        flops=10**6,
+        vmem=16 * 2**20,
+    )
+    ahead = lax.ppermute(ahead, "seq", downward)
+    behind = lax.ppermute(behind, "seq", upward)
+    layer_out, d_normal = call(
         result_kernel,
-        [((rows, width), bf16), ((rows, width), bf16)],
-        (
-            both, norm_gain, gated, out_proj, d_gate, d_xbc, d_edge, ahead, behind, d_step,
-            in_proj, step_turned,
-        ),
-        [pltpu.VMEM((both_rows, channels), bf16)],
+        [((rows, width), bf16), ((both_rows, width), f32)],
+        (both, gated, out_proj, d_gate, d_xbc, d_step, in_proj, step_turned),
         flops=8 * 10**9,
     )
+    from_x, from_y, layer_out, ahead, behind = lax.optimization_barrier((from_x, from_y, layer_out, ahead, behind))
     parts = call(
         first_sum_kernel,
         slots(eighth // SIDE, joined, f32) * 2,
-        (place, *from_x, *from_y, layer_out),
+        (place, *from_x, *from_y),
         [pltpu.VMEM((SIDE, SIDE, 8, joined), f32), pltpu.VMEM((eighth, joined), f32)],
         scalars=1,
         vmem=16 * 2**20,
     )
     first = exchange(parts[:4], stride_y)
     second = exchange(parts[4:], stride_x)
-    parts = call(
+    (grad_input,) = call(
+        input_kernel,
+        [((rows, width), bf16)],
+        (both, norm_gain, d_normal, d_edge, ahead, behind, in_proj),
+        [pltpu.VMEM((both_rows, width), f32)],
+        flops=4 * 10**9,
+    )
+    (by_z,) = call(
         second_sum_kernel,
-        slots(16, joined, f32),
-        (place, *first, *second),
-        [pltpu.VMEM((SIDE, 2, 8, joined), f32)],
-        scalars=1,
+        [((SIDE, 16, joined), bf16)],
+        (*first, *second),
         vmem=16 * 2**20,
     )
-    last = exchange(parts, stride_z)
+    last = transpose_over(by_z, aligned)
     grad_in_proj, grad_out_proj = call(
         last_sum_kernel,
         [((8, inner + channels), f32), ((16, width), f32)],
-        tuple(last),
+        (last,),
         vmem=16 * 2**20,
     )
     return (layer_out, grad_input, grad_in_proj, grad_out_proj)

time: 173 us -> 170 us (0.983)
  starting transfers between devices: 55.2 us -> 47.7 us
  Pallas kernels: 36.4 us -> 39.6 us
  waiting for transfers between devices: 42.9 us -> 45.3 us
    ppermute x15 -> x12, starting transfers between devices: 22 us -> 16 us  [exchange(): lax.ppermute(parts[step], 'seq', axis_pairs(stride, step))]
    all_to_all x2 -> x3, waiting for transfers between devices: 14.4 us -> 20 us  [transpose_over(): return lax.all_to_all(parts, 'seq', 0, 0, axis_index_groups=groups)]
    ppermute x2, starting transfers between devices: 10.9 us -> 5.85 us  [the longest x1 3.93 us: shards(): behind = lax.ppermute(behind, 'seq', upward)]
    ppermute x15 -> x12, waiting for transfers between devices: 18.3 us -> 14.6 us  [exchange(): lax.ppermute(parts[step], 'seq', axis_pairs(stride, step))]
    all_to_all x2 -> x3, starting transfers between devices: 9.47 us -> 13 us  [transpose_over(): return lax.all_to_all(parts, 'seq', 0, 0, axis_index_groups=groups)]
    pallas_call x10 -> x12, Pallas kernels: 36.4 us -> 39.6 us  [call(): pl.pallas_call(used, out_shape=[jax.ShapeDtypeStruct(shape, kind) for sha...]
  transfers between devices with their start and end apart: 21 -> 19, of which waited for: 15 -> 8; matrix products, arithmetic and copies ran while one was open for 1% -> 0% of each run, Pallas kernels for 7% -> 9%
where the time goes in v3:
time: 170 us; the launch traced here: 169 us
  starting transfers between devices  47.7 us (28%)
  waiting for transfers between devices  45.3 us (27%)
  Pallas kernels  39.6 us (23%)
  blocking collectives  31.9 us (19%)
  local copies, waits for them, and re-layouts  3.24 us (2%)
    pallas_call x12, Pallas kernels, call(): pl.pallas_call(used, out_shape=[jax.ShapeDtypeStruct(shape, kind) for sha...  39.6 us
    all_to_all x2, blocking collectives, transpose_over(): return lax.all_to_all(parts, 'seq', 0, 0, axis_index_groups=groups)  31.9 us
    all_to_all x3, waiting for transfers between devices, transpose_over(): return lax.all_to_all(parts, 'seq', 0, 0, axis_index_groups=groups)  20 us
    ppermute x12, starting transfers between devices, exchange(): lax.ppermute(parts[step], 'seq', axis_pairs(stride, step))  16 us
    ppermute x12, waiting for transfers between devices, exchange(): lax.ppermute(parts[step], 'seq', axis_pairs(stride, step))  14.6 us
    all_to_all x3, starting transfers between devices, transpose_over(): return lax.all_to_all(parts, 'seq', 0, 0, axis_index_groups=groups)  13 us
    ppermute x1, starting transfers between devices, shards(): high = lax.ppermute(sequence[:16], 'seq', downward)  10.9 us
    ppermute x1, waiting for transfers between devices, shards(): low = lax.ppermute(sequence[rows - 16:], 'seq', upward)  8.8 us
  transfers between devices with their start and end apart: 19, of which 8 were waited for; matrix products, arithmetic and copies ran while one was open for 0% of the time, Pallas kernels for 9%

profile of v3, /device:TPU:6, one launch (start us, length us, event | category | flops | bytes accessed | tf_op | source)
XLA Modules:
  0.0 169.1 jit_solution(5363541654583986616)
XLA Ops:
  0.6 0.7 fusion
  1.4 10.9 %collective-permute-start.1 = (bf16[16,512]{1,0:T(8,128)(2,1)S(1)}, bf16[16,512]{1,0:T(8,128)(2,1)S(1)}, u32[]{:S(2)}, u32[]{:S(2)}) collective-permute-start(bf16[16,512]{1,0:T(8,128)(2,1)S(1)} %get-tuple-element.114), channel_id=1, source_target_pairs={{4,0},{8,4},{12,8},{16,12},{20,16},{24,20},{28,24},{32,28},{36,32}... | collective-permute-start | bytes 49160 | tf_op jit(solution)/shard_map/ppermute | solution.py:567
  12.3 1.9 %collective-permute-start = (bf16[16,512]{1,0:T(8,128)(2,1)S(1)}, bf16[16,512]{1,0:T(8,128)(2,1)S(1)}, u32[]{:S(2)}, u32[]{:S(2)}) collective-permute-start(bf16[16,512]{1,0:T(8,128)(2,1)S(1)} %get-tuple-element.115), channel_id=1, source_target_pairs={{0,4},{4,8},{8,12},{12,16},{16,20},{20,24},{24,28},{28,32},{32,36}... | collective-permute-start | bytes 49160 | tf_op jit(solution)/shard_map/ppermute | solution.py:566
  14.2 0.0 collective-permute-done.1.refs_3_
  14.2 0.0 copy-start.5
  14.2 8.8 %collective-permute-done.refs_2_ = bf16[16,512]{1,0:T(8,128)(2,1)S(1)} collective-permute-done((bf16[16,512]{1,0:T(8,128)(2,1)S(1)}, bf16[16,512]{1,0:T(8,128)(2,1)S(1)}, u32[]{:S(2)}, u32[]{:S(2)}) %collective-permute-start) | collective-permute-done | bytes 16416 | tf_op jit(solution)/shard_map/ppermute | solution.py:566
  23.0 0.0 copy-done.5
  23.0 0.6 copy-done.6
  23.6 7.0 %shard_map.138 = (bf16[4,1040,128]{2,1,0:T(8,128)(2,1)}, bf16[256,512]{1,0:T(8,128)(2,1)}, bf16[256,512]{1,0:T(8,128)(2,1)}, bf16[32,512]{1,0:T(8,128)(2,1)}, bf...) custom-call(bf16[128,512]{1,0:T(8,128)(2,1)} %refs_0_.1, ...), custom_call_target="tpu_custom_call" | custom-call | flops 1000000000 | bytes 3746944 | tf_op jit(solution)/shard_map/pallas_call | solution.py:28
  30.6 17.6 %all_to_all.25.refs_0_ = bf16[4,1040,128]{2,1,0:T(8,128)(2,1)S(1)} all-to-all(bf16[4,1040,128]{2,1,0:T(8,128)(2,1)} %get-tuple-element.59), channel_id=1, replica_groups={{0,4,8,12},{16,20,24,28},{32,36,40,44},{48,52,56,60},{64,68,72,76},{80,..., dimensions={0} | all-to-all | bytes 2129920 | tf_op jit(solution)/shard_map/all_to_all | solution.py:532
  48.2 0.4 shard_map.139
  48.6 14.2 %all_to_all.26.refs_0_ = bf16[16,72,128]{2,1,0:T(8,128)(2,1)S(1)} all-to-all(bf16[16,72,128]{2,1,0:T(8,128)(2,1)S(1)} %shard_map.139), channel_id=1, replica_groups={{0,16,32,48,64,80,96,112,128,144,160,176,192,208,224,240},{4,20,36,52,6..., dimensions={0} | all-to-all | bytes 589824 | tf_op jit(solution)/shard_map/all_to_all | solution.py:532
  62.9 1.6 shard_map.140
  64.5 5.8 %all-to-all-start.2 = ((bf16[16,64,128]{2,1,0:T(8,128)(2,1)}), bf16[16,64,128]{2,1,0:T(8,128)(2,1)S(1)}, u32[]{:S(2)}, u32[]{:S(2)}) async-start(bf16[16,64,128]{2,1,0:T(8,128)(2,1)} %shard_map.140), calls=%async_computation.2 | async-start | bytes 524288 | tf_op jit(solution)/shard_map/all_to_all | solution.py:532
  70.2 9.8 %all-to-all-done.2.refs_1_ = bf16[16,64,128]{2,1,0:T(8,128)(2,1)S(1)} async-done(((bf16[16,64,128]{2,1,0:T(8,128)(2,1)}), bf16[16,64,128]{2,1,0:T(8,128)(2,1)S(1)}, u32[]{:S(2)}, u32[]{:S(2)}) %all-to-all-start.2) | async-done | bytes 262176 | tf_op jit(solution)/shard_map/all_to_all | solution.py:532
  80.0 1.3 shard_map.141
  81.3 3.7 %all-to-all-start.3 = ((bf16[4,1024,128]{2,1,0:T(8,128)(2,1)}), bf16[4,1024,128]{2,1,0:T(8,128)(2,1)S(1)}, u32[]{:S(2)}, u32[]{:S(2)}) async-start(bf16[4,1024,128]{2,1,0:T(8,128)(2,1)} %shard_map.141), calls=%async_computation.3 | async-start | bytes 2097152 | tf_op jit(solution)/shard_map/all_to_all | solution.py:532
  85.0 0.6 pad_add_fusion.refs_0_
  85.6 5.5 %shard_map.142 = (f32[256,1024]{1,0:T(8,128)}, f32[256,1024]{1,0:T(8,128)}, f32[256,256]{1,0:T(8,128)}, f32[256,16]{1,0:T(8,128)}) custom-call(f32[256,1280]{1,0:T(8,128)} %get-tuple-element.60.refs_0_.refs_2_, f32[256,1024]{1,0:T(8,128)} %get-tuple-element.61.refs_1_.refs_3_, bf16[256,1024]{1,0:T(8,128)(2,1)} %get-tuple-element.62.refs_2_.refs_4_, ...), custom_call_target="tpu_custom_call" | custom-call | flops 8000000000 | bytes 2932736 | tf_op jit(solution)/shard_map/pallas_call | solution.py:28
  91.1 4.6 %all-to-all-done.3.refs_1_ = bf16[4,1024,128]{2,1,0:T(8,128)(2,1)S(1)} async-done(((bf16[4,1024,128]{2,1,0:T(8,128)(2,1)}), bf16[4,1024,128]{2,1,0:T(8,128)(2,1)S(1)}, u32[]{:S(2)}, u32[]{:S(2)}) %all-to-all-start.3) | async-done | bytes 1048608 | tf_op jit(solution)/shard_map/all_to_all | solution.py:532
  95.7 1.0 copy-done.4
  96.7 12.1 %shard_map.143 = (bf16[256,1024]{1,0:T(8,128)(2,1)}, bf16[256,1024]{1,0:T(8,128)(2,1)}, bf16[256,1280]{1,0:T(8,128)(2,1)}, f32[16,1280]{1,0:T(8,128)}, f32[16,12...) custom-call(s32[3]{0:T(128)} %pad_add_fusion.refs_0_, ...), custom_call_target="tpu_custom_call" | custom-call | flops 1000000000 | bytes 6934732 | tf_op jit(solution)/shard_map/pallas_call | solution.py:28
  108.8 0.7 collective-permute-start.5
  109.5 2.4 %collective-permute-start.2 = (bf16[128,1664]{1,0:T(8,128)(2,1)}, bf16[128,1664]{1,0:T(8,128)(2,1)S(1)}, u32[]{:S(2)}, u32[]{:S(2)}) collective-permute-start(bf16[128,1664]{1,0:T(8,128)(2,1)} %get-tuple-element.75), channel_id=1, source_target_pairs={{0,64},{4,68},{8,72},{12,76},{16,80},{20,84},{24,88},{28,92},{32,9... | collective-permute-start | bytes 1277960 | tf_op jit(solution)/shard_map/ppermute | solution.py:528
  111.9 0.2 collective-permute-start.3
  112.1 0.7 collective-permute-start.4
  112.7 2.1 %collective-permute-start.6 = (bf16[128,1664]{1,0:T(8,128)(2,1)}, bf16[128,1664]{1,0:T(8,128)(2,1)S(1)}, u32[]{:S(2)}, u32[]{:S(2)}) collective-permute-start(bf16[128,1664]{1,0:T(8,128)(2,1)} %get-tuple-element.80), channel_id=1, source_target_pairs={{0,8},{4,12},{8,0},{12,4},{16,24},{20,28},{24,16},{28,20},{32,40},... | collective-permute-start | bytes 1277960 | tf_op jit(solution)/shard_map/ppermute | solution.py:528
  114.8 9.6 %collective-permute-done.5.refs_1_.refs_6_ = bf16[128,1664]{1,0:T(8,128)(2,1)S(1)} collective-permute-done((bf16[128,1664]{1,0:T(8,128)(2,1)}, bf16[128,1664]{1,0:T(8,128)(2,1)S(1)}, u32[]{:S(2)}, u32[]{:S(2)}) %collective-permute-start.5) | collective-permute-done | bytes 426016 | tf_op jit(solution)/shard_map/ppermute | solution.py:528
  124.4 0.0 collective-permute-start.7
  124.4 0.9 copy-done
  125.3 0.0 collective-permute-done.2.refs_2_
  125.3 1.9 %collective-permute-start.8 = (f32[8,1280]{1,0:T(8,128)S(1)}, f32[8,1280]{1,0:T(8,128)S(1)}, u32[]{:S(2)}, u32[]{:S(2)}) collective-permute-start(f32[8,1280]{1,0:T(8,128)S(1)} %get-tuple-element.89), channel_id=1, source_target_pairs={{4,0},{8,4},{12,8},{16,12},{20,16},{24,20},{28,24},{32,28},{36,32}... | collective-permute-start | bytes 122888 | tf_op jit(solution)/shard_map/ppermute | solution.py:651
  127.2 0.0 collective-permute-done.3.refs_3_
  127.3 3.9 %collective-permute-start.9 = (f32[8,1280]{1,0:T(8,128)S(1)}, f32[8,1280]{1,0:T(8,128)S(1)}, u32[]{:S(2)}, u32[]{:S(2)}) collective-permute-start(f32[8,1280]{1,0:T(8,128)S(1)} %get-tuple-element.90), channel_id=1, source_target_pairs={{0,4},{4,8},{8,12},{12,16},{16,20},{20,24},{24,28},{28,32},{32,36}... | collective-permute-start | bytes 122888 | tf_op jit(solution)/shard_map/ppermute | solution.py:652
  131.2 0.0 copy-start.1
  131.2 5.2 %shard_map.144 = (bf16[128,512]{1,0:T(8,128)(2,1)}, f32[256,512]{1,0:T(8,128)}) custom-call(bf16[256,512]{1,0:T(8,128)(2,1)} %get-tuple-element.82.refs_0_, bf16[256,1024]{1,0:T(8,128)(2,1)} %get-tuple-element.83.refs_1_, bf16[1024,512]{1,0:T(8,128)(2,1)} %refs_2_.1, bf16[256,1024]{1,0:T(8,128)(2,1)} %get-tuple-element.84.refs_3_, ...), custom_call_target="tpu_custom_call" | custom-call | flops 8000000000 | bytes 5398528 | tf_op jit(solution)/shard_map/pallas_call | solution.py:28
  136.4 0.0 collective-permute-done.4.refs_4_
  136.4 0.0 collective-permute-done.6.refs_7_
  136.4 0.0 collective-permute-done.7.refs_8_
  136.4 0.0 collective-permute-done.8.refs_4_
  136.5 0.0 copy-start.7
  136.5 1.8 %collective-permute-done.9.refs_5_ = f32[8,1280]{1,0:T(8,128)S(1)} collective-permute-done((f32[8,1280]{1,0:T(8,128)S(1)}, f32[8,1280]{1,0:T(8,128)S(1)}, u32[]{:S(2)}, u32[]{:S(2)}) %collective-permute-start.9) | collective-permute-done | bytes 40992 | tf_op jit(solution)/shard_map/ppermute | solution.py:652
  138.3 0.0 copy-done.1
  138.3 0.0 copy-done.3
  138.3 1.3 shard_map.147
  139.7 0.0 copy-done.7
  139.7 0.0 copy-done.8
  139.7 0.3 collective-permute-start.10
  140.0 3.9 %collective-permute-start.11 = (bf16[32,1664]{1,0:T(8,128)(2,1)S(1)}, bf16[32,1664]{1,0:T(8,128)(2,1)S(1)}, u32[]{:S(2)}, u32[]{:S(2)}) collective-permute-start(bf16[32,1664]{1,0:T(8,128)(2,1)S(1)} %get-tuple-element.106), channel_id=1, source_target_pairs={{0,8},{4,12},{8,0},{12,4},{16,24},{20,28},{24,16},{28,20},{32,40},... | collective-permute-start | bytes 319496 | tf_op jit(solution)/shard_map/ppermute | solution.py:528
  143.8 0.0 collective-permute-start.12
  143.8 3.6 %collective-permute-start.13 = (bf16[32,1664]{1,0:T(8,128)(2,1)S(1)}, bf16[32,1664]{1,0:T(8,128)(2,1)S(1)}, u32[]{:S(2)}, u32[]{:S(2)}) collective-permute-start(bf16[32,1664]{1,0:T(8,128)(2,1)S(1)} %get-tuple-element.109), channel_id=1, source_target_pairs={{0,64},{4,68},{8,72},{12,76},{16,80},{20,84},{24,88},{28,92},{32,9... | collective-permute-start | bytes 319496 | tf_op jit(solution)/shard_map/ppermute | solution.py:528
  147.4 0.9 collective-permute-start.14
  148.3 0.0 collective-permute-done.10.refs_1_
  148.3 1.4 collective-permute-start.15
  149.7 0.0 collective-permute-done.11.refs_2_
  149.7 0.0 collective-permute-done.12.refs_3_
  149.7 0.0 collective-permute-done.13.refs_5_
  149.7 3.9 %collective-permute-done.14.refs_6_ = bf16[32,1664]{1,0:T(8,128)(2,1)S(1)} collective-permute-done((bf16[32,1664]{1,0:T(8,128)(2,1)S(1)}, bf16[32,1664]{1,0:T(8,128)(2,1)S(1)}, u32[]{:S(2)}, u32[]{:S(2)}) %collective-permute-start.14) | collective-permute-done | bytes 106528 | tf_op jit(solution)/shard_map/ppermute | solution.py:528
  153.7 1.1 collective-permute-done.15.refs_7_
  154.7 0.8 shard_map.148
  155.5 3.5 %all-to-all-start.4 = ((bf16[4,16,1664]{2,1,0:T(8,128)(2,1)}), bf16[4,16,1664]{2,1,0:T(8,128)(2,1)S(1)}, u32[]{:S(2)}, u32[]{:S(2)}) async-start(bf16[4,16,1664]{2,1,0:T(8,128)(2,1)} %shard_map.148), calls=%async_computation.4 | async-start | bytes 425984 | tf_op jit(solution)/shard_map/all_to_all | solution.py:532
  159.0 3.8 %shard_map.146 = bf16[128,512]{1,0:T(8,128)(2,1)} custom-call(bf16[256,512]{1,0:T(8,128)(2,1)} %get-tuple-element.82.refs_0_, f32[512]{0:T(512)} %refs_1_.3, f32[256,512]{1,0:T(8,128)} %get-tuple-element.92.refs_2_, f32[16,1280]{1,0:T(8,128)} %get-tuple-element.93.refs_3_, f32[8,1280]{1,0:T(8,128)} %copy-done.7, f32[8,1280]{1,0:T(8,128)} %copy-done.8, ...), custom_call_target="tpu_custom_call" | custom-call | flops 4000000000 | bytes 3311616 | tf_op jit(solution)/shard_map/pallas_call | solution.py:28
  162.8 5.6 %all-to-all-done.4.refs_0_ = bf16[4,16,1664]{2,1,0:T(8,128)(2,1)S(1)} async-done(((bf16[4,16,1664]{2,1,0:T(8,128)(2,1)}), bf16[4,16,1664]{2,1,0:T(8,128)(2,1)S(1)}, u32[]{:S(2)}, u32[]{:S(2)}) %all-to-all-start.4) | async-done | bytes 213024 | tf_op jit(solution)/shard_map/all_to_all | solution.py:532
  168.4 0.7 shard_map.149
  (8 shorter events, 0.0 us)
Async XLA Ops:
  1.4 12.9 %collective-permute-start.1 = (bf16[16,512]{1,0:T(8,128)(2,1)S(1)}, bf16[16,512]{1,0:T(8,128)(2,1)S(1)}, u32[]{:S(2)}, u32[]{:S(2)}) collective-permute-start(bf16[16,512]{1,0:T(8,128)(2,1)S(1)} %get-tuple-element.114), channel_id=1, source_target_pairs={{4,0},{8,4},{12,8},{16,12},{20,16},{24,20},{28,24},{32,28},{36,32}... | collective-permute-start | bytes 49160 | tf_op jit(solution)/shard_map/ppermute | solution.py:567
  12.3 10.8 %collective-permute-start = (bf16[16,512]{1,0:T(8,128)(2,1)S(1)}, bf16[16,512]{1,0:T(8,128)(2,1)S(1)}, u32[]{:S(2)}, u32[]{:S(2)}) collective-permute-start(bf16[16,512]{1,0:T(8,128)(2,1)S(1)} %get-tuple-element.115), channel_id=1, source_target_pairs={{0,4},{4,8},{8,12},{12,16},{16,20},{20,24},{24,28},{28,32},{32,36}... | collective-permute-start | bytes 49160 | tf_op jit(solution)/shard_map/ppermute | solution.py:566
  14.2 8.8 %copy-start.5 = (bf16[16,512]{1,0:T(8,128)(2,1)}, bf16[16,512]{1,0:T(8,128)(2,1)S(1)}, u32[]{:S(2)}) copy-start(bf16[16,512]{1,0:T(8,128)(2,1)S(1)} %collective-permute-done.1.refs_3_) | copy-start | bytes 49156
  23.0 0.6 copy-start.6
  64.5 15.5 %all-to-all-start.2 = ((bf16[16,64,128]{2,1,0:T(8,128)(2,1)}), bf16[16,64,128]{2,1,0:T(8,128)(2,1)S(1)}, u32[]{:S(2)}, u32[]{:S(2)}) async-start(bf16[16,64,128]{2,1,0:T(8,128)(2,1)} %shard_map.140), calls=%async_computation.2 | async-start | bytes 524288 | tf_op jit(solution)/shard_map/all_to_all | solution.py:532
  81.3 14.4 %all-to-all-start.3 = ((bf16[4,1024,128]{2,1,0:T(8,128)(2,1)}), bf16[4,1024,128]{2,1,0:T(8,128)(2,1)S(1)}, u32[]{:S(2)}, u32[]{:S(2)}) async-start(bf16[4,1024,128]{2,1,0:T(8,128)(2,1)} %shard_map.141), calls=%async_computation.3 | async-start | bytes 2097152 | tf_op jit(solution)/shard_map/all_to_all | solution.py:532
  95.7 1.0 copy-start.4
  108.8 15.6 %collective-permute-start.5 = (bf16[128,1664]{1,0:T(8,128)(2,1)}, bf16[128,1664]{1,0:T(8,128)(2,1)S(1)}, u32[]{:S(2)}, u32[]{:S(2)}) collective-permute-start(bf16[128,1664]{1,0:T(8,128)(2,1)} %get-tuple-element.79), channel_id=1, source_target_pairs={{0,4},{4,8},{8,12},{12,0},{16,20},{20,24},{24,28},{28,16},{32,36},... | collective-permute-start | bytes 1277960 | tf_op jit(solution)/shard_map/ppermute | solution.py:528
  109.5 15.9 %collective-permute-start.2 = (bf16[128,1664]{1,0:T(8,128)(2,1)}, bf16[128,1664]{1,0:T(8,128)(2,1)S(1)}, u32[]{:S(2)}, u32[]{:S(2)}) collective-permute-start(bf16[128,1664]{1,0:T(8,128)(2,1)} %get-tuple-element.75), channel_id=1, source_target_pairs={{0,64},{4,68},{8,72},{12,76},{16,80},{20,84},{24,88},{28,92},{32,9... | collective-permute-start | bytes 1277960 | tf_op jit(solution)/shard_map/ppermute | solution.py:528
  111.9 15.4 %collective-permute-start.3 = (bf16[128,1664]{1,0:T(8,128)(2,1)}, bf16[128,1664]{1,0:T(8,128)(2,1)S(1)}, u32[]{:S(2)}, u32[]{:S(2)}) collective-permute-start(bf16[128,1664]{1,0:T(8,128)(2,1)} %get-tuple-element.76), channel_id=1, source_target_pairs={{0,128},{4,132},{8,136},{12,140},{16,144},{20,148},{24,152},{28,15... | collective-permute-start | bytes 1277960 | tf_op jit(solution)/shard_map/ppermute | solution.py:528
  112.1 24.4 %collective-permute-start.4 = (bf16[128,1664]{1,0:T(8,128)(2,1)}, bf16[128,1664]{1,0:T(8,128)(2,1)S(1)}, u32[]{:S(2)}, u32[]{:S(2)}) collective-permute-start(bf16[128,1664]{1,0:T(8,128)(2,1)} %get-tuple-element.77), channel_id=1, source_target_pairs={{0,192},{4,196},{8,200},{12,204},{16,208},{20,212},{24,216},{28,22... | collective-permute-start | bytes 1277960 | tf_op jit(solution)/shard_map/ppermute | solution.py:528
  112.7 23.7 %collective-permute-start.6 = (bf16[128,1664]{1,0:T(8,128)(2,1)}, bf16[128,1664]{1,0:T(8,128)(2,1)S(1)}, u32[]{:S(2)}, u32[]{:S(2)}) collective-permute-start(bf16[128,1664]{1,0:T(8,128)(2,1)} %get-tuple-element.80), channel_id=1, source_target_pairs={{0,8},{4,12},{8,0},{12,4},{16,24},{20,28},{24,16},{28,20},{32,40},... | collective-permute-start | bytes 1277960 | tf_op jit(solution)/shard_map/ppermute | solution.py:528
  124.4 12.0 %collective-permute-start.7 = (bf16[128,1664]{1,0:T(8,128)(2,1)}, bf16[128,1664]{1,0:T(8,128)(2,1)S(1)}, u32[]{:S(2)}, u32[]{:S(2)}) collective-permute-start(bf16[128,1664]{1,0:T(8,128)(2,1)} %get-tuple-element.81), channel_id=1, source_target_pairs={{0,12},{4,0},{8,4},{12,8},{16,28},{20,16},{24,20},{28,24},{32,44},... | collective-permute-start | bytes 1277960 | tf_op jit(solution)/shard_map/ppermute | solution.py:528
  124.4 0.9 copy-start
  125.3 11.1 %collective-permute-start.8 = (f32[8,1280]{1,0:T(8,128)S(1)}, f32[8,1280]{1,0:T(8,128)S(1)}, u32[]{:S(2)}, u32[]{:S(2)}) collective-permute-start(f32[8,1280]{1,0:T(8,128)S(1)} %get-tuple-element.89), channel_id=1, source_target_pairs={{4,0},{8,4},{12,8},{16,12},{20,16},{24,20},{28,24},{32,28},{36,32}... | collective-permute-start | bytes 122888 | tf_op jit(solution)/shard_map/ppermute | solution.py:651
  127.3 11.1 %collective-permute-start.9 = (f32[8,1280]{1,0:T(8,128)S(1)}, f32[8,1280]{1,0:T(8,128)S(1)}, u32[]{:S(2)}, u32[]{:S(2)}) collective-permute-start(f32[8,1280]{1,0:T(8,128)S(1)} %get-tuple-element.90), channel_id=1, source_target_pairs={{0,4},{4,8},{8,12},{12,16},{16,20},{20,24},{24,28},{28,32},{32,36}... | collective-permute-start | bytes 122888 | tf_op jit(solution)/shard_map/ppermute | solution.py:652
  131.2 7.1 %copy-start.1 = (s32[3]{0:T(128)S(1)}, s32[3]{0:T(128)}, u32[]{:S(2)}) copy-start(s32[3]{0:T(128)} %pad_add_fusion.refs_0_) | copy-start | bytes 40
  131.2 7.1 %copy-start.2 = (bf16[128,1664]{1,0:T(8,128)(2,1)S(1)}, bf16[128,1664]{1,0:T(8,128)(2,1)}, u32[]{:S(2)}) copy-start(bf16[128,1664]{1,0:T(8,128)(2,1)} %get-tuple-element.96.refs_1_) | copy-start | bytes 1277956
  131.2 7.1 %copy-start.3 = (bf16[128,1664]{1,0:T(8,128)(2,1)S(1)}, bf16[128,1664]{1,0:T(8,128)(2,1)}, u32[]{:S(2)}) copy-start(bf16[128,1664]{1,0:T(8,128)(2,1)} %get-tuple-element.100.refs_5_) | copy-start | bytes 1277956
  136.5 3.2 %copy-start.7 = (f32[8,1280]{1,0:T(8,128)}, f32[8,1280]{1,0:T(8,128)S(1)}, u32[]{:S(2)}) copy-start(f32[8,1280]{1,0:T(8,128)S(1)} %collective-permute-done.8.refs_4_) | copy-start | bytes 122884
  138.3 1.4 copy-start.8
  139.7 8.6 %collective-permute-start.10 = (bf16[32,1664]{1,0:T(8,128)(2,1)S(1)}, bf16[32,1664]{1,0:T(8,128)(2,1)S(1)}, u32[]{:S(2)}, u32[]{:S(2)}) collective-permute-start(bf16[32,1664]{1,0:T(8,128)(2,1)S(1)} %get-tuple-element.105), channel_id=1, source_target_pairs={{0,4},{4,8},{8,12},{12,0},{16,20},{20,24},{24,28},{28,16},{32,36},... | collective-permute-start | bytes 319496 | tf_op jit(solution)/shard_map/ppermute | solution.py:528
  140.0 9.7 %collective-permute-start.11 = (bf16[32,1664]{1,0:T(8,128)(2,1)S(1)}, bf16[32,1664]{1,0:T(8,128)(2,1)S(1)}, u32[]{:S(2)}, u32[]{:S(2)}) collective-permute-start(bf16[32,1664]{1,0:T(8,128)(2,1)S(1)} %get-tuple-element.106), channel_id=1, source_target_pairs={{0,8},{4,12},{8,0},{12,4},{16,24},{20,28},{24,16},{28,20},{32,40},... | collective-permute-start | bytes 319496 | tf_op jit(solution)/shard_map/ppermute | solution.py:528
  143.8 5.9 %collective-permute-start.12 = (bf16[32,1664]{1,0:T(8,128)(2,1)S(1)}, bf16[32,1664]{1,0:T(8,128)(2,1)S(1)}, u32[]{:S(2)}, u32[]{:S(2)}) collective-permute-start(bf16[32,1664]{1,0:T(8,128)(2,1)S(1)} %get-tuple-element.107), channel_id=1, source_target_pairs={{0,12},{4,0},{8,4},{12,8},{16,28},{20,16},{24,20},{28,24},{32,44},... | collective-permute-start | bytes 319496 | tf_op jit(solution)/shard_map/ppermute | solution.py:528
  143.8 5.9 %collective-permute-start.13 = (bf16[32,1664]{1,0:T(8,128)(2,1)S(1)}, bf16[32,1664]{1,0:T(8,128)(2,1)S(1)}, u32[]{:S(2)}, u32[]{:S(2)}) collective-permute-start(bf16[32,1664]{1,0:T(8,128)(2,1)S(1)} %get-tuple-element.109), channel_id=1, source_target_pairs={{0,64},{4,68},{8,72},{12,76},{16,80},{20,84},{24,88},{28,92},{32,9... | collective-permute-start | bytes 319496 | tf_op jit(solution)/shard_map/ppermute | solution.py:528
  147.4 6.3 %collective-permute-start.14 = (bf16[32,1664]{1,0:T(8,128)(2,1)S(1)}, bf16[32,1664]{1,0:T(8,128)(2,1)S(1)}, u32[]{:S(2)}, u32[]{:S(2)}) collective-permute-start(bf16[32,1664]{1,0:T(8,128)(2,1)S(1)} %get-tuple-element.110), channel_id=1, source_target_pairs={{0,128},{4,132},{8,136},{12,140},{16,144},{20,148},{24,152},{28,15... | collective-permute-start | bytes 319496 | tf_op jit(solution)/shard_map/ppermute | solution.py:528
  148.3 6.4 %collective-permute-start.15 = (bf16[32,1664]{1,0:T(8,128)(2,1)S(1)}, bf16[32,1664]{1,0:T(8,128)(2,1)S(1)}, u32[]{:S(2)}, u32[]{:S(2)}) collective-permute-start(bf16[32,1664]{1,0:T(8,128)(2,1)S(1)} %get-tuple-element.111), channel_id=1, source_target_pairs={{0,192},{4,196},{8,200},{12,204},{16,208},{20,212},{24,216},{28,22... | collective-permute-start | bytes 319496 | tf_op jit(solution)/shard_map/ppermute | solution.py:528
  155.5 12.9 %all-to-all-start.4 = ((bf16[4,16,1664]{2,1,0:T(8,128)(2,1)}), bf16[4,16,1664]{2,1,0:T(8,128)(2,1)S(1)}, u32[]{:S(2)}, u32[]{:S(2)}) async-start(bf16[4,16,1664]{2,1,0:T(8,128)(2,1)} %shard_map.148), calls=%async_computation.4 | async-start | bytes 425984 | tf_op jit(solution)/shard_map/all_to_all | solution.py:532

commit v4 on v2

--- a/solution.py
+++ b/solution.py
@@ -15,12 +15,18 @@
 INTERPRET = False
 
 
-def call(body, outs, args, scratch=(), scalars=0, flops=10**9, vmem=58 * 2**20):
+def call(body, outs, args, scratch=(), scalars=0, unused=0, flops=10**9, vmem=58 * 2**20):
+    after = len(args) - unused
     specs = [pl.BlockSpec(memory_space=pltpu.SMEM)] * scalars
-    specs += [pl.BlockSpec(memory_space=pltpu.VMEM)] * (len(args) - scalars)
-    moved = sum(a.size * a.dtype.itemsize for a in args)
+    specs += [pl.BlockSpec(memory_space=pltpu.VMEM)] * (after - scalars)
+    specs += [pl.BlockSpec(memory_space=pl.ANY)] * unused
+    moved = sum(a.size * a.dtype.itemsize for a in args[:after])
+
+    def used(*refs):
+        body(*refs[:after], *refs[len(args) :])
+
     return pl.pallas_call(
-        body,
+        used,
         out_shape=[jax.ShapeDtypeStruct(shape, kind) for shape, kind in outs],
         in_specs=specs,
         out_specs=[pl.BlockSpec(memory_space=pltpu.VMEM)] * len(outs),
@@ -353,7 +359,7 @@
 def post_kernel(
     place, got, conv, gate, d_gated, raw, step, cumul, mixed, d_driven, d_bc, d_cumul, step_bias, decay_log, skip_gain,
     conv_w, cot, normal, normal_halo,
-    gated, d_gate, d_xbc, d_edge, d_ahead, d_step, *refs,
+    gated, d_gate, d_xbc, d_first, d_second, d_step, *refs,
 ):
     by_x, by_y, ext, d_conv_out, whole, parted = refs[:4], refs[4:8], refs[8], refs[9], refs[10], refs[11]
     rows = conv.shape[0] // 2
@@ -414,8 +420,7 @@
             total = part if total is None else total + part
         d_xbc[at, :] = total[margin:].astype(bf16)
         d_conv_out[frame * margin : (frame + 1) * margin, :] = total[:margin].astype(bf16)
-        d_ahead[8 * frame : 8 * frame + 8, :] = total[margin - 8 : margin]
-        d_edge[8 * frame : 8 * frame + 8, :] = total[margin + rows - 8 :]
+        (d_first, d_second)[frame][...] = total[margin - 8 : margin]
     columns = cot.shape[1]
     half = d_xbc.shape[1] // 2
     out_term = mm_rows(gated[...], cot[...]).reshape(COUNT, 2, 8, columns)
@@ -426,8 +431,50 @@
     whole[:, 2 * columns :] = in_term[:, :half]
     parted[:, :, :, :inner] = gate_term
     parted[:, :, :, inner:] = in_term[:, half:].reshape(COUNT // SIDE, SIDE, 8, half)
-    send_x(place, whole, by_x)
-    send_y(place, parted, by_y)
+    ring_out(lambda step: chunk_x(place, whole, step), by_x)
+    ring_out(lambda step: chunk_y(place, parted, step), by_y)
+
+
+def chunk_x(place, whole, step):
+    chunk = whole.shape[0] // SIDE
+    to = lax.rem(place[0] + step, SIDE)
+    return whole[pl.ds(pl.multiple_of(to * chunk, chunk), chunk), :].astype(bf16)
+
+
+def chunk_y(place, parted, step):
+    block = parted[:, lax.rem(place[2] + step, SIDE)]
+    return block.reshape(-1, block.shape[-1]).astype(bf16)
+
+
+def ring_out(chunk_of, slots):
+    keep, base, right, left = slots
+    half = keep.shape[0] // 2
+    keep[...] = chunk_of(0)
+    ahead, opposite, behind = chunk_of(1), chunk_of(2), chunk_of(3)
+    base[:half, :], base[half:, :] = ahead[:half], behind[half:]
+    right[:half, :], right[half:, :] = opposite[:half], ahead[half:]
+    left[:half, :], left[half:, :] = behind[:half], opposite[half:]
+
+
+def relay_kernel(base_x, right_x, left_x, base_y, right_y, left_y, to_low, to_high, *outs):
+    for base, right, left, on_right, on_left in (
+        (base_x, right_x, left_x, outs[0], outs[1]),
+        (base_y, right_y, left_y, outs[2], outs[3]),
+    ):
+        half = base.shape[0] // 2
+        columns = base.shape[1]
+        on_right[:, :columns] = (base[:half, :].astype(f32) + right[:half, :].astype(f32)).astype(bf16)
+        on_left[:, :columns] = (base[half:, :].astype(f32) + left[half:, :].astype(f32)).astype(bf16)
+    for target, edge in ((outs[2], to_high), (outs[3], to_low)):
+        target[:, columns:] = jnp.concatenate([edge[...], jnp.zeros(edge.shape, bf16)], axis=0)
+
+
+def ring_total(keep, right, left, on_right, on_left):
+    half = keep.shape[0] // 2
+    columns = keep.shape[1]
+    first = keep[:half, :].astype(f32) + left[:half, :].astype(f32) + on_right[:, :columns].astype(f32)
+    second = keep[half:, :].astype(f32) + right[half:, :].astype(f32) + on_left[:, :columns].astype(f32)
+    return jnp.concatenate([first, second], axis=0)
 
 
 def send_x(place, whole, slots):
@@ -444,28 +491,48 @@
         slots[step][...] = block.reshape(slots[step].shape).astype(slots[step].dtype)
 
 
+def norm_back(block, d_normal, gain):
+    wide = block.astype(f32)
+    scale = lax.rsqrt(jnp.mean(wide * wide, axis=-1, keepdims=True) + epsilon)
+    d_scaled = d_normal * gain.reshape(1, -1)
+    along = jnp.mean(d_scaled * wide, axis=-1, keepdims=True)
+    return scale * d_scaled - wide * (scale * scale * scale * along)
+
+
+def fold_rows(block):
+    return jnp.concatenate([block[:, 128 * nth : 128 * (nth + 1)] for nth in range(4)], axis=0)
+
+
+def unfold_rows(block):
+    return jnp.concatenate([block[8 * nth : 8 * (nth + 1)] for nth in range(4)], axis=1)
+
+
+def scalar_flag(condition):
+    return jnp.where(condition, 1.0, 0.0)
+
+
 def result_kernel(
-    both, gain, gated, out_proj, d_gate, d_xbc, d_edge, ahead, behind, d_step, in_proj, step_proj,
-    layer, grad, d_whole,
+    place, both, gain, gated, out_proj, d_gate, d_xbc, d_first, d_second, low, high, d_step, in_proj, step_proj,
+    layer, base, to_low, to_high, d_whole,
 ):
     rows = both.shape[0] // 2
     inner = out_proj.shape[0]
     branch = mm(gated[...], out_proj[...])
     layer[...] = (branch[:rows] + mirror_wide(branch[rows:])).astype(bf16)
-    d_whole[...] = d_xbc[...]
-    for frame, halo in enumerate((ahead, behind)):
-        edge = d_edge[8 * frame : 8 * frame + 8, :] + halo[...]
-        keep = d_xbc[(frame + 1) * rows - 16 : (frame + 1) * rows, :].astype(f32)
-        edge = jnp.concatenate([keep[:8], edge], axis=0)
-        d_whole[(frame + 1) * rows - 16 : (frame + 1) * rows, :] = edge.astype(bf16)
-    d_normal = mm_cols(d_gate[...], in_proj[:, :inner]) + mm_cols(d_whole[...], in_proj[:, inner:])
+    d_whole[: 2 * rows, :] = d_xbc[...]
+    edges = jnp.concatenate([d_first[...], d_second[...]], axis=0)
+    d_whole[2 * rows :, :] = edges.astype(bf16)
+    through = mm_cols(d_whole[...], in_proj[:, inner:])
+    d_normal = mm_cols(d_gate[...], in_proj[:, :inner]) + through[: 2 * rows]
     d_normal = d_normal + mm(d_step[...], step_proj[...])
-    wide = both[...].astype(f32)
-    scale = lax.rsqrt(jnp.mean(wide * wide, axis=-1, keepdims=True) + epsilon)
-    d_scaled = d_normal * gain[...].reshape(1, -1)
-    along = jnp.mean(d_scaled * wide, axis=-1, keepdims=True)
-    d_wide = scale * d_scaled - wide * (scale * scale * scale * along)
-    grad[...] = (d_wide[:rows] + mirror_wide(d_wide[rows:])).astype(bf16)
+    d_wide = norm_back(both[...], d_normal, gain[...])
+    base[...] = d_wide[:rows] + mirror_wide(d_wide[rows:])
+    first = norm_back(low[8:, :], through[2 * rows : 2 * rows + 8], gain[...])
+    second = norm_back(mirror_exact(high[...])[8:, :], through[2 * rows + 8 :], gain[...])
+    at_start = (place[0] + place[1] + place[2]) == 0
+    at_end = (place[0] + place[1] + place[2]) == 3 * (SIDE - 1)
+    to_low[...] = fold_rows(first * (1.0 - scalar_flag(at_start))).astype(bf16)
+    to_high[...] = fold_rows(mirror_wide(second) * (1.0 - scalar_flag(at_end))).astype(bf16)
 
 
 def total_of(refs):
@@ -476,29 +543,65 @@
 
 
 def first_sum_kernel(place, *refs):
-    from_x, from_y, by_y, by_x, parted, whole = refs[:4], refs[4:8], refs[9:13], refs[13:17], refs[17], refs[18]
-    parted[...] = total_of(from_x).reshape(parted.shape)
-    whole[...] = total_of(from_y)
+    from_x, from_y, by_y, by_x, kept = refs[:5], refs[5:10], refs[10:14], refs[14:18], refs[18]
+    parted, whole = refs[19], refs[20]
+    parted[...] = ring_total(*from_x).reshape(parted.shape)
+    whole[...] = ring_total(*from_y)
     send_y(place, parted, by_y)
-    send_x(place, whole, by_x)
+    columns = whole.shape[1]
+    chunk = whole.shape[0] // SIDE
+    for step in range(SIDE):
+        to = lax.rem(place[0] + step, SIDE)
+        block = whole[pl.ds(pl.multiple_of(to * chunk, chunk), chunk), :]
+        by_x[step][:, :columns] = block.astype(by_x[step].dtype)
+    high = from_y[3][:32, columns:].astype(f32)
+    low = from_y[4][:32, columns:].astype(f32)
+    on_high = scalar_flag((place[2] == 0) & (place[1] == SIDE - 1))
+    on_low = scalar_flag((place[2] == SIDE - 1) & (place[1] == 0))
+    by_x[1][:, columns:] = (high * on_high).astype(bf16)
+    by_x[3][:, columns:] = (low * on_low).astype(bf16)
+    kept[:32, :] = high * (1.0 - on_high)
+    kept[32:, :] = low * (1.0 - on_low)
 
 
 def second_sum_kernel(place, *refs):
-    first, second, by_z, keep = refs[:4], refs[4:8], refs[8:12], refs[12]
-    keep[:, 0] = total_of(first).reshape(SIDE, 8, -1)
-    keep[:, 1] = total_of(second).reshape(SIDE, 8, -1)
-    for step in range(SIDE):
-        to = lax.rem(place[1] + step, SIDE)
-        by_z[step][...] = keep[to].reshape(by_z[step].shape).astype(by_z[step].dtype)
-
-
-def last_sum_kernel(*refs):
-    grad_in, grad_out = refs[4:]
-    total = total_of(refs[:4])
+    first, second, kept, by_z = refs[:4], refs[4:8], refs[8], refs[9]
+    columns = first[0].shape[1]
+    high = kept[:32, :] + second[1][:, columns:].astype(f32)
+    low = kept[32:, :] + second[3][:, columns:].astype(f32)
+    first = total_of(first).reshape(SIDE, 8, -1)
+    total = second[0][...]
+    for step in range(1, SIDE):
+        total = total + second[step][:, :columns].astype(f32)
+    second = total.reshape(SIDE, 8, -1)
+    above = scalar_flag(place[2] == 0)
+    below = scalar_flag(place[2] == SIDE - 1)
+    for to in range(SIDE):
+        own = scalar_flag(place[1] == to)
+        share_high = own * (1.0 - above) + scalar_flag(lax.rem(place[1] + 1, SIDE) == to) * above
+        share_low = own * (1.0 - below) + scalar_flag(lax.rem(place[1] + SIDE - 1, SIDE) == to) * below
+        edges = [high[:16] * share_high, high[16:] * share_high, low[:16] * share_low, low[16:] * share_low]
+        by_z[to, :, :columns] = jnp.concatenate([first[to], second[to]], axis=0).astype(bf16)
+        by_z[to, :, columns:] = jnp.concatenate(edges, axis=1).astype(bf16)
+
+
+def last_sum_kernel(parts, base, grad_in, grad_out, grad):
+    total = parts[0].astype(f32)
+    for step in range(1, SIDE):
+        total = total + parts[step].astype(f32)
     columns = grad_out.shape[1]
+    joined = total.shape[1] - 512
     grad_out[:8, :] = total[:8, :columns]
     grad_out[8:, :] = total[:8, columns : 2 * columns]
-    grad_in[...] = jnp.concatenate([total[8:, : 2 * columns], total[:8, 2 * columns :], total[8:, 2 * columns :]], axis=1)
+    grad_in[...] = jnp.concatenate(
+        [total[8:, : 2 * columns], total[:8, 2 * columns : joined], total[8:, 2 * columns : joined]], axis=1
+    )
+    edges = total[:, joined:]
+    high = unfold_rows(jnp.concatenate([edges[:, :128], edges[:, 128:256]], axis=0))
+    low = unfold_rows(jnp.concatenate([edges[:, 256:384], edges[:, 384:]], axis=0))
+    rows = base.shape[0]
+    whole = jnp.concatenate([base[:8, :] + high, base[8 : rows - 8, :], base[rows - 8 :, :] + low], axis=0)
+    grad[...] = whole.astype(bf16)
 
 
 def axis_pairs(stride, step):
@@ -511,6 +614,13 @@
 
 def exchange(parts, stride):
     return [parts[0]] + [lax.ppermute(parts[step], "seq", axis_pairs(stride, step)) for step in range(1, SIDE)]
+
+
+def around(to_right, to_left, stride):
+    return (
+        lax.ppermute(to_right, "seq", axis_pairs(stride, 1)),
+        lax.ppermute(to_left, "seq", axis_pairs(stride, SIDE - 1)),
+    )
 
 
 def transpose_over(parts, groups):
@@ -543,6 +653,7 @@
     stride_x, stride_z, stride_y = SIDE * SIDE, SIDE, 1
     index = lax.axis_index("seq")
     place = jnp.stack([index // stride_x, index // stride_z % SIDE, index % SIDE]).astype(jnp.int32)
+    aligned = [[base + SIDE * digit for digit in range(SIDE)] for base in range(COUNT) if base // SIDE % SIDE == 0]
     beside = [[SIDE * base + digit for digit in range(SIDE)] for base in range(COUNT // SIDE)]
     across = [[base + SIDE * digit for digit in range(COUNT // SIDE)] for base in range(SIDE)]
     upward = [(i, i + 1) for i in range(COUNT - 1)]
@@ -599,14 +710,14 @@
     states = transpose_over(spread, beside)
     eighth = 8 * COUNT // SIDE
     joined = inner + channels // 2
-    gated, d_gate, d_xbc, d_edge, d_ahead, d_step, *parts = call(
+    gated, d_gate, d_xbc, d_first, d_second, d_step, *parts = call(
         post_kernel,
         [
             ((both_rows, inner), bf16),
             ((both_rows, inner), bf16),
             ((both_rows, channels), bf16),
-            ((16, channels), f32),
-            ((16, channels), f32),
+            ((8, channels), f32),
+            ((8, channels), f32),
             ((both_rows, heads), bf16),
         ]
         + slots(eighth, joined, bf16) * 2,
@@ -622,43 +733,53 @@
         ],
         scalars=1,
     )
-    from_x = exchange(parts[:4], stride_x)
-    from_y = exchange(parts[4:], stride_y)
-    ahead = lax.ppermute(d_ahead[:8], "seq", downward)
-    behind = lax.ppermute(d_ahead[8:], "seq", upward)
-    layer_out, grad_input = call(
+    layer_out, base, to_low, to_high = call(
         result_kernel,
-        [((rows, width), bf16), ((rows, width), bf16)],
+        [((rows, width), bf16), ((rows, width), f32), ((32, 128), bf16), ((32, 128), bf16)],
         (
-            both, norm_gain, gated, out_proj, d_gate, d_xbc, d_edge, ahead, behind, d_step,
+            place, both, norm_gain, gated, out_proj, d_gate, d_xbc, d_first, d_second, low, high, d_step,
             in_proj, step_turned,
         ),
-        [pltpu.VMEM((both_rows, channels), bf16)],
+        [pltpu.VMEM((both_rows + 16, channels), bf16)],
+        scalars=1,
         flops=8 * 10**9,
     )
-    parts = call(
+    keep_x, base_x, right_x, left_x, keep_y, base_y, right_y, left_y = parts
+    right_x, left_x = around(right_x, left_x, stride_x)
+    right_y, left_y = around(right_y, left_y, stride_y)
+    relayed = call(
+        relay_kernel,
+        [((eighth // 2, joined), bf16)] * 2 + [((eighth // 2, joined + 128), bf16)] * 2,
+        (base_x, right_x, left_x, base_y, right_y, left_y, to_low, to_high),
+        vmem=16 * 2**20,
+    )
+    from_x = [keep_x, right_x, left_x, *around(relayed[0], relayed[1], stride_x)]
+    from_y = [keep_y, right_y, left_y, *around(relayed[2], relayed[3], stride_y)]
+    small = eighth // SIDE
+    *parts, kept = call(
         first_sum_kernel,
-        slots(eighth // SIDE, joined, f32) * 2,
-        (place, *from_x, *from_y, layer_out),
+        slots(small, joined, f32)
+        + [((small, joined), f32), ((small, joined + 128), bf16), ((small, joined), bf16), ((small, joined + 128), bf16)]
+        + [((64, 128), f32)],
+        (place, *from_x, *from_y),
         [pltpu.VMEM((SIDE, SIDE, 8, joined), f32), pltpu.VMEM((eighth, joined), f32)],
         scalars=1,
         vmem=16 * 2**20,
     )
     first = exchange(parts[:4], stride_y)
     second = exchange(parts[4:], stride_x)
-    parts = call(
+    (by_z,) = call(
         second_sum_kernel,
-        slots(16, joined, f32),
-        (place, *first, *second),
-        [pltpu.VMEM((SIDE, 2, 8, joined), f32)],
+        [((SIDE, 16, joined + 512), bf16)],
+        (place, *first, *second, kept),
         scalars=1,
         vmem=16 * 2**20,
     )
-    last = exchange(parts, stride_z)
-    grad_in_proj, grad_out_proj = call(
+    last = transpose_over(by_z, aligned)
+    grad_in_proj, grad_out_proj, grad_input = call(
         last_sum_kernel,
-        [((8, inner + channels), f32), ((16, width), f32)],
-        tuple(last),
+        [((8, inner + channels), f32), ((16, width), f32), ((rows, width), bf16)],
+        (last, base),
         vmem=16 * 2**20,
     )
     return (layer_out, grad_input, grad_in_proj, grad_out_proj)

time: 173 us -> 168 us (0.971)
  starting transfers between devices: 55.2 us -> 41.3 us
  blocking collectives: 31.9 us -> 44.5 us
  waiting for transfers between devices: 42.9 us -> 38.8 us
    ppermute x15 -> x6, starting transfers between devices: 22 us -> 6.1 us  [exchange(): lax.ppermute(parts[step], 'seq', axis_pairs(stride, step))]
    all_to_all x2 -> x3, blocking collectives: 31.9 us -> 44.5 us  [transpose_over(): return lax.all_to_all(parts, 'seq', 0, 0, axis_index_groups=groups)]
    ppermute x15 -> x6, waiting for transfers between devices: 18.3 us -> 6.21 us  [exchange(): lax.ppermute(parts[step], 'seq', axis_pairs(stride, step))]
    ppermute x2 -> x8, waiting for transfers between devices: 1.36 us -> 9.43 us  [the longest x4 4.84 us: around(): lax.ppermute(to_left, 'seq', axis_pairs(stride, SIDE - 1))]
    ppermute x2 -> x8, starting transfers between devices: 10.9 us -> 12.9 us  [the longest x4 6.67 us: around(): lax.ppermute(to_right, 'seq', axis_pairs(stride, 1))]
    pallas_call x10 -> x11, Pallas kernels: 36.4 us -> 37 us  [call(): pl.pallas_call(used, out_shape=[jax.ShapeDtypeStruct(shape, kind) for sha...]
  transfers between devices with their start and end apart: 21 -> 18, of which waited for: 15 -> 9; matrix products, arithmetic and copies ran while one was open for 1% -> 0% of each run, Pallas kernels for 7% -> 7%
where the time goes in v4:
time: 168 us; the launch traced here: 167 us
  blocking collectives  44.5 us (26%)
  starting transfers between devices  41.3 us (25%)
  waiting for transfers between devices  38.8 us (23%)
  Pallas kernels  37 us (22%)
  local copies, waits for them, and re-layouts  3.74 us (2%)
    all_to_all x3, blocking collectives, transpose_over(): return lax.all_to_all(parts, 'seq', 0, 0, axis_index_groups=groups)  44.5 us
    pallas_call x11, Pallas kernels, call(): pl.pallas_call(used, out_shape=[jax.ShapeDtypeStruct(shape, kind) for sha...  37 us
    all_to_all x2, waiting for transfers between devices, transpose_over(): return lax.all_to_all(parts, 'seq', 0, 0, axis_index_groups=groups)  14.4 us
    ppermute x1, starting transfers between devices, shards(): high = lax.ppermute(sequence[:16], 'seq', downward)  10.9 us
    all_to_all x2, starting transfers between devices, transpose_over(): return lax.all_to_all(parts, 'seq', 0, 0, axis_index_groups=groups)  9.47 us
    ppermute x1, waiting for transfers between devices, shards(): low = lax.ppermute(sequence[rows - 16:], 'seq', upward)  8.8 us
    ppermute x4, starting transfers between devices, around(): lax.ppermute(to_right, 'seq', axis_pairs(stride, 1))  6.67 us
    ppermute x4, starting transfers between devices, around(): lax.ppermute(to_left, 'seq', axis_pairs(stride, SIDE - 1))  6.24 us
  transfers between devices with their start and end apart: 18, of which 9 were waited for; matrix products, arithmetic and copies ran while one was open for 0% of the time, Pallas kernels for 7%

profile of v4, /device:TPU:6, one launch (start us, length us, event | category | flops | bytes accessed | tf_op | source)
XLA Modules:
  0.0 166.8 jit_solution(7635768857451385809)
XLA Ops:
  0.6 0.7 fusion
  1.4 10.9 %collective-permute-start.1 = (bf16[16,512]{1,0:T(8,128)(2,1)S(1)}, bf16[16,512]{1,0:T(8,128)(2,1)S(1)}, u32[]{:S(2)}, u32[]{:S(2)}) collective-permute-start(bf16[16,512]{1,0:T(8,128)(2,1)S(1)} %get-tuple-element.104), channel_id=1, source_target_pairs={{4,0},{8,4},{12,8},{16,12},{20,16},{24,20},{28,24},{32,28},{36,32}... | collective-permute-start | bytes 49160 | tf_op jit(solution)/shard_map/ppermute | solution.py:662
  12.3 1.9 %collective-permute-start = (bf16[16,512]{1,0:T(8,128)(2,1)S(1)}, bf16[16,512]{1,0:T(8,128)(2,1)S(1)}, u32[]{:S(2)}, u32[]{:S(2)}) collective-permute-start(bf16[16,512]{1,0:T(8,128)(2,1)S(1)} %get-tuple-element.105), channel_id=1, source_target_pairs={{0,4},{4,8},{8,12},{12,16},{16,20},{20,24},{24,28},{28,32},{32,36}... | collective-permute-start | bytes 49160 | tf_op jit(solution)/shard_map/ppermute | solution.py:661
  14.2 0.0 collective-permute-done.1.refs_3_.refs_10_
  14.2 0.0 copy-start.9
  14.2 8.8 %collective-permute-done.refs_2_.refs_9_ = bf16[16,512]{1,0:T(8,128)(2,1)S(1)} collective-permute-done((bf16[16,512]{1,0:T(8,128)(2,1)S(1)}, bf16[16,512]{1,0:T(8,128)(2,1)S(1)}, u32[]{:S(2)}, u32[]{:S(2)}) %collective-permute-start) | collective-permute-done | bytes 16416 | tf_op jit(solution)/shard_map/ppermute | solution.py:661
  23.0 0.0 copy-done.9
  23.0 0.6 copy-done.10
  23.6 7.0 %shard_map.138 = (bf16[4,1040,128]{2,1,0:T(8,128)(2,1)}, bf16[256,512]{1,0:T(8,128)(2,1)}, bf16[256,512]{1,0:T(8,128)(2,1)}, bf16[32,512]{1,0:T(8,128)(2,1)}, bf...) custom-call(bf16[128,512]{1,0:T(8,128)(2,1)} %refs_0_.1, ...), custom_call_target="tpu_custom_call" | custom-call | flops 1000000000 | bytes 3746944 | tf_op jit(solution)/shard_map/pallas_call | solution.py:28
  30.6 17.6 %all_to_all.25.refs_0_ = bf16[4,1040,128]{2,1,0:T(8,128)(2,1)S(1)} all-to-all(bf16[4,1040,128]{2,1,0:T(8,128)(2,1)} %get-tuple-element.55), channel_id=1, replica_groups={{0,4,8,12},{16,20,24,28},{32,36,40,44},{48,52,56,60},{64,68,72,76},{80,..., dimensions={0} | all-to-all | bytes 2129920 | tf_op jit(solution)/shard_map/all_to_all | solution.py:627
  48.2 0.4 shard_map.139
  48.6 14.2 %all_to_all.26.refs_0_ = bf16[16,72,128]{2,1,0:T(8,128)(2,1)S(1)} all-to-all(bf16[16,72,128]{2,1,0:T(8,128)(2,1)S(1)} %shard_map.139), channel_id=1, replica_groups={{0,16,32,48,64,80,96,112,128,144,160,176,192,208,224,240},{4,20,36,52,6..., dimensions={0} | all-to-all | bytes 589824 | tf_op jit(solution)/shard_map/all_to_all | solution.py:627
  62.9 1.6 shard_map.140
  64.4 5.8 %all-to-all-start.2 = ((bf16[16,64,128]{2,1,0:T(8,128)(2,1)}), bf16[16,64,128]{2,1,0:T(8,128)(2,1)S(1)}, u32[]{:S(2)}, u32[]{:S(2)}) async-start(bf16[16,64,128]{2,1,0:T(8,128)(2,1)} %shard_map.140), calls=%async_computation.2 | async-start | bytes 524288 | tf_op jit(solution)/shard_map/all_to_all | solution.py:627
  70.2 9.8 %all-to-all-done.2.refs_1_ = bf16[16,64,128]{2,1,0:T(8,128)(2,1)S(1)} async-done(((bf16[16,64,128]{2,1,0:T(8,128)(2,1)}), bf16[16,64,128]{2,1,0:T(8,128)(2,1)S(1)}, u32[]{:S(2)}, u32[]{:S(2)}) %all-to-all-start.2) | async-done | bytes 262176 | tf_op jit(solution)/shard_map/all_to_all | solution.py:627
  80.0 1.3 shard_map.141
  81.3 3.7 %all-to-all-start.3 = ((bf16[4,1024,128]{2,1,0:T(8,128)(2,1)}), bf16[4,1024,128]{2,1,0:T(8,128)(2,1)S(1)}, u32[]{:S(2)}, u32[]{:S(2)}) async-start(bf16[4,1024,128]{2,1,0:T(8,128)(2,1)} %shard_map.141), calls=%async_computation.3 | async-start | bytes 2097152 | tf_op jit(solution)/shard_map/all_to_all | solution.py:627
  85.0 0.6 pad_add_fusion.refs_0_
  85.6 5.5 %shard_map.142 = (f32[256,1024]{1,0:T(8,128)}, f32[256,1024]{1,0:T(8,128)}, f32[256,256]{1,0:T(8,128)}, f32[256,16]{1,0:T(8,128)}) custom-call(f32[256,1280]{1,0:T(8,128)} %get-tuple-element.56.refs_0_.refs_2_, f32[256,1024]{1,0:T(8,128)} %get-tuple-element.57.refs_1_.refs_3_, bf16[256,1024]{1,0:T(8,128)(2,1)} %get-tuple-element.58.refs_2_.refs_4_, ...), custom_call_target="tpu_custom_call" | custom-call | flops 8000000000 | bytes 2932736 | tf_op jit(solution)/shard_map/pallas_call | solution.py:28
  91.1 4.6 %all-to-all-done.3.refs_1_ = bf16[4,1024,128]{2,1,0:T(8,128)(2,1)S(1)} async-done(((bf16[4,1024,128]{2,1,0:T(8,128)(2,1)}), bf16[4,1024,128]{2,1,0:T(8,128)(2,1)S(1)}, u32[]{:S(2)}, u32[]{:S(2)}) %all-to-all-start.3) | async-done | bytes 1048608 | tf_op jit(solution)/shard_map/all_to_all | solution.py:627
  95.7 1.0 copy-done.8
  96.7 12.3 %shard_map.143 = (bf16[256,1024]{1,0:T(8,128)(2,1)}, bf16[256,1024]{1,0:T(8,128)(2,1)}, bf16[256,1280]{1,0:T(8,128)(2,1)}, f32[8,1280]{1,0:T(8,128)}, f32[8,1280...) custom-call(s32[3]{0:T(128)} %pad_add_fusion.refs_0_, ...), custom_call_target="tpu_custom_call" | custom-call | flops 1000000000 | bytes 6934732 | tf_op jit(solution)/shard_map/pallas_call | solution.py:28
  109.0 2.5 %collective-permute-start.2 = (bf16[128,1664]{1,0:T(8,128)(2,1)}, bf16[128,1664]{1,0:T(8,128)(2,1)S(1)}, u32[]{:S(2)}, u32[]{:S(2)}) collective-permute-start(bf16[128,1664]{1,0:T(8,128)(2,1)} %get-tuple-element.78), channel_id=1, source_target_pairs={{0,64},{4,68},{8,72},{12,76},{16,80},{20,84},{24,88},{28,92},{32,9... | collective-permute-start | bytes 1277960 | tf_op jit(solution)/shard_map/ppermute | solution.py:621
  111.5 0.0 collective-permute-start.3
  111.5 0.6 collective-permute-start.4
  112.0 2.6 %collective-permute-start.5 = (bf16[128,1664]{1,0:T(8,128)(2,1)}, bf16[128,1664]{1,0:T(8,128)(2,1)S(1)}, u32[]{:S(2)}, u32[]{:S(2)}) collective-permute-start(bf16[128,1664]{1,0:T(8,128)(2,1)} %get-tuple-element.83), channel_id=1, source_target_pairs={{0,12},{4,0},{8,4},{12,8},{16,28},{20,16},{24,20},{28,24},{32,44},... | collective-permute-start | bytes 1277960 | tf_op jit(solution)/shard_map/ppermute | solution.py:622
  114.7 6.4 %shard_map.144 = (bf16[128,512]{1,0:T(8,128)(2,1)}, f32[128,512]{1,0:T(8,128)}, bf16[32,128]{1,0:T(8,128)(2,1)}, bf16[32,128]{1,0:T(8,128)(2,1)}) custom-call(s32[3]{0:T(128)} %pad_add_fusion.refs_0_, bf16[256,512]{1,0:T(8,128)(2,1)} %get-tuple-element.54.refs_1_, f32[512]{0:T(512)} %refs_2_.1, bf16[256,1024]{1,0:T(8,128)(2,1)} %get-tuple-element.70.refs_3_, ...), custom_call_target="tpu_custom_call" | custom-call | flops 8000000000 | bytes 5515276 | tf_op jit(solution)/shard_map/pallas_call | solution.py:28
  121.1 0.0 collective-permute-done.2.refs_1_.refs_2_
  121.1 0.0 collective-permute-done.3.refs_2_.refs_3_
  121.1 1.2 collective-permute-done.4.refs_4_.refs_7_
  122.3 0.0 collective-permute-done.5.refs_5_.refs_8_
  122.3 0.0 copy-done.3
  122.3 0.0 copy-done.4
  122.3 0.0 copy-start.6
  122.4 0.7 copy-done.6
  123.1 0.7 copy-done.7
  123.8 0.2 shard_map.145
  124.0 0.1 collective-permute-start.8
  124.0 3.6 %collective-permute-start.9 = (bf16[64,1792]{1,0:T(8,128)(2,1)S(1)}, bf16[64,1792]{1,0:T(8,128)(2,1)S(1)}, u32[]{:S(2)}, u32[]{:S(2)}) collective-permute-start(bf16[64,1792]{1,0:T(8,128)(2,1)S(1)} %get-tuple-element.90), channel_id=1, source_target_pairs={{0,12},{4,0},{8,4},{12,8},{16,28},{20,16},{24,20},{28,24},{32,44},... | collective-permute-start | bytes 688136 | tf_op jit(solution)/shard_map/ppermute | solution.py:622
  127.6 3.5 %collective-permute-start.6 = (bf16[64,1664]{1,0:T(8,128)(2,1)S(1)}, bf16[64,1664]{1,0:T(8,128)(2,1)S(1)}, u32[]{:S(2)}, u32[]{:S(2)}) collective-permute-start(bf16[64,1664]{1,0:T(8,128)(2,1)S(1)} %get-tuple-element.86), channel_id=1, source_target_pairs={{0,64},{4,68},{8,72},{12,76},{16,80},{20,84},{24,88},{28,92},{32,9... | collective-permute-start | bytes 638984 | tf_op jit(solution)/shard_map/ppermute | solution.py:621
  131.1 0.0 collective-permute-start.7
  131.2 3.4 %collective-permute-done.6.refs_4_ = bf16[64,1664]{1,0:T(8,128)(2,1)S(1)} collective-permute-done((bf16[64,1664]{1,0:T(8,128)(2,1)S(1)}, bf16[64,1664]{1,0:T(8,128)(2,1)S(1)}, u32[]{:S(2)}, u32[]{:S(2)}) %collective-permute-start.6) | collective-permute-done | bytes 213024 | tf_op jit(solution)/shard_map/ppermute | solution.py:621
  134.5 4.8 %collective-permute-done.7.refs_5_ = bf16[64,1664]{1,0:T(8,128)(2,1)S(1)} collective-permute-done((bf16[64,1664]{1,0:T(8,128)(2,1)S(1)}, bf16[64,1664]{1,0:T(8,128)(2,1)S(1)}, u32[]{:S(2)}, u32[]{:S(2)}) %collective-permute-start.7) | collective-permute-done | bytes 213024 | tf_op jit(solution)/shard_map/ppermute | solution.py:622
  139.3 0.0 collective-permute-done.8.refs_9_
  139.3 0.0 collective-permute-done.9.refs_10_
  139.4 0.0 copy-done
  139.4 0.0 copy-done.1
  139.4 1.1 shard_map.146
  140.5 0.1 collective-permute-start.10
  140.5 0.1 collective-permute-start.13
  140.6 2.0 %collective-permute-start.15 = (bf16[32,1792]{1,0:T(8,128)(2,1)S(1)}, bf16[32,1792]{1,0:T(8,128)(2,1)S(1)}, u32[]{:S(2)}, u32[]{:S(2)}) collective-permute-start(bf16[32,1792]{1,0:T(8,128)(2,1)S(1)} %get-tuple-element.98), channel_id=1, source_target_pairs={{0,192},{4,196},{8,200},{12,204},{16,208},{20,212},{24,216},{28,22... | collective-permute-start | bytes 344072 | tf_op jit(solution)/shard_map/ppermute | solution.py:616
  142.6 3.3 %collective-permute-start.11 = (bf16[32,1664]{1,0:T(8,128)(2,1)S(1)}, bf16[32,1664]{1,0:T(8,128)(2,1)S(1)}, u32[]{:S(2)}, u32[]{:S(2)}) collective-permute-start(bf16[32,1664]{1,0:T(8,128)(2,1)S(1)} %get-tuple-element.93), channel_id=1, source_target_pairs={{0,8},{4,12},{8,0},{12,4},{16,24},{20,28},{24,16},{28,20},{32,40},... | collective-permute-start | bytes 319496 | tf_op jit(solution)/shard_map/ppermute | solution.py:616
  146.0 0.6 collective-permute-start.12
  146.6 0.0 collective-permute-done.10.refs_2_
  146.6 0.0 collective-permute-start.14
  146.6 2.3 %collective-permute-done.11.refs_3_ = bf16[32,1664]{1,0:T(8,128)(2,1)S(1)} collective-permute-done((bf16[32,1664]{1,0:T(8,128)(2,1)S(1)}, bf16[32,1664]{1,0:T(8,128)(2,1)S(1)}, u32[]{:S(2)}, u32[]{:S(2)}) %collective-permute-start.11) | collective-permute-done | bytes 106528 | tf_op jit(solution)/shard_map/ppermute | solution.py:616
  148.9 1.8 %collective-permute-done.12.refs_4_ = bf16[32,1664]{1,0:T(8,128)(2,1)S(1)} collective-permute-done((bf16[32,1664]{1,0:T(8,128)(2,1)S(1)}, bf16[32,1664]{1,0:T(8,128)(2,1)S(1)}, u32[]{:S(2)}, u32[]{:S(2)}) %collective-permute-start.12) | collective-permute-done | bytes 106528 | tf_op jit(solution)/shard_map/ppermute | solution.py:616
  150.7 2.1 %collective-permute-done.14.refs_7_ = bf16[32,1664]{1,0:T(8,128)(2,1)S(1)} collective-permute-done((bf16[32,1664]{1,0:T(8,128)(2,1)S(1)}, bf16[32,1664]{1,0:T(8,128)(2,1)S(1)}, u32[]{:S(2)}, u32[]{:S(2)}) %collective-permute-start.14) | collective-permute-done | bytes 106528 | tf_op jit(solution)/shard_map/ppermute | solution.py:616
  152.8 0.0 collective-permute-done.13.refs_6_
  152.8 0.0 collective-permute-done.15.refs_8_
  152.8 0.7 shard_map.147
  153.4 12.6 %all_to_all.27.refs_0_ = bf16[4,16,2176]{2,1,0:T(8,128)(2,1)S(1)} all-to-all(bf16[4,16,2176]{2,1,0:T(8,128)(2,1)S(1)} %shard_map.147), channel_id=1, replica_groups={{0,16,32,48},{4,20,36,52},{8,24,40,56},{12,28,44,60},{64,80,96,112},{68..., dimensions={0} | all-to-all | bytes 557056 | tf_op jit(solution)/shard_map/all_to_all | solution.py:627
  166.1 0.0 copy-done.5
  166.1 0.7 shard_map.148
  (10 shorter events, 0.0 us)
Async XLA Ops:
  1.4 12.9 %collective-permute-start.1 = (bf16[16,512]{1,0:T(8,128)(2,1)S(1)}, bf16[16,512]{1,0:T(8,128)(2,1)S(1)}, u32[]{:S(2)}, u32[]{:S(2)}) collective-permute-start(bf16[16,512]{1,0:T(8,128)(2,1)S(1)} %get-tuple-element.104), channel_id=1, source_target_pairs={{4,0},{8,4},{12,8},{16,12},{20,16},{24,20},{28,24},{32,28},{36,32}... | collective-permute-start | bytes 49160 | tf_op jit(solution)/shard_map/ppermute | solution.py:662
  12.3 10.8 %collective-permute-start = (bf16[16,512]{1,0:T(8,128)(2,1)S(1)}, bf16[16,512]{1,0:T(8,128)(2,1)S(1)}, u32[]{:S(2)}, u32[]{:S(2)}) collective-permute-start(bf16[16,512]{1,0:T(8,128)(2,1)S(1)} %get-tuple-element.105), channel_id=1, source_target_pairs={{0,4},{4,8},{8,12},{12,16},{16,20},{20,24},{24,28},{28,32},{32,36}... | collective-permute-start | bytes 49160 | tf_op jit(solution)/shard_map/ppermute | solution.py:661
  14.2 8.8 %copy-start.9 = (bf16[16,512]{1,0:T(8,128)(2,1)}, bf16[16,512]{1,0:T(8,128)(2,1)S(1)}, u32[]{:S(2)}) copy-start(bf16[16,512]{1,0:T(8,128)(2,1)S(1)} %collective-permute-done.1.refs_3_.refs_10_) | copy-start | bytes 49156
  23.0 0.6 copy-start.10
  64.4 15.5 %all-to-all-start.2 = ((bf16[16,64,128]{2,1,0:T(8,128)(2,1)}), bf16[16,64,128]{2,1,0:T(8,128)(2,1)S(1)}, u32[]{:S(2)}, u32[]{:S(2)}) async-start(bf16[16,64,128]{2,1,0:T(8,128)(2,1)} %shard_map.140), calls=%async_computation.2 | async-start | bytes 524288 | tf_op jit(solution)/shard_map/all_to_all | solution.py:627
  81.3 14.4 %all-to-all-start.3 = ((bf16[4,1024,128]{2,1,0:T(8,128)(2,1)}), bf16[4,1024,128]{2,1,0:T(8,128)(2,1)S(1)}, u32[]{:S(2)}, u32[]{:S(2)}) async-start(bf16[4,1024,128]{2,1,0:T(8,128)(2,1)} %shard_map.141), calls=%async_computation.3 | async-start | bytes 2097152 | tf_op jit(solution)/shard_map/all_to_all | solution.py:627
  95.7 1.0 copy-start.8
  109.0 12.1 %collective-permute-start.2 = (bf16[128,1664]{1,0:T(8,128)(2,1)}, bf16[128,1664]{1,0:T(8,128)(2,1)S(1)}, u32[]{:S(2)}, u32[]{:S(2)}) collective-permute-start(bf16[128,1664]{1,0:T(8,128)(2,1)} %get-tuple-element.78), channel_id=1, source_target_pairs={{0,64},{4,68},{8,72},{12,76},{16,80},{20,84},{24,88},{28,92},{32,9... | collective-permute-start | bytes 1277960 | tf_op jit(solution)/shard_map/ppermute | solution.py:621
  111.5 9.7 %collective-permute-start.3 = (bf16[128,1664]{1,0:T(8,128)(2,1)}, bf16[128,1664]{1,0:T(8,128)(2,1)S(1)}, u32[]{:S(2)}, u32[]{:S(2)}) collective-permute-start(bf16[128,1664]{1,0:T(8,128)(2,1)} %get-tuple-element.79), channel_id=1, source_target_pairs={{0,192},{4,196},{8,200},{12,204},{16,208},{20,212},{24,216},{28,22... | collective-permute-start | bytes 1277960 | tf_op jit(solution)/shard_map/ppermute | solution.py:622
  111.5 10.9 %collective-permute-start.4 = (bf16[128,1664]{1,0:T(8,128)(2,1)}, bf16[128,1664]{1,0:T(8,128)(2,1)S(1)}, u32[]{:S(2)}, u32[]{:S(2)}) collective-permute-start(bf16[128,1664]{1,0:T(8,128)(2,1)} %get-tuple-element.82), channel_id=1, source_target_pairs={{0,4},{4,8},{8,12},{12,0},{16,20},{20,24},{24,28},{28,16},{32,36},... | collective-permute-start | bytes 1277960 | tf_op jit(solution)/shard_map/ppermute | solution.py:621
  112.0 10.3 %collective-permute-start.5 = (bf16[128,1664]{1,0:T(8,128)(2,1)}, bf16[128,1664]{1,0:T(8,128)(2,1)S(1)}, u32[]{:S(2)}, u32[]{:S(2)}) collective-permute-start(bf16[128,1664]{1,0:T(8,128)(2,1)} %get-tuple-element.83), channel_id=1, source_target_pairs={{0,12},{4,0},{8,4},{12,8},{16,28},{20,16},{24,20},{28,24},{32,44},... | collective-permute-start | bytes 1277960 | tf_op jit(solution)/shard_map/ppermute | solution.py:622
  114.7 7.7 %copy-start.3 = (bf16[128,1664]{1,0:T(8,128)(2,1)S(1)}, bf16[128,1664]{1,0:T(8,128)(2,1)}, u32[]{:S(2)}) copy-start(bf16[128,1664]{1,0:T(8,128)(2,1)} %get-tuple-element.80.refs_0_) | copy-start | bytes 1277956
  114.7 7.7 %copy-start.4 = (bf16[128,1664]{1,0:T(8,128)(2,1)S(1)}, bf16[128,1664]{1,0:T(8,128)(2,1)}, u32[]{:S(2)}) copy-start(bf16[128,1664]{1,0:T(8,128)(2,1)} %get-tuple-element.81.refs_3_) | copy-start | bytes 1277956
  122.3 0.7 copy-start.6
  123.0 0.7 copy-start.7
  123.7 15.6 %copy-start = (s32[3]{0:T(128)S(1)}, s32[3]{0:T(128)}, u32[]{:S(2)}) copy-start(s32[3]{0:T(128)} %pad_add_fusion.refs_0_) | copy-start | bytes 40
  123.7 15.6 %copy-start.1 = (bf16[128,1664]{1,0:T(8,128)(2,1)S(1)}, bf16[128,1664]{1,0:T(8,128)(2,1)}, u32[]{:S(2)}) copy-start(bf16[128,1664]{1,0:T(8,128)(2,1)} %get-tuple-element.77.refs_1_) | copy-start | bytes 1277956
  123.8 15.6 %copy-start.2 = (bf16[128,1664]{1,0:T(8,128)(2,1)S(1)}, bf16[128,1664]{1,0:T(8,128)(2,1)}, u32[]{:S(2)}) copy-start(bf16[128,1664]{1,0:T(8,128)(2,1)} %get-tuple-element.88.refs_6_) | copy-start | bytes 1277956
  124.0 15.4 %collective-permute-start.8 = (bf16[64,1792]{1,0:T(8,128)(2,1)S(1)}, bf16[64,1792]{1,0:T(8,128)(2,1)S(1)}, u32[]{:S(2)}, u32[]{:S(2)}) collective-permute-start(bf16[64,1792]{1,0:T(8,128)(2,1)S(1)} %get-tuple-element.89), channel_id=1, source_target_pairs={{0,4},{4,8},{8,12},{12,0},{16,20},{20,24},{24,28},{28,16},{32,36},... | collective-permute-start | bytes 688136 | tf_op jit(solution)/shard_map/ppermute | solution.py:621
  124.0 15.3 %collective-permute-start.9 = (bf16[64,1792]{1,0:T(8,128)(2,1)S(1)}, bf16[64,1792]{1,0:T(8,128)(2,1)S(1)}, u32[]{:S(2)}, u32[]{:S(2)}) collective-permute-start(bf16[64,1792]{1,0:T(8,128)(2,1)S(1)} %get-tuple-element.90), channel_id=1, source_target_pairs={{0,12},{4,0},{8,4},{12,8},{16,28},{20,16},{24,20},{28,24},{32,44},... | collective-permute-start | bytes 688136 | tf_op jit(solution)/shard_map/ppermute | solution.py:622
  127.6 6.9 %collective-permute-start.6 = (bf16[64,1664]{1,0:T(8,128)(2,1)S(1)}, bf16[64,1664]{1,0:T(8,128)(2,1)S(1)}, u32[]{:S(2)}, u32[]{:S(2)}) collective-permute-start(bf16[64,1664]{1,0:T(8,128)(2,1)S(1)} %get-tuple-element.86), channel_id=1, source_target_pairs={{0,64},{4,68},{8,72},{12,76},{16,80},{20,84},{24,88},{28,92},{32,9... | collective-permute-start | bytes 638984 | tf_op jit(solution)/shard_map/ppermute | solution.py:621
  131.1 8.2 %collective-permute-start.7 = (bf16[64,1664]{1,0:T(8,128)(2,1)S(1)}, bf16[64,1664]{1,0:T(8,128)(2,1)S(1)}, u32[]{:S(2)}, u32[]{:S(2)}) collective-permute-start(bf16[64,1664]{1,0:T(8,128)(2,1)S(1)} %get-tuple-element.87), channel_id=1, source_target_pairs={{0,192},{4,196},{8,200},{12,204},{16,208},{20,212},{24,216},{28,22... | collective-permute-start | bytes 638984 | tf_op jit(solution)/shard_map/ppermute | solution.py:622
  140.5 6.1 %collective-permute-start.10 = (bf16[32,1664]{1,0:T(8,128)(2,1)S(1)}, bf16[32,1664]{1,0:T(8,128)(2,1)S(1)}, u32[]{:S(2)}, u32[]{:S(2)}) collective-permute-start(bf16[32,1664]{1,0:T(8,128)(2,1)S(1)} %get-tuple-element.92), channel_id=1, source_target_pairs={{0,4},{4,8},{8,12},{12,0},{16,20},{20,24},{24,28},{28,16},{32,36},... | collective-permute-start | bytes 319496 | tf_op jit(solution)/shard_map/ppermute | solution.py:616
  140.5 12.2 %collective-permute-start.13 = (bf16[32,1792]{1,0:T(8,128)(2,1)S(1)}, bf16[32,1792]{1,0:T(8,128)(2,1)S(1)}, u32[]{:S(2)}, u32[]{:S(2)}) collective-permute-start(bf16[32,1792]{1,0:T(8,128)(2,1)S(1)} %get-tuple-element.96), channel_id=1, source_target_pairs={{0,64},{4,68},{8,72},{12,76},{16,80},{20,84},{24,88},{28,92},{32,9... | collective-permute-start | bytes 344072 | tf_op jit(solution)/shard_map/ppermute | solution.py:616
  140.6 12.1 %collective-permute-start.15 = (bf16[32,1792]{1,0:T(8,128)(2,1)S(1)}, bf16[32,1792]{1,0:T(8,128)(2,1)S(1)}, u32[]{:S(2)}, u32[]{:S(2)}) collective-permute-start(bf16[32,1792]{1,0:T(8,128)(2,1)S(1)} %get-tuple-element.98), channel_id=1, source_target_pairs={{0,192},{4,196},{8,200},{12,204},{16,208},{20,212},{24,216},{28,22... | collective-permute-start | bytes 344072 | tf_op jit(solution)/shard_map/ppermute | solution.py:616
  142.6 6.2 %collective-permute-start.11 = (bf16[32,1664]{1,0:T(8,128)(2,1)S(1)}, bf16[32,1664]{1,0:T(8,128)(2,1)S(1)}, u32[]{:S(2)}, u32[]{:S(2)}) collective-permute-start(bf16[32,1664]{1,0:T(8,128)(2,1)S(1)} %get-tuple-element.93), channel_id=1, source_target_pairs={{0,8},{4,12},{8,0},{12,4},{16,24},{20,28},{24,16},{28,20},{32,40},... | collective-permute-start | bytes 319496 | tf_op jit(solution)/shard_map/ppermute | solution.py:616
  146.0 4.7 %collective-permute-start.12 = (bf16[32,1664]{1,0:T(8,128)(2,1)S(1)}, bf16[32,1664]{1,0:T(8,128)(2,1)S(1)}, u32[]{:S(2)}, u32[]{:S(2)}) collective-permute-start(bf16[32,1664]{1,0:T(8,128)(2,1)S(1)} %get-tuple-element.94), channel_id=1, source_target_pairs={{0,12},{4,0},{8,4},{12,8},{16,28},{20,16},{24,20},{28,24},{32,44},... | collective-permute-start | bytes 319496 | tf_op jit(solution)/shard_map/ppermute | solution.py:616
  146.6 6.2 %collective-permute-start.14 = (bf16[32,1664]{1,0:T(8,128)(2,1)S(1)}, bf16[32,1664]{1,0:T(8,128)(2,1)S(1)}, u32[]{:S(2)}, u32[]{:S(2)}) collective-permute-start(bf16[32,1664]{1,0:T(8,128)(2,1)S(1)} %get-tuple-element.97), channel_id=1, source_target_pairs={{0,128},{4,132},{8,136},{12,140},{16,144},{20,148},{24,152},{28,15... | collective-permute-start | bytes 319496 | tf_op jit(solution)/shard_map/ppermute | solution.py:616
  152.8 13.3 %copy-start.5 = (f32[128,512]{1,0:T(8,128)S(1)}, f32[128,512]{1,0:T(8,128)}, u32[]{:S(2)}) copy-start(f32[128,512]{1,0:T(8,128)} %get-tuple-element.100.refs_1_) | copy-start | bytes 786436

commit v5 on v4

--- a/solution.py
+++ b/solution.py
@@ -133,55 +133,69 @@
     return (wide * scale * gain.reshape(1, -1)).astype(bf16)
 
 
-def pre_kernel(
-    seq, up, low, high, gain, in_proj, step_proj, conv_w, conv_b, step_bias, decay_log, out_proj,
-    payload, both, normal, normal_halo, cot, gate, conv, d_gated, raw, step, cumul, cumul_t,
-    ext,
+def project_kernel(
+    seq, up, gain, in_proj, step_proj, step_bias, decay_log, out_proj,
+    both, normal, xbc, gate, cot, d_gated, raw, step, cumul, cumul_t, weighted,
 ):
     rows = seq.shape[0]
     inner = out_proj.shape[0]
     heads = step_bias.shape[0]
+    both[:rows, :] = seq[...]
+    both[rows:, :] = mirror_exact(seq[...])
+    normal[...] = norm_rows(both[...], gain[...])
+    raw[...] = mm_cols(normal[...], step_proj[...])
+    xbc[...] = mm(normal[...], in_proj[:, inner:]).astype(bf16)
+    gate[...] = mm(normal[...], in_proj[:, :inner])
+    cot[:rows, :] = up[...]
+    cot[rows:, :] = mirror_exact(up[...])
+    d_gated[...] = mm_cols(cot[...], out_proj[...]).astype(bf16)
+    mask = head_mask(heads, inner // heads)
+    for frame in range(2):
+        at = slice(frame * rows, (frame + 1) * rows)
+        size = softplus(raw[at, :] + step_bias[...].reshape(1, -1))
+        decay = -jnp.exp(decay_log[...].reshape(1, -1)) * size
+        upto = tri_sum(triangle(rows, True), decay)
+        step[at, :] = size
+        cumul[at, :] = upto
+        cumul_t[frame * heads : (frame + 1) * heads, :] = tri_sum_turned(triangle(rows, False), decay)
+        wide = gate[at, :]
+        d_mixed = d_gated[at, :].astype(f32) * (wide * sigmoid(wide))
+        weighted[at, :] = (d_mixed * expand(jnp.exp(upto), mask)).astype(bf16)
+
+
+def local_kernel(
+    low, high, xbc, in_proj, step, cumul, weighted, gain, conv_w, conv_b,
+    payload, conv, normal_halo,
+    ext,
+):
+    rows = xbc.shape[0] // 2
+    inner = weighted.shape[1]
+    heads = step.shape[1]
     state = (conv_w.shape[1] - inner) // 2
     taps = conv_w.shape[0]
-    both[:rows, :] = seq[...]
-    both[rows:, :] = mirror_exact(seq[...])
-    cot[:rows, :] = up[...]
-    cot[rows:, :] = mirror_exact(up[...])
+    margin = low.shape[0]
     halo = jnp.concatenate([low[...], mirror_exact(high[...])], axis=0)
-    normal[...] = norm_rows(both[...], gain[...])
     normal_halo[...] = norm_rows(halo, gain[...])
-    gate[...] = mm(normal[...], in_proj[:, :inner])
-    xbc = mm(normal[...], in_proj[:, inner:]).astype(bf16).astype(f32)
     xbc_halo = mm(normal_halo[...], in_proj[:, inner:]).astype(bf16).astype(f32)
-    raw[...] = mm_cols(normal[...], step_proj[...])
-    d_gated[...] = mm_cols(cot[...], out_proj[...]).astype(bf16)
-    margin = low.shape[0]
     mask = head_mask(heads, inner // heads)
     ends = []
     for frame in range(2):
         at = slice(frame * rows, (frame + 1) * rows)
         ext[:8, :] = xbc_halo[(frame + 1) * margin - 8 : (frame + 1) * margin, :]
-        ext[8:, :] = xbc[at, :]
+        ext[8:, :] = xbc[at, :].astype(f32)
         found = conv_b[...].reshape(1, -1)
         for tap in range(taps):
             start = 9 - taps + tap
             found = found + ext[start : start + rows, :] * conv_w[tap : tap + 1, :]
         conv[at, :] = found
         act = found * sigmoid(found)
-        size = softplus(raw[at, :] + step_bias[...].reshape(1, -1))
-        decay = -jnp.exp(decay_log[...].reshape(1, -1)) * size
-        upto = tri_sum(triangle(rows, True), decay)
-        step[at, :] = size
-        cumul[at, :] = upto
-        cumul_t[frame * heads : (frame + 1) * heads, :] = tri_sum_turned(triangle(rows, False), decay)
+        upto = cumul[at, :]
         end = upto[rows - 1 : rows, :]
         ends.append(end)
-        spread = expand(jnp.concatenate([size * jnp.exp(end - upto), jnp.exp(upto)], axis=0), mask)
-        driven = (act[:, :inner] * spread[:rows]).astype(bf16)
+        spread = expand(step[at, :] * jnp.exp(end - upto), mask)
+        driven = (act[:, :inner] * spread).astype(bf16)
         local = mm_rows(driven, act[:, inner : inner + state].astype(bf16))
-        wide = gate[at, :]
-        d_mixed = d_gated[at, :].astype(f32) * (wide * sigmoid(wide))
-        back = mm_rows((d_mixed * spread[rows:]).astype(bf16), act[:, inner + state :].astype(bf16))
+        back = mm_rows(weighted[at, :], act[:, inner + state :].astype(bf16))
         part = inner // SIDE
         for place, block in ((frame, local), (2 + frame, back)):
             block = block.astype(bf16).reshape(SIDE, part, state)
@@ -456,7 +470,7 @@
     left[:half, :], left[half:, :] = behind[:half], opposite[half:]
 
 
-def relay_kernel(base_x, right_x, left_x, base_y, right_y, left_y, to_low, to_high, *outs):
+def relay_kernel(base_x, right_x, left_x, base_y, right_y, left_y, to_both, *outs):
     for base, right, left, on_right, on_left in (
         (base_x, right_x, left_x, outs[0], outs[1]),
         (base_y, right_y, left_y, outs[2], outs[3]),
@@ -465,8 +479,10 @@
         columns = base.shape[1]
         on_right[:, :columns] = (base[:half, :].astype(f32) + right[:half, :].astype(f32)).astype(bf16)
         on_left[:, :columns] = (base[half:, :].astype(f32) + left[half:, :].astype(f32)).astype(bf16)
-    for target, edge in ((outs[2], to_high), (outs[3], to_low)):
-        target[:, columns:] = jnp.concatenate([edge[...], jnp.zeros(edge.shape, bf16)], axis=0)
+    outs[2][:32, columns:] = to_both[:32, :]
+    outs[3][:32, columns:] = to_both[32:, :]
+    for target in outs[2:]:
+        target[32:, columns:] = jnp.zeros((32, 128), bf16)
 
 
 def ring_total(keep, right, left, on_right, on_left):
@@ -513,7 +529,7 @@
 
 def result_kernel(
     place, both, gain, gated, out_proj, d_gate, d_xbc, d_first, d_second, low, high, d_step, in_proj, step_proj,
-    layer, base, to_low, to_high, d_whole,
+    layer, base, to_both, d_whole,
 ):
     rows = both.shape[0] // 2
     inner = out_proj.shape[0]
@@ -531,8 +547,8 @@
     second = norm_back(mirror_exact(high[...])[8:, :], through[2 * rows + 8 :], gain[...])
     at_start = (place[0] + place[1] + place[2]) == 0
     at_end = (place[0] + place[1] + place[2]) == 3 * (SIDE - 1)
-    to_low[...] = fold_rows(first * (1.0 - scalar_flag(at_start))).astype(bf16)
-    to_high[...] = fold_rows(mirror_wide(second) * (1.0 - scalar_flag(at_end))).astype(bf16)
+    to_both[32:, :] = fold_rows(first * (1.0 - scalar_flag(at_start))).astype(bf16)
+    to_both[:32, :] = fold_rows(mirror_wide(second) * (1.0 - scalar_flag(at_end))).astype(bf16)
 
 
 def total_of(refs):
@@ -661,26 +677,32 @@
     low = lax.ppermute(sequence[rows - 16 :], "seq", upward)
     high = lax.ppermute(sequence[:16], "seq", downward)
     step_turned = step_proj.T
-    payload, both, normal, normal_halo, cot, gate, conv, d_gated, raw, step, cumul, cumul_t = call(
-        pre_kernel,
+    both, normal, xbc, gate, cot, d_gated, raw, step, cumul, cumul_t, weighted = call(
+        project_kernel,
         [
-            ((SIDE, inner + 16, state), bf16),
             ((both_rows, width), bf16),
             ((both_rows, width), bf16),
-            ((32, width), bf16),
+            ((both_rows, channels), bf16),
+            ((both_rows, inner), f32),
             ((both_rows, width), bf16),
-            ((both_rows, inner), f32),
-            ((both_rows, channels), f32),
             ((both_rows, inner), bf16),
             ((both_rows, heads), f32),
             ((both_rows, heads), f32),
             ((both_rows, heads), f32),
             ((2 * heads, rows), f32),
+            ((both_rows, inner), bf16),
         ],
-        (
-            sequence, upstream, low, high, norm_gain, in_proj, step_turned,
-            conv_weight, conv_bias, step_bias, decay_log, out_proj,
-        ),
+        (sequence, upstream, norm_gain, in_proj, step_turned, step_bias, decay_log, out_proj),
+        flops=4 * 10**9,
+    )
+    payload, conv, normal_halo = call(
+        local_kernel,
+        [
+            ((SIDE, inner + 16, state), bf16),
+            ((both_rows, channels), f32),
+            ((32, width), bf16),
+        ],
+        (low, high, xbc, in_proj, step, cumul, weighted, norm_gain, conv_weight, conv_bias),
         [pltpu.VMEM((rows + 8, channels), f32)],
     )
     got = transpose_over(payload, beside)
@@ -731,11 +753,12 @@
             pltpu.VMEM((8 * COUNT, joined), f32),
             pltpu.VMEM((COUNT // SIDE, SIDE, 8, joined), f32),
         ],
+        vmem=54 * 2**20,
         scalars=1,
     )
-    layer_out, base, to_low, to_high = call(
+    layer_out, base, to_both = call(
         result_kernel,
-        [((rows, width), bf16), ((rows, width), f32), ((32, 128), bf16), ((32, 128), bf16)],
+        [((rows, width), bf16), ((rows, width), f32), ((64, 128), bf16)],
         (
             place, both, norm_gain, gated, out_proj, d_gate, d_xbc, d_first, d_second, low, high, d_step,
             in_proj, step_turned,
@@ -750,7 +773,7 @@
     relayed = call(
         relay_kernel,
         [((eighth // 2, joined), bf16)] * 2 + [((eighth // 2, joined + 128), bf16)] * 2,
-        (base_x, right_x, left_x, base_y, right_y, left_y, to_low, to_high),
+        (base_x, right_x, left_x, base_y, right_y, left_y, to_both),
         vmem=16 * 2**20,
     )
     from_x = [keep_x, right_x, left_x, *around(relayed[0], relayed[1], stride_x)]

time: 168 us -> 168 us (level)
  waiting for transfers between devices: 38.8 us -> 33.6 us
  Pallas kernels: 37 us -> 41.1 us
  blocking collectives: 44.5 us -> 46.6 us
    ppermute x1, waiting for transfers between devices: 8.8 us -> 3.39 us  [shards(): low = lax.ppermute(sequence[rows - 16:], 'seq', upward)]
    pallas_call x11 -> x12, Pallas kernels: 37 us -> 41.1 us  [call(): pl.pallas_call(used, out_shape=[jax.ShapeDtypeStruct(shape, kind) for sha...]
    all_to_all x3, blocking collectives: 44.5 us -> 46.6 us  [transpose_over(): return lax.all_to_all(parts, 'seq', 0, 0, axis_index_groups=groups)]
  transfers between devices with their start and end apart: 18 -> 18, of which waited for: 9 -> 9; matrix products, arithmetic and copies ran while one was open for 0% -> 0% of each run, Pallas kernels for 7% -> 10%
where the time goes in v5:
time: 168 us; the launch traced here: 167 us
  blocking collectives  46.6 us (28%)
  starting transfers between devices  41.4 us (25%)
  Pallas kernels  41.1 us (24%)
  waiting for transfers between devices  33.6 us (20%)
  local copies, waits for them, and re-layouts  3.06 us (2%)
    all_to_all x3, blocking collectives, transpose_over(): return lax.all_to_all(parts, 'seq', 0, 0, axis_index_groups=groups)  46.6 us
    pallas_call x12, Pallas kernels, call(): pl.pallas_call(used, out_shape=[jax.ShapeDtypeStruct(shape, kind) for sha...  41.1 us
    all_to_all x2, waiting for transfers between devices, transpose_over(): return lax.all_to_all(parts, 'seq', 0, 0, axis_index_groups=groups)  14.4 us
    ppermute x1, starting transfers between devices, shards(): high = lax.ppermute(sequence[:16], 'seq', downward)  10.9 us
    all_to_all x2, starting transfers between devices, transpose_over(): return lax.all_to_all(parts, 'seq', 0, 0, axis_index_groups=groups)  9.47 us
    ppermute x4, starting transfers between devices, around(): lax.ppermute(to_right, 'seq', axis_pairs(stride, 1))  6.66 us
    ppermute x4, starting transfers between devices, around(): lax.ppermute(to_left, 'seq', axis_pairs(stride, SIDE - 1))  6.24 us
    ppermute x6, starting transfers between devices, exchange(): lax.ppermute(parts[step], 'seq', axis_pairs(stride, step))  6.24 us
  transfers between devices with their start and end apart: 18, of which 9 were waited for; matrix products, arithmetic and copies ran while one was open for 0% of the time, Pallas kernels for 10%

profile of v5, /device:TPU:6, one launch (start us, length us, event | category | flops | bytes accessed | tf_op | source)
XLA Modules:
  0.0 167.1 jit_solution(9766868567537883146)
XLA Ops:
  0.6 0.7 fusion
  1.4 10.9 %collective-permute-start.1 = (bf16[16,512]{1,0:T(8,128)(2,1)S(1)}, bf16[16,512]{1,0:T(8,128)(2,1)S(1)}, u32[]{:S(2)}, u32[]{:S(2)}) collective-permute-start(bf16[16,512]{1,0:T(8,128)(2,1)S(1)} %get-tuple-element.106), channel_id=1, source_target_pairs={{4,0},{8,4},{12,8},{16,12},{20,16},{24,20},{28,24},{32,28},{36,32}... | collective-permute-start | bytes 49160 | tf_op jit(solution)/shard_map/ppermute | solution.py:678
  12.3 1.9 %collective-permute-start = (bf16[16,512]{1,0:T(8,128)(2,1)S(1)}, bf16[16,512]{1,0:T(8,128)(2,1)S(1)}, u32[]{:S(2)}, u32[]{:S(2)}) collective-permute-start(bf16[16,512]{1,0:T(8,128)(2,1)S(1)} %get-tuple-element.107), channel_id=1, source_target_pairs={{0,4},{4,8},{8,12},{12,16},{16,20},{20,24},{24,28},{28,32},{32,36}... | collective-permute-start | bytes 49160 | tf_op jit(solution)/shard_map/ppermute | solution.py:677
  14.2 5.4 %shard_map.138 = (bf16[256,512]{1,0:T(8,128)(2,1)}, bf16[256,512]{1,0:T(8,128)(2,1)}, bf16[256,1280]{1,0:T(8,128)(2,1)}, f32[256,1024]{1,0:T(8,128)}, bf16[256,5...) custom-call(bf16[128,512]{1,0:T(8,128)(2,1)} %refs_0_.1, ...), custom_call_target="tpu_custom_call" | custom-call | flops 4000000000 | bytes 3688576 | tf_op jit(solution)/shard_map/pallas_call | solution.py:28
  19.6 0.0 collective-permute-done.1.refs_1_.refs_10_
  19.6 0.0 copy-start.8
  19.7 3.4 %collective-permute-done.refs_0_.refs_9_ = bf16[16,512]{1,0:T(8,128)(2,1)S(1)} collective-permute-done((bf16[16,512]{1,0:T(8,128)(2,1)S(1)}, bf16[16,512]{1,0:T(8,128)(2,1)S(1)}, u32[]{:S(2)}, u32[]{:S(2)}) %collective-permute-start) | collective-permute-done | bytes 16416 | tf_op jit(solution)/shard_map/ppermute | solution.py:677
  23.0 0.0 copy-done.8
  23.0 0.6 copy-done.9
  23.6 5.6 %shard_map.139 = (bf16[4,1040,128]{2,1,0:T(8,128)(2,1)}, f32[256,1280]{1,0:T(8,128)}, bf16[32,512]{1,0:T(8,128)(2,1)}) custom-call(bf16[16,512]{1,0:T(8,128)(2,1)} %copy-done.9, bf16[16,512]{1,0:T(8,128)(2,1)} %copy-done.8, bf16[256,1280]{1,0:T(8,128)(2,1)} %get-tuple-element.56.refs_2_, bf16[512,2304]{1,0:T(8,128)(2,1)} %refs_12_.3, ...), custom_call_target="tpu_custom_call" | custom-call | flops 1000000000 | bytes 3632128 | tf_op jit(solution)/shard_map/pallas_call | solution.py:28
  29.2 17.6 %all_to_all.25.refs_0_ = bf16[4,1040,128]{2,1,0:T(8,128)(2,1)S(1)} all-to-all(bf16[4,1040,128]{2,1,0:T(8,128)(2,1)} %get-tuple-element.60), channel_id=1, replica_groups={{0,4,8,12},{16,20,24,28},{32,36,40,44},{48,52,56,60},{64,68,72,76},{80,..., dimensions={0} | all-to-all | bytes 2129920 | tf_op jit(solution)/shard_map/all_to_all | solution.py:643
  46.8 0.4 shard_map.140
  47.2 16.4 %all_to_all.26.refs_0_ = bf16[16,72,128]{2,1,0:T(8,128)(2,1)S(1)} all-to-all(bf16[16,72,128]{2,1,0:T(8,128)(2,1)S(1)} %shard_map.140), channel_id=1, replica_groups={{0,16,32,48,64,80,96,112,128,144,160,176,192,208,224,240},{4,20,36,52,6..., dimensions={0} | all-to-all | bytes 589824 | tf_op jit(solution)/shard_map/all_to_all | solution.py:643
  63.6 1.6 shard_map.141
  65.2 5.8 %all-to-all-start.2 = ((bf16[16,64,128]{2,1,0:T(8,128)(2,1)}), bf16[16,64,128]{2,1,0:T(8,128)(2,1)S(1)}, u32[]{:S(2)}, u32[]{:S(2)}) async-start(bf16[16,64,128]{2,1,0:T(8,128)(2,1)} %shard_map.141), calls=%async_computation.2 | async-start | bytes 524288 | tf_op jit(solution)/shard_map/all_to_all | solution.py:643
  70.9 9.6 %all-to-all-done.2.refs_1_ = bf16[16,64,128]{2,1,0:T(8,128)(2,1)S(1)} async-done(((bf16[16,64,128]{2,1,0:T(8,128)(2,1)}), bf16[16,64,128]{2,1,0:T(8,128)(2,1)S(1)}, u32[]{:S(2)}, u32[]{:S(2)}) %all-to-all-start.2) | async-done | bytes 262176 | tf_op jit(solution)/shard_map/all_to_all | solution.py:643
  80.5 1.3 shard_map.142
  81.8 3.7 %all-to-all-start.3 = ((bf16[4,1024,128]{2,1,0:T(8,128)(2,1)}), bf16[4,1024,128]{2,1,0:T(8,128)(2,1)S(1)}, u32[]{:S(2)}, u32[]{:S(2)}) async-start(bf16[4,1024,128]{2,1,0:T(8,128)(2,1)} %shard_map.142), calls=%async_computation.3 | async-start | bytes 2097152 | tf_op jit(solution)/shard_map/all_to_all | solution.py:643
  85.6 0.6 pad_add_fusion.refs_0_
  86.2 5.5 %shard_map.143 = (f32[256,1024]{1,0:T(8,128)}, f32[256,1024]{1,0:T(8,128)}, f32[256,256]{1,0:T(8,128)}, f32[256,16]{1,0:T(8,128)}) custom-call(f32[256,1280]{1,0:T(8,128)} %get-tuple-element.61.refs_0_.refs_2_, f32[256,1024]{1,0:T(8,128)} %get-tuple-element.62.refs_1_.refs_3_, bf16[256,1024]{1,0:T(8,128)(2,1)} %get-tuple-element.63.refs_2_.refs_4_, ...), custom_call_target="tpu_custom_call" | custom-call | flops 8000000000 | bytes 2932736 | tf_op jit(solution)/shard_map/pallas_call | solution.py:28
  91.6 4.9 %all-to-all-done.3.refs_1_ = bf16[4,1024,128]{2,1,0:T(8,128)(2,1)S(1)} async-done(((bf16[4,1024,128]{2,1,0:T(8,128)(2,1)}), bf16[4,1024,128]{2,1,0:T(8,128)(2,1)S(1)}, u32[]{:S(2)}, u32[]{:S(2)}) %all-to-all-start.3) | async-done | bytes 1048608 | tf_op jit(solution)/shard_map/all_to_all | solution.py:643
  96.5 1.0 copy-done.7
  97.5 12.3 %shard_map.144 = (bf16[256,1024]{1,0:T(8,128)(2,1)}, bf16[256,1024]{1,0:T(8,128)(2,1)}, bf16[256,1280]{1,0:T(8,128)(2,1)}, f32[8,1280]{1,0:T(8,128)}, f32[8,1280...) custom-call(s32[3]{0:T(128)} %pad_add_fusion.refs_0_, ...), custom_call_target="tpu_custom_call" | custom-call | flops 1000000000 | bytes 6934732 | tf_op jit(solution)/shard_map/pallas_call | solution.py:28
  109.8 2.5 %collective-permute-start.2 = (bf16[128,1664]{1,0:T(8,128)(2,1)}, bf16[128,1664]{1,0:T(8,128)(2,1)S(1)}, u32[]{:S(2)}, u32[]{:S(2)}) collective-permute-start(bf16[128,1664]{1,0:T(8,128)(2,1)} %get-tuple-element.81), channel_id=1, source_target_pairs={{0,64},{4,68},{8,72},{12,76},{16,80},{20,84},{24,88},{28,92},{32,9... | collective-permute-start | bytes 1277960 | tf_op jit(solution)/shard_map/ppermute | solution.py:637
  112.2 0.0 collective-permute-start.3
  112.2 0.6 collective-permute-start.4
  112.8 2.6 %collective-permute-start.5 = (bf16[128,1664]{1,0:T(8,128)(2,1)}, bf16[128,1664]{1,0:T(8,128)(2,1)S(1)}, u32[]{:S(2)}, u32[]{:S(2)}) collective-permute-start(bf16[128,1664]{1,0:T(8,128)(2,1)} %get-tuple-element.86), channel_id=1, source_target_pairs={{0,12},{4,0},{8,4},{12,8},{16,28},{20,16},{24,20},{28,24},{32,44},... | collective-permute-start | bytes 1277960 | tf_op jit(solution)/shard_map/ppermute | solution.py:638
  115.5 6.4 %shard_map.145 = (bf16[128,512]{1,0:T(8,128)(2,1)}, f32[128,512]{1,0:T(8,128)}, bf16[64,128]{1,0:T(8,128)(2,1)}) custom-call(s32[3]{0:T(128)} %pad_add_fusion.refs_0_, bf16[256,512]{1,0:T(8,128)(2,1)} %get-tuple-element.55.refs_1_, f32[512]{0:T(512)} %refs_2_.3, bf16[256,1024]{1,0:T(8,128)(2,1)} %get-tuple-element.73.refs_3_, bf16[1024,512]{1,0:T(8,128)(2,1)} %refs_4_.1, ...), custom_call_target="tpu_custom_call" | custom-call | flops 8000000000 | bytes 5515276 | tf_op jit(solution)/shard_map/pallas_call | solution.py:28
  121.9 0.0 collective-permute-done.2.refs_1_.refs_2_
  121.9 0.0 collective-permute-done.3.refs_2_.refs_3_
  121.9 1.3 collective-permute-done.4.refs_4_.refs_7_
  123.2 0.0 collective-permute-done.5.refs_5_.refs_8_
  123.2 0.0 copy-done.3
  123.2 0.0 copy-done.4
  123.2 0.0 copy-start.6
  123.2 0.7 copy-done.6
  124.0 0.2 shard_map.146
  124.2 0.1 collective-permute-start.8
  124.3 3.6 %collective-permute-start.9 = (bf16[64,1792]{1,0:T(8,128)(2,1)S(1)}, bf16[64,1792]{1,0:T(8,128)(2,1)S(1)}, u32[]{:S(2)}, u32[]{:S(2)}) collective-permute-start(bf16[64,1792]{1,0:T(8,128)(2,1)S(1)} %get-tuple-element.92), channel_id=1, source_target_pairs={{0,12},{4,0},{8,4},{12,8},{16,28},{20,16},{24,20},{28,24},{32,44},... | collective-permute-start | bytes 688136 | tf_op jit(solution)/shard_map/ppermute | solution.py:638
  127.8 3.5 %collective-permute-start.6 = (bf16[64,1664]{1,0:T(8,128)(2,1)S(1)}, bf16[64,1664]{1,0:T(8,128)(2,1)S(1)}, u32[]{:S(2)}, u32[]{:S(2)}) collective-permute-start(bf16[64,1664]{1,0:T(8,128)(2,1)S(1)} %get-tuple-element.88), channel_id=1, source_target_pairs={{0,64},{4,68},{8,72},{12,76},{16,80},{20,84},{24,88},{28,92},{32,9... | collective-permute-start | bytes 638984 | tf_op jit(solution)/shard_map/ppermute | solution.py:637
  131.4 0.0 collective-permute-start.7
  131.4 3.6 %collective-permute-done.6.refs_4_ = bf16[64,1664]{1,0:T(8,128)(2,1)S(1)} collective-permute-done((bf16[64,1664]{1,0:T(8,128)(2,1)S(1)}, bf16[64,1664]{1,0:T(8,128)(2,1)S(1)}, u32[]{:S(2)}, u32[]{:S(2)}) %collective-permute-start.6) | collective-permute-done | bytes 213024 | tf_op jit(solution)/shard_map/ppermute | solution.py:637
  134.9 4.6 %collective-permute-done.7.refs_5_ = bf16[64,1664]{1,0:T(8,128)(2,1)S(1)} collective-permute-done((bf16[64,1664]{1,0:T(8,128)(2,1)S(1)}, bf16[64,1664]{1,0:T(8,128)(2,1)S(1)}, u32[]{:S(2)}, u32[]{:S(2)}) %collective-permute-start.7) | collective-permute-done | bytes 213024 | tf_op jit(solution)/shard_map/ppermute | solution.py:638
  139.6 0.0 collective-permute-done.8.refs_9_
  139.6 0.0 collective-permute-done.9.refs_10_
  139.6 0.0 copy-done
  139.6 0.0 copy-done.1
  139.6 0.0 copy-done.2
  139.6 1.1 shard_map.147
  140.7 0.1 collective-permute-start.10
  140.8 0.1 collective-permute-start.13
  140.8 2.0 %collective-permute-start.15 = (bf16[32,1792]{1,0:T(8,128)(2,1)S(1)}, bf16[32,1792]{1,0:T(8,128)(2,1)S(1)}, u32[]{:S(2)}, u32[]{:S(2)}) collective-permute-start(bf16[32,1792]{1,0:T(8,128)(2,1)S(1)} %get-tuple-element.100), channel_id=1, source_target_pairs={{0,192},{4,196},{8,200},{12,204},{16,208},{20,212},{24,216},{28,22... | collective-permute-start | bytes 344072 | tf_op jit(solution)/shard_map/ppermute | solution.py:632
  142.9 3.3 %collective-permute-start.11 = (bf16[32,1664]{1,0:T(8,128)(2,1)S(1)}, bf16[32,1664]{1,0:T(8,128)(2,1)S(1)}, u32[]{:S(2)}, u32[]{:S(2)}) collective-permute-start(bf16[32,1664]{1,0:T(8,128)(2,1)S(1)} %get-tuple-element.95), channel_id=1, source_target_pairs={{0,8},{4,12},{8,0},{12,4},{16,24},{20,28},{24,16},{28,20},{32,40},... | collective-permute-start | bytes 319496 | tf_op jit(solution)/shard_map/ppermute | solution.py:632
  146.2 0.8 collective-permute-start.12
  146.9 0.0 collective-permute-done.10.refs_2_
  146.9 0.0 collective-permute-start.14
  146.9 2.1 %collective-permute-done.11.refs_3_ = bf16[32,1664]{1,0:T(8,128)(2,1)S(1)} collective-permute-done((bf16[32,1664]{1,0:T(8,128)(2,1)S(1)}, bf16[32,1664]{1,0:T(8,128)(2,1)S(1)}, u32[]{:S(2)}, u32[]{:S(2)}) %collective-permute-start.11) | collective-permute-done | bytes 106528 | tf_op jit(solution)/shard_map/ppermute | solution.py:632
  149.1 1.8 %collective-permute-done.12.refs_4_ = bf16[32,1664]{1,0:T(8,128)(2,1)S(1)} collective-permute-done((bf16[32,1664]{1,0:T(8,128)(2,1)S(1)}, bf16[32,1664]{1,0:T(8,128)(2,1)S(1)}, u32[]{:S(2)}, u32[]{:S(2)}) %collective-permute-start.12) | collective-permute-done | bytes 106528 | tf_op jit(solution)/shard_map/ppermute | solution.py:632
  150.9 2.3 %collective-permute-done.14.refs_7_ = bf16[32,1664]{1,0:T(8,128)(2,1)S(1)} collective-permute-done((bf16[32,1664]{1,0:T(8,128)(2,1)S(1)}, bf16[32,1664]{1,0:T(8,128)(2,1)S(1)}, u32[]{:S(2)}, u32[]{:S(2)}) %collective-permute-start.14) | collective-permute-done | bytes 106528 | tf_op jit(solution)/shard_map/ppermute | solution.py:632
  153.1 0.0 collective-permute-done.13.refs_6_
  153.1 0.0 collective-permute-done.15.refs_8_
  153.1 0.7 shard_map.148
  153.8 12.6 %all_to_all.27.refs_0_ = bf16[4,16,2176]{2,1,0:T(8,128)(2,1)S(1)} all-to-all(bf16[4,16,2176]{2,1,0:T(8,128)(2,1)S(1)} %shard_map.148), channel_id=1, replica_groups={{0,16,32,48},{4,20,36,52},{8,24,40,56},{12,28,44,60},{64,80,96,112},{68..., dimensions={0} | all-to-all | bytes 557056 | tf_op jit(solution)/shard_map/all_to_all | solution.py:643
  166.4 0.7 shard_map.149
  (9 shorter events, 0.0 us)
Async XLA Ops:
  1.4 18.3 %collective-permute-start.1 = (bf16[16,512]{1,0:T(8,128)(2,1)S(1)}, bf16[16,512]{1,0:T(8,128)(2,1)S(1)}, u32[]{:S(2)}, u32[]{:S(2)}) collective-permute-start(bf16[16,512]{1,0:T(8,128)(2,1)S(1)} %get-tuple-element.106), channel_id=1, source_target_pairs={{4,0},{8,4},{12,8},{16,12},{20,16},{24,20},{28,24},{32,28},{36,32}... | collective-permute-start | bytes 49160 | tf_op jit(solution)/shard_map/ppermute | solution.py:678
  12.3 10.8 %collective-permute-start = (bf16[16,512]{1,0:T(8,128)(2,1)S(1)}, bf16[16,512]{1,0:T(8,128)(2,1)S(1)}, u32[]{:S(2)}, u32[]{:S(2)}) collective-permute-start(bf16[16,512]{1,0:T(8,128)(2,1)S(1)} %get-tuple-element.107), channel_id=1, source_target_pairs={{0,4},{4,8},{8,12},{12,16},{16,20},{20,24},{24,28},{28,32},{32,36}... | collective-permute-start | bytes 49160 | tf_op jit(solution)/shard_map/ppermute | solution.py:677
  19.6 3.4 %copy-start.8 = (bf16[16,512]{1,0:T(8,128)(2,1)}, bf16[16,512]{1,0:T(8,128)(2,1)S(1)}, u32[]{:S(2)}) copy-start(bf16[16,512]{1,0:T(8,128)(2,1)S(1)} %collective-permute-done.1.refs_1_.refs_10_) | copy-start | bytes 49156
  23.0 0.6 copy-start.9
  65.2 15.4 %all-to-all-start.2 = ((bf16[16,64,128]{2,1,0:T(8,128)(2,1)}), bf16[16,64,128]{2,1,0:T(8,128)(2,1)S(1)}, u32[]{:S(2)}, u32[]{:S(2)}) async-start(bf16[16,64,128]{2,1,0:T(8,128)(2,1)} %shard_map.141), calls=%async_computation.2 | async-start | bytes 524288 | tf_op jit(solution)/shard_map/all_to_all | solution.py:643
  81.8 14.6 %all-to-all-start.3 = ((bf16[4,1024,128]{2,1,0:T(8,128)(2,1)}), bf16[4,1024,128]{2,1,0:T(8,128)(2,1)S(1)}, u32[]{:S(2)}, u32[]{:S(2)}) async-start(bf16[4,1024,128]{2,1,0:T(8,128)(2,1)} %shard_map.142), calls=%async_computation.3 | async-start | bytes 2097152 | tf_op jit(solution)/shard_map/all_to_all | solution.py:643
  96.5 1.0 copy-start.7
  109.8 12.1 %collective-permute-start.2 = (bf16[128,1664]{1,0:T(8,128)(2,1)}, bf16[128,1664]{1,0:T(8,128)(2,1)S(1)}, u32[]{:S(2)}, u32[]{:S(2)}) collective-permute-start(bf16[128,1664]{1,0:T(8,128)(2,1)} %get-tuple-element.81), channel_id=1, source_target_pairs={{0,64},{4,68},{8,72},{12,76},{16,80},{20,84},{24,88},{28,92},{32,9... | collective-permute-start | bytes 1277960 | tf_op jit(solution)/shard_map/ppermute | solution.py:637
  112.2 9.7 %collective-permute-start.3 = (bf16[128,1664]{1,0:T(8,128)(2,1)}, bf16[128,1664]{1,0:T(8,128)(2,1)S(1)}, u32[]{:S(2)}, u32[]{:S(2)}) collective-permute-start(bf16[128,1664]{1,0:T(8,128)(2,1)} %get-tuple-element.82), channel_id=1, source_target_pairs={{0,192},{4,196},{8,200},{12,204},{16,208},{20,212},{24,216},{28,22... | collective-permute-start | bytes 1277960 | tf_op jit(solution)/shard_map/ppermute | solution.py:638
  112.2 11.0 %collective-permute-start.4 = (bf16[128,1664]{1,0:T(8,128)(2,1)}, bf16[128,1664]{1,0:T(8,128)(2,1)S(1)}, u32[]{:S(2)}, u32[]{:S(2)}) collective-permute-start(bf16[128,1664]{1,0:T(8,128)(2,1)} %get-tuple-element.85), channel_id=1, source_target_pairs={{0,4},{4,8},{8,12},{12,0},{16,20},{20,24},{24,28},{28,16},{32,36},... | collective-permute-start | bytes 1277960 | tf_op jit(solution)/shard_map/ppermute | solution.py:637
  112.8 10.4 %collective-permute-start.5 = (bf16[128,1664]{1,0:T(8,128)(2,1)}, bf16[128,1664]{1,0:T(8,128)(2,1)S(1)}, u32[]{:S(2)}, u32[]{:S(2)}) collective-permute-start(bf16[128,1664]{1,0:T(8,128)(2,1)} %get-tuple-element.86), channel_id=1, source_target_pairs={{0,12},{4,0},{8,4},{12,8},{16,28},{20,16},{24,20},{28,24},{32,44},... | collective-permute-start | bytes 1277960 | tf_op jit(solution)/shard_map/ppermute | solution.py:638
  115.5 7.8 %copy-start.3 = (bf16[128,1664]{1,0:T(8,128)(2,1)S(1)}, bf16[128,1664]{1,0:T(8,128)(2,1)}, u32[]{:S(2)}) copy-start(bf16[128,1664]{1,0:T(8,128)(2,1)} %get-tuple-element.83.refs_0_) | copy-start | bytes 1277956
  115.5 7.8 %copy-start.4 = (bf16[128,1664]{1,0:T(8,128)(2,1)S(1)}, bf16[128,1664]{1,0:T(8,128)(2,1)}, u32[]{:S(2)}) copy-start(bf16[128,1664]{1,0:T(8,128)(2,1)} %get-tuple-element.84.refs_3_) | copy-start | bytes 1277956
  123.2 0.7 copy-start.6
  124.0 15.6 %copy-start = (s32[3]{0:T(128)S(1)}, s32[3]{0:T(128)}, u32[]{:S(2)}) copy-start(s32[3]{0:T(128)} %pad_add_fusion.refs_0_) | copy-start | bytes 40
  124.0 15.6 %copy-start.1 = (bf16[128,1664]{1,0:T(8,128)(2,1)S(1)}, bf16[128,1664]{1,0:T(8,128)(2,1)}, u32[]{:S(2)}) copy-start(bf16[128,1664]{1,0:T(8,128)(2,1)} %get-tuple-element.80.refs_1_) | copy-start | bytes 1277956
  124.0 15.6 %copy-start.2 = (bf16[128,1664]{1,0:T(8,128)(2,1)S(1)}, bf16[128,1664]{1,0:T(8,128)(2,1)}, u32[]{:S(2)}) copy-start(bf16[128,1664]{1,0:T(8,128)(2,1)} %get-tuple-element.90.refs_6_) | copy-start | bytes 1277956
  124.2 15.4 %collective-permute-start.8 = (bf16[64,1792]{1,0:T(8,128)(2,1)S(1)}, bf16[64,1792]{1,0:T(8,128)(2,1)S(1)}, u32[]{:S(2)}, u32[]{:S(2)}) collective-permute-start(bf16[64,1792]{1,0:T(8,128)(2,1)S(1)} %get-tuple-element.91), channel_id=1, source_target_pairs={{0,4},{4,8},{8,12},{12,0},{16,20},{20,24},{24,28},{28,16},{32,36},... | collective-permute-start | bytes 688136 | tf_op jit(solution)/shard_map/ppermute | solution.py:637
  124.3 15.3 %collective-permute-start.9 = (bf16[64,1792]{1,0:T(8,128)(2,1)S(1)}, bf16[64,1792]{1,0:T(8,128)(2,1)S(1)}, u32[]{:S(2)}, u32[]{:S(2)}) collective-permute-start(bf16[64,1792]{1,0:T(8,128)(2,1)S(1)} %get-tuple-element.92), channel_id=1, source_target_pairs={{0,12},{4,0},{8,4},{12,8},{16,28},{20,16},{24,20},{28,24},{32,44},... | collective-permute-start | bytes 688136 | tf_op jit(solution)/shard_map/ppermute | solution.py:638
  127.8 7.1 %collective-permute-start.6 = (bf16[64,1664]{1,0:T(8,128)(2,1)S(1)}, bf16[64,1664]{1,0:T(8,128)(2,1)S(1)}, u32[]{:S(2)}, u32[]{:S(2)}) collective-permute-start(bf16[64,1664]{1,0:T(8,128)(2,1)S(1)} %get-tuple-element.88), channel_id=1, source_target_pairs={{0,64},{4,68},{8,72},{12,76},{16,80},{20,84},{24,88},{28,92},{32,9... | collective-permute-start | bytes 638984 | tf_op jit(solution)/shard_map/ppermute | solution.py:637
  131.4 8.2 %collective-permute-start.7 = (bf16[64,1664]{1,0:T(8,128)(2,1)S(1)}, bf16[64,1664]{1,0:T(8,128)(2,1)S(1)}, u32[]{:S(2)}, u32[]{:S(2)}) collective-permute-start(bf16[64,1664]{1,0:T(8,128)(2,1)S(1)} %get-tuple-element.89), channel_id=1, source_target_pairs={{0,192},{4,196},{8,200},{12,204},{16,208},{20,212},{24,216},{28,22... | collective-permute-start | bytes 638984 | tf_op jit(solution)/shard_map/ppermute | solution.py:638
  140.7 6.3 %collective-permute-start.10 = (bf16[32,1664]{1,0:T(8,128)(2,1)S(1)}, bf16[32,1664]{1,0:T(8,128)(2,1)S(1)}, u32[]{:S(2)}, u32[]{:S(2)}) collective-permute-start(bf16[32,1664]{1,0:T(8,128)(2,1)S(1)} %get-tuple-element.94), channel_id=1, source_target_pairs={{0,4},{4,8},{8,12},{12,0},{16,20},{20,24},{24,28},{28,16},{32,36},... | collective-permute-start | bytes 319496 | tf_op jit(solution)/shard_map/ppermute | solution.py:632
  140.8 12.4 %collective-permute-start.13 = (bf16[32,1792]{1,0:T(8,128)(2,1)S(1)}, bf16[32,1792]{1,0:T(8,128)(2,1)S(1)}, u32[]{:S(2)}, u32[]{:S(2)}) collective-permute-start(bf16[32,1792]{1,0:T(8,128)(2,1)S(1)} %get-tuple-element.98), channel_id=1, source_target_pairs={{0,64},{4,68},{8,72},{12,76},{16,80},{20,84},{24,88},{28,92},{32,9... | collective-permute-start | bytes 344072 | tf_op jit(solution)/shard_map/ppermute | solution.py:632
  140.8 12.3 %collective-permute-start.15 = (bf16[32,1792]{1,0:T(8,128)(2,1)S(1)}, bf16[32,1792]{1,0:T(8,128)(2,1)S(1)}, u32[]{:S(2)}, u32[]{:S(2)}) collective-permute-start(bf16[32,1792]{1,0:T(8,128)(2,1)S(1)} %get-tuple-element.100), channel_id=1, source_target_pairs={{0,192},{4,196},{8,200},{12,204},{16,208},{20,212},{24,216},{28,22... | collective-permute-start | bytes 344072 | tf_op jit(solution)/shard_map/ppermute | solution.py:632
  142.9 6.2 %collective-permute-start.11 = (bf16[32,1664]{1,0:T(8,128)(2,1)S(1)}, bf16[32,1664]{1,0:T(8,128)(2,1)S(1)}, u32[]{:S(2)}, u32[]{:S(2)}) collective-permute-start(bf16[32,1664]{1,0:T(8,128)(2,1)S(1)} %get-tuple-element.95), channel_id=1, source_target_pairs={{0,8},{4,12},{8,0},{12,4},{16,24},{20,28},{24,16},{28,20},{32,40},... | collective-permute-start | bytes 319496 | tf_op jit(solution)/shard_map/ppermute | solution.py:632
  146.2 4.7 %collective-permute-start.12 = (bf16[32,1664]{1,0:T(8,128)(2,1)S(1)}, bf16[32,1664]{1,0:T(8,128)(2,1)S(1)}, u32[]{:S(2)}, u32[]{:S(2)}) collective-permute-start(bf16[32,1664]{1,0:T(8,128)(2,1)S(1)} %get-tuple-element.96), channel_id=1, source_target_pairs={{0,12},{4,0},{8,4},{12,8},{16,28},{20,16},{24,20},{28,24},{32,44},... | collective-permute-start | bytes 319496 | tf_op jit(solution)/shard_map/ppermute | solution.py:632
  146.9 6.2 %collective-permute-start.14 = (bf16[32,1664]{1,0:T(8,128)(2,1)S(1)}, bf16[32,1664]{1,0:T(8,128)(2,1)S(1)}, u32[]{:S(2)}, u32[]{:S(2)}) collective-permute-start(bf16[32,1664]{1,0:T(8,128)(2,1)S(1)} %get-tuple-element.99), channel_id=1, source_target_pairs={{0,128},{4,132},{8,136},{12,140},{16,144},{20,148},{24,152},{28,15... | collective-permute-start | bytes 319496 | tf_op jit(solution)/shard_map/ppermute | solution.py:632
  153.1 13.3 %copy-start.5 = (f32[128,512]{1,0:T(8,128)S(1)}, f32[128,512]{1,0:T(8,128)}, u32[]{:S(2)}) copy-start(f32[128,512]{1,0:T(8,128)} %get-tuple-element.102.refs_1_) | copy-start | bytes 786436

commit v6 on v4

--- a/solution.py
+++ b/solution.py
@@ -150,7 +150,7 @@
     halo = jnp.concatenate([low[...], mirror_exact(high[...])], axis=0)
     normal[...] = norm_rows(both[...], gain[...])
     normal_halo[...] = norm_rows(halo, gain[...])
-    gate[...] = mm(normal[...], in_proj[:, :inner])
+    gate[...] = mm(normal[...], in_proj[:, :inner]).astype(bf16)
     xbc = mm(normal[...], in_proj[:, inner:]).astype(bf16).astype(f32)
     xbc_halo = mm(normal_halo[...], in_proj[:, inner:]).astype(bf16).astype(f32)
     raw[...] = mm_cols(normal[...], step_proj[...])
@@ -166,7 +166,7 @@
         for tap in range(taps):
             start = 9 - taps + tap
             found = found + ext[start : start + rows, :] * conv_w[tap : tap + 1, :]
-        conv[at, :] = found
+        conv[at, :] = found.astype(bf16)
         act = found * sigmoid(found)
         size = softplus(raw[at, :] + step_bias[...].reshape(1, -1))
         decay = -jnp.exp(decay_log[...].reshape(1, -1)) * size
@@ -179,7 +179,7 @@
         spread = expand(jnp.concatenate([size * jnp.exp(end - upto), jnp.exp(upto)], axis=0), mask)
         driven = (act[:, :inner] * spread[:rows]).astype(bf16)
         local = mm_rows(driven, act[:, inner : inner + state].astype(bf16))
-        wide = gate[at, :]
+        wide = gate[at, :].astype(f32)
         d_mixed = d_gated[at, :].astype(f32) * (wide * sigmoid(wide))
         back = mm_rows((d_mixed * spread[rows:]).astype(bf16), act[:, inner + state :].astype(bf16))
         part = inner // SIDE
@@ -317,12 +317,12 @@
     wide_pair = 2 * inner // heads
     for frame in range(2):
         at = slice(frame * rows, (frame + 1) * rows)
-        found = conv[at, :]
+        found = conv[at, :].astype(f32)
         act = found * sigmoid(found)
         bmat = act[:, inner : inner + state].astype(bf16)
         cmat = act[:, inner + state :].astype(bf16)
         driven = act[:, :inner] * expand(step[at, :], mask)
-        wide = gate[at, :]
+        wide = gate[at, :].astype(f32)
         d_mixed = d_gated[at, :].astype(f32) * (wide * sigmoid(wide))
         scores = mm_cols(cmat, bmat)
         upto, line = cumul[at, :], cumul_t[frame * heads : (frame + 1) * heads, :]
@@ -347,8 +347,8 @@
             d_weights = mm_cols(d_mix_two, drive_bf)
             d_drive = mm_rows(jnp.concatenate(weights, axis=0), d_mix_two)
             d_scores = d_scores + decays[0] * d_weights[:rows] + decays[1] * d_weights[rows:]
-            mixed[at, lanes] = mix
-            d_driven[at, lanes] = d_drive
+            mixed[at, lanes] = mix.astype(bf16)
+            d_driven[at, lanes] = d_drive.astype(bf16)
             sums.append(d_mix_bf.astype(f32) * mix - drive_bf.astype(f32) * d_drive)
         d_scores = d_scores.astype(bf16)
         d_bc[at, :state] = mm_rows(d_scores, cmat)
@@ -370,7 +370,7 @@
     skip = expand(jnp.broadcast_to(skip_gain[...].reshape(1, -1), (8, heads)), mask)[:1]
     for frame in range(2):
         at = slice(frame * rows, (frame + 1) * rows)
-        found = conv[at, :]
+        found = conv[at, :].astype(f32)
         share = sigmoid(found)
         act = found * share
         inputs = act[:, :inner]
@@ -384,8 +384,8 @@
         carried = got[:, frame * part : (frame + 1) * part, :].reshape(inner, state)
         reach = got[:, (2 + frame) * part : (3 + frame) * part, :].reshape(inner, state)
         inter = grown * mm_cols(cmat, carried)
-        full = mixed[at, :] + inter + skip * inputs
-        wide = gate[at, :]
+        full = mixed[at, :].astype(f32) + inter + skip * inputs
+        wide = gate[at, :].astype(f32)
         opened = sigmoid(wide)
         silu = wide * opened
         gated[at, :] = (full * silu).astype(bf16)
@@ -395,7 +395,7 @@
         d_cmat = d_bc[at, state:] + mm((d_mixed * grown).astype(bf16), carried)
         answer = left * mm_cols(bmat, reach)
         driven = inputs * sizes
-        d_drive = d_driven[at, :] + answer
+        d_drive = d_driven[at, :].astype(f32) + answer
         d_bmat = d_bc[at, :state] + mm((left * driven).astype(bf16), reach)
         products = carried.astype(f32) * reach.astype(f32)
         met = jnp.sum(products.reshape(heads, inner // heads, state), axis=1)
@@ -456,7 +456,7 @@
     left[:half, :], left[half:, :] = behind[:half], opposite[half:]
 
 
-def relay_kernel(base_x, right_x, left_x, base_y, right_y, left_y, to_low, to_high, *outs):
+def relay_kernel(base_x, right_x, left_x, base_y, right_y, left_y, to_both, *outs):
     for base, right, left, on_right, on_left in (
         (base_x, right_x, left_x, outs[0], outs[1]),
         (base_y, right_y, left_y, outs[2], outs[3]),
@@ -465,8 +465,10 @@
         columns = base.shape[1]
         on_right[:, :columns] = (base[:half, :].astype(f32) + right[:half, :].astype(f32)).astype(bf16)
         on_left[:, :columns] = (base[half:, :].astype(f32) + left[half:, :].astype(f32)).astype(bf16)
-    for target, edge in ((outs[2], to_high), (outs[3], to_low)):
-        target[:, columns:] = jnp.concatenate([edge[...], jnp.zeros(edge.shape, bf16)], axis=0)
+    outs[2][:32, columns:] = to_both[:32, :]
+    outs[3][:32, columns:] = to_both[32:, :]
+    for target in outs[2:]:
+        target[32:, columns:] = jnp.zeros((32, 128), bf16)
 
 
 def ring_total(keep, right, left, on_right, on_left):
@@ -513,7 +515,7 @@
 
 def result_kernel(
     place, both, gain, gated, out_proj, d_gate, d_xbc, d_first, d_second, low, high, d_step, in_proj, step_proj,
-    layer, base, to_low, to_high, d_whole,
+    layer, base, to_both, d_whole,
 ):
     rows = both.shape[0] // 2
     inner = out_proj.shape[0]
@@ -531,8 +533,8 @@
     second = norm_back(mirror_exact(high[...])[8:, :], through[2 * rows + 8 :], gain[...])
     at_start = (place[0] + place[1] + place[2]) == 0
     at_end = (place[0] + place[1] + place[2]) == 3 * (SIDE - 1)
-    to_low[...] = fold_rows(first * (1.0 - scalar_flag(at_start))).astype(bf16)
-    to_high[...] = fold_rows(mirror_wide(second) * (1.0 - scalar_flag(at_end))).astype(bf16)
+    to_both[32:, :] = fold_rows(first * (1.0 - scalar_flag(at_start))).astype(bf16)
+    to_both[:32, :] = fold_rows(mirror_wide(second) * (1.0 - scalar_flag(at_end))).astype(bf16)
 
 
 def total_of(refs):
@@ -565,7 +567,7 @@
 
 
 def second_sum_kernel(place, *refs):
-    first, second, kept, by_z = refs[:4], refs[4:8], refs[8], refs[9]
+    first, second, kept, by_z, kept_on, keep = refs[:4], refs[4:8], refs[8], refs[9:13], refs[13], refs[14]
     columns = first[0].shape[1]
     high = kept[:32, :] + second[1][:, columns:].astype(f32)
     low = kept[32:, :] + second[3][:, columns:].astype(f32)
@@ -576,31 +578,32 @@
     second = total.reshape(SIDE, 8, -1)
     above = scalar_flag(place[2] == 0)
     below = scalar_flag(place[2] == SIDE - 1)
-    for to in range(SIDE):
-        own = scalar_flag(place[1] == to)
-        share_high = own * (1.0 - above) + scalar_flag(lax.rem(place[1] + 1, SIDE) == to) * above
-        share_low = own * (1.0 - below) + scalar_flag(lax.rem(place[1] + SIDE - 1, SIDE) == to) * below
-        edges = [high[:16] * share_high, high[16:] * share_high, low[:16] * share_low, low[16:] * share_low]
-        by_z[to, :, :columns] = jnp.concatenate([first[to], second[to]], axis=0).astype(bf16)
-        by_z[to, :, columns:] = jnp.concatenate(edges, axis=1).astype(bf16)
-
-
-def last_sum_kernel(parts, base, grad_in, grad_out, grad):
-    total = parts[0].astype(f32)
-    for step in range(1, SIDE):
-        total = total + parts[step].astype(f32)
+    keep[:, 0] = first
+    keep[:, 1] = second
+    for step in range(SIDE):
+        block = keep[lax.rem(place[1] + step, SIDE)].reshape(16, columns)
+        by_z[step][:, :columns] = block.astype(by_z[step].dtype)
+    for step, edge, share in ((1, high, above), (3, low, below)):
+        edge = edge * share
+        by_z[step][:, columns:] = jnp.concatenate([edge[:16], edge[16:]], axis=1).astype(bf16)
+    kept_on[:32, :] = high * (1.0 - above)
+    kept_on[32:, :] = low * (1.0 - below)
+
+
+def last_sum_kernel(own, up, across, down, kept, base, grad_in, grad_out, grad):
+    joined = own.shape[1]
+    total = own[...] + up[:, :joined].astype(f32) + across[...].astype(f32) + down[:, :joined].astype(f32)
     columns = grad_out.shape[1]
-    joined = total.shape[1] - 512
     grad_out[:8, :] = total[:8, :columns]
     grad_out[8:, :] = total[:8, columns : 2 * columns]
-    grad_in[...] = jnp.concatenate(
-        [total[8:, : 2 * columns], total[:8, 2 * columns : joined], total[8:, 2 * columns : joined]], axis=1
-    )
-    edges = total[:, joined:]
-    high = unfold_rows(jnp.concatenate([edges[:, :128], edges[:, 128:256]], axis=0))
-    low = unfold_rows(jnp.concatenate([edges[:, 256:384], edges[:, 384:]], axis=0))
+    grad_in[...] = jnp.concatenate([total[8:, : 2 * columns], total[:8, 2 * columns :], total[8:, 2 * columns :]], axis=1)
+    edges = []
+    for nth, recv in enumerate((up, down)):
+        recv = recv[:, joined:].astype(f32)
+        recv = jnp.concatenate([recv[:, :128], recv[:, 128:]], axis=0)
+        edges.append(unfold_rows(kept[32 * nth : 32 * nth + 32, :] + recv))
     rows = base.shape[0]
-    whole = jnp.concatenate([base[:8, :] + high, base[8 : rows - 8, :], base[rows - 8 :, :] + low], axis=0)
+    whole = jnp.concatenate([base[:8, :] + edges[0], base[8 : rows - 8, :], base[rows - 8 :, :] + edges[1]], axis=0)
     grad[...] = whole.astype(bf16)
 
 
@@ -653,7 +656,6 @@
     stride_x, stride_z, stride_y = SIDE * SIDE, SIDE, 1
     index = lax.axis_index("seq")
     place = jnp.stack([index // stride_x, index // stride_z % SIDE, index % SIDE]).astype(jnp.int32)
-    aligned = [[base + SIDE * digit for digit in range(SIDE)] for base in range(COUNT) if base // SIDE % SIDE == 0]
     beside = [[SIDE * base + digit for digit in range(SIDE)] for base in range(COUNT // SIDE)]
     across = [[base + SIDE * digit for digit in range(COUNT // SIDE)] for base in range(SIDE)]
     upward = [(i, i + 1) for i in range(COUNT - 1)]
@@ -669,8 +671,8 @@
             ((both_rows, width), bf16),
             ((32, width), bf16),
             ((both_rows, width), bf16),
-            ((both_rows, inner), f32),
-            ((both_rows, channels), f32),
+            ((both_rows, inner), bf16),
+            ((both_rows, channels), bf16),
             ((both_rows, inner), bf16),
             ((both_rows, heads), f32),
             ((both_rows, heads), f32),
@@ -689,8 +691,8 @@
     mixed, d_driven, d_bc, d_cumul = call(
         intra_kernel,
         [
-            ((both_rows, inner), f32),
-            ((both_rows, inner), f32),
+            ((both_rows, inner), bf16),
+            ((both_rows, inner), bf16),
             ((both_rows, 2 * state), f32),
             ((both_rows, heads), f32),
         ],
@@ -733,9 +735,9 @@
         ],
         scalars=1,
     )
-    layer_out, base, to_low, to_high = call(
+    layer_out, base, to_both = call(
         result_kernel,
-        [((rows, width), bf16), ((rows, width), f32), ((32, 128), bf16), ((32, 128), bf16)],
+        [((rows, width), bf16), ((rows, width), f32), ((64, 128), bf16)],
         (
             place, both, norm_gain, gated, out_proj, d_gate, d_xbc, d_first, d_second, low, high, d_step,
             in_proj, step_turned,
@@ -750,7 +752,7 @@
     relayed = call(
         relay_kernel,
         [((eighth // 2, joined), bf16)] * 2 + [((eighth // 2, joined + 128), bf16)] * 2,
-        (base_x, right_x, left_x, base_y, right_y, left_y, to_low, to_high),
+        (base_x, right_x, left_x, base_y, right_y, left_y, to_both),
         vmem=16 * 2**20,
     )
     from_x = [keep_x, right_x, left_x, *around(relayed[0], relayed[1], stride_x)]
@@ -768,18 +770,20 @@
     )
     first = exchange(parts[:4], stride_y)
     second = exchange(parts[4:], stride_x)
-    (by_z,) = call(
+    *parts, kept = call(
         second_sum_kernel,
-        [((SIDE, 16, joined + 512), bf16)],
+        [((16, joined), f32), ((16, joined + 256), bf16), ((16, joined), bf16), ((16, joined + 256), bf16)]
+        + [((64, 128), f32)],
         (place, *first, *second, kept),
+        [pltpu.VMEM((SIDE, 2, 8, joined), f32)],
         scalars=1,
         vmem=16 * 2**20,
     )
-    last = transpose_over(by_z, aligned)
+    last = exchange(parts, stride_z)
     grad_in_proj, grad_out_proj, grad_input = call(
         last_sum_kernel,
         [((8, inner + channels), f32), ((16, width), f32), ((rows, width), bf16)],
-        (last, base),
+        (*last, kept, base),
         vmem=16 * 2**20,
     )
     return (layer_out, grad_input, grad_in_proj, grad_out_proj)

time: 168 us -> 167 us (level)
  blocking collectives: 44.5 us -> 31.9 us
  waiting for transfers between devices: 38.8 us -> 47 us
  starting transfers between devices: 41.3 us -> 46.2 us
    all_to_all x3 -> x2, blocking collectives: 44.5 us -> 31.9 us  [transpose_over(): return lax.all_to_all(parts, 'seq', 0, 0, axis_index_groups=groups)]
    ppermute x6 -> x9, waiting for transfers between devices: 6.21 us -> 13.6 us  [exchange(): lax.ppermute(parts[step], 'seq', axis_pairs(stride, step))]
    ppermute x6 -> x9, starting transfers between devices: 6.1 us -> 11 us  [exchange(): lax.ppermute(parts[step], 'seq', axis_pairs(stride, step))]
  transfers between devices with their start and end apart: 18 -> 21, of which waited for: 9 -> 10; matrix products, arithmetic and copies ran while one was open for 0% -> 0% of each run, Pallas kernels for 7% -> 7%
where the time goes in v6:
time: 167 us; the launch traced here: 165 us
  waiting for transfers between devices  47 us (28%)
  starting transfers between devices  46.2 us (28%)
  Pallas kernels  35.7 us (21%)
  blocking collectives  31.9 us (19%)
  local copies, waits for them, and re-layouts  3.06 us (2%)
    pallas_call x11, Pallas kernels, call(): pl.pallas_call(used, out_shape=[jax.ShapeDtypeStruct(shape, kind) for sha...  35.7 us
    all_to_all x2, blocking collectives, transpose_over(): return lax.all_to_all(parts, 'seq', 0, 0, axis_index_groups=groups)  31.9 us
    all_to_all x2, waiting for transfers between devices, transpose_over(): return lax.all_to_all(parts, 'seq', 0, 0, axis_index_groups=groups)  14.7 us
    ppermute x9, waiting for transfers between devices, exchange(): lax.ppermute(parts[step], 'seq', axis_pairs(stride, step))  13.6 us
    ppermute x9, starting transfers between devices, exchange(): lax.ppermute(parts[step], 'seq', axis_pairs(stride, step))  11 us
    ppermute x1, starting transfers between devices, shards(): high = lax.ppermute(sequence[:16], 'seq', downward)  10.9 us
    all_to_all x2, starting transfers between devices, transpose_over(): return lax.all_to_all(parts, 'seq', 0, 0, axis_index_groups=groups)  9.47 us
    ppermute x1, waiting for transfers between devices, shards(): low = lax.ppermute(sequence[rows - 16:], 'seq', upward)  8.8 us
  transfers between devices with their start and end apart: 21, of which 10 were waited for; matrix products, arithmetic and copies ran while one was open for 0% of the time, Pallas kernels for 7%

profile of v6, /device:TPU:6, one launch (start us, length us, event | category | flops | bytes accessed | tf_op | source)
XLA Modules:
  0.0 165.4 jit_solution(7390026786192463023)
XLA Ops:
  0.6 0.7 fusion
  1.4 10.9 %collective-permute-start.1 = (bf16[16,512]{1,0:T(8,128)(2,1)S(1)}, bf16[16,512]{1,0:T(8,128)(2,1)S(1)}, u32[]{:S(2)}, u32[]{:S(2)}) collective-permute-start(bf16[16,512]{1,0:T(8,128)(2,1)S(1)} %get-tuple-element.112), channel_id=1, source_target_pairs={{4,0},{8,4},{12,8},{16,12},{20,16},{24,20},{28,24},{32,28},{36,32}... | collective-permute-start | bytes 49160 | tf_op jit(solution)/shard_map/ppermute | solution.py:664
  12.3 1.9 %collective-permute-start = (bf16[16,512]{1,0:T(8,128)(2,1)S(1)}, bf16[16,512]{1,0:T(8,128)(2,1)S(1)}, u32[]{:S(2)}, u32[]{:S(2)}) collective-permute-start(bf16[16,512]{1,0:T(8,128)(2,1)S(1)} %get-tuple-element.113), channel_id=1, source_target_pairs={{0,4},{4,8},{8,12},{12,16},{16,20},{20,24},{24,28},{28,32},{32,36}... | collective-permute-start | bytes 49160 | tf_op jit(solution)/shard_map/ppermute | solution.py:663
  14.2 0.0 collective-permute-done.1.refs_3_.refs_10_
  14.2 0.0 copy-start.8
  14.2 8.8 %collective-permute-done.refs_2_.refs_9_ = bf16[16,512]{1,0:T(8,128)(2,1)S(1)} collective-permute-done((bf16[16,512]{1,0:T(8,128)(2,1)S(1)}, bf16[16,512]{1,0:T(8,128)(2,1)S(1)}, u32[]{:S(2)}, u32[]{:S(2)}) %collective-permute-start) | collective-permute-done | bytes 16416 | tf_op jit(solution)/shard_map/ppermute | solution.py:663
  23.0 0.0 copy-done.8
  23.0 0.6 copy-done.9
  23.6 7.0 %shard_map.138 = (bf16[4,1040,128]{2,1,0:T(8,128)(2,1)}, bf16[256,512]{1,0:T(8,128)(2,1)}, bf16[256,512]{1,0:T(8,128)(2,1)}, bf16[32,512]{1,0:T(8,128)(2,1)}, bf...) custom-call(bf16[128,512]{1,0:T(8,128)(2,1)} %refs_0_.1, ...), custom_call_target="tpu_custom_call" | custom-call | flops 1000000000 | bytes 3746944 | tf_op jit(solution)/shard_map/pallas_call | solution.py:28
  30.6 17.6 %all_to_all.20.refs_0_ = bf16[4,1040,128]{2,1,0:T(8,128)(2,1)S(1)} all-to-all(bf16[4,1040,128]{2,1,0:T(8,128)(2,1)} %get-tuple-element.59), channel_id=1, replica_groups={{0,4,8,12},{16,20,24,28},{32,36,40,44},{48,52,56,60},{64,68,72,76},{80,..., dimensions={0} | all-to-all | bytes 2129920 | tf_op jit(solution)/shard_map/all_to_all | solution.py:630
  48.3 0.4 shard_map.139
  48.6 14.2 %all_to_all.21.refs_0_ = bf16[16,72,128]{2,1,0:T(8,128)(2,1)S(1)} all-to-all(bf16[16,72,128]{2,1,0:T(8,128)(2,1)S(1)} %shard_map.139), channel_id=1, replica_groups={{0,16,32,48,64,80,96,112,128,144,160,176,192,208,224,240},{4,20,36,52,6..., dimensions={0} | all-to-all | bytes 589824 | tf_op jit(solution)/shard_map/all_to_all | solution.py:630
  62.9 1.6 shard_map.140
  64.5 5.8 %all-to-all-start.2 = ((bf16[16,64,128]{2,1,0:T(8,128)(2,1)}), bf16[16,64,128]{2,1,0:T(8,128)(2,1)S(1)}, u32[]{:S(2)}, u32[]{:S(2)}) async-start(bf16[16,64,128]{2,1,0:T(8,128)(2,1)} %shard_map.140), calls=%async_computation.2 | async-start | bytes 524288 | tf_op jit(solution)/shard_map/all_to_all | solution.py:630
  70.2 9.6 %all-to-all-done.2.refs_1_ = bf16[16,64,128]{2,1,0:T(8,128)(2,1)S(1)} async-done(((bf16[16,64,128]{2,1,0:T(8,128)(2,1)}), bf16[16,64,128]{2,1,0:T(8,128)(2,1)S(1)}, u32[]{:S(2)}, u32[]{:S(2)}) %all-to-all-start.2) | async-done | bytes 262176 | tf_op jit(solution)/shard_map/all_to_all | solution.py:630
  79.8 1.3 shard_map.141
  81.2 3.7 %all-to-all-start.3 = ((bf16[4,1024,128]{2,1,0:T(8,128)(2,1)}), bf16[4,1024,128]{2,1,0:T(8,128)(2,1)S(1)}, u32[]{:S(2)}, u32[]{:S(2)}) async-start(bf16[4,1024,128]{2,1,0:T(8,128)(2,1)} %shard_map.141), calls=%async_computation.3 | async-start | bytes 2097152 | tf_op jit(solution)/shard_map/all_to_all | solution.py:630
  84.9 0.7 pad_add_fusion.refs_0_
  85.5 4.9 %shard_map.142 = (bf16[256,1024]{1,0:T(8,128)(2,1)}, bf16[256,1024]{1,0:T(8,128)(2,1)}, f32[256,256]{1,0:T(8,128)}, f32[256,16]{1,0:T(8,128)}) custom-call(bf16[256,1280]{1,0:T(8,128)(2,1)} %get-tuple-element.60.refs_0_.refs_2_, bf16[256,1024]{1,0:T(8,128)(2,1)} %get-tuple-element.61.refs_1_.refs_3_, bf16[256,1024]{1,0:T(8,128)(2,1)} %get-tuple-element.62.refs_2_.refs_4_, ...), custom_call_target="tpu_custom_call" | custom-call | flops 8000000000 | bytes 1753088 | tf_op jit(solution)/shard_map/pallas_call | solution.py:28
  90.4 5.2 %all-to-all-done.3.refs_1_ = bf16[4,1024,128]{2,1,0:T(8,128)(2,1)S(1)} async-done(((bf16[4,1024,128]{2,1,0:T(8,128)(2,1)}), bf16[4,1024,128]{2,1,0:T(8,128)(2,1)S(1)}, u32[]{:S(2)}, u32[]{:S(2)}) %all-to-all-start.3) | async-done | bytes 1048608 | tf_op jit(solution)/shard_map/all_to_all | solution.py:630
  95.5 1.0 copy-done.7
  96.5 11.5 %shard_map.143 = (bf16[256,1024]{1,0:T(8,128)(2,1)}, bf16[256,1024]{1,0:T(8,128)(2,1)}, bf16[256,1280]{1,0:T(8,128)(2,1)}, f32[8,1280]{1,0:T(8,128)}, f32[8,1280...) custom-call(s32[3]{0:T(128)} %pad_add_fusion.refs_0_, ...), custom_call_target="tpu_custom_call" | custom-call | flops 1000000000 | bytes 4706508 | tf_op jit(solution)/shard_map/pallas_call | solution.py:28
  108.0 2.5 %collective-permute-start.2 = (bf16[128,1664]{1,0:T(8,128)(2,1)}, bf16[128,1664]{1,0:T(8,128)(2,1)S(1)}, u32[]{:S(2)}, u32[]{:S(2)}) collective-permute-start(bf16[128,1664]{1,0:T(8,128)(2,1)} %get-tuple-element.82), channel_id=1, source_target_pairs={{0,64},{4,68},{8,72},{12,76},{16,80},{20,84},{24,88},{28,92},{32,9... | collective-permute-start | bytes 1277960 | tf_op jit(solution)/shard_map/ppermute | solution.py:624
  110.5 0.0 collective-permute-start.3
  110.5 0.6 collective-permute-start.4
  111.1 2.6 %collective-permute-start.5 = (bf16[128,1664]{1,0:T(8,128)(2,1)}, bf16[128,1664]{1,0:T(8,128)(2,1)S(1)}, u32[]{:S(2)}, u32[]{:S(2)}) collective-permute-start(bf16[128,1664]{1,0:T(8,128)(2,1)} %get-tuple-element.87), channel_id=1, source_target_pairs={{0,12},{4,0},{8,4},{12,8},{16,28},{20,16},{24,20},{28,24},{32,44},... | collective-permute-start | bytes 1277960 | tf_op jit(solution)/shard_map/ppermute | solution.py:625
  113.8 6.4 %shard_map.144 = (bf16[128,512]{1,0:T(8,128)(2,1)}, f32[128,512]{1,0:T(8,128)}, bf16[64,128]{1,0:T(8,128)(2,1)}) custom-call(s32[3]{0:T(128)} %pad_add_fusion.refs_0_, bf16[256,512]{1,0:T(8,128)(2,1)} %get-tuple-element.58.refs_1_, f32[512]{0:T(512)} %refs_2_.1, bf16[256,1024]{1,0:T(8,128)(2,1)} %get-tuple-element.74.refs_3_, bf16[1024,512]{1,0:T(8,128)(2,1)} %refs_4_.3, ...), custom_call_target="tpu_custom_call" | custom-call | flops 8000000000 | bytes 5515276 | tf_op jit(solution)/shard_map/pallas_call | solution.py:28
  120.2 0.0 collective-permute-done.2.refs_1_.refs_2_
  120.2 0.0 collective-permute-done.3.refs_2_.refs_3_
  120.2 1.7 %collective-permute-done.4.refs_4_.refs_7_ = bf16[128,1664]{1,0:T(8,128)(2,1)S(1)} collective-permute-done((bf16[128,1664]{1,0:T(8,128)(2,1)}, bf16[128,1664]{1,0:T(8,128)(2,1)S(1)}, u32[]{:S(2)}, u32[]{:S(2)}) %collective-permute-start.4) | collective-permute-done | bytes 426016 | tf_op jit(solution)/shard_map/ppermute | solution.py:624
  121.9 0.0 collective-permute-done.5.refs_5_.refs_8_
  121.9 0.0 copy-done.3
  121.9 0.0 copy-start.6
  121.9 0.7 copy-done.6
  122.6 0.2 shard_map.145
  122.8 0.1 collective-permute-start.8
  122.9 3.6 %collective-permute-start.9 = (bf16[64,1792]{1,0:T(8,128)(2,1)S(1)}, bf16[64,1792]{1,0:T(8,128)(2,1)S(1)}, u32[]{:S(2)}, u32[]{:S(2)}) collective-permute-start(bf16[64,1792]{1,0:T(8,128)(2,1)S(1)} %get-tuple-element.93), channel_id=1, source_target_pairs={{0,12},{4,0},{8,4},{12,8},{16,28},{20,16},{24,20},{28,24},{32,44},... | collective-permute-start | bytes 688136 | tf_op jit(solution)/shard_map/ppermute | solution.py:625
  126.5 3.5 %collective-permute-start.6 = (bf16[64,1664]{1,0:T(8,128)(2,1)S(1)}, bf16[64,1664]{1,0:T(8,128)(2,1)S(1)}, u32[]{:S(2)}, u32[]{:S(2)}) collective-permute-start(bf16[64,1664]{1,0:T(8,128)(2,1)S(1)} %get-tuple-element.89), channel_id=1, source_target_pairs={{0,64},{4,68},{8,72},{12,76},{16,80},{20,84},{24,88},{28,92},{32,9... | collective-permute-start | bytes 638984 | tf_op jit(solution)/shard_map/ppermute | solution.py:624
  130.0 0.0 collective-permute-start.7
  130.0 3.4 %collective-permute-done.6.refs_4_ = bf16[64,1664]{1,0:T(8,128)(2,1)S(1)} collective-permute-done((bf16[64,1664]{1,0:T(8,128)(2,1)S(1)}, bf16[64,1664]{1,0:T(8,128)(2,1)S(1)}, u32[]{:S(2)}, u32[]{:S(2)}) %collective-permute-start.6) | collective-permute-done | bytes 213024 | tf_op jit(solution)/shard_map/ppermute | solution.py:624
  133.4 4.8 %collective-permute-done.7.refs_5_ = bf16[64,1664]{1,0:T(8,128)(2,1)S(1)} collective-permute-done((bf16[64,1664]{1,0:T(8,128)(2,1)S(1)}, bf16[64,1664]{1,0:T(8,128)(2,1)S(1)}, u32[]{:S(2)}, u32[]{:S(2)}) %collective-permute-start.7) | collective-permute-done | bytes 213024 | tf_op jit(solution)/shard_map/ppermute | solution.py:625
  138.2 0.0 collective-permute-done.8.refs_9_
  138.2 0.0 collective-permute-done.9.refs_10_
  138.3 1.1 shard_map.146
  139.3 0.1 collective-permute-start.10
  139.4 0.1 collective-permute-start.13
  139.5 2.0 %collective-permute-start.15 = (bf16[32,1792]{1,0:T(8,128)(2,1)S(1)}, bf16[32,1792]{1,0:T(8,128)(2,1)S(1)}, u32[]{:S(2)}, u32[]{:S(2)}) collective-permute-start(bf16[32,1792]{1,0:T(8,128)(2,1)S(1)} %get-tuple-element.101), channel_id=1, source_target_pairs={{0,192},{4,196},{8,200},{12,204},{16,208},{20,212},{24,216},{28,22... | collective-permute-start | bytes 344072 | tf_op jit(solution)/shard_map/ppermute | solution.py:619
  141.5 3.3 %collective-permute-start.11 = (bf16[32,1664]{1,0:T(8,128)(2,1)S(1)}, bf16[32,1664]{1,0:T(8,128)(2,1)S(1)}, u32[]{:S(2)}, u32[]{:S(2)}) collective-permute-start(bf16[32,1664]{1,0:T(8,128)(2,1)S(1)} %get-tuple-element.96), channel_id=1, source_target_pairs={{0,8},{4,12},{8,0},{12,4},{16,24},{20,28},{24,16},{28,20},{32,40},... | collective-permute-start | bytes 319496 | tf_op jit(solution)/shard_map/ppermute | solution.py:619
  144.8 0.6 collective-permute-start.12
  145.5 0.0 collective-permute-done.10.refs_2_
  145.5 0.0 collective-permute-start.14
  145.5 2.3 %collective-permute-done.11.refs_3_ = bf16[32,1664]{1,0:T(8,128)(2,1)S(1)} collective-permute-done((bf16[32,1664]{1,0:T(8,128)(2,1)S(1)}, bf16[32,1664]{1,0:T(8,128)(2,1)S(1)}, u32[]{:S(2)}, u32[]{:S(2)}) %collective-permute-start.11) | collective-permute-done | bytes 106528 | tf_op jit(solution)/shard_map/ppermute | solution.py:619
  147.7 1.8 %collective-permute-done.12.refs_4_ = bf16[32,1664]{1,0:T(8,128)(2,1)S(1)} collective-permute-done((bf16[32,1664]{1,0:T(8,128)(2,1)S(1)}, bf16[32,1664]{1,0:T(8,128)(2,1)S(1)}, u32[]{:S(2)}, u32[]{:S(2)}) %collective-permute-start.12) | collective-permute-done | bytes 106528 | tf_op jit(solution)/shard_map/ppermute | solution.py:619
  149.6 2.1 %collective-permute-done.14.refs_7_ = bf16[32,1664]{1,0:T(8,128)(2,1)S(1)} collective-permute-done((bf16[32,1664]{1,0:T(8,128)(2,1)S(1)}, bf16[32,1664]{1,0:T(8,128)(2,1)S(1)}, u32[]{:S(2)}, u32[]{:S(2)}) %collective-permute-start.14) | collective-permute-done | bytes 106528 | tf_op jit(solution)/shard_map/ppermute | solution.py:619
  151.7 0.0 collective-permute-done.13.refs_6_
  151.7 0.0 collective-permute-done.15.refs_8_
  151.7 0.7 shard_map.147
  152.4 0.1 collective-permute-start.16
  152.5 4.1 %collective-permute-start.18 = (bf16[16,1920]{1,0:T(8,128)(2,1)S(1)}, bf16[16,1920]{1,0:T(8,128)(2,1)S(1)}, u32[]{:S(2)}, u32[]{:S(2)}) collective-permute-start(bf16[16,1920]{1,0:T(8,128)(2,1)S(1)} %get-tuple-element.106), channel_id=1, source_target_pairs={{0,48},{4,52},{8,56},{12,60},{16,0},{20,4},{24,8},{28,12},{32,16},... | collective-permute-start | bytes 184328 | tf_op jit(solution)/shard_map/ppermute | solution.py:619
  156.6 0.7 collective-permute-start.17
  157.3 7.3 %collective-permute-done.17.refs_2_ = bf16[16,1664]{1,0:T(8,128)(2,1)S(1)} collective-permute-done((bf16[16,1664]{1,0:T(8,128)(2,1)S(1)}, bf16[16,1664]{1,0:T(8,128)(2,1)S(1)}, u32[]{:S(2)}, u32[]{:S(2)}) %collective-permute-start.17) | collective-permute-done | bytes 53280 | tf_op jit(solution)/shard_map/ppermute | solution.py:619
  164.7 0.0 collective-permute-done.16.refs_1_
  164.7 0.0 collective-permute-done.18.refs_3_
  164.7 0.7 shard_map.148
  (13 shorter events, 0.0 us)
Async XLA Ops:
  1.4 12.9 %collective-permute-start.1 = (bf16[16,512]{1,0:T(8,128)(2,1)S(1)}, bf16[16,512]{1,0:T(8,128)(2,1)S(1)}, u32[]{:S(2)}, u32[]{:S(2)}) collective-permute-start(bf16[16,512]{1,0:T(8,128)(2,1)S(1)} %get-tuple-element.112), channel_id=1, source_target_pairs={{4,0},{8,4},{12,8},{16,12},{20,16},{24,20},{28,24},{32,28},{36,32}... | collective-permute-start | bytes 49160 | tf_op jit(solution)/shard_map/ppermute | solution.py:664
  12.3 10.8 %collective-permute-start = (bf16[16,512]{1,0:T(8,128)(2,1)S(1)}, bf16[16,512]{1,0:T(8,128)(2,1)S(1)}, u32[]{:S(2)}, u32[]{:S(2)}) collective-permute-start(bf16[16,512]{1,0:T(8,128)(2,1)S(1)} %get-tuple-element.113), channel_id=1, source_target_pairs={{0,4},{4,8},{8,12},{12,16},{16,20},{20,24},{24,28},{28,32},{32,36}... | collective-permute-start | bytes 49160 | tf_op jit(solution)/shard_map/ppermute | solution.py:663
  14.2 8.8 %copy-start.8 = (bf16[16,512]{1,0:T(8,128)(2,1)}, bf16[16,512]{1,0:T(8,128)(2,1)S(1)}, u32[]{:S(2)}) copy-start(bf16[16,512]{1,0:T(8,128)(2,1)S(1)} %collective-permute-done.1.refs_3_.refs_10_) | copy-start | bytes 49156
  23.0 0.6 copy-start.9
  64.5 15.3 %all-to-all-start.2 = ((bf16[16,64,128]{2,1,0:T(8,128)(2,1)}), bf16[16,64,128]{2,1,0:T(8,128)(2,1)S(1)}, u32[]{:S(2)}, u32[]{:S(2)}) async-start(bf16[16,64,128]{2,1,0:T(8,128)(2,1)} %shard_map.140), calls=%async_computation.2 | async-start | bytes 524288 | tf_op jit(solution)/shard_map/all_to_all | solution.py:630
  81.2 14.4 %all-to-all-start.3 = ((bf16[4,1024,128]{2,1,0:T(8,128)(2,1)}), bf16[4,1024,128]{2,1,0:T(8,128)(2,1)S(1)}, u32[]{:S(2)}, u32[]{:S(2)}) async-start(bf16[4,1024,128]{2,1,0:T(8,128)(2,1)} %shard_map.141), calls=%async_computation.3 | async-start | bytes 2097152 | tf_op jit(solution)/shard_map/all_to_all | solution.py:630
  95.5 1.0 copy-start.7
  108.0 12.1 %collective-permute-start.2 = (bf16[128,1664]{1,0:T(8,128)(2,1)}, bf16[128,1664]{1,0:T(8,128)(2,1)S(1)}, u32[]{:S(2)}, u32[]{:S(2)}) collective-permute-start(bf16[128,1664]{1,0:T(8,128)(2,1)} %get-tuple-element.82), channel_id=1, source_target_pairs={{0,64},{4,68},{8,72},{12,76},{16,80},{20,84},{24,88},{28,92},{32,9... | collective-permute-start | bytes 1277960 | tf_op jit(solution)/shard_map/ppermute | solution.py:624
  110.5 9.7 %collective-permute-start.3 = (bf16[128,1664]{1,0:T(8,128)(2,1)}, bf16[128,1664]{1,0:T(8,128)(2,1)S(1)}, u32[]{:S(2)}, u32[]{:S(2)}) collective-permute-start(bf16[128,1664]{1,0:T(8,128)(2,1)} %get-tuple-element.83), channel_id=1, source_target_pairs={{0,192},{4,196},{8,200},{12,204},{16,208},{20,212},{24,216},{28,22... | collective-permute-start | bytes 1277960 | tf_op jit(solution)/shard_map/ppermute | solution.py:625
  110.5 11.4 %collective-permute-start.4 = (bf16[128,1664]{1,0:T(8,128)(2,1)}, bf16[128,1664]{1,0:T(8,128)(2,1)S(1)}, u32[]{:S(2)}, u32[]{:S(2)}) collective-permute-start(bf16[128,1664]{1,0:T(8,128)(2,1)} %get-tuple-element.86), channel_id=1, source_target_pairs={{0,4},{4,8},{8,12},{12,0},{16,20},{20,24},{24,28},{28,16},{32,36},... | collective-permute-start | bytes 1277960 | tf_op jit(solution)/shard_map/ppermute | solution.py:624
  111.1 10.8 %collective-permute-start.5 = (bf16[128,1664]{1,0:T(8,128)(2,1)}, bf16[128,1664]{1,0:T(8,128)(2,1)S(1)}, u32[]{:S(2)}, u32[]{:S(2)}) collective-permute-start(bf16[128,1664]{1,0:T(8,128)(2,1)} %get-tuple-element.87), channel_id=1, source_target_pairs={{0,12},{4,0},{8,4},{12,8},{16,28},{20,16},{24,20},{28,24},{32,44},... | collective-permute-start | bytes 1277960 | tf_op jit(solution)/shard_map/ppermute | solution.py:625
  113.8 8.1 %copy-start.3 = (bf16[128,1664]{1,0:T(8,128)(2,1)S(1)}, bf16[128,1664]{1,0:T(8,128)(2,1)}, u32[]{:S(2)}) copy-start(bf16[128,1664]{1,0:T(8,128)(2,1)} %get-tuple-element.84.refs_0_) | copy-start | bytes 1277956
  113.8 8.1 %copy-start.4 = (bf16[128,1664]{1,0:T(8,128)(2,1)S(1)}, bf16[128,1664]{1,0:T(8,128)(2,1)}, u32[]{:S(2)}) copy-start(bf16[128,1664]{1,0:T(8,128)(2,1)} %get-tuple-element.85.refs_3_) | copy-start | bytes 1277956
  121.9 0.7 copy-start.6
  122.6 15.6 %copy-start = (s32[3]{0:T(128)S(1)}, s32[3]{0:T(128)}, u32[]{:S(2)}) copy-start(s32[3]{0:T(128)} %pad_add_fusion.refs_0_) | copy-start | bytes 40
  122.6 15.6 %copy-start.1 = (bf16[128,1664]{1,0:T(8,128)(2,1)S(1)}, bf16[128,1664]{1,0:T(8,128)(2,1)}, u32[]{:S(2)}) copy-start(bf16[128,1664]{1,0:T(8,128)(2,1)} %get-tuple-element.81.refs_1_) | copy-start | bytes 1277956
  122.6 15.6 %copy-start.2 = (bf16[128,1664]{1,0:T(8,128)(2,1)S(1)}, bf16[128,1664]{1,0:T(8,128)(2,1)}, u32[]{:S(2)}) copy-start(bf16[128,1664]{1,0:T(8,128)(2,1)} %get-tuple-element.91.refs_6_) | copy-start | bytes 1277956
  122.8 15.4 %collective-permute-start.8 = (bf16[64,1792]{1,0:T(8,128)(2,1)S(1)}, bf16[64,1792]{1,0:T(8,128)(2,1)S(1)}, u32[]{:S(2)}, u32[]{:S(2)}) collective-permute-start(bf16[64,1792]{1,0:T(8,128)(2,1)S(1)} %get-tuple-element.92), channel_id=1, source_target_pairs={{0,4},{4,8},{8,12},{12,0},{16,20},{20,24},{24,28},{28,16},{32,36},... | collective-permute-start | bytes 688136 | tf_op jit(solution)/shard_map/ppermute | solution.py:624
  122.9 15.3 %collective-permute-start.9 = (bf16[64,1792]{1,0:T(8,128)(2,1)S(1)}, bf16[64,1792]{1,0:T(8,128)(2,1)S(1)}, u32[]{:S(2)}, u32[]{:S(2)}) collective-permute-start(bf16[64,1792]{1,0:T(8,128)(2,1)S(1)} %get-tuple-element.93), channel_id=1, source_target_pairs={{0,12},{4,0},{8,4},{12,8},{16,28},{20,16},{24,20},{28,24},{32,44},... | collective-permute-start | bytes 688136 | tf_op jit(solution)/shard_map/ppermute | solution.py:625
  126.5 6.9 %collective-permute-start.6 = (bf16[64,1664]{1,0:T(8,128)(2,1)S(1)}, bf16[64,1664]{1,0:T(8,128)(2,1)S(1)}, u32[]{:S(2)}, u32[]{:S(2)}) collective-permute-start(bf16[64,1664]{1,0:T(8,128)(2,1)S(1)} %get-tuple-element.89), channel_id=1, source_target_pairs={{0,64},{4,68},{8,72},{12,76},{16,80},{20,84},{24,88},{28,92},{32,9... | collective-permute-start | bytes 638984 | tf_op jit(solution)/shard_map/ppermute | solution.py:624
  130.0 8.2 %collective-permute-start.7 = (bf16[64,1664]{1,0:T(8,128)(2,1)S(1)}, bf16[64,1664]{1,0:T(8,128)(2,1)S(1)}, u32[]{:S(2)}, u32[]{:S(2)}) collective-permute-start(bf16[64,1664]{1,0:T(8,128)(2,1)S(1)} %get-tuple-element.90), channel_id=1, source_target_pairs={{0,192},{4,196},{8,200},{12,204},{16,208},{20,212},{24,216},{28,22... | collective-permute-start | bytes 638984 | tf_op jit(solution)/shard_map/ppermute | solution.py:625
  139.3 6.1 %collective-permute-start.10 = (bf16[32,1664]{1,0:T(8,128)(2,1)S(1)}, bf16[32,1664]{1,0:T(8,128)(2,1)S(1)}, u32[]{:S(2)}, u32[]{:S(2)}) collective-permute-start(bf16[32,1664]{1,0:T(8,128)(2,1)S(1)} %get-tuple-element.95), channel_id=1, source_target_pairs={{0,4},{4,8},{8,12},{12,0},{16,20},{20,24},{24,28},{28,16},{32,36},... | collective-permute-start | bytes 319496 | tf_op jit(solution)/shard_map/ppermute | solution.py:619
  139.4 12.2 %collective-permute-start.13 = (bf16[32,1792]{1,0:T(8,128)(2,1)S(1)}, bf16[32,1792]{1,0:T(8,128)(2,1)S(1)}, u32[]{:S(2)}, u32[]{:S(2)}) collective-permute-start(bf16[32,1792]{1,0:T(8,128)(2,1)S(1)} %get-tuple-element.99), channel_id=1, source_target_pairs={{0,64},{4,68},{8,72},{12,76},{16,80},{20,84},{24,88},{28,92},{32,9... | collective-permute-start | bytes 344072 | tf_op jit(solution)/shard_map/ppermute | solution.py:619
  139.5 12.1 %collective-permute-start.15 = (bf16[32,1792]{1,0:T(8,128)(2,1)S(1)}, bf16[32,1792]{1,0:T(8,128)(2,1)S(1)}, u32[]{:S(2)}, u32[]{:S(2)}) collective-permute-start(bf16[32,1792]{1,0:T(8,128)(2,1)S(1)} %get-tuple-element.101), channel_id=1, source_target_pairs={{0,192},{4,196},{8,200},{12,204},{16,208},{20,212},{24,216},{28,22... | collective-permute-start | bytes 344072 | tf_op jit(solution)/shard_map/ppermute | solution.py:619
  141.5 6.2 %collective-permute-start.11 = (bf16[32,1664]{1,0:T(8,128)(2,1)S(1)}, bf16[32,1664]{1,0:T(8,128)(2,1)S(1)}, u32[]{:S(2)}, u32[]{:S(2)}) collective-permute-start(bf16[32,1664]{1,0:T(8,128)(2,1)S(1)} %get-tuple-element.96), channel_id=1, source_target_pairs={{0,8},{4,12},{8,0},{12,4},{16,24},{20,28},{24,16},{28,20},{32,40},... | collective-permute-start | bytes 319496 | tf_op jit(solution)/shard_map/ppermute | solution.py:619
  144.8 4.7 %collective-permute-start.12 = (bf16[32,1664]{1,0:T(8,128)(2,1)S(1)}, bf16[32,1664]{1,0:T(8,128)(2,1)S(1)}, u32[]{:S(2)}, u32[]{:S(2)}) collective-permute-start(bf16[32,1664]{1,0:T(8,128)(2,1)S(1)} %get-tuple-element.97), channel_id=1, source_target_pairs={{0,12},{4,0},{8,4},{12,8},{16,28},{20,16},{24,20},{28,24},{32,44},... | collective-permute-start | bytes 319496 | tf_op jit(solution)/shard_map/ppermute | solution.py:619
  145.5 6.2 %collective-permute-start.14 = (bf16[32,1664]{1,0:T(8,128)(2,1)S(1)}, bf16[32,1664]{1,0:T(8,128)(2,1)S(1)}, u32[]{:S(2)}, u32[]{:S(2)}) collective-permute-start(bf16[32,1664]{1,0:T(8,128)(2,1)S(1)} %get-tuple-element.100), channel_id=1, source_target_pairs={{0,128},{4,132},{8,136},{12,140},{16,144},{20,148},{24,152},{28,15... | collective-permute-start | bytes 319496 | tf_op jit(solution)/shard_map/ppermute | solution.py:619
  151.7 13.0 %copy-start.5 = (f32[128,512]{1,0:T(8,128)S(1)}, f32[128,512]{1,0:T(8,128)}, u32[]{:S(2)}) copy-start(f32[128,512]{1,0:T(8,128)} %get-tuple-element.108.refs_5_) | copy-start | bytes 786436
  152.4 12.3 %collective-permute-start.16 = (bf16[16,1920]{1,0:T(8,128)(2,1)S(1)}, bf16[16,1920]{1,0:T(8,128)(2,1)S(1)}, u32[]{:S(2)}, u32[]{:S(2)}) collective-permute-start(bf16[16,1920]{1,0:T(8,128)(2,1)S(1)} %get-tuple-element.104), channel_id=1, source_target_pairs={{0,16},{4,20},{8,24},{12,28},{16,32},{20,36},{24,40},{28,44},{32,4... | collective-permute-start | bytes 184328 | tf_op jit(solution)/shard_map/ppermute | solution.py:619
  152.5 12.2 %collective-permute-start.18 = (bf16[16,1920]{1,0:T(8,128)(2,1)S(1)}, bf16[16,1920]{1,0:T(8,128)(2,1)S(1)}, u32[]{:S(2)}, u32[]{:S(2)}) collective-permute-start(bf16[16,1920]{1,0:T(8,128)(2,1)S(1)} %get-tuple-element.106), channel_id=1, source_target_pairs={{0,48},{4,52},{8,56},{12,60},{16,0},{20,4},{24,8},{28,12},{32,16},... | collective-permute-start | bytes 184328 | tf_op jit(solution)/shard_map/ppermute | solution.py:619
  156.6 8.1 %collective-permute-start.17 = (bf16[16,1664]{1,0:T(8,128)(2,1)S(1)}, bf16[16,1664]{1,0:T(8,128)(2,1)S(1)}, u32[]{:S(2)}, u32[]{:S(2)}) collective-permute-start(bf16[16,1664]{1,0:T(8,128)(2,1)S(1)} %get-tuple-element.105), channel_id=1, source_target_pairs={{0,32},{4,36},{8,40},{12,44},{16,48},{20,52},{24,56},{28,60},{32,0... | collective-permute-start | bytes 159752 | tf_op jit(solution)/shard_map/ppermute | solution.py:619

commit v7 on v6

--- a/solution.py
+++ b/solution.py
@@ -90,9 +90,9 @@
     return mm(jnp.concatenate(found, axis=1), jnp.concatenate([mask] * 3, axis=0))
 
 
-def fold(value, mask):
+def fold(value, mask, count=2):
     total = None
-    for piece in pieces_of(value, 2):
+    for piece in pieces_of(value, count):
         part = mm_cols(piece, mask)
         total = part if total is None else total + part
     return total
@@ -306,7 +306,14 @@
     out[...] = done[...].reshape(count, 64, state).astype(bf16)
 
 
-def intra_kernel(conv, gate, d_gated, step, cumul, cumul_t, mixed, d_driven, d_bc, d_cumul):
+def intra_kernel(
+    conv, gate, d_gated, step, cumul, cumul_t, normal, normal_halo,
+    mixed, d_driven, d_bc, d_cumul, normal_t, halo_t,
+):
+    for source, target in ((normal, normal_t), (normal_halo, halo_t)):
+        count = source.shape[0]
+        same = iota((count, count), 0) == iota((count, count), 1)
+        target[...] = mm_rows(source[...], ones_where(same)).astype(bf16)
     rows = conv.shape[0] // 2
     inner = gate.shape[1]
     heads = step.shape[1]
@@ -358,7 +365,7 @@
 
 def post_kernel(
     place, got, conv, gate, d_gated, raw, step, cumul, mixed, d_driven, d_bc, d_cumul, step_bias, decay_log, skip_gain,
-    conv_w, cot, normal, normal_halo,
+    conv_w, cot, normal_t, halo_t,
     gated, d_gate, d_xbc, d_first, d_second, d_step, *refs,
 ):
     by_x, by_y, ext, d_conv_out, whole, parted = refs[:4], refs[4:8], refs[8], refs[9], refs[10], refs[11]
@@ -401,14 +408,14 @@
         met = jnp.sum(products.reshape(heads, inner // heads, state), axis=1)
         met = jnp.sum(met, axis=1, keepdims=True)
         met = jnp.sum(jnp.where(iota((heads, heads), 0) == iota((heads, heads), 1), met, 0.0), axis=0, keepdims=True)
-        folded = fold(jnp.concatenate([driven * answer, d_mixed * inter, d_drive * inputs], axis=0), mask)
+        folded = fold(jnp.concatenate([driven * answer, d_mixed * inter, d_drive * inputs], axis=0), mask, 1)
         held, entered, by_size = folded[:rows], folded[rows : 2 * rows], folded[2 * rows :]
         d_end = jnp.exp(end) * met + jnp.sum(held, axis=0, keepdims=True)
         d_decay = tri_sum(triangle(rows, False), d_cumul[at, :] + entered - held) + d_end
         d_size = by_size - jnp.exp(decay_log[...].reshape(1, -1)) * d_decay
         d_step[at, :] = (d_size * sigmoid(raw[at, :] + step_bias[...].reshape(1, -1))).astype(bf16)
         d_act = jnp.concatenate([skip * d_mixed + d_drive * sizes, d_bmat, d_cmat], axis=1)
-        margin = normal_halo.shape[0] // 2
+        margin = halo_t.shape[1] // 2
         ext[:margin, :] = jnp.zeros((margin, ext.shape[1]), f32)
         ext[margin : margin + rows, :] = d_act * (share * (1.0 + found * (1.0 - share)))
         ext[margin + rows :, :] = jnp.zeros((8, ext.shape[1]), f32)
@@ -424,11 +431,11 @@
     columns = cot.shape[1]
     half = d_xbc.shape[1] // 2
     out_term = mm_rows(gated[...], cot[...]).reshape(COUNT, 2, 8, columns)
-    gate_term = mm_rows(normal[...], d_gate[...]).reshape(COUNT // SIDE, SIDE, 8, inner)
-    in_term = mm_rows(normal[...], d_xbc[...]) + mm_rows(normal_halo[...], d_conv_out[...])
-    whole[:, :columns] = out_term[:, 0].reshape(-1, columns)
-    whole[:, columns : 2 * columns] = out_term[:, 1].reshape(-1, columns)
-    whole[:, 2 * columns :] = in_term[:, :half]
+    gate_term = mm(normal_t[...], d_gate[...]).reshape(COUNT // SIDE, SIDE, 8, inner)
+    in_term = mm(normal_t[...], d_xbc[...]) + mm(halo_t[...], d_conv_out[...])
+    whole[:, :columns] = out_term[:, 0].reshape(-1, columns).astype(bf16)
+    whole[:, columns : 2 * columns] = out_term[:, 1].reshape(-1, columns).astype(bf16)
+    whole[:, 2 * columns :] = in_term[:, :half].astype(bf16)
     parted[:, :, :, :inner] = gate_term
     parted[:, :, :, inner:] = in_term[:, half:].reshape(COUNT // SIDE, SIDE, 8, half)
     ring_out(lambda step: chunk_x(place, whole, step), by_x)
@@ -688,15 +695,17 @@
     got = transpose_over(payload, beside)
     (summary,) = call(group_kernel, [((COUNT // SIDE, 72, state), bf16)], (got,), vmem=16 * 2**20)
     summaries = transpose_over(summary, across)
-    mixed, d_driven, d_bc, d_cumul = call(
+    mixed, d_driven, d_bc, d_cumul, normal_t, halo_t = call(
         intra_kernel,
         [
             ((both_rows, inner), bf16),
             ((both_rows, inner), bf16),
             ((both_rows, 2 * state), f32),
             ((both_rows, heads), f32),
+            ((width, both_rows), bf16),
+            ((width, 32), bf16),
         ],
-        (conv, gate, d_gated, step, cumul, cumul_t),
+        (conv, gate, d_gated, step, cumul, cumul_t, normal, normal_halo),
         flops=8 * 10**9,
     )
     groups = COUNT // SIDE
@@ -725,12 +734,12 @@
         + slots(eighth, joined, bf16) * 2,
         (
             place, states, conv, gate, d_gated, raw, step, cumul, mixed, d_driven, d_bc, d_cumul,
-            step_bias, decay_log, skip_gain, conv_weight, cot, normal, normal_halo,
+            step_bias, decay_log, skip_gain, conv_weight, cot, normal_t, halo_t,
         ),
         [
             pltpu.VMEM((rows + 24, channels), f32),
             pltpu.VMEM((32, channels), bf16),
-            pltpu.VMEM((8 * COUNT, joined), f32),
+            pltpu.VMEM((8 * COUNT, joined), bf16),
             pltpu.VMEM((COUNT // SIDE, SIDE, 8, joined), f32),
         ],
         scalars=1,

time: 167 us -> 165 us (0.988)
  no operation moved by 1% of the time
where the time goes in v7:
time: 165 us; the launch traced here: 164 us
  waiting for transfers between devices  46.7 us (28%)
  starting transfers between devices  46.2 us (28%)
  Pallas kernels  34.9 us (21%)
  blocking collectives  31.9 us (19%)
  local copies, waits for them, and re-layouts  3.06 us (2%)
    pallas_call x11, Pallas kernels, call(): pl.pallas_call(used, out_shape=[jax.ShapeDtypeStruct(shape, kind) for sha...  34.9 us
    all_to_all x2, blocking collectives, transpose_over(): return lax.all_to_all(parts, 'seq', 0, 0, axis_index_groups=groups)  31.9 us
    all_to_all x2, waiting for transfers between devices, transpose_over(): return lax.all_to_all(parts, 'seq', 0, 0, axis_index_groups=groups)  14.4 us
    ppermute x9, waiting for transfers between devices, exchange(): lax.ppermute(parts[step], 'seq', axis_pairs(stride, step))  13.6 us
    ppermute x9, starting transfers between devices, exchange(): lax.ppermute(parts[step], 'seq', axis_pairs(stride, step))  11 us
    ppermute x1, starting transfers between devices, shards(): high = lax.ppermute(sequence[:16], 'seq', downward)  10.9 us
    all_to_all x2, starting transfers between devices, transpose_over(): return lax.all_to_all(parts, 'seq', 0, 0, axis_index_groups=groups)  9.47 us
    ppermute x1, waiting for transfers between devices, shards(): low = lax.ppermute(sequence[rows - 16:], 'seq', upward)  8.8 us
  transfers between devices with their start and end apart: 21, of which 10 were waited for; matrix products, arithmetic and copies ran while one was open for 0% of the time, Pallas kernels for 7%

profile of v7, /device:TPU:6, one launch (start us, length us, event | category | flops | bytes accessed | tf_op | source)
XLA Modules:
  0.0 164.2 jit_solution(15824185620499149856)
XLA Ops:
  0.6 0.7 fusion
  1.4 10.9 %collective-permute-start.1 = (bf16[16,512]{1,0:T(8,128)(2,1)S(1)}, bf16[16,512]{1,0:T(8,128)(2,1)S(1)}, u32[]{:S(2)}, u32[]{:S(2)}) collective-permute-start(bf16[16,512]{1,0:T(8,128)(2,1)S(1)} %get-tuple-element.116), channel_id=1, source_target_pairs={{4,0},{8,4},{12,8},{16,12},{20,16},{24,20},{28,24},{32,28},{36,32}... | collective-permute-start | bytes 49160 | tf_op jit(solution)/shard_map/ppermute | solution.py:671
  12.3 1.9 %collective-permute-start = (bf16[16,512]{1,0:T(8,128)(2,1)S(1)}, bf16[16,512]{1,0:T(8,128)(2,1)S(1)}, u32[]{:S(2)}, u32[]{:S(2)}) collective-permute-start(bf16[16,512]{1,0:T(8,128)(2,1)S(1)} %get-tuple-element.117), channel_id=1, source_target_pairs={{0,4},{4,8},{8,12},{12,16},{16,20},{20,24},{24,28},{28,32},{32,36}... | collective-permute-start | bytes 49160 | tf_op jit(solution)/shard_map/ppermute | solution.py:670
  14.2 0.0 collective-permute-done.1.refs_3_.refs_10_
  14.2 8.8 %collective-permute-done.refs_2_.refs_9_ = bf16[16,512]{1,0:T(8,128)(2,1)S(1)} collective-permute-done((bf16[16,512]{1,0:T(8,128)(2,1)S(1)}, bf16[16,512]{1,0:T(8,128)(2,1)S(1)}, u32[]{:S(2)}, u32[]{:S(2)}) %collective-permute-start) | collective-permute-done | bytes 16416 | tf_op jit(solution)/shard_map/ppermute | solution.py:670
  23.0 0.0 copy-done.8
  23.0 0.6 copy-done.9
  23.6 7.0 %shard_map.138 = (bf16[4,1040,128]{2,1,0:T(8,128)(2,1)}, bf16[256,512]{1,0:T(8,128)(2,1)}, bf16[256,512]{1,0:T(8,128)(2,1)}, bf16[32,512]{1,0:T(8,128)(2,1)}, bf...) custom-call(bf16[128,512]{1,0:T(8,128)(2,1)} %refs_0_.1, ...), custom_call_target="tpu_custom_call" | custom-call | flops 1000000000 | bytes 3746944 | tf_op jit(solution)/shard_map/pallas_call | solution.py:28
  30.6 17.6 %all_to_all.20.refs_0_ = bf16[4,1040,128]{2,1,0:T(8,128)(2,1)S(1)} all-to-all(bf16[4,1040,128]{2,1,0:T(8,128)(2,1)} %get-tuple-element.61), channel_id=1, replica_groups={{0,4,8,12},{16,20,24,28},{32,36,40,44},{48,52,56,60},{64,68,72,76},{80,..., dimensions={0} | all-to-all | bytes 2129920 | tf_op jit(solution)/shard_map/all_to_all | solution.py:637
  48.3 0.4 shard_map.139
  48.6 14.2 %all_to_all.21.refs_0_ = bf16[16,72,128]{2,1,0:T(8,128)(2,1)S(1)} all-to-all(bf16[16,72,128]{2,1,0:T(8,128)(2,1)S(1)} %shard_map.139), channel_id=1, replica_groups={{0,16,32,48,64,80,96,112,128,144,160,176,192,208,224,240},{4,20,36,52,6..., dimensions={0} | all-to-all | bytes 589824 | tf_op jit(solution)/shard_map/all_to_all | solution.py:637
  62.9 1.6 shard_map.140
  64.5 5.8 %all-to-all-start.2 = ((bf16[16,64,128]{2,1,0:T(8,128)(2,1)}), bf16[16,64,128]{2,1,0:T(8,128)(2,1)S(1)}, u32[]{:S(2)}, u32[]{:S(2)}) async-start(bf16[16,64,128]{2,1,0:T(8,128)(2,1)} %shard_map.140), calls=%async_computation.2 | async-start | bytes 524288 | tf_op jit(solution)/shard_map/all_to_all | solution.py:637
  70.2 9.6 %all-to-all-done.2.refs_1_ = bf16[16,64,128]{2,1,0:T(8,128)(2,1)S(1)} async-done(((bf16[16,64,128]{2,1,0:T(8,128)(2,1)}), bf16[16,64,128]{2,1,0:T(8,128)(2,1)S(1)}, u32[]{:S(2)}, u32[]{:S(2)}) %all-to-all-start.2) | async-done | bytes 262176 | tf_op jit(solution)/shard_map/all_to_all | solution.py:637
  79.8 1.3 shard_map.141
  81.2 3.7 %all-to-all-start.3 = ((bf16[4,1024,128]{2,1,0:T(8,128)(2,1)}), bf16[4,1024,128]{2,1,0:T(8,128)(2,1)S(1)}, u32[]{:S(2)}, u32[]{:S(2)}) async-start(bf16[4,1024,128]{2,1,0:T(8,128)(2,1)} %shard_map.141), calls=%async_computation.3 | async-start | bytes 2097152 | tf_op jit(solution)/shard_map/all_to_all | solution.py:637
  84.9 0.7 pad_add_fusion.refs_0_
  85.5 5.2 %shard_map.142 = (bf16[256,1024]{1,0:T(8,128)(2,1)}, bf16[256,1024]{1,0:T(8,128)(2,1)}, f32[256,256]{1,0:T(8,128)}, f32[256,16]{1,0:T(8,128)}, bf16[512,256]{1,0:T(8,128)(2,1)}, /*index=5*/bf16[512,32]{1,0:T(8,128)(2,1)}) custom-call(bf16[256,1280]{1,0:T(8,128)(2,1)} %get-tuple-element.62.refs_0_.refs_2_, ...), custom_call_target="tpu_custom_call" | custom-call | flops 8000000000 | bytes 2048000 | tf_op jit(solution)/shard_map/pallas_call | solution.py:28
  90.7 4.9 %all-to-all-done.3.refs_1_ = bf16[4,1024,128]{2,1,0:T(8,128)(2,1)S(1)} async-done(((bf16[4,1024,128]{2,1,0:T(8,128)(2,1)}), bf16[4,1024,128]{2,1,0:T(8,128)(2,1)S(1)}, u32[]{:S(2)}, u32[]{:S(2)}) %all-to-all-start.3) | async-done | bytes 1048608 | tf_op jit(solution)/shard_map/all_to_all | solution.py:637
  95.5 1.0 copy-done.7
  96.5 10.4 %shard_map.143 = (bf16[256,1024]{1,0:T(8,128)(2,1)}, bf16[256,1024]{1,0:T(8,128)(2,1)}, bf16[256,1280]{1,0:T(8,128)(2,1)}, f32[8,1280]{1,0:T(8,128)}, f32[8,1280...) custom-call(s32[3]{0:T(128)} %pad_add_fusion.refs_0_, ...), custom_call_target="tpu_custom_call" | custom-call | flops 1000000000 | bytes 4706508 | tf_op jit(solution)/shard_map/pallas_call | solution.py:28
  106.9 2.5 %collective-permute-start.2 = (bf16[128,1664]{1,0:T(8,128)(2,1)}, bf16[128,1664]{1,0:T(8,128)(2,1)S(1)}, u32[]{:S(2)}, u32[]{:S(2)}) collective-permute-start(bf16[128,1664]{1,0:T(8,128)(2,1)} %get-tuple-element.86), channel_id=1, source_target_pairs={{0,64},{4,68},{8,72},{12,76},{16,80},{20,84},{24,88},{28,92},{32,9... | collective-permute-start | bytes 1277960 | tf_op jit(solution)/shard_map/ppermute | solution.py:631
  109.4 0.0 collective-permute-start.3
  109.4 0.6 collective-permute-start.4
  110.0 2.7 %collective-permute-start.5 = (bf16[128,1664]{1,0:T(8,128)(2,1)}, bf16[128,1664]{1,0:T(8,128)(2,1)S(1)}, u32[]{:S(2)}, u32[]{:S(2)}) collective-permute-start(bf16[128,1664]{1,0:T(8,128)(2,1)} %get-tuple-element.91), channel_id=1, source_target_pairs={{0,12},{4,0},{8,4},{12,8},{16,28},{20,16},{24,20},{28,24},{32,44},... | collective-permute-start | bytes 1277960 | tf_op jit(solution)/shard_map/ppermute | solution.py:632
  112.6 6.4 %shard_map.144 = (bf16[128,512]{1,0:T(8,128)(2,1)}, f32[128,512]{1,0:T(8,128)}, bf16[64,128]{1,0:T(8,128)(2,1)}) custom-call(s32[3]{0:T(128)} %pad_add_fusion.refs_0_, bf16[256,512]{1,0:T(8,128)(2,1)} %get-tuple-element.60.refs_1_, f32[512]{0:T(512)} %refs_2_.1, bf16[256,1024]{1,0:T(8,128)(2,1)} %get-tuple-element.78.refs_3_, bf16[1024,512]{1,0:T(8,128)(2,1)} %refs_4_.3, ...), custom_call_target="tpu_custom_call" | custom-call | flops 8000000000 | bytes 5515276 | tf_op jit(solution)/shard_map/pallas_call | solution.py:28
  119.0 0.0 collective-permute-done.2.refs_1_.refs_2_
  119.0 0.0 collective-permute-done.3.refs_2_.refs_3_
  119.0 1.7 %collective-permute-done.4.refs_4_.refs_7_ = bf16[128,1664]{1,0:T(8,128)(2,1)S(1)} collective-permute-done((bf16[128,1664]{1,0:T(8,128)(2,1)}, bf16[128,1664]{1,0:T(8,128)(2,1)S(1)}, u32[]{:S(2)}, u32[]{:S(2)}) %collective-permute-start.4) | collective-permute-done | bytes 426016 | tf_op jit(solution)/shard_map/ppermute | solution.py:631
  120.7 0.0 collective-permute-done.5.refs_5_.refs_8_
  120.8 0.0 copy-done.4
  120.8 0.0 copy-start.6
  120.8 0.7 copy-done.6
  121.5 0.2 shard_map.145
  121.7 0.1 collective-permute-start.8
  121.8 3.6 %collective-permute-start.9 = (bf16[64,1792]{1,0:T(8,128)(2,1)S(1)}, bf16[64,1792]{1,0:T(8,128)(2,1)S(1)}, u32[]{:S(2)}, u32[]{:S(2)}) collective-permute-start(bf16[64,1792]{1,0:T(8,128)(2,1)S(1)} %get-tuple-element.97), channel_id=1, source_target_pairs={{0,12},{4,0},{8,4},{12,8},{16,28},{20,16},{24,20},{28,24},{32,44},... | collective-permute-start | bytes 688136 | tf_op jit(solution)/shard_map/ppermute | solution.py:632
  125.4 3.5 %collective-permute-start.6 = (bf16[64,1664]{1,0:T(8,128)(2,1)S(1)}, bf16[64,1664]{1,0:T(8,128)(2,1)S(1)}, u32[]{:S(2)}, u32[]{:S(2)}) collective-permute-start(bf16[64,1664]{1,0:T(8,128)(2,1)S(1)} %get-tuple-element.93), channel_id=1, source_target_pairs={{0,64},{4,68},{8,72},{12,76},{16,80},{20,84},{24,88},{28,92},{32,9... | collective-permute-start | bytes 638984 | tf_op jit(solution)/shard_map/ppermute | solution.py:631
  128.9 0.0 collective-permute-start.7
  128.9 3.4 %collective-permute-done.6.refs_4_ = bf16[64,1664]{1,0:T(8,128)(2,1)S(1)} collective-permute-done((bf16[64,1664]{1,0:T(8,128)(2,1)S(1)}, bf16[64,1664]{1,0:T(8,128)(2,1)S(1)}, u32[]{:S(2)}, u32[]{:S(2)}) %collective-permute-start.6) | collective-permute-done | bytes 213024 | tf_op jit(solution)/shard_map/ppermute | solution.py:631
  132.3 4.8 %collective-permute-done.7.refs_5_ = bf16[64,1664]{1,0:T(8,128)(2,1)S(1)} collective-permute-done((bf16[64,1664]{1,0:T(8,128)(2,1)S(1)}, bf16[64,1664]{1,0:T(8,128)(2,1)S(1)}, u32[]{:S(2)}, u32[]{:S(2)}) %collective-permute-start.7) | collective-permute-done | bytes 213024 | tf_op jit(solution)/shard_map/ppermute | solution.py:632
  137.1 0.0 collective-permute-done.8.refs_9_
  137.1 0.0 collective-permute-done.9.refs_10_
  137.1 0.0 copy-done.1
  137.1 1.1 shard_map.146
  138.2 0.1 collective-permute-start.10
  138.3 0.1 collective-permute-start.13
  138.4 2.0 %collective-permute-start.15 = (bf16[32,1792]{1,0:T(8,128)(2,1)S(1)}, bf16[32,1792]{1,0:T(8,128)(2,1)S(1)}, u32[]{:S(2)}, u32[]{:S(2)}) collective-permute-start(bf16[32,1792]{1,0:T(8,128)(2,1)S(1)} %get-tuple-element.105), channel_id=1, source_target_pairs={{0,192},{4,196},{8,200},{12,204},{16,208},{20,212},{24,216},{28,22... | collective-permute-start | bytes 344072 | tf_op jit(solution)/shard_map/ppermute | solution.py:626
  140.4 3.3 %collective-permute-start.11 = (bf16[32,1664]{1,0:T(8,128)(2,1)S(1)}, bf16[32,1664]{1,0:T(8,128)(2,1)S(1)}, u32[]{:S(2)}, u32[]{:S(2)}) collective-permute-start(bf16[32,1664]{1,0:T(8,128)(2,1)S(1)} %get-tuple-element.100), channel_id=1, source_target_pairs={{0,8},{4,12},{8,0},{12,4},{16,24},{20,28},{24,16},{28,20},{32,40},... | collective-permute-start | bytes 319496 | tf_op jit(solution)/shard_map/ppermute | solution.py:626
  143.7 0.6 collective-permute-start.12
  144.3 0.0 collective-permute-done.10.refs_2_
  144.3 0.0 collective-permute-start.14
  144.3 2.3 %collective-permute-done.11.refs_3_ = bf16[32,1664]{1,0:T(8,128)(2,1)S(1)} collective-permute-done((bf16[32,1664]{1,0:T(8,128)(2,1)S(1)}, bf16[32,1664]{1,0:T(8,128)(2,1)S(1)}, u32[]{:S(2)}, u32[]{:S(2)}) %collective-permute-start.11) | collective-permute-done | bytes 106528 | tf_op jit(solution)/shard_map/ppermute | solution.py:626
  146.6 1.8 %collective-permute-done.12.refs_4_ = bf16[32,1664]{1,0:T(8,128)(2,1)S(1)} collective-permute-done((bf16[32,1664]{1,0:T(8,128)(2,1)S(1)}, bf16[32,1664]{1,0:T(8,128)(2,1)S(1)}, u32[]{:S(2)}, u32[]{:S(2)}) %collective-permute-start.12) | collective-permute-done | bytes 106528 | tf_op jit(solution)/shard_map/ppermute | solution.py:626
  148.4 2.1 %collective-permute-done.14.refs_7_ = bf16[32,1664]{1,0:T(8,128)(2,1)S(1)} collective-permute-done((bf16[32,1664]{1,0:T(8,128)(2,1)S(1)}, bf16[32,1664]{1,0:T(8,128)(2,1)S(1)}, u32[]{:S(2)}, u32[]{:S(2)}) %collective-permute-start.14) | collective-permute-done | bytes 106528 | tf_op jit(solution)/shard_map/ppermute | solution.py:626
  150.5 0.0 collective-permute-done.13.refs_6_
  150.5 0.0 collective-permute-done.15.refs_8_
  150.5 0.7 shard_map.147
  151.2 0.1 collective-permute-start.16
  151.3 4.1 %collective-permute-start.18 = (bf16[16,1920]{1,0:T(8,128)(2,1)S(1)}, bf16[16,1920]{1,0:T(8,128)(2,1)S(1)}, u32[]{:S(2)}, u32[]{:S(2)}) collective-permute-start(bf16[16,1920]{1,0:T(8,128)(2,1)S(1)} %get-tuple-element.110), channel_id=1, source_target_pairs={{0,48},{4,52},{8,56},{12,60},{16,0},{20,4},{24,8},{28,12},{32,16},... | collective-permute-start | bytes 184328 | tf_op jit(solution)/shard_map/ppermute | solution.py:626
  155.4 0.7 collective-permute-start.17
  156.2 7.3 %collective-permute-done.17.refs_2_ = bf16[16,1664]{1,0:T(8,128)(2,1)S(1)} collective-permute-done((bf16[16,1664]{1,0:T(8,128)(2,1)S(1)}, bf16[16,1664]{1,0:T(8,128)(2,1)S(1)}, u32[]{:S(2)}, u32[]{:S(2)}) %collective-permute-start.17) | collective-permute-done | bytes 53280 | tf_op jit(solution)/shard_map/ppermute | solution.py:626
  163.5 0.0 collective-permute-done.16.refs_1_
  163.5 0.0 collective-permute-done.18.refs_3_
  163.5 0.7 shard_map.148
  (13 shorter events, 0.0 us)
Async XLA Ops:
  1.4 12.9 %collective-permute-start.1 = (bf16[16,512]{1,0:T(8,128)(2,1)S(1)}, bf16[16,512]{1,0:T(8,128)(2,1)S(1)}, u32[]{:S(2)}, u32[]{:S(2)}) collective-permute-start(bf16[16,512]{1,0:T(8,128)(2,1)S(1)} %get-tuple-element.116), channel_id=1, source_target_pairs={{4,0},{8,4},{12,8},{16,12},{20,16},{24,20},{28,24},{32,28},{36,32}... | collective-permute-start | bytes 49160 | tf_op jit(solution)/shard_map/ppermute | solution.py:671
  12.3 10.8 %collective-permute-start = (bf16[16,512]{1,0:T(8,128)(2,1)S(1)}, bf16[16,512]{1,0:T(8,128)(2,1)S(1)}, u32[]{:S(2)}, u32[]{:S(2)}) collective-permute-start(bf16[16,512]{1,0:T(8,128)(2,1)S(1)} %get-tuple-element.117), channel_id=1, source_target_pairs={{0,4},{4,8},{8,12},{12,16},{16,20},{20,24},{24,28},{28,32},{32,36}... | collective-permute-start | bytes 49160 | tf_op jit(solution)/shard_map/ppermute | solution.py:670
  14.2 8.8 %copy-start.8 = (bf16[16,512]{1,0:T(8,128)(2,1)}, bf16[16,512]{1,0:T(8,128)(2,1)S(1)}, u32[]{:S(2)}) copy-start(bf16[16,512]{1,0:T(8,128)(2,1)S(1)} %collective-permute-done.1.refs_3_.refs_10_) | copy-start | bytes 49156
  23.0 0.6 copy-start.9
  64.5 15.3 %all-to-all-start.2 = ((bf16[16,64,128]{2,1,0:T(8,128)(2,1)}), bf16[16,64,128]{2,1,0:T(8,128)(2,1)S(1)}, u32[]{:S(2)}, u32[]{:S(2)}) async-start(bf16[16,64,128]{2,1,0:T(8,128)(2,1)} %shard_map.140), calls=%async_computation.2 | async-start | bytes 524288 | tf_op jit(solution)/shard_map/all_to_all | solution.py:637
  81.2 14.4 %all-to-all-start.3 = ((bf16[4,1024,128]{2,1,0:T(8,128)(2,1)}), bf16[4,1024,128]{2,1,0:T(8,128)(2,1)S(1)}, u32[]{:S(2)}, u32[]{:S(2)}) async-start(bf16[4,1024,128]{2,1,0:T(8,128)(2,1)} %shard_map.141), calls=%async_computation.3 | async-start | bytes 2097152 | tf_op jit(solution)/shard_map/all_to_all | solution.py:637
  95.5 1.0 copy-start.7
  106.9 12.1 %collective-permute-start.2 = (bf16[128,1664]{1,0:T(8,128)(2,1)}, bf16[128,1664]{1,0:T(8,128)(2,1)S(1)}, u32[]{:S(2)}, u32[]{:S(2)}) collective-permute-start(bf16[128,1664]{1,0:T(8,128)(2,1)} %get-tuple-element.86), channel_id=1, source_target_pairs={{0,64},{4,68},{8,72},{12,76},{16,80},{20,84},{24,88},{28,92},{32,9... | collective-permute-start | bytes 1277960 | tf_op jit(solution)/shard_map/ppermute | solution.py:631
  109.4 9.7 %collective-permute-start.3 = (bf16[128,1664]{1,0:T(8,128)(2,1)}, bf16[128,1664]{1,0:T(8,128)(2,1)S(1)}, u32[]{:S(2)}, u32[]{:S(2)}) collective-permute-start(bf16[128,1664]{1,0:T(8,128)(2,1)} %get-tuple-element.87), channel_id=1, source_target_pairs={{0,192},{4,196},{8,200},{12,204},{16,208},{20,212},{24,216},{28,22... | collective-permute-start | bytes 1277960 | tf_op jit(solution)/shard_map/ppermute | solution.py:632
  109.4 11.4 %collective-permute-start.4 = (bf16[128,1664]{1,0:T(8,128)(2,1)}, bf16[128,1664]{1,0:T(8,128)(2,1)S(1)}, u32[]{:S(2)}, u32[]{:S(2)}) collective-permute-start(bf16[128,1664]{1,0:T(8,128)(2,1)} %get-tuple-element.90), channel_id=1, source_target_pairs={{0,4},{4,8},{8,12},{12,0},{16,20},{20,24},{24,28},{28,16},{32,36},... | collective-permute-start | bytes 1277960 | tf_op jit(solution)/shard_map/ppermute | solution.py:631
  110.0 10.8 %collective-permute-start.5 = (bf16[128,1664]{1,0:T(8,128)(2,1)}, bf16[128,1664]{1,0:T(8,128)(2,1)S(1)}, u32[]{:S(2)}, u32[]{:S(2)}) collective-permute-start(bf16[128,1664]{1,0:T(8,128)(2,1)} %get-tuple-element.91), channel_id=1, source_target_pairs={{0,12},{4,0},{8,4},{12,8},{16,28},{20,16},{24,20},{28,24},{32,44},... | collective-permute-start | bytes 1277960 | tf_op jit(solution)/shard_map/ppermute | solution.py:632
  112.6 8.1 %copy-start.3 = (bf16[128,1664]{1,0:T(8,128)(2,1)S(1)}, bf16[128,1664]{1,0:T(8,128)(2,1)}, u32[]{:S(2)}) copy-start(bf16[128,1664]{1,0:T(8,128)(2,1)} %get-tuple-element.88.refs_0_) | copy-start | bytes 1277956
  112.6 8.1 %copy-start.4 = (bf16[128,1664]{1,0:T(8,128)(2,1)S(1)}, bf16[128,1664]{1,0:T(8,128)(2,1)}, u32[]{:S(2)}) copy-start(bf16[128,1664]{1,0:T(8,128)(2,1)} %get-tuple-element.89.refs_3_) | copy-start | bytes 1277956
  120.8 0.7 copy-start.6
  121.5 15.6 %copy-start = (s32[3]{0:T(128)S(1)}, s32[3]{0:T(128)}, u32[]{:S(2)}) copy-start(s32[3]{0:T(128)} %pad_add_fusion.refs_0_) | copy-start | bytes 40
  121.5 15.6 %copy-start.1 = (bf16[128,1664]{1,0:T(8,128)(2,1)S(1)}, bf16[128,1664]{1,0:T(8,128)(2,1)}, u32[]{:S(2)}) copy-start(bf16[128,1664]{1,0:T(8,128)(2,1)} %get-tuple-element.85.refs_1_) | copy-start | bytes 1277956
  121.5 15.6 %copy-start.2 = (bf16[128,1664]{1,0:T(8,128)(2,1)S(1)}, bf16[128,1664]{1,0:T(8,128)(2,1)}, u32[]{:S(2)}) copy-start(bf16[128,1664]{1,0:T(8,128)(2,1)} %get-tuple-element.95.refs_6_) | copy-start | bytes 1277956
  121.7 15.4 %collective-permute-start.8 = (bf16[64,1792]{1,0:T(8,128)(2,1)S(1)}, bf16[64,1792]{1,0:T(8,128)(2,1)S(1)}, u32[]{:S(2)}, u32[]{:S(2)}) collective-permute-start(bf16[64,1792]{1,0:T(8,128)(2,1)S(1)} %get-tuple-element.96), channel_id=1, source_target_pairs={{0,4},{4,8},{8,12},{12,0},{16,20},{20,24},{24,28},{28,16},{32,36},... | collective-permute-start | bytes 688136 | tf_op jit(solution)/shard_map/ppermute | solution.py:631
  121.8 15.3 %collective-permute-start.9 = (bf16[64,1792]{1,0:T(8,128)(2,1)S(1)}, bf16[64,1792]{1,0:T(8,128)(2,1)S(1)}, u32[]{:S(2)}, u32[]{:S(2)}) collective-permute-start(bf16[64,1792]{1,0:T(8,128)(2,1)S(1)} %get-tuple-element.97), channel_id=1, source_target_pairs={{0,12},{4,0},{8,4},{12,8},{16,28},{20,16},{24,20},{28,24},{32,44},... | collective-permute-start | bytes 688136 | tf_op jit(solution)/shard_map/ppermute | solution.py:632
  125.4 6.9 %collective-permute-start.6 = (bf16[64,1664]{1,0:T(8,128)(2,1)S(1)}, bf16[64,1664]{1,0:T(8,128)(2,1)S(1)}, u32[]{:S(2)}, u32[]{:S(2)}) collective-permute-start(bf16[64,1664]{1,0:T(8,128)(2,1)S(1)} %get-tuple-element.93), channel_id=1, source_target_pairs={{0,64},{4,68},{8,72},{12,76},{16,80},{20,84},{24,88},{28,92},{32,9... | collective-permute-start | bytes 638984 | tf_op jit(solution)/shard_map/ppermute | solution.py:631
  128.9 8.2 %collective-permute-start.7 = (bf16[64,1664]{1,0:T(8,128)(2,1)S(1)}, bf16[64,1664]{1,0:T(8,128)(2,1)S(1)}, u32[]{:S(2)}, u32[]{:S(2)}) collective-permute-start(bf16[64,1664]{1,0:T(8,128)(2,1)S(1)} %get-tuple-element.94), channel_id=1, source_target_pairs={{0,192},{4,196},{8,200},{12,204},{16,208},{20,212},{24,216},{28,22... | collective-permute-start | bytes 638984 | tf_op jit(solution)/shard_map/ppermute | solution.py:632
  138.2 6.1 %collective-permute-start.10 = (bf16[32,1664]{1,0:T(8,128)(2,1)S(1)}, bf16[32,1664]{1,0:T(8,128)(2,1)S(1)}, u32[]{:S(2)}, u32[]{:S(2)}) collective-permute-start(bf16[32,1664]{1,0:T(8,128)(2,1)S(1)} %get-tuple-element.99), channel_id=1, source_target_pairs={{0,4},{4,8},{8,12},{12,0},{16,20},{20,24},{24,28},{28,16},{32,36},... | collective-permute-start | bytes 319496 | tf_op jit(solution)/shard_map/ppermute | solution.py:626
  138.3 12.2 %collective-permute-start.13 = (bf16[32,1792]{1,0:T(8,128)(2,1)S(1)}, bf16[32,1792]{1,0:T(8,128)(2,1)S(1)}, u32[]{:S(2)}, u32[]{:S(2)}) collective-permute-start(bf16[32,1792]{1,0:T(8,128)(2,1)S(1)} %get-tuple-element.103), channel_id=1, source_target_pairs={{0,64},{4,68},{8,72},{12,76},{16,80},{20,84},{24,88},{28,92},{32,9... | collective-permute-start | bytes 344072 | tf_op jit(solution)/shard_map/ppermute | solution.py:626
  138.4 12.1 %collective-permute-start.15 = (bf16[32,1792]{1,0:T(8,128)(2,1)S(1)}, bf16[32,1792]{1,0:T(8,128)(2,1)S(1)}, u32[]{:S(2)}, u32[]{:S(2)}) collective-permute-start(bf16[32,1792]{1,0:T(8,128)(2,1)S(1)} %get-tuple-element.105), channel_id=1, source_target_pairs={{0,192},{4,196},{8,200},{12,204},{16,208},{20,212},{24,216},{28,22... | collective-permute-start | bytes 344072 | tf_op jit(solution)/shard_map/ppermute | solution.py:626
  140.4 6.2 %collective-permute-start.11 = (bf16[32,1664]{1,0:T(8,128)(2,1)S(1)}, bf16[32,1664]{1,0:T(8,128)(2,1)S(1)}, u32[]{:S(2)}, u32[]{:S(2)}) collective-permute-start(bf16[32,1664]{1,0:T(8,128)(2,1)S(1)} %get-tuple-element.100), channel_id=1, source_target_pairs={{0,8},{4,12},{8,0},{12,4},{16,24},{20,28},{24,16},{28,20},{32,40},... | collective-permute-start | bytes 319496 | tf_op jit(solution)/shard_map/ppermute | solution.py:626
  143.7 4.7 %collective-permute-start.12 = (bf16[32,1664]{1,0:T(8,128)(2,1)S(1)}, bf16[32,1664]{1,0:T(8,128)(2,1)S(1)}, u32[]{:S(2)}, u32[]{:S(2)}) collective-permute-start(bf16[32,1664]{1,0:T(8,128)(2,1)S(1)} %get-tuple-element.101), channel_id=1, source_target_pairs={{0,12},{4,0},{8,4},{12,8},{16,28},{20,16},{24,20},{28,24},{32,44},... | collective-permute-start | bytes 319496 | tf_op jit(solution)/shard_map/ppermute | solution.py:626
  144.3 6.2 %collective-permute-start.14 = (bf16[32,1664]{1,0:T(8,128)(2,1)S(1)}, bf16[32,1664]{1,0:T(8,128)(2,1)S(1)}, u32[]{:S(2)}, u32[]{:S(2)}) collective-permute-start(bf16[32,1664]{1,0:T(8,128)(2,1)S(1)} %get-tuple-element.104), channel_id=1, source_target_pairs={{0,128},{4,132},{8,136},{12,140},{16,144},{20,148},{24,152},{28,15... | collective-permute-start | bytes 319496 | tf_op jit(solution)/shard_map/ppermute | solution.py:626
  150.5 13.0 %copy-start.5 = (f32[128,512]{1,0:T(8,128)S(1)}, f32[128,512]{1,0:T(8,128)}, u32[]{:S(2)}) copy-start(f32[128,512]{1,0:T(8,128)} %get-tuple-element.112.refs_5_) | copy-start | bytes 786436
  151.2 12.3 %collective-permute-start.16 = (bf16[16,1920]{1,0:T(8,128)(2,1)S(1)}, bf16[16,1920]{1,0:T(8,128)(2,1)S(1)}, u32[]{:S(2)}, u32[]{:S(2)}) collective-permute-start(bf16[16,1920]{1,0:T(8,128)(2,1)S(1)} %get-tuple-element.108), channel_id=1, source_target_pairs={{0,16},{4,20},{8,24},{12,28},{16,32},{20,36},{24,40},{28,44},{32,4... | collective-permute-start | bytes 184328 | tf_op jit(solution)/shard_map/ppermute | solution.py:626
  151.3 12.2 %collective-permute-start.18 = (bf16[16,1920]{1,0:T(8,128)(2,1)S(1)}, bf16[16,1920]{1,0:T(8,128)(2,1)S(1)}, u32[]{:S(2)}, u32[]{:S(2)}) collective-permute-start(bf16[16,1920]{1,0:T(8,128)(2,1)S(1)} %get-tuple-element.110), channel_id=1, source_target_pairs={{0,48},{4,52},{8,56},{12,60},{16,0},{20,4},{24,8},{28,12},{32,16},... | collective-permute-start | bytes 184328 | tf_op jit(solution)/shard_map/ppermute | solution.py:626
  155.4 8.1 %collective-permute-start.17 = (bf16[16,1664]{1,0:T(8,128)(2,1)S(1)}, bf16[16,1664]{1,0:T(8,128)(2,1)S(1)}, u32[]{:S(2)}, u32[]{:S(2)}) collective-permute-start(bf16[16,1664]{1,0:T(8,128)(2,1)S(1)} %get-tuple-element.109), channel_id=1, source_target_pairs={{0,32},{4,36},{8,40},{12,44},{16,48},{20,52},{24,56},{28,60},{32,0... | collective-permute-start | bytes 159752 | tf_op jit(solution)/shard_map/ppermute | solution.py:626

commit v8 on v7

--- a/solution.py
+++ b/solution.py
@@ -307,8 +307,8 @@
 
 
 def intra_kernel(
-    conv, gate, d_gated, step, cumul, cumul_t, normal, normal_halo,
-    mixed, d_driven, d_bc, d_cumul, normal_t, halo_t,
+    conv, gate, d_gated, step, cumul, cumul_t, normal, normal_halo, skip_gain,
+    silus, d_gates, pushed, mixed, d_inputs, lefts, held_back, d_convs, bc, d_bc, sums_out, normal_t, halo_t,
 ):
     for source, target in ((normal, normal_t), (normal_halo, halo_t)):
         count = source.shape[0]
@@ -322,19 +322,35 @@
     lower = triangle(rows, True)
     first = iota((rows, 2 * inner // heads), 1) < inner // heads
     wide_pair = 2 * inner // heads
+    skip = expand(jnp.broadcast_to(skip_gain[...].reshape(1, -1), (8, heads)), mask)[:1]
     for frame in range(2):
         at = slice(frame * rows, (frame + 1) * rows)
         found = conv[at, :].astype(f32)
-        act = found * sigmoid(found)
-        bmat = act[:, inner : inner + state].astype(bf16)
-        cmat = act[:, inner + state :].astype(bf16)
-        driven = act[:, :inner] * expand(step[at, :], mask)
+        share = sigmoid(found)
+        act = found * share
+        d_convs[at, :] = (share * (1.0 + found * (1.0 - share))).astype(bf16)
+        bc[at, :] = act[:, inner:].astype(bf16)
+        bmat, cmat = bc[at, :state], bc[at, state:]
+        upto = cumul[at, :]
+        end = upto[rows - 1 : rows, :]
+        spread = expand(jnp.concatenate([step[at, :], jnp.exp(upto), jnp.exp(end - upto)], axis=0), mask)
+        sizes, grown, left = spread[:rows], spread[rows : 2 * rows], spread[2 * rows :]
+        inputs = act[:, :inner]
+        driven = inputs * sizes
+        lefts[at, :] = (left * inputs).astype(bf16)
+        held_back[at, :] = (left * driven).astype(bf16)
         wide = gate[at, :].astype(f32)
-        d_mixed = d_gated[at, :].astype(f32) * (wide * sigmoid(wide))
+        opened = sigmoid(wide)
+        silu = wide * opened
+        silus[at, :] = silu.astype(bf16)
+        d_out = d_gated[at, :].astype(f32)
+        d_gates[at, :] = (d_out * (opened * (1.0 + wide * (1.0 - opened)))).astype(bf16)
+        d_mixed = d_out * silu
+        pushed[at, :] = (d_mixed * grown).astype(bf16)
         scores = mm_cols(cmat, bmat)
-        upto, line = cumul[at, :], cumul_t[frame * heads : (frame + 1) * heads, :]
+        line = cumul_t[frame * heads : (frame + 1) * heads, :]
         d_scores = jnp.zeros((rows, rows), f32)
-        sums = []
+        sums, by_size = [], []
         for pair in range(heads // 2):
             lanes = slice(pair * wide_pair, (pair + 1) * wide_pair)
             decays = []
@@ -354,70 +370,61 @@
             d_weights = mm_cols(d_mix_two, drive_bf)
             d_drive = mm_rows(jnp.concatenate(weights, axis=0), d_mix_two)
             d_scores = d_scores + decays[0] * d_weights[:rows] + decays[1] * d_weights[rows:]
-            mixed[at, lanes] = mix.astype(bf16)
-            d_driven[at, lanes] = d_drive.astype(bf16)
+            mixed[at, lanes] = (mix + skip[:, lanes] * inputs[:, lanes]).astype(bf16)
+            d_inputs[at, lanes] = (skip[:, lanes] * d_mix + d_drive * sizes[:, lanes]).astype(bf16)
+            by_size.append(d_drive * inputs[:, lanes])
             sums.append(d_mix_bf.astype(f32) * mix - drive_bf.astype(f32) * d_drive)
         d_scores = d_scores.astype(bf16)
         d_bc[at, :state] = mm_rows(d_scores, cmat)
         d_bc[at, state:] = mm(d_scores, bmat)
-        d_cumul[at, :] = fold(jnp.concatenate(sums, axis=1), mask)
+        sums_out[at, :heads] = fold(jnp.concatenate(sums, axis=1), mask)
+        sums_out[at, heads:] = fold(jnp.concatenate(by_size, axis=1), mask)
 
 
 def post_kernel(
-    place, got, conv, gate, d_gated, raw, step, cumul, mixed, d_driven, d_bc, d_cumul, step_bias, decay_log, skip_gain,
-    conv_w, cot, normal_t, halo_t,
+    place, got, silus, d_gates, pushed, mixed, d_inputs, lefts, held_back, d_convs, bc, d_bc, sums,
+    raw, step, cumul, step_bias, decay_log, conv_w, cot, normal_t, halo_t,
     gated, d_gate, d_xbc, d_first, d_second, d_step, *refs,
 ):
     by_x, by_y, ext, d_conv_out, whole, parted = refs[:4], refs[4:8], refs[8], refs[9], refs[10], refs[11]
-    rows = conv.shape[0] // 2
-    inner = gate.shape[1]
+    rows = silus.shape[0] // 2
+    inner = silus.shape[1]
     heads = step.shape[1]
-    state = (conv.shape[1] - inner) // 2
+    state = bc.shape[1] // 2
     mask = head_mask(heads, inner // heads)
-    skip = expand(jnp.broadcast_to(skip_gain[...].reshape(1, -1), (8, heads)), mask)[:1]
     for frame in range(2):
         at = slice(frame * rows, (frame + 1) * rows)
-        found = conv[at, :].astype(f32)
-        share = sigmoid(found)
-        act = found * share
-        inputs = act[:, :inner]
-        bmat = act[:, inner : inner + state].astype(bf16)
-        cmat = act[:, inner + state :].astype(bf16)
         upto = cumul[at, :]
+        size = step[at, :]
         end = upto[rows - 1 : rows, :]
-        spread = expand(jnp.concatenate([step[at, :], jnp.exp(upto), jnp.exp(end - upto)], axis=0), mask)
-        sizes, grown, left = spread[:rows], spread[rows : 2 * rows], spread[2 * rows :]
+        spread = expand(jnp.concatenate([jnp.exp(upto), size * jnp.exp(end - upto)], axis=0), mask)
         part = inner // SIDE
         carried = got[:, frame * part : (frame + 1) * part, :].reshape(inner, state)
         reach = got[:, (2 + frame) * part : (3 + frame) * part, :].reshape(inner, state)
-        inter = grown * mm_cols(cmat, carried)
-        full = mixed[at, :].astype(f32) + inter + skip * inputs
-        wide = gate[at, :].astype(f32)
-        opened = sigmoid(wide)
-        silu = wide * opened
-        gated[at, :] = (full * silu).astype(bf16)
-        d_out = d_gated[at, :].astype(f32)
-        d_gate[at, :] = (d_out * full * (opened * (1.0 + wide * (1.0 - opened)))).astype(bf16)
-        d_mixed = d_out * silu
-        d_cmat = d_bc[at, state:] + mm((d_mixed * grown).astype(bf16), carried)
-        answer = left * mm_cols(bmat, reach)
-        driven = inputs * sizes
-        d_drive = d_driven[at, :].astype(f32) + answer
-        d_bmat = d_bc[at, :state] + mm((left * driven).astype(bf16), reach)
+        read = mm_cols(bc[at, state:], carried)
+        full = mixed[at, :].astype(f32) + spread[:rows] * read
+        gated[at, :] = (full * silus[at, :].astype(f32)).astype(bf16)
+        d_gate[at, :] = (full * d_gates[at, :].astype(f32)).astype(bf16)
+        d_cmat = d_bc[at, state:] + mm(pushed[at, :], carried)
+        answer = mm_cols(bc[at, :state], reach)
+        d_bmat = d_bc[at, :state] + mm(held_back[at, :], reach)
         products = carried.astype(f32) * reach.astype(f32)
         met = jnp.sum(products.reshape(heads, inner // heads, state), axis=1)
         met = jnp.sum(met, axis=1, keepdims=True)
         met = jnp.sum(jnp.where(iota((heads, heads), 0) == iota((heads, heads), 1), met, 0.0), axis=0, keepdims=True)
-        folded = fold(jnp.concatenate([driven * answer, d_mixed * inter, d_drive * inputs], axis=0), mask, 1)
-        held, entered, by_size = folded[:rows], folded[rows : 2 * rows], folded[2 * rows :]
+        folded = fold(
+            jnp.concatenate([lefts[at, :].astype(f32) * answer, pushed[at, :].astype(f32) * read], axis=0), mask, 1
+        )
+        by_size, entered = folded[:rows], folded[rows:]
+        held = by_size * size
         d_end = jnp.exp(end) * met + jnp.sum(held, axis=0, keepdims=True)
-        d_decay = tri_sum(triangle(rows, False), d_cumul[at, :] + entered - held) + d_end
-        d_size = by_size - jnp.exp(decay_log[...].reshape(1, -1)) * d_decay
+        d_decay = tri_sum(triangle(rows, False), sums[at, :heads] + entered - held) + d_end
+        d_size = sums[at, heads:] + by_size - jnp.exp(decay_log[...].reshape(1, -1)) * d_decay
         d_step[at, :] = (d_size * sigmoid(raw[at, :] + step_bias[...].reshape(1, -1))).astype(bf16)
-        d_act = jnp.concatenate([skip * d_mixed + d_drive * sizes, d_bmat, d_cmat], axis=1)
+        d_act = jnp.concatenate([d_inputs[at, :].astype(f32) + spread[rows:] * answer, d_bmat, d_cmat], axis=1)
         margin = halo_t.shape[1] // 2
         ext[:margin, :] = jnp.zeros((margin, ext.shape[1]), f32)
-        ext[margin : margin + rows, :] = d_act * (share * (1.0 + found * (1.0 - share)))
+        ext[margin : margin + rows, :] = d_act * d_convs[at, :].astype(f32)
         ext[margin + rows :, :] = jnp.zeros((8, ext.shape[1]), f32)
         taps = conv_w.shape[0]
         total = None
@@ -695,19 +702,21 @@
     got = transpose_over(payload, beside)
     (summary,) = call(group_kernel, [((COUNT // SIDE, 72, state), bf16)], (got,), vmem=16 * 2**20)
     summaries = transpose_over(summary, across)
-    mixed, d_driven, d_bc, d_cumul, normal_t, halo_t = call(
+    inner_values = call(
         intra_kernel,
-        [
-            ((both_rows, inner), bf16),
-            ((both_rows, inner), bf16),
+        [((both_rows, inner), bf16)] * 7
+        + [
+            ((both_rows, channels), bf16),
+            ((both_rows, 2 * state), bf16),
             ((both_rows, 2 * state), f32),
-            ((both_rows, heads), f32),
+            ((both_rows, 2 * heads), f32),
             ((width, both_rows), bf16),
             ((width, 32), bf16),
         ],
-        (conv, gate, d_gated, step, cumul, cumul_t, normal, normal_halo),
+        (conv, gate, d_gated, step, cumul, cumul_t, normal, normal_halo, skip_gain),
         flops=8 * 10**9,
     )
+    normal_t, halo_t = inner_values[-2:]
     groups = COUNT // SIDE
     (scanned,) = call(
         scan_kernel,
@@ -733,8 +742,8 @@
         ]
         + slots(eighth, joined, bf16) * 2,
         (
-            place, states, conv, gate, d_gated, raw, step, cumul, mixed, d_driven, d_bc, d_cumul,
-            step_bias, decay_log, skip_gain, conv_weight, cot, normal_t, halo_t,
+            place, states, *inner_values[:-2], raw, step, cumul,
+            step_bias, decay_log, conv_weight, cot, normal_t, halo_t,
         ),
         [
             pltpu.VMEM((rows + 24, channels), f32),

time: 165 us -> 165 us (level)
  transfers between devices with their start and end apart: 21 -> 21, of which waited for: 10 -> 10; matrix products, arithmetic and copies ran while one was open for 0% -> 0% of each run, Pallas kernels for 7% -> 8%
where the time goes in v8:
time: 165 us; the launch traced here: 164 us
  waiting for transfers between devices  46.3 us (28%)
  starting transfers between devices  45.8 us (28%)
  Pallas kernels  35 us (21%)
  blocking collectives  31.9 us (19%)
  local copies, waits for them, and re-layouts  3.06 us (2%)
    pallas_call x11, Pallas kernels, call(): pl.pallas_call(used, out_shape=[jax.ShapeDtypeStruct(shape, kind) for sha...  35 us
    all_to_all x2, blocking collectives, transpose_over(): return lax.all_to_all(parts, 'seq', 0, 0, axis_index_groups=groups)  31.9 us
    ppermute x9, waiting for transfers between devices, exchange(): lax.ppermute(parts[step], 'seq', axis_pairs(stride, step))  13.8 us
    all_to_all x2, waiting for transfers between devices, transpose_over(): return lax.all_to_all(parts, 'seq', 0, 0, axis_index_groups=groups)  13.6 us
    ppermute x1, starting transfers between devices, shards(): high = lax.ppermute(sequence[:16], 'seq', downward)  10.9 us
    ppermute x9, starting transfers between devices, exchange(): lax.ppermute(parts[step], 'seq', axis_pairs(stride, step))  10.8 us
    all_to_all x2, starting transfers between devices, transpose_over(): return lax.all_to_all(parts, 'seq', 0, 0, axis_index_groups=groups)  9.47 us
    ppermute x1, waiting for transfers between devices, shards(): low = lax.ppermute(sequence[rows - 16:], 'seq', upward)  8.8 us
  transfers between devices with their start and end apart: 21, of which 10 were waited for; matrix products, arithmetic and copies ran while one was open for 0% of the time, Pallas kernels for 8%

profile of v8, /device:TPU:6, one launch (start us, length us, event | category | flops | bytes accessed | tf_op | source)
XLA Modules:
  0.0 163.6 jit_solution(3025974690924808722)
XLA Ops:
  0.6 0.7 fusion
  1.4 10.9 %collective-permute-start.1 = (bf16[16,512]{1,0:T(8,128)(2,1)S(1)}, bf16[16,512]{1,0:T(8,128)(2,1)S(1)}, u32[]{:S(2)}, u32[]{:S(2)}) collective-permute-start(bf16[16,512]{1,0:T(8,128)(2,1)S(1)} %get-tuple-element.130), channel_id=1, source_target_pairs={{4,0},{8,4},{12,8},{16,12},{20,16},{24,20},{28,24},{32,28},{36,32}... | collective-permute-start | bytes 49160 | tf_op jit(solution)/shard_map/ppermute | solution.py:678
  12.3 1.9 %collective-permute-start = (bf16[16,512]{1,0:T(8,128)(2,1)S(1)}, bf16[16,512]{1,0:T(8,128)(2,1)S(1)}, u32[]{:S(2)}, u32[]{:S(2)}) collective-permute-start(bf16[16,512]{1,0:T(8,128)(2,1)S(1)} %get-tuple-element.131), channel_id=1, source_target_pairs={{0,4},{4,8},{8,12},{12,16},{16,20},{20,24},{24,28},{28,32},{32,36}... | collective-permute-start | bytes 49160 | tf_op jit(solution)/shard_map/ppermute | solution.py:677
  14.2 0.0 collective-permute-done.1.refs_3_.refs_10_
  14.2 8.8 %collective-permute-done.refs_2_.refs_9_ = bf16[16,512]{1,0:T(8,128)(2,1)S(1)} collective-permute-done((bf16[16,512]{1,0:T(8,128)(2,1)S(1)}, bf16[16,512]{1,0:T(8,128)(2,1)S(1)}, u32[]{:S(2)}, u32[]{:S(2)}) %collective-permute-start) | collective-permute-done | bytes 16416 | tf_op jit(solution)/shard_map/ppermute | solution.py:677
  23.0 0.0 copy-done.8
  23.0 0.6 copy-done.9
  23.6 7.0 %shard_map.138 = (bf16[4,1040,128]{2,1,0:T(8,128)(2,1)}, bf16[256,512]{1,0:T(8,128)(2,1)}, bf16[256,512]{1,0:T(8,128)(2,1)}, bf16[32,512]{1,0:T(8,128)(2,1)}, bf...) custom-call(bf16[128,512]{1,0:T(8,128)(2,1)} %refs_0_.1, ...), custom_call_target="tpu_custom_call" | custom-call | flops 1000000000 | bytes 3746944 | tf_op jit(solution)/shard_map/pallas_call | solution.py:28
  30.6 17.6 %all_to_all.20.refs_0_ = bf16[4,1040,128]{2,1,0:T(8,128)(2,1)S(1)} all-to-all(bf16[4,1040,128]{2,1,0:T(8,128)(2,1)} %get-tuple-element.68), channel_id=1, replica_groups={{0,4,8,12},{16,20,24,28},{32,36,40,44},{48,52,56,60},{64,68,72,76},{80,..., dimensions={0} | all-to-all | bytes 2129920 | tf_op jit(solution)/shard_map/all_to_all | solution.py:644
  48.3 0.4 shard_map.139
  48.6 14.2 %all_to_all.21.refs_0_ = bf16[16,72,128]{2,1,0:T(8,128)(2,1)S(1)} all-to-all(bf16[16,72,128]{2,1,0:T(8,128)(2,1)S(1)} %shard_map.139), channel_id=1, replica_groups={{0,16,32,48,64,80,96,112,128,144,160,176,192,208,224,240},{4,20,36,52,6..., dimensions={0} | all-to-all | bytes 589824 | tf_op jit(solution)/shard_map/all_to_all | solution.py:644
  62.9 1.6 shard_map.140
  64.5 5.8 %all-to-all-start.2 = ((bf16[16,64,128]{2,1,0:T(8,128)(2,1)}), bf16[16,64,128]{2,1,0:T(8,128)(2,1)S(1)}, u32[]{:S(2)}, u32[]{:S(2)}) async-start(bf16[16,64,128]{2,1,0:T(8,128)(2,1)} %shard_map.140), calls=%async_computation.2 | async-start | bytes 524288 | tf_op jit(solution)/shard_map/all_to_all | solution.py:644
  70.2 9.8 %all-to-all-done.2.refs_1_ = bf16[16,64,128]{2,1,0:T(8,128)(2,1)S(1)} async-done(((bf16[16,64,128]{2,1,0:T(8,128)(2,1)}), bf16[16,64,128]{2,1,0:T(8,128)(2,1)S(1)}, u32[]{:S(2)}, u32[]{:S(2)}) %all-to-all-start.2) | async-done | bytes 262176 | tf_op jit(solution)/shard_map/all_to_all | solution.py:644
  80.0 1.3 shard_map.141
  81.3 3.7 %all-to-all-start.3 = ((bf16[4,1024,128]{2,1,0:T(8,128)(2,1)}), bf16[4,1024,128]{2,1,0:T(8,128)(2,1)S(1)}, u32[]{:S(2)}, u32[]{:S(2)}) async-start(bf16[4,1024,128]{2,1,0:T(8,128)(2,1)} %shard_map.141), calls=%async_computation.3 | async-start | bytes 2097152 | tf_op jit(solution)/shard_map/all_to_all | solution.py:644
  85.0 0.7 pad_add_fusion.refs_0_
  85.7 6.2 %shard_map.142 = (bf16[256,1024]{1,0:T(8,128)(2,1)}, bf16[256,1024]{1,0:T(8,128)(2,1)}, bf16[256,1024]{1,0:T(8,128)(2,1)}, bf16[256,1024]{1,0:T(8,128)(2,1)}, bf...) custom-call(bf16[256,1280]{1,0:T(8,128)(2,1)} %get-tuple-element.69., ...), custom_call_target="tpu_custom_call" | custom-call | flops 8000000000 | bytes 2048064 | tf_op jit(solution)/shard_map/pallas_call | solution.py:28
  91.9 3.8 %all-to-all-done.3.refs_1_ = bf16[4,1024,128]{2,1,0:T(8,128)(2,1)S(1)} async-done(((bf16[4,1024,128]{2,1,0:T(8,128)(2,1)}), bf16[4,1024,128]{2,1,0:T(8,128)(2,1)S(1)}, u32[]{:S(2)}, u32[]{:S(2)}) %all-to-all-start.3) | async-done | bytes 1048608 | tf_op jit(solution)/shard_map/all_to_all | solution.py:644
  95.7 1.0 copy-done.7
  96.7 9.4 %shard_map.143 = (bf16[256,1024]{1,0:T(8,128)(2,1)}, bf16[256,1024]{1,0:T(8,128)(2,1)}, bf16[256,1280]{1,0:T(8,128)(2,1)}, f32[8,1280]{1,0:T(8,128)}, f32[8,1280...) custom-call(s32[3]{0:T(128)} %pad_add_fusion.refs_0_, ...), custom_call_target="tpu_custom_call" | custom-call | flops 1000000000 | bytes 6426764 | tf_op jit(solution)/shard_map/pallas_call | solution.py:28
  106.2 2.5 %collective-permute-start.2 = (bf16[128,1664]{1,0:T(8,128)(2,1)}, bf16[128,1664]{1,0:T(8,128)(2,1)S(1)}, u32[]{:S(2)}, u32[]{:S(2)}) collective-permute-start(bf16[128,1664]{1,0:T(8,128)(2,1)} %get-tuple-element.100), channel_id=1, source_target_pairs={{0,64},{4,68},{8,72},{12,76},{16,80},{20,84},{24,88},{28,92},{32,9... | collective-permute-start | bytes 1277960 | tf_op jit(solution)/shard_map/ppermute | solution.py:638
  108.6 0.0 collective-permute-start.3
  108.6 0.6 collective-permute-start.4
  109.2 2.7 %collective-permute-start.5 = (bf16[128,1664]{1,0:T(8,128)(2,1)}, bf16[128,1664]{1,0:T(8,128)(2,1)S(1)}, u32[]{:S(2)}, u32[]{:S(2)}) collective-permute-start(bf16[128,1664]{1,0:T(8,128)(2,1)} %get-tuple-element.105), channel_id=1, source_target_pairs={{0,12},{4,0},{8,4},{12,8},{16,28},{20,16},{24,20},{28,24},{32,44},... | collective-permute-start | bytes 1277960 | tf_op jit(solution)/shard_map/ppermute | solution.py:639
  111.9 6.4 %shard_map.144 = (bf16[128,512]{1,0:T(8,128)(2,1)}, f32[128,512]{1,0:T(8,128)}, bf16[64,128]{1,0:T(8,128)(2,1)}) custom-call(s32[3]{0:T(128)} %pad_add_fusion.refs_0_, bf16[256,512]{1,0:T(8,128)(2,1)} %get-tuple-element.67.refs_1_, f32[512]{0:T(512)} %refs_2_.1, bf16[256,1024]{1,0:T(8,128)(2,1)} %get-tuple-element.92.refs_3_, bf16[1024,512]{1,0:T(8,128)(2,1)} %refs_4_.3, ...), custom_call_target="tpu_custom_call" | custom-call | flops 8000000000 | bytes 5515276 | tf_op jit(solution)/shard_map/pallas_call | solution.py:28
  118.3 0.0 collective-permute-done.2.refs_1_.refs_2_
  118.3 0.0 collective-permute-done.3.refs_2_.refs_3_
  118.3 1.9 %collective-permute-done.4.refs_4_.refs_7_ = bf16[128,1664]{1,0:T(8,128)(2,1)S(1)} collective-permute-done((bf16[128,1664]{1,0:T(8,128)(2,1)}, bf16[128,1664]{1,0:T(8,128)(2,1)S(1)}, u32[]{:S(2)}, u32[]{:S(2)}) %collective-permute-start.4) | collective-permute-done | bytes 426016 | tf_op jit(solution)/shard_map/ppermute | solution.py:638
  120.2 0.0 collective-permute-done.5.refs_5_.refs_8_
  120.2 0.0 copy-start.6
  120.2 0.7 copy-done.6
  121.0 0.2 shard_map.145
  121.2 0.1 collective-permute-start.8
  121.3 3.6 %collective-permute-start.9 = (bf16[64,1792]{1,0:T(8,128)(2,1)S(1)}, bf16[64,1792]{1,0:T(8,128)(2,1)S(1)}, u32[]{:S(2)}, u32[]{:S(2)}) collective-permute-start(bf16[64,1792]{1,0:T(8,128)(2,1)S(1)} %get-tuple-element.111), channel_id=1, source_target_pairs={{0,12},{4,0},{8,4},{12,8},{16,28},{20,16},{24,20},{28,24},{32,44},... | collective-permute-start | bytes 688136 | tf_op jit(solution)/shard_map/ppermute | solution.py:639
  124.8 3.4 %collective-permute-start.6 = (bf16[64,1664]{1,0:T(8,128)(2,1)S(1)}, bf16[64,1664]{1,0:T(8,128)(2,1)S(1)}, u32[]{:S(2)}, u32[]{:S(2)}) collective-permute-start(bf16[64,1664]{1,0:T(8,128)(2,1)S(1)} %get-tuple-element.107), channel_id=1, source_target_pairs={{0,64},{4,68},{8,72},{12,76},{16,80},{20,84},{24,88},{28,92},{32,9... | collective-permute-start | bytes 638984 | tf_op jit(solution)/shard_map/ppermute | solution.py:638
  128.2 0.0 collective-permute-start.7
  128.2 3.4 %collective-permute-done.6.refs_4_ = bf16[64,1664]{1,0:T(8,128)(2,1)S(1)} collective-permute-done((bf16[64,1664]{1,0:T(8,128)(2,1)S(1)}, bf16[64,1664]{1,0:T(8,128)(2,1)S(1)}, u32[]{:S(2)}, u32[]{:S(2)}) %collective-permute-start.6) | collective-permute-done | bytes 213024 | tf_op jit(solution)/shard_map/ppermute | solution.py:638
  131.6 4.8 %collective-permute-done.7.refs_5_ = bf16[64,1664]{1,0:T(8,128)(2,1)S(1)} collective-permute-done((bf16[64,1664]{1,0:T(8,128)(2,1)S(1)}, bf16[64,1664]{1,0:T(8,128)(2,1)S(1)}, u32[]{:S(2)}, u32[]{:S(2)}) %collective-permute-start.7) | collective-permute-done | bytes 213024 | tf_op jit(solution)/shard_map/ppermute | solution.py:639
  136.4 0.0 collective-permute-done.8.refs_9_
  136.4 0.0 collective-permute-done.9.refs_10_
  136.4 0.0 copy-done.1
  136.4 0.0 copy-done.2
  136.5 1.1 shard_map.146
  137.5 0.1 collective-permute-start.10
  137.6 0.1 collective-permute-start.13
  137.7 2.0 %collective-permute-start.15 = (bf16[32,1792]{1,0:T(8,128)(2,1)S(1)}, bf16[32,1792]{1,0:T(8,128)(2,1)S(1)}, u32[]{:S(2)}, u32[]{:S(2)}) collective-permute-start(bf16[32,1792]{1,0:T(8,128)(2,1)S(1)} %get-tuple-element.119), channel_id=1, source_target_pairs={{0,192},{4,196},{8,200},{12,204},{16,208},{20,212},{24,216},{28,22... | collective-permute-start | bytes 344072 | tf_op jit(solution)/shard_map/ppermute | solution.py:633
  139.7 3.3 %collective-permute-start.11 = (bf16[32,1664]{1,0:T(8,128)(2,1)S(1)}, bf16[32,1664]{1,0:T(8,128)(2,1)S(1)}, u32[]{:S(2)}, u32[]{:S(2)}) collective-permute-start(bf16[32,1664]{1,0:T(8,128)(2,1)S(1)} %get-tuple-element.114), channel_id=1, source_target_pairs={{0,8},{4,12},{8,0},{12,4},{16,24},{20,28},{24,16},{28,20},{32,40},... | collective-permute-start | bytes 319496 | tf_op jit(solution)/shard_map/ppermute | solution.py:633
  143.0 0.6 collective-permute-start.12
  143.6 0.0 collective-permute-done.10.refs_2_
  143.6 0.0 collective-permute-start.14
  143.6 2.3 %collective-permute-done.11.refs_3_ = bf16[32,1664]{1,0:T(8,128)(2,1)S(1)} collective-permute-done((bf16[32,1664]{1,0:T(8,128)(2,1)S(1)}, bf16[32,1664]{1,0:T(8,128)(2,1)S(1)}, u32[]{:S(2)}, u32[]{:S(2)}) %collective-permute-start.11) | collective-permute-done | bytes 106528 | tf_op jit(solution)/shard_map/ppermute | solution.py:633
  145.9 1.8 %collective-permute-done.12.refs_4_ = bf16[32,1664]{1,0:T(8,128)(2,1)S(1)} collective-permute-done((bf16[32,1664]{1,0:T(8,128)(2,1)S(1)}, bf16[32,1664]{1,0:T(8,128)(2,1)S(1)}, u32[]{:S(2)}, u32[]{:S(2)}) %collective-permute-start.12) | collective-permute-done | bytes 106528 | tf_op jit(solution)/shard_map/ppermute | solution.py:633
  147.7 2.1 %collective-permute-done.14.refs_7_ = bf16[32,1664]{1,0:T(8,128)(2,1)S(1)} collective-permute-done((bf16[32,1664]{1,0:T(8,128)(2,1)S(1)}, bf16[32,1664]{1,0:T(8,128)(2,1)S(1)}, u32[]{:S(2)}, u32[]{:S(2)}) %collective-permute-start.14) | collective-permute-done | bytes 106528 | tf_op jit(solution)/shard_map/ppermute | solution.py:633
  149.9 0.0 collective-permute-done.13.refs_6_
  149.9 0.0 collective-permute-done.15.refs_8_
  149.9 0.7 shard_map.147
  150.6 0.1 collective-permute-start.16
  150.7 4.1 %collective-permute-start.18 = (bf16[16,1920]{1,0:T(8,128)(2,1)S(1)}, bf16[16,1920]{1,0:T(8,128)(2,1)S(1)}, u32[]{:S(2)}, u32[]{:S(2)}) collective-permute-start(bf16[16,1920]{1,0:T(8,128)(2,1)S(1)} %get-tuple-element.124), channel_id=1, source_target_pairs={{0,48},{4,52},{8,56},{12,60},{16,0},{20,4},{24,8},{28,12},{32,16},... | collective-permute-start | bytes 184328 | tf_op jit(solution)/shard_map/ppermute | solution.py:633
  154.8 0.5 collective-permute-start.17
  155.2 7.6 %collective-permute-done.17.refs_2_ = bf16[16,1664]{1,0:T(8,128)(2,1)S(1)} collective-permute-done((bf16[16,1664]{1,0:T(8,128)(2,1)S(1)}, bf16[16,1664]{1,0:T(8,128)(2,1)S(1)}, u32[]{:S(2)}, u32[]{:S(2)}) %collective-permute-start.17) | collective-permute-done | bytes 53280 | tf_op jit(solution)/shard_map/ppermute | solution.py:633
  162.8 0.0 collective-permute-done.16.refs_1_
  162.9 0.0 collective-permute-done.18.refs_3_
  162.9 0.7 shard_map.148
  (13 shorter events, 0.0 us)
Async XLA Ops:
  1.4 12.9 %collective-permute-start.1 = (bf16[16,512]{1,0:T(8,128)(2,1)S(1)}, bf16[16,512]{1,0:T(8,128)(2,1)S(1)}, u32[]{:S(2)}, u32[]{:S(2)}) collective-permute-start(bf16[16,512]{1,0:T(8,128)(2,1)S(1)} %get-tuple-element.130), channel_id=1, source_target_pairs={{4,0},{8,4},{12,8},{16,12},{20,16},{24,20},{28,24},{32,28},{36,32}... | collective-permute-start | bytes 49160 | tf_op jit(solution)/shard_map/ppermute | solution.py:678
  12.3 10.8 %collective-permute-start = (bf16[16,512]{1,0:T(8,128)(2,1)S(1)}, bf16[16,512]{1,0:T(8,128)(2,1)S(1)}, u32[]{:S(2)}, u32[]{:S(2)}) collective-permute-start(bf16[16,512]{1,0:T(8,128)(2,1)S(1)} %get-tuple-element.131), channel_id=1, source_target_pairs={{0,4},{4,8},{8,12},{12,16},{16,20},{20,24},{24,28},{28,32},{32,36}... | collective-permute-start | bytes 49160 | tf_op jit(solution)/shard_map/ppermute | solution.py:677
  14.2 8.8 %copy-start.8 = (bf16[16,512]{1,0:T(8,128)(2,1)}, bf16[16,512]{1,0:T(8,128)(2,1)S(1)}, u32[]{:S(2)}) copy-start(bf16[16,512]{1,0:T(8,128)(2,1)S(1)} %collective-permute-done.1.refs_3_.refs_10_) | copy-start | bytes 49156
  23.0 0.6 copy-start.9
  64.5 15.5 %all-to-all-start.2 = ((bf16[16,64,128]{2,1,0:T(8,128)(2,1)}), bf16[16,64,128]{2,1,0:T(8,128)(2,1)S(1)}, u32[]{:S(2)}, u32[]{:S(2)}) async-start(bf16[16,64,128]{2,1,0:T(8,128)(2,1)} %shard_map.140), calls=%async_computation.2 | async-start | bytes 524288 | tf_op jit(solution)/shard_map/all_to_all | solution.py:644
  81.3 14.4 %all-to-all-start.3 = ((bf16[4,1024,128]{2,1,0:T(8,128)(2,1)}), bf16[4,1024,128]{2,1,0:T(8,128)(2,1)S(1)}, u32[]{:S(2)}, u32[]{:S(2)}) async-start(bf16[4,1024,128]{2,1,0:T(8,128)(2,1)} %shard_map.141), calls=%async_computation.3 | async-start | bytes 2097152 | tf_op jit(solution)/shard_map/all_to_all | solution.py:644
  95.7 1.0 copy-start.7
  106.2 12.1 %collective-permute-start.2 = (bf16[128,1664]{1,0:T(8,128)(2,1)}, bf16[128,1664]{1,0:T(8,128)(2,1)S(1)}, u32[]{:S(2)}, u32[]{:S(2)}) collective-permute-start(bf16[128,1664]{1,0:T(8,128)(2,1)} %get-tuple-element.100), channel_id=1, source_target_pairs={{0,64},{4,68},{8,72},{12,76},{16,80},{20,84},{24,88},{28,92},{32,9... | collective-permute-start | bytes 1277960 | tf_op jit(solution)/shard_map/ppermute | solution.py:638
  108.6 9.7 %collective-permute-start.3 = (bf16[128,1664]{1,0:T(8,128)(2,1)}, bf16[128,1664]{1,0:T(8,128)(2,1)S(1)}, u32[]{:S(2)}, u32[]{:S(2)}) collective-permute-start(bf16[128,1664]{1,0:T(8,128)(2,1)} %get-tuple-element.101), channel_id=1, source_target_pairs={{0,192},{4,196},{8,200},{12,204},{16,208},{20,212},{24,216},{28,22... | collective-permute-start | bytes 1277960 | tf_op jit(solution)/shard_map/ppermute | solution.py:639
  108.6 11.6 %collective-permute-start.4 = (bf16[128,1664]{1,0:T(8,128)(2,1)}, bf16[128,1664]{1,0:T(8,128)(2,1)S(1)}, u32[]{:S(2)}, u32[]{:S(2)}) collective-permute-start(bf16[128,1664]{1,0:T(8,128)(2,1)} %get-tuple-element.104), channel_id=1, source_target_pairs={{0,4},{4,8},{8,12},{12,0},{16,20},{20,24},{24,28},{28,16},{32,36},... | collective-permute-start | bytes 1277960 | tf_op jit(solution)/shard_map/ppermute | solution.py:638
  109.2 11.0 %collective-permute-start.5 = (bf16[128,1664]{1,0:T(8,128)(2,1)}, bf16[128,1664]{1,0:T(8,128)(2,1)S(1)}, u32[]{:S(2)}, u32[]{:S(2)}) collective-permute-start(bf16[128,1664]{1,0:T(8,128)(2,1)} %get-tuple-element.105), channel_id=1, source_target_pairs={{0,12},{4,0},{8,4},{12,8},{16,28},{20,16},{24,20},{28,24},{32,44},... | collective-permute-start | bytes 1277960 | tf_op jit(solution)/shard_map/ppermute | solution.py:639
  111.9 8.3 %copy-start.3 = (bf16[128,1664]{1,0:T(8,128)(2,1)S(1)}, bf16[128,1664]{1,0:T(8,128)(2,1)}, u32[]{:S(2)}) copy-start(bf16[128,1664]{1,0:T(8,128)(2,1)} %get-tuple-element.102.refs_0_) | copy-start | bytes 1277956
  111.9 8.3 %copy-start.4 = (bf16[128,1664]{1,0:T(8,128)(2,1)S(1)}, bf16[128,1664]{1,0:T(8,128)(2,1)}, u32[]{:S(2)}) copy-start(bf16[128,1664]{1,0:T(8,128)(2,1)} %get-tuple-element.103.refs_3_) | copy-start | bytes 1277956
  120.2 0.7 copy-start.6
  121.0 15.5 %copy-start = (s32[3]{0:T(128)S(1)}, s32[3]{0:T(128)}, u32[]{:S(2)}) copy-start(s32[3]{0:T(128)} %pad_add_fusion.refs_0_) | copy-start | bytes 40
  121.0 15.5 %copy-start.1 = (bf16[128,1664]{1,0:T(8,128)(2,1)S(1)}, bf16[128,1664]{1,0:T(8,128)(2,1)}, u32[]{:S(2)}) copy-start(bf16[128,1664]{1,0:T(8,128)(2,1)} %get-tuple-element.99.refs_1_) | copy-start | bytes 1277956
  121.0 15.5 %copy-start.2 = (bf16[128,1664]{1,0:T(8,128)(2,1)S(1)}, bf16[128,1664]{1,0:T(8,128)(2,1)}, u32[]{:S(2)}) copy-start(bf16[128,1664]{1,0:T(8,128)(2,1)} %get-tuple-element.109.refs_6_) | copy-start | bytes 1277956
  121.2 15.3 %collective-permute-start.8 = (bf16[64,1792]{1,0:T(8,128)(2,1)S(1)}, bf16[64,1792]{1,0:T(8,128)(2,1)S(1)}, u32[]{:S(2)}, u32[]{:S(2)}) collective-permute-start(bf16[64,1792]{1,0:T(8,128)(2,1)S(1)} %get-tuple-element.110), channel_id=1, source_target_pairs={{0,4},{4,8},{8,12},{12,0},{16,20},{20,24},{24,28},{28,16},{32,36},... | collective-permute-start | bytes 688136 | tf_op jit(solution)/shard_map/ppermute | solution.py:638
  121.3 15.2 %collective-permute-start.9 = (bf16[64,1792]{1,0:T(8,128)(2,1)S(1)}, bf16[64,1792]{1,0:T(8,128)(2,1)S(1)}, u32[]{:S(2)}, u32[]{:S(2)}) collective-permute-start(bf16[64,1792]{1,0:T(8,128)(2,1)S(1)} %get-tuple-element.111), channel_id=1, source_target_pairs={{0,12},{4,0},{8,4},{12,8},{16,28},{20,16},{24,20},{28,24},{32,44},... | collective-permute-start | bytes 688136 | tf_op jit(solution)/shard_map/ppermute | solution.py:639
  124.8 6.7 %collective-permute-start.6 = (bf16[64,1664]{1,0:T(8,128)(2,1)S(1)}, bf16[64,1664]{1,0:T(8,128)(2,1)S(1)}, u32[]{:S(2)}, u32[]{:S(2)}) collective-permute-start(bf16[64,1664]{1,0:T(8,128)(2,1)S(1)} %get-tuple-element.107), channel_id=1, source_target_pairs={{0,64},{4,68},{8,72},{12,76},{16,80},{20,84},{24,88},{28,92},{32,9... | collective-permute-start | bytes 638984 | tf_op jit(solution)/shard_map/ppermute | solution.py:638
  128.2 8.2 %collective-permute-start.7 = (bf16[64,1664]{1,0:T(8,128)(2,1)S(1)}, bf16[64,1664]{1,0:T(8,128)(2,1)S(1)}, u32[]{:S(2)}, u32[]{:S(2)}) collective-permute-start(bf16[64,1664]{1,0:T(8,128)(2,1)S(1)} %get-tuple-element.108), channel_id=1, source_target_pairs={{0,192},{4,196},{8,200},{12,204},{16,208},{20,212},{24,216},{28,22... | collective-permute-start | bytes 638984 | tf_op jit(solution)/shard_map/ppermute | solution.py:639
  137.5 6.1 %collective-permute-start.10 = (bf16[32,1664]{1,0:T(8,128)(2,1)S(1)}, bf16[32,1664]{1,0:T(8,128)(2,1)S(1)}, u32[]{:S(2)}, u32[]{:S(2)}) collective-permute-start(bf16[32,1664]{1,0:T(8,128)(2,1)S(1)} %get-tuple-element.113), channel_id=1, source_target_pairs={{0,4},{4,8},{8,12},{12,0},{16,20},{20,24},{24,28},{28,16},{32,36},... | collective-permute-start | bytes 319496 | tf_op jit(solution)/shard_map/ppermute | solution.py:633
  137.6 12.2 %collective-permute-start.13 = (bf16[32,1792]{1,0:T(8,128)(2,1)S(1)}, bf16[32,1792]{1,0:T(8,128)(2,1)S(1)}, u32[]{:S(2)}, u32[]{:S(2)}) collective-permute-start(bf16[32,1792]{1,0:T(8,128)(2,1)S(1)} %get-tuple-element.117), channel_id=1, source_target_pairs={{0,64},{4,68},{8,72},{12,76},{16,80},{20,84},{24,88},{28,92},{32,9... | collective-permute-start | bytes 344072 | tf_op jit(solution)/shard_map/ppermute | solution.py:633
  137.7 12.1 %collective-permute-start.15 = (bf16[32,1792]{1,0:T(8,128)(2,1)S(1)}, bf16[32,1792]{1,0:T(8,128)(2,1)S(1)}, u32[]{:S(2)}, u32[]{:S(2)}) collective-permute-start(bf16[32,1792]{1,0:T(8,128)(2,1)S(1)} %get-tuple-element.119), channel_id=1, source_target_pairs={{0,192},{4,196},{8,200},{12,204},{16,208},{20,212},{24,216},{28,22... | collective-permute-start | bytes 344072 | tf_op jit(solution)/shard_map/ppermute | solution.py:633
  139.7 6.2 %collective-permute-start.11 = (bf16[32,1664]{1,0:T(8,128)(2,1)S(1)}, bf16[32,1664]{1,0:T(8,128)(2,1)S(1)}, u32[]{:S(2)}, u32[]{:S(2)}) collective-permute-start(bf16[32,1664]{1,0:T(8,128)(2,1)S(1)} %get-tuple-element.114), channel_id=1, source_target_pairs={{0,8},{4,12},{8,0},{12,4},{16,24},{20,28},{24,16},{28,20},{32,40},... | collective-permute-start | bytes 319496 | tf_op jit(solution)/shard_map/ppermute | solution.py:633
  143.0 4.7 %collective-permute-start.12 = (bf16[32,1664]{1,0:T(8,128)(2,1)S(1)}, bf16[32,1664]{1,0:T(8,128)(2,1)S(1)}, u32[]{:S(2)}, u32[]{:S(2)}) collective-permute-start(bf16[32,1664]{1,0:T(8,128)(2,1)S(1)} %get-tuple-element.115), channel_id=1, source_target_pairs={{0,12},{4,0},{8,4},{12,8},{16,28},{20,16},{24,20},{28,24},{32,44},... | collective-permute-start | bytes 319496 | tf_op jit(solution)/shard_map/ppermute | solution.py:633
  143.6 6.2 %collective-permute-start.14 = (bf16[32,1664]{1,0:T(8,128)(2,1)S(1)}, bf16[32,1664]{1,0:T(8,128)(2,1)S(1)}, u32[]{:S(2)}, u32[]{:S(2)}) collective-permute-start(bf16[32,1664]{1,0:T(8,128)(2,1)S(1)} %get-tuple-element.118), channel_id=1, source_target_pairs={{0,128},{4,132},{8,136},{12,140},{16,144},{20,148},{24,152},{28,15... | collective-permute-start | bytes 319496 | tf_op jit(solution)/shard_map/ppermute | solution.py:633
  149.9 13.0 %copy-start.5 = (f32[128,512]{1,0:T(8,128)S(1)}, f32[128,512]{1,0:T(8,128)}, u32[]{:S(2)}) copy-start(f32[128,512]{1,0:T(8,128)} %get-tuple-element.126.refs_5_) | copy-start | bytes 786436
  150.6 12.3 %collective-permute-start.16 = (bf16[16,1920]{1,0:T(8,128)(2,1)S(1)}, bf16[16,1920]{1,0:T(8,128)(2,1)S(1)}, u32[]{:S(2)}, u32[]{:S(2)}) collective-permute-start(bf16[16,1920]{1,0:T(8,128)(2,1)S(1)} %get-tuple-element.122), channel_id=1, source_target_pairs={{0,16},{4,20},{8,24},{12,28},{16,32},{20,36},{24,40},{28,44},{32,4... | collective-permute-start | bytes 184328 | tf_op jit(solution)/shard_map/ppermute | solution.py:633
  150.7 12.2 %collective-permute-start.18 = (bf16[16,1920]{1,0:T(8,128)(2,1)S(1)}, bf16[16,1920]{1,0:T(8,128)(2,1)S(1)}, u32[]{:S(2)}, u32[]{:S(2)}) collective-permute-start(bf16[16,1920]{1,0:T(8,128)(2,1)S(1)} %get-tuple-element.124), channel_id=1, source_target_pairs={{0,48},{4,52},{8,56},{12,60},{16,0},{20,4},{24,8},{28,12},{32,16},... | collective-permute-start | bytes 184328 | tf_op jit(solution)/shard_map/ppermute | solution.py:633
  154.8 8.1 %collective-permute-start.17 = (bf16[16,1664]{1,0:T(8,128)(2,1)S(1)}, bf16[16,1664]{1,0:T(8,128)(2,1)S(1)}, u32[]{:S(2)}, u32[]{:S(2)}) collective-permute-start(bf16[16,1664]{1,0:T(8,128)(2,1)S(1)} %get-tuple-element.123), channel_id=1, source_target_pairs={{0,32},{4,36},{8,40},{12,44},{16,48},{20,52},{24,56},{28,60},{32,0... | collective-permute-start | bytes 159752 | tf_op jit(solution)/shard_map/ppermute | solution.py:633

commit v9 on v8

--- a/solution.py
+++ b/solution.py
@@ -104,19 +104,15 @@
 
 
 def tri_sum(mask, value):
-    total = None
-    for piece in pieces_of(value, 3):
-        part = mm(ones_where(mask), piece)
-        total = part if total is None else total + part
-    return total
+    width = value.shape[1]
+    total = mm(ones_where(mask), jnp.concatenate(pieces_of(value, 3), axis=1))
+    return total[:, :width] + total[:, width : 2 * width] + total[:, 2 * width :]
 
 
 def tri_sum_turned(mask, value):
-    total = None
-    for piece in pieces_of(value, 3):
-        part = mm_rows(piece, ones_where(mask))
-        total = part if total is None else total + part
-    return total
+    width = value.shape[1]
+    total = mm_rows(jnp.concatenate(pieces_of(value, 3), axis=1), ones_where(mask))
+    return total[:width] + total[width : 2 * width] + total[2 * width :]
 
 
 def softplus(value):
@@ -135,7 +131,7 @@
 
 def pre_kernel(
     seq, up, low, high, gain, in_proj, step_proj, conv_w, conv_b, step_bias, decay_log, out_proj,
-    payload, both, normal, normal_halo, cot, gate, conv, d_gated, raw, step, cumul, cumul_t,
+    payload, both, normal, normal_halo, cot, gate, conv, d_gated, raw, step, cumul,
     ext,
 ):
     rows = seq.shape[0]
@@ -143,11 +139,13 @@
     heads = step_bias.shape[0]
     state = (conv_w.shape[1] - inner) // 2
     taps = conv_w.shape[0]
+    turned = mm(jnp.concatenate([seq[...], up[...], high[...]], axis=0), anti(seq.shape[1])).astype(bf16)
+    flip = anti(rows)
     both[:rows, :] = seq[...]
-    both[rows:, :] = mirror_exact(seq[...])
+    both[rows:, :] = mm(flip, turned[:rows]).astype(bf16)
     cot[:rows, :] = up[...]
-    cot[rows:, :] = mirror_exact(up[...])
-    halo = jnp.concatenate([low[...], mirror_exact(high[...])], axis=0)
+    cot[rows:, :] = mm(flip, turned[rows : 2 * rows]).astype(bf16)
+    halo = jnp.concatenate([low[...], mm(anti(high.shape[0]), turned[2 * rows :]).astype(bf16)], axis=0)
     normal[...] = norm_rows(both[...], gain[...])
     normal_halo[...] = norm_rows(halo, gain[...])
     gate[...] = mm(normal[...], in_proj[:, :inner]).astype(bf16)
@@ -173,7 +171,6 @@
         upto = tri_sum(triangle(rows, True), decay)
         step[at, :] = size
         cumul[at, :] = upto
-        cumul_t[frame * heads : (frame + 1) * heads, :] = tri_sum_turned(triangle(rows, False), decay)
         end = upto[rows - 1 : rows, :]
         ends.append(end)
         spread = expand(jnp.concatenate([size * jnp.exp(end - upto), jnp.exp(upto)], axis=0), mask)
@@ -307,7 +304,7 @@
 
 
 def intra_kernel(
-    conv, gate, d_gated, step, cumul, cumul_t, normal, normal_halo, skip_gain,
+    conv, gate, d_gated, step, cumul, decay_log, normal, normal_halo, skip_gain,
     silus, d_gates, pushed, mixed, d_inputs, lefts, held_back, d_convs, bc, d_bc, sums_out, normal_t, halo_t,
 ):
     for source, target in ((normal, normal_t), (normal_halo, halo_t)):
@@ -348,7 +345,7 @@
         d_mixed = d_out * silu
         pushed[at, :] = (d_mixed * grown).astype(bf16)
         scores = mm_cols(cmat, bmat)
-        line = cumul_t[frame * heads : (frame + 1) * heads, :]
+        line = tri_sum_turned(triangle(rows, False), -jnp.exp(decay_log[...].reshape(1, -1)) * step[at, :])
         d_scores = jnp.zeros((rows, rows), f32)
         sums, by_size = [], []
         for pair in range(heads // 2):
@@ -677,7 +674,7 @@
     low = lax.ppermute(sequence[rows - 16 :], "seq", upward)
     high = lax.ppermute(sequence[:16], "seq", downward)
     step_turned = step_proj.T
-    payload, both, normal, normal_halo, cot, gate, conv, d_gated, raw, step, cumul, cumul_t = call(
+    payload, both, normal, normal_halo, cot, gate, conv, d_gated, raw, step, cumul = call(
         pre_kernel,
         [
             ((SIDE, inner + 16, state), bf16),
@@ -691,7 +688,6 @@
             ((both_rows, heads), f32),
             ((both_rows, heads), f32),
             ((both_rows, heads), f32),
-            ((2 * heads, rows), f32),
         ],
         (
             sequence, upstream, low, high, norm_gain, in_proj, step_turned,
@@ -713,7 +709,7 @@
             ((width, both_rows), bf16),
             ((width, 32), bf16),
         ],
-        (conv, gate, d_gated, step, cumul, cumul_t, normal, normal_halo, skip_gain),
+        (conv, gate, d_gated, step, cumul, decay_log, normal, normal_halo, skip_gain),
         flops=8 * 10**9,
     )
     normal_t, halo_t = inner_values[-2:]

time: 165 us -> 165 us (level)
  no operation moved by 1% of the time
where the time goes in v9:
time: 165 us; the launch traced here: 164 us
  waiting for transfers between devices  46.2 us (28%)
  starting transfers between devices  45.9 us (28%)
  Pallas kernels  35.5 us (22%)
  blocking collectives  31.9 us (19%)
  local copies, waits for them, and re-layouts  3.06 us (2%)
    pallas_call x11, Pallas kernels, call(): pl.pallas_call(used, out_shape=[jax.ShapeDtypeStruct(shape, kind) for sha...  35.5 us
    all_to_all x2, blocking collectives, transpose_over(): return lax.all_to_all(parts, 'seq', 0, 0, axis_index_groups=groups)  31.9 us
    ppermute x9, waiting for transfers between devices, exchange(): lax.ppermute(parts[step], 'seq', axis_pairs(stride, step))  13.8 us
    all_to_all x2, waiting for transfers between devices, transpose_over(): return lax.all_to_all(parts, 'seq', 0, 0, axis_index_groups=groups)  13.5 us
    ppermute x1, starting transfers between devices, shards(): high = lax.ppermute(sequence[:16], 'seq', downward)  10.9 us
    ppermute x9, starting transfers between devices, exchange(): lax.ppermute(parts[step], 'seq', axis_pairs(stride, step))  10.8 us
    all_to_all x2, starting transfers between devices, transpose_over(): return lax.all_to_all(parts, 'seq', 0, 0, axis_index_groups=groups)  9.47 us
    ppermute x1, waiting for transfers between devices, shards(): low = lax.ppermute(sequence[rows - 16:], 'seq', upward)  8.8 us
  transfers between devices with their start and end apart: 21, of which 10 were waited for; matrix products, arithmetic and copies ran while one was open for 0% of the time, Pallas kernels for 8%

profile of v9, /device:TPU:6, one launch (start us, length us, event | category | flops | bytes accessed | tf_op | source)
XLA Modules:
  0.0 164.0 jit_solution(17575481135317309567)
XLA Ops:
  0.6 0.7 fusion
  1.4 10.9 %collective-permute-start.1 = (bf16[16,512]{1,0:T(8,128)(2,1)S(1)}, bf16[16,512]{1,0:T(8,128)(2,1)S(1)}, u32[]{:S(2)}, u32[]{:S(2)}) collective-permute-start(bf16[16,512]{1,0:T(8,128)(2,1)S(1)} %get-tuple-element.128), channel_id=1, source_target_pairs={{4,0},{8,4},{12,8},{16,12},{20,16},{24,20},{28,24},{32,28},{36,32}... | collective-permute-start | bytes 49160 | tf_op jit(solution)/shard_map/ppermute | solution.py:675
  12.3 1.9 %collective-permute-start = (bf16[16,512]{1,0:T(8,128)(2,1)S(1)}, bf16[16,512]{1,0:T(8,128)(2,1)S(1)}, u32[]{:S(2)}, u32[]{:S(2)}) collective-permute-start(bf16[16,512]{1,0:T(8,128)(2,1)S(1)} %get-tuple-element.129), channel_id=1, source_target_pairs={{0,4},{4,8},{8,12},{12,16},{16,20},{20,24},{24,28},{28,32},{32,36}... | collective-permute-start | bytes 49160 | tf_op jit(solution)/shard_map/ppermute | solution.py:674
  14.2 0.0 collective-permute-done.1.refs_3_.refs_10_
  14.2 8.8 %collective-permute-done.refs_2_.refs_9_ = bf16[16,512]{1,0:T(8,128)(2,1)S(1)} collective-permute-done((bf16[16,512]{1,0:T(8,128)(2,1)S(1)}, bf16[16,512]{1,0:T(8,128)(2,1)S(1)}, u32[]{:S(2)}, u32[]{:S(2)}) %collective-permute-start) | collective-permute-done | bytes 16416 | tf_op jit(solution)/shard_map/ppermute | solution.py:674
  23.0 0.0 copy-done.8
  23.0 0.6 copy-done.9
  23.6 7.2 %shard_map.138 = (bf16[4,1040,128]{2,1,0:T(8,128)(2,1)}, bf16[256,512]{1,0:T(8,128)(2,1)}, bf16[256,512]{1,0:T(8,128)(2,1)}, bf16[32,512]{1,0:T(8,128)(2,1)}, bf...) custom-call(bf16[128,512]{1,0:T(8,128)(2,1)} %refs_0_.1, ...), custom_call_target="tpu_custom_call" | custom-call | flops 1000000000 | bytes 3746944 | tf_op jit(solution)/shard_map/pallas_call | solution.py:28
  30.8 17.6 %all_to_all.20.refs_0_ = bf16[4,1040,128]{2,1,0:T(8,128)(2,1)S(1)} all-to-all(bf16[4,1040,128]{2,1,0:T(8,128)(2,1)} %get-tuple-element.67), channel_id=1, replica_groups={{0,4,8,12},{16,20,24,28},{32,36,40,44},{48,52,56,60},{64,68,72,76},{80,..., dimensions={0} | all-to-all | bytes 2129920 | tf_op jit(solution)/shard_map/all_to_all | solution.py:641
  48.5 0.4 shard_map.139
  48.8 14.2 %all_to_all.21.refs_0_ = bf16[16,72,128]{2,1,0:T(8,128)(2,1)S(1)} all-to-all(bf16[16,72,128]{2,1,0:T(8,128)(2,1)S(1)} %shard_map.139), channel_id=1, replica_groups={{0,16,32,48,64,80,96,112,128,144,160,176,192,208,224,240},{4,20,36,52,6..., dimensions={0} | all-to-all | bytes 589824 | tf_op jit(solution)/shard_map/all_to_all | solution.py:641
  63.1 1.6 shard_map.140
  64.7 5.8 %all-to-all-start.2 = ((bf16[16,64,128]{2,1,0:T(8,128)(2,1)}), bf16[16,64,128]{2,1,0:T(8,128)(2,1)S(1)}, u32[]{:S(2)}, u32[]{:S(2)}) async-start(bf16[16,64,128]{2,1,0:T(8,128)(2,1)} %shard_map.140), calls=%async_computation.2 | async-start | bytes 524288 | tf_op jit(solution)/shard_map/all_to_all | solution.py:641
  70.4 9.8 %all-to-all-done.2.refs_1_ = bf16[16,64,128]{2,1,0:T(8,128)(2,1)S(1)} async-done(((bf16[16,64,128]{2,1,0:T(8,128)(2,1)}), bf16[16,64,128]{2,1,0:T(8,128)(2,1)S(1)}, u32[]{:S(2)}, u32[]{:S(2)}) %all-to-all-start.2) | async-done | bytes 262176 | tf_op jit(solution)/shard_map/all_to_all | solution.py:641
  80.2 1.3 shard_map.141
  81.5 3.7 %all-to-all-start.3 = ((bf16[4,1024,128]{2,1,0:T(8,128)(2,1)}), bf16[4,1024,128]{2,1,0:T(8,128)(2,1)S(1)}, u32[]{:S(2)}, u32[]{:S(2)}) async-start(bf16[4,1024,128]{2,1,0:T(8,128)(2,1)} %shard_map.141), calls=%async_computation.3 | async-start | bytes 2097152 | tf_op jit(solution)/shard_map/all_to_all | solution.py:641
  85.2 0.7 pad_add_fusion.refs_0_
  85.9 6.3 %shard_map.142 = (bf16[256,1024]{1,0:T(8,128)(2,1)}, bf16[256,1024]{1,0:T(8,128)(2,1)}, bf16[256,1024]{1,0:T(8,128)(2,1)}, bf16[256,1024]{1,0:T(8,128)(2,1)}, bf...) custom-call(bf16[256,1280]{1,0:T(8,128)(2,1)} %get-tuple-element.68., ...), custom_call_target="tpu_custom_call" | custom-call | flops 8000000000 | bytes 2031744 | tf_op jit(solution)/shard_map/pallas_call | solution.py:28
  92.2 3.7 %all-to-all-done.3.refs_1_ = bf16[4,1024,128]{2,1,0:T(8,128)(2,1)S(1)} async-done(((bf16[4,1024,128]{2,1,0:T(8,128)(2,1)}), bf16[4,1024,128]{2,1,0:T(8,128)(2,1)S(1)}, u32[]{:S(2)}, u32[]{:S(2)}) %all-to-all-start.3) | async-done | bytes 1048608 | tf_op jit(solution)/shard_map/all_to_all | solution.py:641
  95.9 1.0 copy-done.7
  96.9 9.7 %shard_map.143 = (bf16[256,1024]{1,0:T(8,128)(2,1)}, bf16[256,1024]{1,0:T(8,128)(2,1)}, bf16[256,1280]{1,0:T(8,128)(2,1)}, f32[8,1280]{1,0:T(8,128)}, f32[8,1280...) custom-call(s32[3]{0:T(128)} %pad_add_fusion.refs_0_, ...), custom_call_target="tpu_custom_call" | custom-call | flops 1000000000 | bytes 6426764 | tf_op jit(solution)/shard_map/pallas_call | solution.py:28
  106.6 2.5 %collective-permute-start.2 = (bf16[128,1664]{1,0:T(8,128)(2,1)}, bf16[128,1664]{1,0:T(8,128)(2,1)S(1)}, u32[]{:S(2)}, u32[]{:S(2)}) collective-permute-start(bf16[128,1664]{1,0:T(8,128)(2,1)} %get-tuple-element.98), channel_id=1, source_target_pairs={{0,64},{4,68},{8,72},{12,76},{16,80},{20,84},{24,88},{28,92},{32,9... | collective-permute-start | bytes 1277960 | tf_op jit(solution)/shard_map/ppermute | solution.py:635
  109.0 0.0 collective-permute-start.3
  109.0 0.6 collective-permute-start.4
  109.6 2.7 %collective-permute-start.5 = (bf16[128,1664]{1,0:T(8,128)(2,1)}, bf16[128,1664]{1,0:T(8,128)(2,1)S(1)}, u32[]{:S(2)}, u32[]{:S(2)}) collective-permute-start(bf16[128,1664]{1,0:T(8,128)(2,1)} %get-tuple-element.103), channel_id=1, source_target_pairs={{0,12},{4,0},{8,4},{12,8},{16,28},{20,16},{24,20},{28,24},{32,44},... | collective-permute-start | bytes 1277960 | tf_op jit(solution)/shard_map/ppermute | solution.py:636
  112.3 6.4 %shard_map.144 = (bf16[128,512]{1,0:T(8,128)(2,1)}, f32[128,512]{1,0:T(8,128)}, bf16[64,128]{1,0:T(8,128)(2,1)}) custom-call(s32[3]{0:T(128)} %pad_add_fusion.refs_0_, bf16[256,512]{1,0:T(8,128)(2,1)} %get-tuple-element.66.refs_1_, f32[512]{0:T(512)} %refs_2_.1, bf16[256,1024]{1,0:T(8,128)(2,1)} %get-tuple-element.90.refs_3_, bf16[1024,512]{1,0:T(8,128)(2,1)} %refs_4_.3, ...), custom_call_target="tpu_custom_call" | custom-call | flops 8000000000 | bytes 5515276 | tf_op jit(solution)/shard_map/pallas_call | solution.py:28
  118.7 0.0 collective-permute-done.2.refs_1_.refs_2_
  118.7 0.0 collective-permute-done.3.refs_2_.refs_3_
  118.7 1.9 %collective-permute-done.4.refs_4_.refs_7_ = bf16[128,1664]{1,0:T(8,128)(2,1)S(1)} collective-permute-done((bf16[128,1664]{1,0:T(8,128)(2,1)}, bf16[128,1664]{1,0:T(8,128)(2,1)S(1)}, u32[]{:S(2)}, u32[]{:S(2)}) %collective-permute-start.4) | collective-permute-done | bytes 426016 | tf_op jit(solution)/shard_map/ppermute | solution.py:635
  120.6 0.0 collective-permute-done.5.refs_5_.refs_8_
  120.6 0.0 copy-done.3
  120.6 0.0 copy-start.6
  120.6 0.7 copy-done.6
  121.3 0.2 shard_map.145
  121.5 0.1 collective-permute-start.8
  121.6 3.6 %collective-permute-start.9 = (bf16[64,1792]{1,0:T(8,128)(2,1)S(1)}, bf16[64,1792]{1,0:T(8,128)(2,1)S(1)}, u32[]{:S(2)}, u32[]{:S(2)}) collective-permute-start(bf16[64,1792]{1,0:T(8,128)(2,1)S(1)} %get-tuple-element.109), channel_id=1, source_target_pairs={{0,12},{4,0},{8,4},{12,8},{16,28},{20,16},{24,20},{28,24},{32,44},... | collective-permute-start | bytes 688136 | tf_op jit(solution)/shard_map/ppermute | solution.py:636
  125.2 3.4 %collective-permute-start.6 = (bf16[64,1664]{1,0:T(8,128)(2,1)S(1)}, bf16[64,1664]{1,0:T(8,128)(2,1)S(1)}, u32[]{:S(2)}, u32[]{:S(2)}) collective-permute-start(bf16[64,1664]{1,0:T(8,128)(2,1)S(1)} %get-tuple-element.105), channel_id=1, source_target_pairs={{0,64},{4,68},{8,72},{12,76},{16,80},{20,84},{24,88},{28,92},{32,9... | collective-permute-start | bytes 638984 | tf_op jit(solution)/shard_map/ppermute | solution.py:635
  128.6 0.0 collective-permute-start.7
  128.6 3.4 %collective-permute-done.6.refs_4_ = bf16[64,1664]{1,0:T(8,128)(2,1)S(1)} collective-permute-done((bf16[64,1664]{1,0:T(8,128)(2,1)S(1)}, bf16[64,1664]{1,0:T(8,128)(2,1)S(1)}, u32[]{:S(2)}, u32[]{:S(2)}) %collective-permute-start.6) | collective-permute-done | bytes 213024 | tf_op jit(solution)/shard_map/ppermute | solution.py:635
  132.0 4.8 %collective-permute-done.7.refs_5_ = bf16[64,1664]{1,0:T(8,128)(2,1)S(1)} collective-permute-done((bf16[64,1664]{1,0:T(8,128)(2,1)S(1)}, bf16[64,1664]{1,0:T(8,128)(2,1)S(1)}, u32[]{:S(2)}, u32[]{:S(2)}) %collective-permute-start.7) | collective-permute-done | bytes 213024 | tf_op jit(solution)/shard_map/ppermute | solution.py:636
  136.8 0.0 collective-permute-done.8.refs_9_
  136.8 0.0 collective-permute-done.9.refs_10_
  136.8 0.0 copy-done
  136.8 1.1 shard_map.146
  137.9 0.1 collective-permute-start.10
  138.0 0.1 collective-permute-start.13
  138.1 2.0 %collective-permute-start.15 = (bf16[32,1792]{1,0:T(8,128)(2,1)S(1)}, bf16[32,1792]{1,0:T(8,128)(2,1)S(1)}, u32[]{:S(2)}, u32[]{:S(2)}) collective-permute-start(bf16[32,1792]{1,0:T(8,128)(2,1)S(1)} %get-tuple-element.117), channel_id=1, source_target_pairs={{0,192},{4,196},{8,200},{12,204},{16,208},{20,212},{24,216},{28,22... | collective-permute-start | bytes 344072 | tf_op jit(solution)/shard_map/ppermute | solution.py:630
  140.1 3.3 %collective-permute-start.11 = (bf16[32,1664]{1,0:T(8,128)(2,1)S(1)}, bf16[32,1664]{1,0:T(8,128)(2,1)S(1)}, u32[]{:S(2)}, u32[]{:S(2)}) collective-permute-start(bf16[32,1664]{1,0:T(8,128)(2,1)S(1)} %get-tuple-element.112), channel_id=1, source_target_pairs={{0,8},{4,12},{8,0},{12,4},{16,24},{20,28},{24,16},{28,20},{32,40},... | collective-permute-start | bytes 319496 | tf_op jit(solution)/shard_map/ppermute | solution.py:630
  143.4 0.6 collective-permute-start.12
  144.0 0.0 collective-permute-done.10.refs_2_
  144.0 0.0 collective-permute-start.14
  144.0 2.3 %collective-permute-done.11.refs_3_ = bf16[32,1664]{1,0:T(8,128)(2,1)S(1)} collective-permute-done((bf16[32,1664]{1,0:T(8,128)(2,1)S(1)}, bf16[32,1664]{1,0:T(8,128)(2,1)S(1)}, u32[]{:S(2)}, u32[]{:S(2)}) %collective-permute-start.11) | collective-permute-done | bytes 106528 | tf_op jit(solution)/shard_map/ppermute | solution.py:630
  146.3 1.8 %collective-permute-done.12.refs_4_ = bf16[32,1664]{1,0:T(8,128)(2,1)S(1)} collective-permute-done((bf16[32,1664]{1,0:T(8,128)(2,1)S(1)}, bf16[32,1664]{1,0:T(8,128)(2,1)S(1)}, u32[]{:S(2)}, u32[]{:S(2)}) %collective-permute-start.12) | collective-permute-done | bytes 106528 | tf_op jit(solution)/shard_map/ppermute | solution.py:630
  148.1 2.1 %collective-permute-done.14.refs_7_ = bf16[32,1664]{1,0:T(8,128)(2,1)S(1)} collective-permute-done((bf16[32,1664]{1,0:T(8,128)(2,1)S(1)}, bf16[32,1664]{1,0:T(8,128)(2,1)S(1)}, u32[]{:S(2)}, u32[]{:S(2)}) %collective-permute-start.14) | collective-permute-done | bytes 106528 | tf_op jit(solution)/shard_map/ppermute | solution.py:630
  150.2 0.0 collective-permute-done.13.refs_6_
  150.2 0.0 collective-permute-done.15.refs_8_
  150.3 0.7 shard_map.147
  151.0 0.1 collective-permute-start.16
  151.1 4.1 %collective-permute-start.18 = (bf16[16,1920]{1,0:T(8,128)(2,1)S(1)}, bf16[16,1920]{1,0:T(8,128)(2,1)S(1)}, u32[]{:S(2)}, u32[]{:S(2)}) collective-permute-start(bf16[16,1920]{1,0:T(8,128)(2,1)S(1)} %get-tuple-element.122), channel_id=1, source_target_pairs={{0,48},{4,52},{8,56},{12,60},{16,0},{20,4},{24,8},{28,12},{32,16},... | collective-permute-start | bytes 184328 | tf_op jit(solution)/shard_map/ppermute | solution.py:630
  155.2 0.5 collective-permute-start.17
  155.7 7.6 %collective-permute-done.17.refs_2_ = bf16[16,1664]{1,0:T(8,128)(2,1)S(1)} collective-permute-done((bf16[16,1664]{1,0:T(8,128)(2,1)S(1)}, bf16[16,1664]{1,0:T(8,128)(2,1)S(1)}, u32[]{:S(2)}, u32[]{:S(2)}) %collective-permute-start.17) | collective-permute-done | bytes 53280 | tf_op jit(solution)/shard_map/ppermute | solution.py:630
  163.2 0.0 collective-permute-done.16.refs_1_
  163.2 0.0 collective-permute-done.18.refs_3_
  163.2 0.7 shard_map.148
  (13 shorter events, 0.0 us)
Async XLA Ops:
  1.4 12.9 %collective-permute-start.1 = (bf16[16,512]{1,0:T(8,128)(2,1)S(1)}, bf16[16,512]{1,0:T(8,128)(2,1)S(1)}, u32[]{:S(2)}, u32[]{:S(2)}) collective-permute-start(bf16[16,512]{1,0:T(8,128)(2,1)S(1)} %get-tuple-element.128), channel_id=1, source_target_pairs={{4,0},{8,4},{12,8},{16,12},{20,16},{24,20},{28,24},{32,28},{36,32}... | collective-permute-start | bytes 49160 | tf_op jit(solution)/shard_map/ppermute | solution.py:675
  12.3 10.8 %collective-permute-start = (bf16[16,512]{1,0:T(8,128)(2,1)S(1)}, bf16[16,512]{1,0:T(8,128)(2,1)S(1)}, u32[]{:S(2)}, u32[]{:S(2)}) collective-permute-start(bf16[16,512]{1,0:T(8,128)(2,1)S(1)} %get-tuple-element.129), channel_id=1, source_target_pairs={{0,4},{4,8},{8,12},{12,16},{16,20},{20,24},{24,28},{28,32},{32,36}... | collective-permute-start | bytes 49160 | tf_op jit(solution)/shard_map/ppermute | solution.py:674
  14.2 8.8 %copy-start.8 = (bf16[16,512]{1,0:T(8,128)(2,1)}, bf16[16,512]{1,0:T(8,128)(2,1)S(1)}, u32[]{:S(2)}) copy-start(bf16[16,512]{1,0:T(8,128)(2,1)S(1)} %collective-permute-done.1.refs_3_.refs_10_) | copy-start | bytes 49156
  23.0 0.6 copy-start.9
  64.7 15.5 %all-to-all-start.2 = ((bf16[16,64,128]{2,1,0:T(8,128)(2,1)}), bf16[16,64,128]{2,1,0:T(8,128)(2,1)S(1)}, u32[]{:S(2)}, u32[]{:S(2)}) async-start(bf16[16,64,128]{2,1,0:T(8,128)(2,1)} %shard_map.140), calls=%async_computation.2 | async-start | bytes 524288 | tf_op jit(solution)/shard_map/all_to_all | solution.py:641
  81.5 14.4 %all-to-all-start.3 = ((bf16[4,1024,128]{2,1,0:T(8,128)(2,1)}), bf16[4,1024,128]{2,1,0:T(8,128)(2,1)S(1)}, u32[]{:S(2)}, u32[]{:S(2)}) async-start(bf16[4,1024,128]{2,1,0:T(8,128)(2,1)} %shard_map.141), calls=%async_computation.3 | async-start | bytes 2097152 | tf_op jit(solution)/shard_map/all_to_all | solution.py:641
  95.9 1.0 copy-start.7
  106.6 12.1 %collective-permute-start.2 = (bf16[128,1664]{1,0:T(8,128)(2,1)}, bf16[128,1664]{1,0:T(8,128)(2,1)S(1)}, u32[]{:S(2)}, u32[]{:S(2)}) collective-permute-start(bf16[128,1664]{1,0:T(8,128)(2,1)} %get-tuple-element.98), channel_id=1, source_target_pairs={{0,64},{4,68},{8,72},{12,76},{16,80},{20,84},{24,88},{28,92},{32,9... | collective-permute-start | bytes 1277960 | tf_op jit(solution)/shard_map/ppermute | solution.py:635
  109.0 9.7 %collective-permute-start.3 = (bf16[128,1664]{1,0:T(8,128)(2,1)}, bf16[128,1664]{1,0:T(8,128)(2,1)S(1)}, u32[]{:S(2)}, u32[]{:S(2)}) collective-permute-start(bf16[128,1664]{1,0:T(8,128)(2,1)} %get-tuple-element.99), channel_id=1, source_target_pairs={{0,192},{4,196},{8,200},{12,204},{16,208},{20,212},{24,216},{28,22... | collective-permute-start | bytes 1277960 | tf_op jit(solution)/shard_map/ppermute | solution.py:636
  109.0 11.6 %collective-permute-start.4 = (bf16[128,1664]{1,0:T(8,128)(2,1)}, bf16[128,1664]{1,0:T(8,128)(2,1)S(1)}, u32[]{:S(2)}, u32[]{:S(2)}) collective-permute-start(bf16[128,1664]{1,0:T(8,128)(2,1)} %get-tuple-element.102), channel_id=1, source_target_pairs={{0,4},{4,8},{8,12},{12,0},{16,20},{20,24},{24,28},{28,16},{32,36},... | collective-permute-start | bytes 1277960 | tf_op jit(solution)/shard_map/ppermute | solution.py:635
  109.6 11.0 %collective-permute-start.5 = (bf16[128,1664]{1,0:T(8,128)(2,1)}, bf16[128,1664]{1,0:T(8,128)(2,1)S(1)}, u32[]{:S(2)}, u32[]{:S(2)}) collective-permute-start(bf16[128,1664]{1,0:T(8,128)(2,1)} %get-tuple-element.103), channel_id=1, source_target_pairs={{0,12},{4,0},{8,4},{12,8},{16,28},{20,16},{24,20},{28,24},{32,44},... | collective-permute-start | bytes 1277960 | tf_op jit(solution)/shard_map/ppermute | solution.py:636
  112.3 8.3 %copy-start.3 = (bf16[128,1664]{1,0:T(8,128)(2,1)S(1)}, bf16[128,1664]{1,0:T(8,128)(2,1)}, u32[]{:S(2)}) copy-start(bf16[128,1664]{1,0:T(8,128)(2,1)} %get-tuple-element.100.refs_0_) | copy-start | bytes 1277956
  112.3 8.3 %copy-start.4 = (bf16[128,1664]{1,0:T(8,128)(2,1)S(1)}, bf16[128,1664]{1,0:T(8,128)(2,1)}, u32[]{:S(2)}) copy-start(bf16[128,1664]{1,0:T(8,128)(2,1)} %get-tuple-element.101.refs_3_) | copy-start | bytes 1277956
  120.6 0.7 copy-start.6
  121.3 15.5 %copy-start = (s32[3]{0:T(128)S(1)}, s32[3]{0:T(128)}, u32[]{:S(2)}) copy-start(s32[3]{0:T(128)} %pad_add_fusion.refs_0_) | copy-start | bytes 40
  121.3 15.5 %copy-start.1 = (bf16[128,1664]{1,0:T(8,128)(2,1)S(1)}, bf16[128,1664]{1,0:T(8,128)(2,1)}, u32[]{:S(2)}) copy-start(bf16[128,1664]{1,0:T(8,128)(2,1)} %get-tuple-element.97.refs_1_) | copy-start | bytes 1277956
  121.3 15.5 %copy-start.2 = (bf16[128,1664]{1,0:T(8,128)(2,1)S(1)}, bf16[128,1664]{1,0:T(8,128)(2,1)}, u32[]{:S(2)}) copy-start(bf16[128,1664]{1,0:T(8,128)(2,1)} %get-tuple-element.107.refs_6_) | copy-start | bytes 1277956
  121.5 15.3 %collective-permute-start.8 = (bf16[64,1792]{1,0:T(8,128)(2,1)S(1)}, bf16[64,1792]{1,0:T(8,128)(2,1)S(1)}, u32[]{:S(2)}, u32[]{:S(2)}) collective-permute-start(bf16[64,1792]{1,0:T(8,128)(2,1)S(1)} %get-tuple-element.108), channel_id=1, source_target_pairs={{0,4},{4,8},{8,12},{12,0},{16,20},{20,24},{24,28},{28,16},{32,36},... | collective-permute-start | bytes 688136 | tf_op jit(solution)/shard_map/ppermute | solution.py:635
  121.6 15.2 %collective-permute-start.9 = (bf16[64,1792]{1,0:T(8,128)(2,1)S(1)}, bf16[64,1792]{1,0:T(8,128)(2,1)S(1)}, u32[]{:S(2)}, u32[]{:S(2)}) collective-permute-start(bf16[64,1792]{1,0:T(8,128)(2,1)S(1)} %get-tuple-element.109), channel_id=1, source_target_pairs={{0,12},{4,0},{8,4},{12,8},{16,28},{20,16},{24,20},{28,24},{32,44},... | collective-permute-start | bytes 688136 | tf_op jit(solution)/shard_map/ppermute | solution.py:636
  125.2 6.8 %collective-permute-start.6 = (bf16[64,1664]{1,0:T(8,128)(2,1)S(1)}, bf16[64,1664]{1,0:T(8,128)(2,1)S(1)}, u32[]{:S(2)}, u32[]{:S(2)}) collective-permute-start(bf16[64,1664]{1,0:T(8,128)(2,1)S(1)} %get-tuple-element.105), channel_id=1, source_target_pairs={{0,64},{4,68},{8,72},{12,76},{16,80},{20,84},{24,88},{28,92},{32,9... | collective-permute-start | bytes 638984 | tf_op jit(solution)/shard_map/ppermute | solution.py:635
  128.6 8.2 %collective-permute-start.7 = (bf16[64,1664]{1,0:T(8,128)(2,1)S(1)}, bf16[64,1664]{1,0:T(8,128)(2,1)S(1)}, u32[]{:S(2)}, u32[]{:S(2)}) collective-permute-start(bf16[64,1664]{1,0:T(8,128)(2,1)S(1)} %get-tuple-element.106), channel_id=1, source_target_pairs={{0,192},{4,196},{8,200},{12,204},{16,208},{20,212},{24,216},{28,22... | collective-permute-start | bytes 638984 | tf_op jit(solution)/shard_map/ppermute | solution.py:636
  137.9 6.1 %collective-permute-start.10 = (bf16[32,1664]{1,0:T(8,128)(2,1)S(1)}, bf16[32,1664]{1,0:T(8,128)(2,1)S(1)}, u32[]{:S(2)}, u32[]{:S(2)}) collective-permute-start(bf16[32,1664]{1,0:T(8,128)(2,1)S(1)} %get-tuple-element.111), channel_id=1, source_target_pairs={{0,4},{4,8},{8,12},{12,0},{16,20},{20,24},{24,28},{28,16},{32,36},... | collective-permute-start | bytes 319496 | tf_op jit(solution)/shard_map/ppermute | solution.py:630
  138.0 12.2 %collective-permute-start.13 = (bf16[32,1792]{1,0:T(8,128)(2,1)S(1)}, bf16[32,1792]{1,0:T(8,128)(2,1)S(1)}, u32[]{:S(2)}, u32[]{:S(2)}) collective-permute-start(bf16[32,1792]{1,0:T(8,128)(2,1)S(1)} %get-tuple-element.115), channel_id=1, source_target_pairs={{0,64},{4,68},{8,72},{12,76},{16,80},{20,84},{24,88},{28,92},{32,9... | collective-permute-start | bytes 344072 | tf_op jit(solution)/shard_map/ppermute | solution.py:630
  138.1 12.1 %collective-permute-start.15 = (bf16[32,1792]{1,0:T(8,128)(2,1)S(1)}, bf16[32,1792]{1,0:T(8,128)(2,1)S(1)}, u32[]{:S(2)}, u32[]{:S(2)}) collective-permute-start(bf16[32,1792]{1,0:T(8,128)(2,1)S(1)} %get-tuple-element.117), channel_id=1, source_target_pairs={{0,192},{4,196},{8,200},{12,204},{16,208},{20,212},{24,216},{28,22... | collective-permute-start | bytes 344072 | tf_op jit(solution)/shard_map/ppermute | solution.py:630
  140.1 6.2 %collective-permute-start.11 = (bf16[32,1664]{1,0:T(8,128)(2,1)S(1)}, bf16[32,1664]{1,0:T(8,128)(2,1)S(1)}, u32[]{:S(2)}, u32[]{:S(2)}) collective-permute-start(bf16[32,1664]{1,0:T(8,128)(2,1)S(1)} %get-tuple-element.112), channel_id=1, source_target_pairs={{0,8},{4,12},{8,0},{12,4},{16,24},{20,28},{24,16},{28,20},{32,40},... | collective-permute-start | bytes 319496 | tf_op jit(solution)/shard_map/ppermute | solution.py:630
  143.4 4.7 %collective-permute-start.12 = (bf16[32,1664]{1,0:T(8,128)(2,1)S(1)}, bf16[32,1664]{1,0:T(8,128)(2,1)S(1)}, u32[]{:S(2)}, u32[]{:S(2)}) collective-permute-start(bf16[32,1664]{1,0:T(8,128)(2,1)S(1)} %get-tuple-element.113), channel_id=1, source_target_pairs={{0,12},{4,0},{8,4},{12,8},{16,28},{20,16},{24,20},{28,24},{32,44},... | collective-permute-start | bytes 319496 | tf_op jit(solution)/shard_map/ppermute | solution.py:630
  144.0 6.2 %collective-permute-start.14 = (bf16[32,1664]{1,0:T(8,128)(2,1)S(1)}, bf16[32,1664]{1,0:T(8,128)(2,1)S(1)}, u32[]{:S(2)}, u32[]{:S(2)}) collective-permute-start(bf16[32,1664]{1,0:T(8,128)(2,1)S(1)} %get-tuple-element.116), channel_id=1, source_target_pairs={{0,128},{4,132},{8,136},{12,140},{16,144},{20,148},{24,152},{28,15... | collective-permute-start | bytes 319496 | tf_op jit(solution)/shard_map/ppermute | solution.py:630
  150.2 13.0 %copy-start.5 = (f32[128,512]{1,0:T(8,128)S(1)}, f32[128,512]{1,0:T(8,128)}, u32[]{:S(2)}) copy-start(f32[128,512]{1,0:T(8,128)} %get-tuple-element.124.refs_5_) | copy-start | bytes 786436
  151.0 12.3 %collective-permute-start.16 = (bf16[16,1920]{1,0:T(8,128)(2,1)S(1)}, bf16[16,1920]{1,0:T(8,128)(2,1)S(1)}, u32[]{:S(2)}, u32[]{:S(2)}) collective-permute-start(bf16[16,1920]{1,0:T(8,128)(2,1)S(1)} %get-tuple-element.120), channel_id=1, source_target_pairs={{0,16},{4,20},{8,24},{12,28},{16,32},{20,36},{24,40},{28,44},{32,4... | collective-permute-start | bytes 184328 | tf_op jit(solution)/shard_map/ppermute | solution.py:630
  151.1 12.2 %collective-permute-start.18 = (bf16[16,1920]{1,0:T(8,128)(2,1)S(1)}, bf16[16,1920]{1,0:T(8,128)(2,1)S(1)}, u32[]{:S(2)}, u32[]{:S(2)}) collective-permute-start(bf16[16,1920]{1,0:T(8,128)(2,1)S(1)} %get-tuple-element.122), channel_id=1, source_target_pairs={{0,48},{4,52},{8,56},{12,60},{16,0},{20,4},{24,8},{28,12},{32,16},... | collective-permute-start | bytes 184328 | tf_op jit(solution)/shard_map/ppermute | solution.py:630
  155.2 8.1 %collective-permute-start.17 = (bf16[16,1664]{1,0:T(8,128)(2,1)S(1)}, bf16[16,1664]{1,0:T(8,128)(2,1)S(1)}, u32[]{:S(2)}, u32[]{:S(2)}) collective-permute-start(bf16[16,1664]{1,0:T(8,128)(2,1)S(1)} %get-tuple-element.121), channel_id=1, source_target_pairs={{0,32},{4,36},{8,40},{12,44},{16,48},{20,52},{24,56},{28,60},{32,0... | collective-permute-start | bytes 159752 | tf_op jit(solution)/shard_map/ppermute | solution.py:630

commit v10 on v8

--- a/solution.py
+++ b/solution.py
@@ -559,36 +559,37 @@
 
 
 def first_sum_kernel(place, *refs):
-    from_x, from_y, by_y, by_x, kept = refs[:5], refs[5:10], refs[10:14], refs[14:18], refs[18]
-    parted, whole = refs[19], refs[20]
+    from_x, from_y, by_y, by_x, kept = refs[:5], refs[5:10], refs[10:14], refs[14], refs[15]
+    parted, whole = refs[16], refs[17]
     parted[...] = ring_total(*from_x).reshape(parted.shape)
     whole[...] = ring_total(*from_y)
     send_y(place, parted, by_y)
     columns = whole.shape[1]
-    chunk = whole.shape[0] // SIDE
-    for step in range(SIDE):
-        to = lax.rem(place[0] + step, SIDE)
-        block = whole[pl.ds(pl.multiple_of(to * chunk, chunk), chunk), :]
-        by_x[step][:, :columns] = block.astype(by_x[step].dtype)
     high = from_y[3][:32, columns:].astype(f32)
     low = from_y[4][:32, columns:].astype(f32)
     on_high = scalar_flag((place[2] == 0) & (place[1] == SIDE - 1))
     on_low = scalar_flag((place[2] == SIDE - 1) & (place[1] == 0))
-    by_x[1][:, columns:] = (high * on_high).astype(bf16)
-    by_x[3][:, columns:] = (low * on_low).astype(bf16)
+    by_x[:, :, :columns] = whole[...].astype(bf16).reshape(SIDE, -1, columns)
+    for to in range(SIDE):
+        up = on_high * scalar_flag(lax.rem(place[0] + 1, SIDE) == to)
+        down = on_low * scalar_flag(lax.rem(place[0] + SIDE - 1, SIDE) == to)
+        by_x[to, :, columns:] = (high * up + low * down).astype(bf16)
     kept[:32, :] = high * (1.0 - on_high)
     kept[32:, :] = low * (1.0 - on_low)
 
 
 def second_sum_kernel(place, *refs):
-    first, second, kept, by_z, kept_on, keep = refs[:4], refs[4:8], refs[8], refs[9:13], refs[13], refs[14]
+    first, second, kept, by_z, kept_on, keep = refs[:4], refs[4], refs[5], refs[6:10], refs[10], refs[11]
     columns = first[0].shape[1]
-    high = kept[:32, :] + second[1][:, columns:].astype(f32)
-    low = kept[32:, :] + second[3][:, columns:].astype(f32)
+    high, low = kept[:32, :], kept[32:, :]
+    total = None
+    for source in range(SIDE):
+        block = second[source].astype(f32)
+        edge = block[:, columns:]
+        high = high + edge * scalar_flag(lax.rem(place[0] + SIDE - 1, SIDE) == source)
+        low = low + edge * scalar_flag(lax.rem(place[0] + 1, SIDE) == source)
+        total = block[:, :columns] if total is None else total + block[:, :columns]
     first = total_of(first).reshape(SIDE, 8, -1)
-    total = second[0][...]
-    for step in range(1, SIDE):
-        total = total + second[step][:, :columns].astype(f32)
     second = total.reshape(SIDE, 8, -1)
     above = scalar_flag(place[2] == 0)
     below = scalar_flag(place[2] == SIDE - 1)
@@ -670,6 +671,7 @@
     stride_x, stride_z, stride_y = SIDE * SIDE, SIDE, 1
     index = lax.axis_index("seq")
     place = jnp.stack([index // stride_x, index // stride_z % SIDE, index % SIDE]).astype(jnp.int32)
+    lined = [[base + stride_x * digit for digit in range(SIDE)] for base in range(stride_x)]
     beside = [[SIDE * base + digit for digit in range(SIDE)] for base in range(COUNT // SIDE)]
     across = [[base + SIDE * digit for digit in range(COUNT // SIDE)] for base in range(SIDE)]
     upward = [(i, i + 1) for i in range(COUNT - 1)]
@@ -779,7 +781,7 @@
     *parts, kept = call(
         first_sum_kernel,
         slots(small, joined, f32)
-        + [((small, joined), f32), ((small, joined + 128), bf16), ((small, joined), bf16), ((small, joined + 128), bf16)]
+        + [((SIDE, small, joined + 128), bf16)]
         + [((64, 128), f32)],
         (place, *from_x, *from_y),
         [pltpu.VMEM((SIDE, SIDE, 8, joined), f32), pltpu.VMEM((eighth, joined), f32)],
@@ -787,12 +789,12 @@
         vmem=16 * 2**20,
     )
     first = exchange(parts[:4], stride_y)
-    second = exchange(parts[4:], stride_x)
+    second = transpose_over(parts[4], lined)
     *parts, kept = call(
         second_sum_kernel,
         [((16, joined), f32), ((16, joined + 256), bf16), ((16, joined), bf16), ((16, joined + 256), bf16)]
         + [((64, 128), f32)],
-        (place, *first, *second, kept),
+        (place, *first, second, kept),
         [pltpu.VMEM((SIDE, 2, 8, joined), f32)],
         scalars=1,
         vmem=16 * 2**20,

time: 165 us -> 165 us (level)
  starting transfers between devices: 45.8 us -> 48.5 us
  waiting for transfers between devices: 46.3 us -> 44.1 us
    all_to_all x2 -> x3, starting transfers between devices: 9.47 us -> 14.1 us  [transpose_over(): return lax.all_to_all(parts, 'seq', 0, 0, axis_index_groups=groups)]
    ppermute x4, waiting for transfers between devices: 5.28 us -> 7.76 us  [around(): lax.ppermute(to_right, 'seq', axis_pairs(stride, 1))]
    ppermute x4, waiting for transfers between devices: 4.84 us -> 2.44 us  [around(): lax.ppermute(to_left, 'seq', axis_pairs(stride, SIDE - 1))]
    ppermute x9 -> x6, waiting for transfers between devices: 13.8 us -> 11.5 us  [exchange(): lax.ppermute(parts[step], 'seq', axis_pairs(stride, step))]
    ppermute x9 -> x6, starting transfers between devices: 10.8 us -> 8.69 us  [exchange(): lax.ppermute(parts[step], 'seq', axis_pairs(stride, step))]
    all_to_all x2 -> x3, waiting for transfers between devices: 13.6 us -> 13.6 us  [transpose_over(): return lax.all_to_all(parts, 'seq', 0, 0, axis_index_groups=groups)]
  transfers between devices with their start and end apart: 21 -> 19, of which waited for: 10 -> 10; matrix products, arithmetic and copies ran while one was open for 0% -> 0% of each run, Pallas kernels for 8% -> 8%
where the time goes in v10:
time: 165 us
  starting transfers between devices  48.5 us (29%)
  waiting for transfers between devices  44.1 us (27%)
  Pallas kernels  35.8 us (22%)
  blocking collectives  31.9 us (19%)
  local copies, waits for them, and re-layouts  3.06 us (2%)
    pallas_call x11, Pallas kernels, call(): pl.pallas_call(used, out_shape=[jax.ShapeDtypeStruct(shape, kind) for sha...  35.8 us
    all_to_all x2, blocking collectives, transpose_over(): return lax.all_to_all(parts, 'seq', 0, 0, axis_index_groups=groups)  31.9 us
    all_to_all x3, starting transfers between devices, transpose_over(): return lax.all_to_all(parts, 'seq', 0, 0, axis_index_groups=groups)  14.1 us
    all_to_all x3, waiting for transfers between devices, transpose_over(): return lax.all_to_all(parts, 'seq', 0, 0, axis_index_groups=groups)  13.6 us
    ppermute x6, waiting for transfers between devices, exchange(): lax.ppermute(parts[step], 'seq', axis_pairs(stride, step))  11.5 us
    ppermute x1, starting transfers between devices, shards(): high = lax.ppermute(sequence[:16], 'seq', downward)  10.9 us
    ppermute x1, waiting for transfers between devices, shards(): low = lax.ppermute(sequence[rows - 16:], 'seq', upward)  8.8 us
    ppermute x6, starting transfers between devices, exchange(): lax.ppermute(parts[step], 'seq', axis_pairs(stride, step))  8.69 us
  transfers between devices with their start and end apart: 19, of which 10 were waited for; matrix products, arithmetic and copies ran while one was open for 0% of the time, Pallas kernels for 8%

profile of v10, /device:TPU:6, one launch (start us, length us, event | category | flops | bytes accessed | tf_op | source)
XLA Modules:
  0.0 164.7 jit_solution(8757207547879537315)
XLA Ops:
  0.6 0.7 fusion
  1.4 10.9 %collective-permute-start.1 = (bf16[16,512]{1,0:T(8,128)(2,1)S(1)}, bf16[16,512]{1,0:T(8,128)(2,1)S(1)}, u32[]{:S(2)}, u32[]{:S(2)}) collective-permute-start(bf16[16,512]{1,0:T(8,128)(2,1)S(1)} %get-tuple-element.124), channel_id=1, source_target_pairs={{4,0},{8,4},{12,8},{16,12},{20,16},{24,20},{28,24},{32,28},{36,32}... | collective-permute-start | bytes 49160 | tf_op jit(solution)/shard_map/ppermute | solution.py:680
  12.3 1.9 %collective-permute-start = (bf16[16,512]{1,0:T(8,128)(2,1)S(1)}, bf16[16,512]{1,0:T(8,128)(2,1)S(1)}, u32[]{:S(2)}, u32[]{:S(2)}) collective-permute-start(bf16[16,512]{1,0:T(8,128)(2,1)S(1)} %get-tuple-element.125), channel_id=1, source_target_pairs={{0,4},{4,8},{8,12},{12,16},{16,20},{20,24},{24,28},{28,32},{32,36}... | collective-permute-start | bytes 49160 | tf_op jit(solution)/shard_map/ppermute | solution.py:679
  14.2 0.0 collective-permute-done.1.refs_3_.refs_10_
  14.2 0.0 copy-start.8
  14.2 8.8 %collective-permute-done.refs_2_.refs_9_ = bf16[16,512]{1,0:T(8,128)(2,1)S(1)} collective-permute-done((bf16[16,512]{1,0:T(8,128)(2,1)S(1)}, bf16[16,512]{1,0:T(8,128)(2,1)S(1)}, u32[]{:S(2)}, u32[]{:S(2)}) %collective-permute-start) | collective-permute-done | bytes 16416 | tf_op jit(solution)/shard_map/ppermute | solution.py:679
  23.0 0.0 copy-done.8
  23.0 0.6 copy-done.9
  23.6 7.0 %shard_map.138 = (bf16[4,1040,128]{2,1,0:T(8,128)(2,1)}, bf16[256,512]{1,0:T(8,128)(2,1)}, bf16[256,512]{1,0:T(8,128)(2,1)}, bf16[32,512]{1,0:T(8,128)(2,1)}, bf...) custom-call(bf16[128,512]{1,0:T(8,128)(2,1)} %refs_0_.1, ...), custom_call_target="tpu_custom_call" | custom-call | flops 1000000000 | bytes 3746944 | tf_op jit(solution)/shard_map/pallas_call | solution.py:28
  30.6 17.6 %all_to_all.25.refs_0_ = bf16[4,1040,128]{2,1,0:T(8,128)(2,1)S(1)} all-to-all(bf16[4,1040,128]{2,1,0:T(8,128)(2,1)} %get-tuple-element.65), channel_id=1, replica_groups={{0,4,8,12},{16,20,24,28},{32,36,40,44},{48,52,56,60},{64,68,72,76},{80,..., dimensions={0} | all-to-all | bytes 2129920 | tf_op jit(solution)/shard_map/all_to_all | solution.py:645
  48.3 0.4 shard_map.139
  48.6 14.2 %all_to_all.26.refs_0_ = bf16[16,72,128]{2,1,0:T(8,128)(2,1)S(1)} all-to-all(bf16[16,72,128]{2,1,0:T(8,128)(2,1)S(1)} %shard_map.139), channel_id=1, replica_groups={{0,16,32,48,64,80,96,112,128,144,160,176,192,208,224,240},{4,20,36,52,6..., dimensions={0} | all-to-all | bytes 589824 | tf_op jit(solution)/shard_map/all_to_all | solution.py:645
  62.9 1.6 shard_map.140
  64.5 5.8 %all-to-all-start.2 = ((bf16[16,64,128]{2,1,0:T(8,128)(2,1)}), bf16[16,64,128]{2,1,0:T(8,128)(2,1)S(1)}, u32[]{:S(2)}, u32[]{:S(2)}) async-start(bf16[16,64,128]{2,1,0:T(8,128)(2,1)} %shard_map.140), calls=%async_computation.2 | async-start | bytes 524288 | tf_op jit(solution)/shard_map/all_to_all | solution.py:645
  70.2 9.8 %all-to-all-done.2.refs_1_ = bf16[16,64,128]{2,1,0:T(8,128)(2,1)S(1)} async-done(((bf16[16,64,128]{2,1,0:T(8,128)(2,1)}), bf16[16,64,128]{2,1,0:T(8,128)(2,1)S(1)}, u32[]{:S(2)}, u32[]{:S(2)}) %all-to-all-start.2) | async-done | bytes 262176 | tf_op jit(solution)/shard_map/all_to_all | solution.py:645
  80.0 1.3 shard_map.141
  81.3 3.7 %all-to-all-start.3 = ((bf16[4,1024,128]{2,1,0:T(8,128)(2,1)}), bf16[4,1024,128]{2,1,0:T(8,128)(2,1)S(1)}, u32[]{:S(2)}, u32[]{:S(2)}) async-start(bf16[4,1024,128]{2,1,0:T(8,128)(2,1)} %shard_map.141), calls=%async_computation.3 | async-start | bytes 2097152 | tf_op jit(solution)/shard_map/all_to_all | solution.py:645
  85.0 0.7 pad_add_fusion.refs_0_
  85.7 6.2 %shard_map.142 = (bf16[256,1024]{1,0:T(8,128)(2,1)}, bf16[256,1024]{1,0:T(8,128)(2,1)}, bf16[256,1024]{1,0:T(8,128)(2,1)}, bf16[256,1024]{1,0:T(8,128)(2,1)}, bf...) custom-call(bf16[256,1280]{1,0:T(8,128)(2,1)} %get-tuple-element.66., ...), custom_call_target="tpu_custom_call" | custom-call | flops 8000000000 | bytes 2048064 | tf_op jit(solution)/shard_map/pallas_call | solution.py:28
  91.9 3.8 %all-to-all-done.3.refs_1_ = bf16[4,1024,128]{2,1,0:T(8,128)(2,1)S(1)} async-done(((bf16[4,1024,128]{2,1,0:T(8,128)(2,1)}), bf16[4,1024,128]{2,1,0:T(8,128)(2,1)S(1)}, u32[]{:S(2)}, u32[]{:S(2)}) %all-to-all-start.3) | async-done | bytes 1048608 | tf_op jit(solution)/shard_map/all_to_all | solution.py:645
  95.7 1.0 copy-done.7
  96.7 9.4 %shard_map.143 = (bf16[256,1024]{1,0:T(8,128)(2,1)}, bf16[256,1024]{1,0:T(8,128)(2,1)}, bf16[256,1280]{1,0:T(8,128)(2,1)}, f32[8,1280]{1,0:T(8,128)}, f32[8,1280...) custom-call(s32[3]{0:T(128)} %pad_add_fusion.refs_0_, ...), custom_call_target="tpu_custom_call" | custom-call | flops 1000000000 | bytes 6426764 | tf_op jit(solution)/shard_map/pallas_call | solution.py:28
  106.1 2.5 %collective-permute-start.2 = (bf16[128,1664]{1,0:T(8,128)(2,1)}, bf16[128,1664]{1,0:T(8,128)(2,1)S(1)}, u32[]{:S(2)}, u32[]{:S(2)}) collective-permute-start(bf16[128,1664]{1,0:T(8,128)(2,1)} %get-tuple-element.97), channel_id=1, source_target_pairs={{0,64},{4,68},{8,72},{12,76},{16,80},{20,84},{24,88},{28,92},{32,9... | collective-permute-start | bytes 1277960 | tf_op jit(solution)/shard_map/ppermute | solution.py:639
  108.6 0.0 collective-permute-start.3
  108.6 0.6 collective-permute-start.4
  109.2 2.7 %collective-permute-start.5 = (bf16[128,1664]{1,0:T(8,128)(2,1)}, bf16[128,1664]{1,0:T(8,128)(2,1)S(1)}, u32[]{:S(2)}, u32[]{:S(2)}) collective-permute-start(bf16[128,1664]{1,0:T(8,128)(2,1)} %get-tuple-element.102), channel_id=1, source_target_pairs={{0,12},{4,0},{8,4},{12,8},{16,28},{20,16},{24,20},{28,24},{32,44},... | collective-permute-start | bytes 1277960 | tf_op jit(solution)/shard_map/ppermute | solution.py:640
  111.8 6.4 %shard_map.144 = (bf16[128,512]{1,0:T(8,128)(2,1)}, f32[128,512]{1,0:T(8,128)}, bf16[64,128]{1,0:T(8,128)(2,1)}) custom-call(s32[3]{0:T(128)} %pad_add_fusion.refs_0_, bf16[256,512]{1,0:T(8,128)(2,1)} %get-tuple-element.64.refs_1_, f32[512]{0:T(512)} %refs_2_.1, bf16[256,1024]{1,0:T(8,128)(2,1)} %get-tuple-element.89.refs_3_, bf16[1024,512]{1,0:T(8,128)(2,1)} %refs_4_.3, ...), custom_call_target="tpu_custom_call" | custom-call | flops 8000000000 | bytes 5515276 | tf_op jit(solution)/shard_map/pallas_call | solution.py:28
  118.2 0.0 collective-permute-done.2.refs_1_.refs_2_
  118.2 0.0 collective-permute-done.3.refs_2_.refs_3_
  118.2 1.9 %collective-permute-done.4.refs_4_.refs_7_ = bf16[128,1664]{1,0:T(8,128)(2,1)S(1)} collective-permute-done((bf16[128,1664]{1,0:T(8,128)(2,1)}, bf16[128,1664]{1,0:T(8,128)(2,1)S(1)}, u32[]{:S(2)}, u32[]{:S(2)}) %collective-permute-start.4) | collective-permute-done | bytes 426016 | tf_op jit(solution)/shard_map/ppermute | solution.py:639
  120.1 0.0 collective-permute-done.5.refs_5_.refs_8_
  120.1 0.0 copy-done.3
  120.2 0.0 copy-done.4
  120.2 0.0 copy-start.6
  120.2 0.7 copy-done.6
  120.9 0.2 shard_map.145
  121.1 0.1 collective-permute-start.8
  121.2 3.6 %collective-permute-start.9 = (bf16[64,1792]{1,0:T(8,128)(2,1)S(1)}, bf16[64,1792]{1,0:T(8,128)(2,1)S(1)}, u32[]{:S(2)}, u32[]{:S(2)}) collective-permute-start(bf16[64,1792]{1,0:T(8,128)(2,1)S(1)} %get-tuple-element.108), channel_id=1, source_target_pairs={{0,12},{4,0},{8,4},{12,8},{16,28},{20,16},{24,20},{28,24},{32,44},... | collective-permute-start | bytes 688136 | tf_op jit(solution)/shard_map/ppermute | solution.py:640
  124.8 3.4 %collective-permute-start.6 = (bf16[64,1664]{1,0:T(8,128)(2,1)S(1)}, bf16[64,1664]{1,0:T(8,128)(2,1)S(1)}, u32[]{:S(2)}, u32[]{:S(2)}) collective-permute-start(bf16[64,1664]{1,0:T(8,128)(2,1)S(1)} %get-tuple-element.104), channel_id=1, source_target_pairs={{0,64},{4,68},{8,72},{12,76},{16,80},{20,84},{24,88},{28,92},{32,9... | collective-permute-start | bytes 638984 | tf_op jit(solution)/shard_map/ppermute | solution.py:639
  128.2 0.0 collective-permute-start.7
  128.2 5.9 %collective-permute-done.6.refs_4_ = bf16[64,1664]{1,0:T(8,128)(2,1)S(1)} collective-permute-done((bf16[64,1664]{1,0:T(8,128)(2,1)S(1)}, bf16[64,1664]{1,0:T(8,128)(2,1)S(1)}, u32[]{:S(2)}, u32[]{:S(2)}) %collective-permute-start.6) | collective-permute-done | bytes 213024 | tf_op jit(solution)/shard_map/ppermute | solution.py:639
  134.0 2.4 %collective-permute-done.7.refs_5_ = bf16[64,1664]{1,0:T(8,128)(2,1)S(1)} collective-permute-done((bf16[64,1664]{1,0:T(8,128)(2,1)S(1)}, bf16[64,1664]{1,0:T(8,128)(2,1)S(1)}, u32[]{:S(2)}, u32[]{:S(2)}) %collective-permute-start.7) | collective-permute-done | bytes 213024 | tf_op jit(solution)/shard_map/ppermute | solution.py:640
  136.5 0.0 collective-permute-done.8.refs_9_
  136.5 0.0 collective-permute-done.9.refs_10_
  136.5 0.0 copy-done
  136.5 0.0 copy-done.1
  136.5 0.0 copy-done.2
  136.5 1.9 %shard_map.146 = (f32[32,1664]{1,0:T(8,128)S(1)}, bf16[32,1664]{1,0:T(8,128)(2,1)S(1)}, bf16[32,1664]{1,0:T(8,128)(2,1)S(1)}, bf16[32,1664]{1,0:T(8,128)(2,1)S(1...) custom-call(s32[3]{0:T(128)S(1)} %copy-done, bf16[128,1664]{1,0:T(8,128)(2,1)S(1)} %copy-done.1, ...), custom_call_target="tpu_custom_call" | custom-call | flops 1000000000 | bytes 3440652 | tf_op jit(solution)/shard_map/pallas_call | solution.py:28
  138.3 4.7 %all-to-all-start.4 = ((bf16[4,32,1792]{2,1,0:T(8,128)(2,1)}), bf16[4,32,1792]{2,1,0:T(8,128)(2,1)S(1)}, u32[]{:S(2)}, u32[]{:S(2)}) async-start(bf16[4,32,1792]{2,1,0:T(8,128)(2,1)} %get-tuple-element.113), calls=%async_computation.4 | async-start | bytes 917504 | tf_op jit(solution)/shard_map/all_to_all | solution.py:645
  143.0 0.0 collective-permute-start.10
  143.0 3.2 %collective-permute-start.11 = (bf16[32,1664]{1,0:T(8,128)(2,1)S(1)}, bf16[32,1664]{1,0:T(8,128)(2,1)S(1)}, u32[]{:S(2)}, u32[]{:S(2)}) collective-permute-start(bf16[32,1664]{1,0:T(8,128)(2,1)S(1)} %get-tuple-element.111), channel_id=1, source_target_pairs={{0,8},{4,12},{8,0},{12,4},{16,24},{20,28},{24,16},{28,20},{32,40},... | collective-permute-start | bytes 319496 | tf_op jit(solution)/shard_map/ppermute | solution.py:634
  146.2 0.8 collective-permute-start.12
  147.0 1.9 %collective-permute-done.10.refs_2_ = bf16[32,1664]{1,0:T(8,128)(2,1)S(1)} collective-permute-done((bf16[32,1664]{1,0:T(8,128)(2,1)S(1)}, bf16[32,1664]{1,0:T(8,128)(2,1)S(1)}, u32[]{:S(2)}, u32[]{:S(2)}) %collective-permute-start.10) | collective-permute-done | bytes 106528 | tf_op jit(solution)/shard_map/ppermute | solution.py:634
  148.9 1.1 collective-permute-done.11.refs_3_
  150.1 0.9 collective-permute-done.12.refs_4_
  150.9 0.0 all-to-all-done.4.refs_5_
  150.9 0.7 shard_map.147
  151.7 0.1 collective-permute-start.13
  151.8 4.1 %collective-permute-start.15 = (bf16[16,1920]{1,0:T(8,128)(2,1)S(1)}, bf16[16,1920]{1,0:T(8,128)(2,1)S(1)}, u32[]{:S(2)}, u32[]{:S(2)}) collective-permute-start(bf16[16,1920]{1,0:T(8,128)(2,1)S(1)} %get-tuple-element.118), channel_id=1, source_target_pairs={{0,48},{4,52},{8,56},{12,60},{16,0},{20,4},{24,8},{28,12},{32,16},... | collective-permute-start | bytes 184328 | tf_op jit(solution)/shard_map/ppermute | solution.py:634
  155.9 0.5 collective-permute-start.14
  156.3 7.6 %collective-permute-done.14.refs_2_ = bf16[16,1664]{1,0:T(8,128)(2,1)S(1)} collective-permute-done((bf16[16,1664]{1,0:T(8,128)(2,1)S(1)}, bf16[16,1664]{1,0:T(8,128)(2,1)S(1)}, u32[]{:S(2)}, u32[]{:S(2)}) %collective-permute-start.14) | collective-permute-done | bytes 53280 | tf_op jit(solution)/shard_map/ppermute | solution.py:634
  163.9 0.0 collective-permute-done.13.refs_1_
  163.9 0.0 collective-permute-done.15.refs_3_
  164.0 0.7 shard_map.148
  (9 shorter events, 0.0 us)
Async XLA Ops:
  1.4 12.9 %collective-permute-start.1 = (bf16[16,512]{1,0:T(8,128)(2,1)S(1)}, bf16[16,512]{1,0:T(8,128)(2,1)S(1)}, u32[]{:S(2)}, u32[]{:S(2)}) collective-permute-start(bf16[16,512]{1,0:T(8,128)(2,1)S(1)} %get-tuple-element.124), channel_id=1, source_target_pairs={{4,0},{8,4},{12,8},{16,12},{20,16},{24,20},{28,24},{32,28},{36,32}... | collective-permute-start | bytes 49160 | tf_op jit(solution)/shard_map/ppermute | solution.py:680
  12.3 10.8 %collective-permute-start = (bf16[16,512]{1,0:T(8,128)(2,1)S(1)}, bf16[16,512]{1,0:T(8,128)(2,1)S(1)}, u32[]{:S(2)}, u32[]{:S(2)}) collective-permute-start(bf16[16,512]{1,0:T(8,128)(2,1)S(1)} %get-tuple-element.125), channel_id=1, source_target_pairs={{0,4},{4,8},{8,12},{12,16},{16,20},{20,24},{24,28},{28,32},{32,36}... | collective-permute-start | bytes 49160 | tf_op jit(solution)/shard_map/ppermute | solution.py:679
  14.2 8.8 %copy-start.8 = (bf16[16,512]{1,0:T(8,128)(2,1)}, bf16[16,512]{1,0:T(8,128)(2,1)S(1)}, u32[]{:S(2)}) copy-start(bf16[16,512]{1,0:T(8,128)(2,1)S(1)} %collective-permute-done.1.refs_3_.refs_10_) | copy-start | bytes 49156
  23.0 0.6 copy-start.9
  64.5 15.5 %all-to-all-start.2 = ((bf16[16,64,128]{2,1,0:T(8,128)(2,1)}), bf16[16,64,128]{2,1,0:T(8,128)(2,1)S(1)}, u32[]{:S(2)}, u32[]{:S(2)}) async-start(bf16[16,64,128]{2,1,0:T(8,128)(2,1)} %shard_map.140), calls=%async_computation.2 | async-start | bytes 524288 | tf_op jit(solution)/shard_map/all_to_all | solution.py:645
  81.3 14.4 %all-to-all-start.3 = ((bf16[4,1024,128]{2,1,0:T(8,128)(2,1)}), bf16[4,1024,128]{2,1,0:T(8,128)(2,1)S(1)}, u32[]{:S(2)}, u32[]{:S(2)}) async-start(bf16[4,1024,128]{2,1,0:T(8,128)(2,1)} %shard_map.141), calls=%async_computation.3 | async-start | bytes 2097152 | tf_op jit(solution)/shard_map/all_to_all | solution.py:645
  95.7 1.0 copy-start.7
  106.1 12.1 %collective-permute-start.2 = (bf16[128,1664]{1,0:T(8,128)(2,1)}, bf16[128,1664]{1,0:T(8,128)(2,1)S(1)}, u32[]{:S(2)}, u32[]{:S(2)}) collective-permute-start(bf16[128,1664]{1,0:T(8,128)(2,1)} %get-tuple-element.97), channel_id=1, source_target_pairs={{0,64},{4,68},{8,72},{12,76},{16,80},{20,84},{24,88},{28,92},{32,9... | collective-permute-start | bytes 1277960 | tf_op jit(solution)/shard_map/ppermute | solution.py:639
  108.6 9.7 %collective-permute-start.3 = (bf16[128,1664]{1,0:T(8,128)(2,1)}, bf16[128,1664]{1,0:T(8,128)(2,1)S(1)}, u32[]{:S(2)}, u32[]{:S(2)}) collective-permute-start(bf16[128,1664]{1,0:T(8,128)(2,1)} %get-tuple-element.98), channel_id=1, source_target_pairs={{0,192},{4,196},{8,200},{12,204},{16,208},{20,212},{24,216},{28,22... | collective-permute-start | bytes 1277960 | tf_op jit(solution)/shard_map/ppermute | solution.py:640
  108.6 11.6 %collective-permute-start.4 = (bf16[128,1664]{1,0:T(8,128)(2,1)}, bf16[128,1664]{1,0:T(8,128)(2,1)S(1)}, u32[]{:S(2)}, u32[]{:S(2)}) collective-permute-start(bf16[128,1664]{1,0:T(8,128)(2,1)} %get-tuple-element.101), channel_id=1, source_target_pairs={{0,4},{4,8},{8,12},{12,0},{16,20},{20,24},{24,28},{28,16},{32,36},... | collective-permute-start | bytes 1277960 | tf_op jit(solution)/shard_map/ppermute | solution.py:639
  109.2 11.0 %collective-permute-start.5 = (bf16[128,1664]{1,0:T(8,128)(2,1)}, bf16[128,1664]{1,0:T(8,128)(2,1)S(1)}, u32[]{:S(2)}, u32[]{:S(2)}) collective-permute-start(bf16[128,1664]{1,0:T(8,128)(2,1)} %get-tuple-element.102), channel_id=1, source_target_pairs={{0,12},{4,0},{8,4},{12,8},{16,28},{20,16},{24,20},{28,24},{32,44},... | collective-permute-start | bytes 1277960 | tf_op jit(solution)/shard_map/ppermute | solution.py:640
  111.8 8.3 %copy-start.3 = (bf16[128,1664]{1,0:T(8,128)(2,1)S(1)}, bf16[128,1664]{1,0:T(8,128)(2,1)}, u32[]{:S(2)}) copy-start(bf16[128,1664]{1,0:T(8,128)(2,1)} %get-tuple-element.99.refs_0_) | copy-start | bytes 1277956
  111.8 8.3 %copy-start.4 = (bf16[128,1664]{1,0:T(8,128)(2,1)S(1)}, bf16[128,1664]{1,0:T(8,128)(2,1)}, u32[]{:S(2)}) copy-start(bf16[128,1664]{1,0:T(8,128)(2,1)} %get-tuple-element.100.refs_3_) | copy-start | bytes 1277956
  120.2 0.7 copy-start.6
  120.9 15.6 %copy-start = (s32[3]{0:T(128)S(1)}, s32[3]{0:T(128)}, u32[]{:S(2)}) copy-start(s32[3]{0:T(128)} %pad_add_fusion.refs_0_) | copy-start | bytes 40
  120.9 15.6 %copy-start.1 = (bf16[128,1664]{1,0:T(8,128)(2,1)S(1)}, bf16[128,1664]{1,0:T(8,128)(2,1)}, u32[]{:S(2)}) copy-start(bf16[128,1664]{1,0:T(8,128)(2,1)} %get-tuple-element.96.refs_1_) | copy-start | bytes 1277956
  120.9 15.6 %copy-start.2 = (bf16[128,1664]{1,0:T(8,128)(2,1)S(1)}, bf16[128,1664]{1,0:T(8,128)(2,1)}, u32[]{:S(2)}) copy-start(bf16[128,1664]{1,0:T(8,128)(2,1)} %get-tuple-element.106.refs_6_) | copy-start | bytes 1277956
  121.1 15.4 %collective-permute-start.8 = (bf16[64,1792]{1,0:T(8,128)(2,1)S(1)}, bf16[64,1792]{1,0:T(8,128)(2,1)S(1)}, u32[]{:S(2)}, u32[]{:S(2)}) collective-permute-start(bf16[64,1792]{1,0:T(8,128)(2,1)S(1)} %get-tuple-element.107), channel_id=1, source_target_pairs={{0,4},{4,8},{8,12},{12,0},{16,20},{20,24},{24,28},{28,16},{32,36},... | collective-permute-start | bytes 688136 | tf_op jit(solution)/shard_map/ppermute | solution.py:639
  121.2 15.3 %collective-permute-start.9 = (bf16[64,1792]{1,0:T(8,128)(2,1)S(1)}, bf16[64,1792]{1,0:T(8,128)(2,1)S(1)}, u32[]{:S(2)}, u32[]{:S(2)}) collective-permute-start(bf16[64,1792]{1,0:T(8,128)(2,1)S(1)} %get-tuple-element.108), channel_id=1, source_target_pairs={{0,12},{4,0},{8,4},{12,8},{16,28},{20,16},{24,20},{28,24},{32,44},... | collective-permute-start | bytes 688136 | tf_op jit(solution)/shard_map/ppermute | solution.py:640
  124.8 9.3 %collective-permute-start.6 = (bf16[64,1664]{1,0:T(8,128)(2,1)S(1)}, bf16[64,1664]{1,0:T(8,128)(2,1)S(1)}, u32[]{:S(2)}, u32[]{:S(2)}) collective-permute-start(bf16[64,1664]{1,0:T(8,128)(2,1)S(1)} %get-tuple-element.104), channel_id=1, source_target_pairs={{0,64},{4,68},{8,72},{12,76},{16,80},{20,84},{24,88},{28,92},{32,9... | collective-permute-start | bytes 638984 | tf_op jit(solution)/shard_map/ppermute | solution.py:639
  128.2 8.3 %collective-permute-start.7 = (bf16[64,1664]{1,0:T(8,128)(2,1)S(1)}, bf16[64,1664]{1,0:T(8,128)(2,1)S(1)}, u32[]{:S(2)}, u32[]{:S(2)}) collective-permute-start(bf16[64,1664]{1,0:T(8,128)(2,1)S(1)} %get-tuple-element.105), channel_id=1, source_target_pairs={{0,192},{4,196},{8,200},{12,204},{16,208},{20,212},{24,216},{28,22... | collective-permute-start | bytes 638984 | tf_op jit(solution)/shard_map/ppermute | solution.py:640
  138.3 12.6 %all-to-all-start.4 = ((bf16[4,32,1792]{2,1,0:T(8,128)(2,1)}), bf16[4,32,1792]{2,1,0:T(8,128)(2,1)S(1)}, u32[]{:S(2)}, u32[]{:S(2)}) async-start(bf16[4,32,1792]{2,1,0:T(8,128)(2,1)} %get-tuple-element.113), calls=%async_computation.4 | async-start | bytes 917504 | tf_op jit(solution)/shard_map/all_to_all | solution.py:645
  143.0 5.9 %collective-permute-start.10 = (bf16[32,1664]{1,0:T(8,128)(2,1)S(1)}, bf16[32,1664]{1,0:T(8,128)(2,1)S(1)}, u32[]{:S(2)}, u32[]{:S(2)}) collective-permute-start(bf16[32,1664]{1,0:T(8,128)(2,1)S(1)} %get-tuple-element.110), channel_id=1, source_target_pairs={{0,4},{4,8},{8,12},{12,0},{16,20},{20,24},{24,28},{28,16},{32,36},... | collective-permute-start | bytes 319496 | tf_op jit(solution)/shard_map/ppermute | solution.py:634
  143.0 7.1 %collective-permute-start.11 = (bf16[32,1664]{1,0:T(8,128)(2,1)S(1)}, bf16[32,1664]{1,0:T(8,128)(2,1)S(1)}, u32[]{:S(2)}, u32[]{:S(2)}) collective-permute-start(bf16[32,1664]{1,0:T(8,128)(2,1)S(1)} %get-tuple-element.111), channel_id=1, source_target_pairs={{0,8},{4,12},{8,0},{12,4},{16,24},{20,28},{24,16},{28,20},{32,40},... | collective-permute-start | bytes 319496 | tf_op jit(solution)/shard_map/ppermute | solution.py:634
  146.2 4.7 %collective-permute-start.12 = (bf16[32,1664]{1,0:T(8,128)(2,1)S(1)}, bf16[32,1664]{1,0:T(8,128)(2,1)S(1)}, u32[]{:S(2)}, u32[]{:S(2)}) collective-permute-start(bf16[32,1664]{1,0:T(8,128)(2,1)S(1)} %get-tuple-element.112), channel_id=1, source_target_pairs={{0,12},{4,0},{8,4},{12,8},{16,28},{20,16},{24,20},{28,24},{32,44},... | collective-permute-start | bytes 319496 | tf_op jit(solution)/shard_map/ppermute | solution.py:634
  150.9 13.0 %copy-start.5 = (f32[128,512]{1,0:T(8,128)S(1)}, f32[128,512]{1,0:T(8,128)}, u32[]{:S(2)}) copy-start(f32[128,512]{1,0:T(8,128)} %get-tuple-element.120.refs_5_) | copy-start | bytes 786436
  151.7 12.3 %collective-permute-start.13 = (bf16[16,1920]{1,0:T(8,128)(2,1)S(1)}, bf16[16,1920]{1,0:T(8,128)(2,1)S(1)}, u32[]{:S(2)}, u32[]{:S(2)}) collective-permute-start(bf16[16,1920]{1,0:T(8,128)(2,1)S(1)} %get-tuple-element.116), channel_id=1, source_target_pairs={{0,16},{4,20},{8,24},{12,28},{16,32},{20,36},{24,40},{28,44},{32,4... | collective-permute-start | bytes 184328 | tf_op jit(solution)/shard_map/ppermute | solution.py:634
  151.8 12.2 %collective-permute-start.15 = (bf16[16,1920]{1,0:T(8,128)(2,1)S(1)}, bf16[16,1920]{1,0:T(8,128)(2,1)S(1)}, u32[]{:S(2)}, u32[]{:S(2)}) collective-permute-start(bf16[16,1920]{1,0:T(8,128)(2,1)S(1)} %get-tuple-element.118), channel_id=1, source_target_pairs={{0,48},{4,52},{8,56},{12,60},{16,0},{20,4},{24,8},{28,12},{32,16},... | collective-permute-start | bytes 184328 | tf_op jit(solution)/shard_map/ppermute | solution.py:634
  155.9 8.1 %collective-permute-start.14 = (bf16[16,1664]{1,0:T(8,128)(2,1)S(1)}, bf16[16,1664]{1,0:T(8,128)(2,1)S(1)}, u32[]{:S(2)}, u32[]{:S(2)}) collective-permute-start(bf16[16,1664]{1,0:T(8,128)(2,1)S(1)} %get-tuple-element.117), channel_id=1, source_target_pairs={{0,32},{4,36},{8,40},{12,44},{16,48},{20,52},{24,56},{28,60},{32,0... | collective-permute-start | bytes 159752 | tf_op jit(solution)/shard_map/ppermute | solution.py:634

commit v11 on v8

--- a/solution.py
+++ b/solution.py
@@ -135,7 +135,7 @@
 
 def pre_kernel(
     seq, up, low, high, gain, in_proj, step_proj, conv_w, conv_b, step_bias, decay_log, out_proj,
-    payload, both, normal, normal_halo, cot, gate, conv, d_gated, raw, step, cumul, cumul_t,
+    payload, both, normal, normal_halo, cot, gate, conv, d_gated, raw, step, cumul,
     ext,
 ):
     rows = seq.shape[0]
@@ -173,7 +173,6 @@
         upto = tri_sum(triangle(rows, True), decay)
         step[at, :] = size
         cumul[at, :] = upto
-        cumul_t[frame * heads : (frame + 1) * heads, :] = tri_sum_turned(triangle(rows, False), decay)
         end = upto[rows - 1 : rows, :]
         ends.append(end)
         spread = expand(jnp.concatenate([size * jnp.exp(end - upto), jnp.exp(upto)], axis=0), mask)
@@ -245,9 +244,10 @@
     inner = got.shape[1] - 16
     part = inner // SIDE
     totals = tails_of(got, inner)
+    blocks = []
     for place in range(4):
         block = chain(got, totals, place, jnp.zeros((part, state), f32), lambda at, value: None)
-        out[:, 16 * place : 16 * place + 16, :] = block.reshape(16, 16, state).astype(bf16)
+        blocks.append(block.reshape(16, 16, state))
     lanes = iota((16, state), 1)
     packed = jnp.zeros((16, state), f32)
     for frame in range(2):
@@ -257,7 +257,8 @@
         packed = pack_column(packed, column, lanes, frame)
     chosen = ones_where(iota((16, 16), 1) == iota((16, 16), 0) // SIDE)
     packed = mm(chosen, packed.astype(bf16))
-    out[:, 64:, :] = jnp.broadcast_to(packed.reshape(16, 1, state), (16, 8, state)).astype(bf16)
+    blocks.append(jnp.broadcast_to(packed.reshape(16, 1, state), (16, 8, state)))
+    out[...] = jnp.concatenate(blocks, axis=1).astype(bf16)
 
 
 def spread_kernel(got, entering, out):
@@ -307,7 +308,7 @@
 
 
 def intra_kernel(
-    conv, gate, d_gated, step, cumul, cumul_t, normal, normal_halo, skip_gain,
+    conv, gate, d_gated, step, cumul, decay_log, normal, normal_halo, skip_gain,
     silus, d_gates, pushed, mixed, d_inputs, lefts, held_back, d_convs, bc, d_bc, sums_out, normal_t, halo_t,
 ):
     for source, target in ((normal, normal_t), (normal_halo, halo_t)):
@@ -348,7 +349,7 @@
         d_mixed = d_out * silu
         pushed[at, :] = (d_mixed * grown).astype(bf16)
         scores = mm_cols(cmat, bmat)
-        line = cumul_t[frame * heads : (frame + 1) * heads, :]
+        line = tri_sum_turned(triangle(rows, False), -jnp.exp(decay_log[...].reshape(1, -1)) * step[at, :])
         d_scores = jnp.zeros((rows, rows), f32)
         sums, by_size = [], []
         for pair in range(heads // 2):
@@ -543,8 +544,8 @@
     d_normal = d_normal + mm(d_step[...], step_proj[...])
     d_wide = norm_back(both[...], d_normal, gain[...])
     base[...] = d_wide[:rows] + mirror_wide(d_wide[rows:])
-    first = norm_back(low[8:, :], through[2 * rows : 2 * rows + 8], gain[...])
-    second = norm_back(mirror_exact(high[...])[8:, :], through[2 * rows + 8 :], gain[...])
+    first = norm_back(low[...].astype(f32)[8:], through[2 * rows : 2 * rows + 8], gain[...])
+    second = norm_back(mirror_exact(high[...]).astype(f32)[8:], through[2 * rows + 8 :], gain[...])
     at_start = (place[0] + place[1] + place[2]) == 0
     at_end = (place[0] + place[1] + place[2]) == 3 * (SIDE - 1)
     to_both[32:, :] = fold_rows(first * (1.0 - scalar_flag(at_start))).astype(bf16)
@@ -677,7 +678,7 @@
     low = lax.ppermute(sequence[rows - 16 :], "seq", upward)
     high = lax.ppermute(sequence[:16], "seq", downward)
     step_turned = step_proj.T
-    payload, both, normal, normal_halo, cot, gate, conv, d_gated, raw, step, cumul, cumul_t = call(
+    payload, both, normal, normal_halo, cot, gate, conv, d_gated, raw, step, cumul = call(
         pre_kernel,
         [
             ((SIDE, inner + 16, state), bf16),
@@ -691,7 +692,6 @@
             ((both_rows, heads), f32),
             ((both_rows, heads), f32),
             ((both_rows, heads), f32),
-            ((2 * heads, rows), f32),
         ],
         (
             sequence, upstream, low, high, norm_gain, in_proj, step_turned,
@@ -713,7 +713,7 @@
             ((width, both_rows), bf16),
             ((width, 32), bf16),
         ],
-        (conv, gate, d_gated, step, cumul, cumul_t, normal, normal_halo, skip_gain),
+        (conv, gate, d_gated, step, cumul, decay_log, normal, normal_halo, skip_gain),
         flops=8 * 10**9,
     )
     normal_t, halo_t = inner_values[-2:]

time: 165 us -> 165 us (level)
  no operation moved by 1% of the time
where the time goes in v11:
time: 165 us; the launch traced here: 164 us
  waiting for transfers between devices  46.3 us (28%)
  starting transfers between devices  45.8 us (28%)
  Pallas kernels  35.4 us (21%)
  blocking collectives  31.9 us (19%)
  local copies, waits for them, and re-layouts  3.06 us (2%)
    pallas_call x11, Pallas kernels, call(): pl.pallas_call(used, out_shape=[jax.ShapeDtypeStruct(shape, kind) for sha...  35.4 us
    all_to_all x2, blocking collectives, transpose_over(): return lax.all_to_all(parts, 'seq', 0, 0, axis_index_groups=groups)  31.9 us
    ppermute x9, waiting for transfers between devices, exchange(): lax.ppermute(parts[step], 'seq', axis_pairs(stride, step))  13.8 us
    all_to_all x2, waiting for transfers between devices, transpose_over(): return lax.all_to_all(parts, 'seq', 0, 0, axis_index_groups=groups)  13.5 us
    ppermute x1, starting transfers between devices, shards(): high = lax.ppermute(sequence[:16], 'seq', downward)  10.9 us
    ppermute x9, starting transfers between devices, exchange(): lax.ppermute(parts[step], 'seq', axis_pairs(stride, step))  10.8 us
    all_to_all x2, starting transfers between devices, transpose_over(): return lax.all_to_all(parts, 'seq', 0, 0, axis_index_groups=groups)  9.47 us
    ppermute x1, waiting for transfers between devices, shards(): low = lax.ppermute(sequence[rows - 16:], 'seq', upward)  8.8 us
  transfers between devices with their start and end apart: 21, of which 10 were waited for; matrix products, arithmetic and copies ran while one was open for 0% of the time, Pallas kernels for 8%

profile of v11, /device:TPU:6, one launch (start us, length us, event | category | flops | bytes accessed | tf_op | source)
XLA Modules:
  0.0 163.9 jit_solution(832786078026039559)
XLA Ops:
  0.6 0.7 fusion
  1.4 10.9 %collective-permute-start.1 = (bf16[16,512]{1,0:T(8,128)(2,1)S(1)}, bf16[16,512]{1,0:T(8,128)(2,1)S(1)}, u32[]{:S(2)}, u32[]{:S(2)}) collective-permute-start(bf16[16,512]{1,0:T(8,128)(2,1)S(1)} %get-tuple-element.128), channel_id=1, source_target_pairs={{4,0},{8,4},{12,8},{16,12},{20,16},{24,20},{28,24},{32,28},{36,32}... | collective-permute-start | bytes 49160 | tf_op jit(solution)/shard_map/ppermute | solution.py:679
  12.3 1.9 %collective-permute-start = (bf16[16,512]{1,0:T(8,128)(2,1)S(1)}, bf16[16,512]{1,0:T(8,128)(2,1)S(1)}, u32[]{:S(2)}, u32[]{:S(2)}) collective-permute-start(bf16[16,512]{1,0:T(8,128)(2,1)S(1)} %get-tuple-element.129), channel_id=1, source_target_pairs={{0,4},{4,8},{8,12},{12,16},{16,20},{20,24},{24,28},{28,32},{32,36}... | collective-permute-start | bytes 49160 | tf_op jit(solution)/shard_map/ppermute | solution.py:678
  14.2 0.0 collective-permute-done.1.refs_3_.refs_10_
  14.2 8.8 %collective-permute-done.refs_2_.refs_9_ = bf16[16,512]{1,0:T(8,128)(2,1)S(1)} collective-permute-done((bf16[16,512]{1,0:T(8,128)(2,1)S(1)}, bf16[16,512]{1,0:T(8,128)(2,1)S(1)}, u32[]{:S(2)}, u32[]{:S(2)}) %collective-permute-start) | collective-permute-done | bytes 16416 | tf_op jit(solution)/shard_map/ppermute | solution.py:678
  23.0 0.0 copy-done.8
  23.0 0.6 copy-done.9
  23.6 7.3 %shard_map.138 = (bf16[4,1040,128]{2,1,0:T(8,128)(2,1)}, bf16[256,512]{1,0:T(8,128)(2,1)}, bf16[256,512]{1,0:T(8,128)(2,1)}, bf16[32,512]{1,0:T(8,128)(2,1)}, bf...) custom-call(bf16[128,512]{1,0:T(8,128)(2,1)} %refs_0_.1, ...), custom_call_target="tpu_custom_call" | custom-call | flops 1000000000 | bytes 3746944 | tf_op jit(solution)/shard_map/pallas_call | solution.py:28
  31.0 17.6 %all_to_all.20.refs_0_ = bf16[4,1040,128]{2,1,0:T(8,128)(2,1)S(1)} all-to-all(bf16[4,1040,128]{2,1,0:T(8,128)(2,1)} %get-tuple-element.67), channel_id=1, replica_groups={{0,4,8,12},{16,20,24,28},{32,36,40,44},{48,52,56,60},{64,68,72,76},{80,..., dimensions={0} | all-to-all | bytes 2129920 | tf_op jit(solution)/shard_map/all_to_all | solution.py:645
  48.6 0.4 shard_map.139
  49.0 14.2 %all_to_all.21.refs_0_ = bf16[16,72,128]{2,1,0:T(8,128)(2,1)S(1)} all-to-all(bf16[16,72,128]{2,1,0:T(8,128)(2,1)S(1)} %shard_map.139), channel_id=1, replica_groups={{0,16,32,48,64,80,96,112,128,144,160,176,192,208,224,240},{4,20,36,52,6..., dimensions={0} | all-to-all | bytes 589824 | tf_op jit(solution)/shard_map/all_to_all | solution.py:645
  63.2 1.6 shard_map.140
  64.8 5.8 %all-to-all-start.2 = ((bf16[16,64,128]{2,1,0:T(8,128)(2,1)}), bf16[16,64,128]{2,1,0:T(8,128)(2,1)S(1)}, u32[]{:S(2)}, u32[]{:S(2)}) async-start(bf16[16,64,128]{2,1,0:T(8,128)(2,1)} %shard_map.140), calls=%async_computation.2 | async-start | bytes 524288 | tf_op jit(solution)/shard_map/all_to_all | solution.py:645
  70.6 9.8 %all-to-all-done.2.refs_1_ = bf16[16,64,128]{2,1,0:T(8,128)(2,1)S(1)} async-done(((bf16[16,64,128]{2,1,0:T(8,128)(2,1)}), bf16[16,64,128]{2,1,0:T(8,128)(2,1)S(1)}, u32[]{:S(2)}, u32[]{:S(2)}) %all-to-all-start.2) | async-done | bytes 262176 | tf_op jit(solution)/shard_map/all_to_all | solution.py:645
  80.3 1.3 shard_map.141
  81.7 3.7 %all-to-all-start.3 = ((bf16[4,1024,128]{2,1,0:T(8,128)(2,1)}), bf16[4,1024,128]{2,1,0:T(8,128)(2,1)S(1)}, u32[]{:S(2)}, u32[]{:S(2)}) async-start(bf16[4,1024,128]{2,1,0:T(8,128)(2,1)} %shard_map.141), calls=%async_computation.3 | async-start | bytes 2097152 | tf_op jit(solution)/shard_map/all_to_all | solution.py:645
  85.4 0.7 pad_add_fusion.refs_0_
  86.0 6.2 %shard_map.142 = (bf16[256,1024]{1,0:T(8,128)(2,1)}, bf16[256,1024]{1,0:T(8,128)(2,1)}, bf16[256,1024]{1,0:T(8,128)(2,1)}, bf16[256,1024]{1,0:T(8,128)(2,1)}, bf...) custom-call(bf16[256,1280]{1,0:T(8,128)(2,1)} %get-tuple-element.68., ...), custom_call_target="tpu_custom_call" | custom-call | flops 8000000000 | bytes 2031744 | tf_op jit(solution)/shard_map/pallas_call | solution.py:28
  92.3 3.8 %all-to-all-done.3.refs_1_ = bf16[4,1024,128]{2,1,0:T(8,128)(2,1)S(1)} async-done(((bf16[4,1024,128]{2,1,0:T(8,128)(2,1)}), bf16[4,1024,128]{2,1,0:T(8,128)(2,1)S(1)}, u32[]{:S(2)}, u32[]{:S(2)}) %all-to-all-start.3) | async-done | bytes 1048608 | tf_op jit(solution)/shard_map/all_to_all | solution.py:645
  96.0 1.0 copy-done.7
  97.0 9.4 %shard_map.143 = (bf16[256,1024]{1,0:T(8,128)(2,1)}, bf16[256,1024]{1,0:T(8,128)(2,1)}, bf16[256,1280]{1,0:T(8,128)(2,1)}, f32[8,1280]{1,0:T(8,128)}, f32[8,1280...) custom-call(s32[3]{0:T(128)} %pad_add_fusion.refs_0_, ...), custom_call_target="tpu_custom_call" | custom-call | flops 1000000000 | bytes 6426764 | tf_op jit(solution)/shard_map/pallas_call | solution.py:28
  106.5 2.5 %collective-permute-start.2 = (bf16[128,1664]{1,0:T(8,128)(2,1)}, bf16[128,1664]{1,0:T(8,128)(2,1)S(1)}, u32[]{:S(2)}, u32[]{:S(2)}) collective-permute-start(bf16[128,1664]{1,0:T(8,128)(2,1)} %get-tuple-element.98), channel_id=1, source_target_pairs={{0,64},{4,68},{8,72},{12,76},{16,80},{20,84},{24,88},{28,92},{32,9... | collective-permute-start | bytes 1277960 | tf_op jit(solution)/shard_map/ppermute | solution.py:639
  109.0 0.0 collective-permute-start.3
  109.0 0.6 collective-permute-start.4
  109.6 2.7 %collective-permute-start.5 = (bf16[128,1664]{1,0:T(8,128)(2,1)}, bf16[128,1664]{1,0:T(8,128)(2,1)S(1)}, u32[]{:S(2)}, u32[]{:S(2)}) collective-permute-start(bf16[128,1664]{1,0:T(8,128)(2,1)} %get-tuple-element.103), channel_id=1, source_target_pairs={{0,12},{4,0},{8,4},{12,8},{16,28},{20,16},{24,20},{28,24},{32,44},... | collective-permute-start | bytes 1277960 | tf_op jit(solution)/shard_map/ppermute | solution.py:640
  112.2 6.4 %shard_map.144 = (bf16[128,512]{1,0:T(8,128)(2,1)}, f32[128,512]{1,0:T(8,128)}, bf16[64,128]{1,0:T(8,128)(2,1)}) custom-call(s32[3]{0:T(128)} %pad_add_fusion.refs_0_, bf16[256,512]{1,0:T(8,128)(2,1)} %get-tuple-element.66.refs_1_, f32[512]{0:T(512)} %refs_2_.1, bf16[256,1024]{1,0:T(8,128)(2,1)} %get-tuple-element.90.refs_3_, bf16[1024,512]{1,0:T(8,128)(2,1)} %refs_4_.3, ...), custom_call_target="tpu_custom_call" | custom-call | flops 8000000000 | bytes 5515276 | tf_op jit(solution)/shard_map/pallas_call | solution.py:28
  118.6 0.0 collective-permute-done.2.refs_1_.refs_2_
  118.6 0.0 collective-permute-done.3.refs_2_.refs_3_
  118.6 1.9 %collective-permute-done.4.refs_4_.refs_7_ = bf16[128,1664]{1,0:T(8,128)(2,1)S(1)} collective-permute-done((bf16[128,1664]{1,0:T(8,128)(2,1)}, bf16[128,1664]{1,0:T(8,128)(2,1)S(1)}, u32[]{:S(2)}, u32[]{:S(2)}) %collective-permute-start.4) | collective-permute-done | bytes 426016 | tf_op jit(solution)/shard_map/ppermute | solution.py:639
  120.6 0.0 collective-permute-done.5.refs_5_.refs_8_
  120.6 0.0 copy-start.6
  120.6 0.7 copy-done.6
  121.3 0.2 shard_map.145
  121.5 0.1 collective-permute-start.8
  121.6 3.6 %collective-permute-start.9 = (bf16[64,1792]{1,0:T(8,128)(2,1)S(1)}, bf16[64,1792]{1,0:T(8,128)(2,1)S(1)}, u32[]{:S(2)}, u32[]{:S(2)}) collective-permute-start(bf16[64,1792]{1,0:T(8,128)(2,1)S(1)} %get-tuple-element.109), channel_id=1, source_target_pairs={{0,12},{4,0},{8,4},{12,8},{16,28},{20,16},{24,20},{28,24},{32,44},... | collective-permute-start | bytes 688136 | tf_op jit(solution)/shard_map/ppermute | solution.py:640
  125.2 3.4 %collective-permute-start.6 = (bf16[64,1664]{1,0:T(8,128)(2,1)S(1)}, bf16[64,1664]{1,0:T(8,128)(2,1)S(1)}, u32[]{:S(2)}, u32[]{:S(2)}) collective-permute-start(bf16[64,1664]{1,0:T(8,128)(2,1)S(1)} %get-tuple-element.105), channel_id=1, source_target_pairs={{0,64},{4,68},{8,72},{12,76},{16,80},{20,84},{24,88},{28,92},{32,9... | collective-permute-start | bytes 638984 | tf_op jit(solution)/shard_map/ppermute | solution.py:639
  128.6 0.0 collective-permute-start.7
  128.6 3.4 %collective-permute-done.6.refs_4_ = bf16[64,1664]{1,0:T(8,128)(2,1)S(1)} collective-permute-done((bf16[64,1664]{1,0:T(8,128)(2,1)S(1)}, bf16[64,1664]{1,0:T(8,128)(2,1)S(1)}, u32[]{:S(2)}, u32[]{:S(2)}) %collective-permute-start.6) | collective-permute-done | bytes 213024 | tf_op jit(solution)/shard_map/ppermute | solution.py:639
  131.9 4.8 %collective-permute-done.7.refs_5_ = bf16[64,1664]{1,0:T(8,128)(2,1)S(1)} collective-permute-done((bf16[64,1664]{1,0:T(8,128)(2,1)S(1)}, bf16[64,1664]{1,0:T(8,128)(2,1)S(1)}, u32[]{:S(2)}, u32[]{:S(2)}) %collective-permute-start.7) | collective-permute-done | bytes 213024 | tf_op jit(solution)/shard_map/ppermute | solution.py:640
  136.8 0.0 collective-permute-done.8.refs_9_
  136.8 0.0 collective-permute-done.9.refs_10_
  136.8 0.0 copy-done.1
  136.8 0.0 copy-done.2
  136.8 1.1 shard_map.146
  137.9 0.1 collective-permute-start.10
  137.9 0.1 collective-permute-start.13
  138.0 2.0 %collective-permute-start.15 = (bf16[32,1792]{1,0:T(8,128)(2,1)S(1)}, bf16[32,1792]{1,0:T(8,128)(2,1)S(1)}, u32[]{:S(2)}, u32[]{:S(2)}) collective-permute-start(bf16[32,1792]{1,0:T(8,128)(2,1)S(1)} %get-tuple-element.117), channel_id=1, source_target_pairs={{0,192},{4,196},{8,200},{12,204},{16,208},{20,212},{24,216},{28,22... | collective-permute-start | bytes 344072 | tf_op jit(solution)/shard_map/ppermute | solution.py:634
  140.1 3.3 %collective-permute-start.11 = (bf16[32,1664]{1,0:T(8,128)(2,1)S(1)}, bf16[32,1664]{1,0:T(8,128)(2,1)S(1)}, u32[]{:S(2)}, u32[]{:S(2)}) collective-permute-start(bf16[32,1664]{1,0:T(8,128)(2,1)S(1)} %get-tuple-element.112), channel_id=1, source_target_pairs={{0,8},{4,12},{8,0},{12,4},{16,24},{20,28},{24,16},{28,20},{32,40},... | collective-permute-start | bytes 319496 | tf_op jit(solution)/shard_map/ppermute | solution.py:634
  143.4 0.6 collective-permute-start.12
  144.0 0.0 collective-permute-done.10.refs_2_
  144.0 0.0 collective-permute-start.14
  144.0 2.3 %collective-permute-done.11.refs_3_ = bf16[32,1664]{1,0:T(8,128)(2,1)S(1)} collective-permute-done((bf16[32,1664]{1,0:T(8,128)(2,1)S(1)}, bf16[32,1664]{1,0:T(8,128)(2,1)S(1)}, u32[]{:S(2)}, u32[]{:S(2)}) %collective-permute-start.11) | collective-permute-done | bytes 106528 | tf_op jit(solution)/shard_map/ppermute | solution.py:634
  146.3 1.8 %collective-permute-done.12.refs_4_ = bf16[32,1664]{1,0:T(8,128)(2,1)S(1)} collective-permute-done((bf16[32,1664]{1,0:T(8,128)(2,1)S(1)}, bf16[32,1664]{1,0:T(8,128)(2,1)S(1)}, u32[]{:S(2)}, u32[]{:S(2)}) %collective-permute-start.12) | collective-permute-done | bytes 106528 | tf_op jit(solution)/shard_map/ppermute | solution.py:634
  148.1 2.1 %collective-permute-done.14.refs_7_ = bf16[32,1664]{1,0:T(8,128)(2,1)S(1)} collective-permute-done((bf16[32,1664]{1,0:T(8,128)(2,1)S(1)}, bf16[32,1664]{1,0:T(8,128)(2,1)S(1)}, u32[]{:S(2)}, u32[]{:S(2)}) %collective-permute-start.14) | collective-permute-done | bytes 106528 | tf_op jit(solution)/shard_map/ppermute | solution.py:634
  150.2 0.0 collective-permute-done.13.refs_6_
  150.2 0.0 collective-permute-done.15.refs_8_
  150.2 0.7 shard_map.147
  150.9 0.1 collective-permute-start.16
  151.0 4.1 %collective-permute-start.18 = (bf16[16,1920]{1,0:T(8,128)(2,1)S(1)}, bf16[16,1920]{1,0:T(8,128)(2,1)S(1)}, u32[]{:S(2)}, u32[]{:S(2)}) collective-permute-start(bf16[16,1920]{1,0:T(8,128)(2,1)S(1)} %get-tuple-element.122), channel_id=1, source_target_pairs={{0,48},{4,52},{8,56},{12,60},{16,0},{20,4},{24,8},{28,12},{32,16},... | collective-permute-start | bytes 184328 | tf_op jit(solution)/shard_map/ppermute | solution.py:634
  155.1 0.5 collective-permute-start.17
  155.6 7.6 %collective-permute-done.17.refs_2_ = bf16[16,1664]{1,0:T(8,128)(2,1)S(1)} collective-permute-done((bf16[16,1664]{1,0:T(8,128)(2,1)S(1)}, bf16[16,1664]{1,0:T(8,128)(2,1)S(1)}, u32[]{:S(2)}, u32[]{:S(2)}) %collective-permute-start.17) | collective-permute-done | bytes 53280 | tf_op jit(solution)/shard_map/ppermute | solution.py:634
  163.2 0.0 collective-permute-done.16.refs_1_
  163.2 0.0 collective-permute-done.18.refs_3_
  163.2 0.7 shard_map.148
  (13 shorter events, 0.0 us)
Async XLA Ops:
  1.4 12.9 %collective-permute-start.1 = (bf16[16,512]{1,0:T(8,128)(2,1)S(1)}, bf16[16,512]{1,0:T(8,128)(2,1)S(1)}, u32[]{:S(2)}, u32[]{:S(2)}) collective-permute-start(bf16[16,512]{1,0:T(8,128)(2,1)S(1)} %get-tuple-element.128), channel_id=1, source_target_pairs={{4,0},{8,4},{12,8},{16,12},{20,16},{24,20},{28,24},{32,28},{36,32}... | collective-permute-start | bytes 49160 | tf_op jit(solution)/shard_map/ppermute | solution.py:679
  12.3 10.8 %collective-permute-start = (bf16[16,512]{1,0:T(8,128)(2,1)S(1)}, bf16[16,512]{1,0:T(8,128)(2,1)S(1)}, u32[]{:S(2)}, u32[]{:S(2)}) collective-permute-start(bf16[16,512]{1,0:T(8,128)(2,1)S(1)} %get-tuple-element.129), channel_id=1, source_target_pairs={{0,4},{4,8},{8,12},{12,16},{16,20},{20,24},{24,28},{28,32},{32,36}... | collective-permute-start | bytes 49160 | tf_op jit(solution)/shard_map/ppermute | solution.py:678
  14.2 8.8 %copy-start.8 = (bf16[16,512]{1,0:T(8,128)(2,1)}, bf16[16,512]{1,0:T(8,128)(2,1)S(1)}, u32[]{:S(2)}) copy-start(bf16[16,512]{1,0:T(8,128)(2,1)S(1)} %collective-permute-done.1.refs_3_.refs_10_) | copy-start | bytes 49156
  23.0 0.6 copy-start.9
  64.8 15.5 %all-to-all-start.2 = ((bf16[16,64,128]{2,1,0:T(8,128)(2,1)}), bf16[16,64,128]{2,1,0:T(8,128)(2,1)S(1)}, u32[]{:S(2)}, u32[]{:S(2)}) async-start(bf16[16,64,128]{2,1,0:T(8,128)(2,1)} %shard_map.140), calls=%async_computation.2 | async-start | bytes 524288 | tf_op jit(solution)/shard_map/all_to_all | solution.py:645
  81.7 14.4 %all-to-all-start.3 = ((bf16[4,1024,128]{2,1,0:T(8,128)(2,1)}), bf16[4,1024,128]{2,1,0:T(8,128)(2,1)S(1)}, u32[]{:S(2)}, u32[]{:S(2)}) async-start(bf16[4,1024,128]{2,1,0:T(8,128)(2,1)} %shard_map.141), calls=%async_computation.3 | async-start | bytes 2097152 | tf_op jit(solution)/shard_map/all_to_all | solution.py:645
  96.0 1.0 copy-start.7
  106.5 12.1 %collective-permute-start.2 = (bf16[128,1664]{1,0:T(8,128)(2,1)}, bf16[128,1664]{1,0:T(8,128)(2,1)S(1)}, u32[]{:S(2)}, u32[]{:S(2)}) collective-permute-start(bf16[128,1664]{1,0:T(8,128)(2,1)} %get-tuple-element.98), channel_id=1, source_target_pairs={{0,64},{4,68},{8,72},{12,76},{16,80},{20,84},{24,88},{28,92},{32,9... | collective-permute-start | bytes 1277960 | tf_op jit(solution)/shard_map/ppermute | solution.py:639
  109.0 9.7 %collective-permute-start.3 = (bf16[128,1664]{1,0:T(8,128)(2,1)}, bf16[128,1664]{1,0:T(8,128)(2,1)S(1)}, u32[]{:S(2)}, u32[]{:S(2)}) collective-permute-start(bf16[128,1664]{1,0:T(8,128)(2,1)} %get-tuple-element.99), channel_id=1, source_target_pairs={{0,192},{4,196},{8,200},{12,204},{16,208},{20,212},{24,216},{28,22... | collective-permute-start | bytes 1277960 | tf_op jit(solution)/shard_map/ppermute | solution.py:640
  109.0 11.6 %collective-permute-start.4 = (bf16[128,1664]{1,0:T(8,128)(2,1)}, bf16[128,1664]{1,0:T(8,128)(2,1)S(1)}, u32[]{:S(2)}, u32[]{:S(2)}) collective-permute-start(bf16[128,1664]{1,0:T(8,128)(2,1)} %get-tuple-element.102), channel_id=1, source_target_pairs={{0,4},{4,8},{8,12},{12,0},{16,20},{20,24},{24,28},{28,16},{32,36},... | collective-permute-start | bytes 1277960 | tf_op jit(solution)/shard_map/ppermute | solution.py:639
  109.6 11.0 %collective-permute-start.5 = (bf16[128,1664]{1,0:T(8,128)(2,1)}, bf16[128,1664]{1,0:T(8,128)(2,1)S(1)}, u32[]{:S(2)}, u32[]{:S(2)}) collective-permute-start(bf16[128,1664]{1,0:T(8,128)(2,1)} %get-tuple-element.103), channel_id=1, source_target_pairs={{0,12},{4,0},{8,4},{12,8},{16,28},{20,16},{24,20},{28,24},{32,44},... | collective-permute-start | bytes 1277960 | tf_op jit(solution)/shard_map/ppermute | solution.py:640
  112.2 8.3 %copy-start.3 = (bf16[128,1664]{1,0:T(8,128)(2,1)S(1)}, bf16[128,1664]{1,0:T(8,128)(2,1)}, u32[]{:S(2)}) copy-start(bf16[128,1664]{1,0:T(8,128)(2,1)} %get-tuple-element.100.refs_0_) | copy-start | bytes 1277956
  112.2 8.3 %copy-start.4 = (bf16[128,1664]{1,0:T(8,128)(2,1)S(1)}, bf16[128,1664]{1,0:T(8,128)(2,1)}, u32[]{:S(2)}) copy-start(bf16[128,1664]{1,0:T(8,128)(2,1)} %get-tuple-element.101.refs_3_) | copy-start | bytes 1277956
  120.6 0.7 copy-start.6
  121.3 15.5 %copy-start = (s32[3]{0:T(128)S(1)}, s32[3]{0:T(128)}, u32[]{:S(2)}) copy-start(s32[3]{0:T(128)} %pad_add_fusion.refs_0_) | copy-start | bytes 40
  121.3 15.5 %copy-start.1 = (bf16[128,1664]{1,0:T(8,128)(2,1)S(1)}, bf16[128,1664]{1,0:T(8,128)(2,1)}, u32[]{:S(2)}) copy-start(bf16[128,1664]{1,0:T(8,128)(2,1)} %get-tuple-element.97.refs_1_) | copy-start | bytes 1277956
  121.3 15.5 %copy-start.2 = (bf16[128,1664]{1,0:T(8,128)(2,1)S(1)}, bf16[128,1664]{1,0:T(8,128)(2,1)}, u32[]{:S(2)}) copy-start(bf16[128,1664]{1,0:T(8,128)(2,1)} %get-tuple-element.107.refs_6_) | copy-start | bytes 1277956
  121.5 15.3 %collective-permute-start.8 = (bf16[64,1792]{1,0:T(8,128)(2,1)S(1)}, bf16[64,1792]{1,0:T(8,128)(2,1)S(1)}, u32[]{:S(2)}, u32[]{:S(2)}) collective-permute-start(bf16[64,1792]{1,0:T(8,128)(2,1)S(1)} %get-tuple-element.108), channel_id=1, source_target_pairs={{0,4},{4,8},{8,12},{12,0},{16,20},{20,24},{24,28},{28,16},{32,36},... | collective-permute-start | bytes 688136 | tf_op jit(solution)/shard_map/ppermute | solution.py:639
  121.6 15.2 %collective-permute-start.9 = (bf16[64,1792]{1,0:T(8,128)(2,1)S(1)}, bf16[64,1792]{1,0:T(8,128)(2,1)S(1)}, u32[]{:S(2)}, u32[]{:S(2)}) collective-permute-start(bf16[64,1792]{1,0:T(8,128)(2,1)S(1)} %get-tuple-element.109), channel_id=1, source_target_pairs={{0,12},{4,0},{8,4},{12,8},{16,28},{20,16},{24,20},{28,24},{32,44},... | collective-permute-start | bytes 688136 | tf_op jit(solution)/shard_map/ppermute | solution.py:640
  125.2 6.7 %collective-permute-start.6 = (bf16[64,1664]{1,0:T(8,128)(2,1)S(1)}, bf16[64,1664]{1,0:T(8,128)(2,1)S(1)}, u32[]{:S(2)}, u32[]{:S(2)}) collective-permute-start(bf16[64,1664]{1,0:T(8,128)(2,1)S(1)} %get-tuple-element.105), channel_id=1, source_target_pairs={{0,64},{4,68},{8,72},{12,76},{16,80},{20,84},{24,88},{28,92},{32,9... | collective-permute-start | bytes 638984 | tf_op jit(solution)/shard_map/ppermute | solution.py:639
  128.6 8.2 %collective-permute-start.7 = (bf16[64,1664]{1,0:T(8,128)(2,1)S(1)}, bf16[64,1664]{1,0:T(8,128)(2,1)S(1)}, u32[]{:S(2)}, u32[]{:S(2)}) collective-permute-start(bf16[64,1664]{1,0:T(8,128)(2,1)S(1)} %get-tuple-element.106), channel_id=1, source_target_pairs={{0,192},{4,196},{8,200},{12,204},{16,208},{20,212},{24,216},{28,22... | collective-permute-start | bytes 638984 | tf_op jit(solution)/shard_map/ppermute | solution.py:640
  137.9 6.1 %collective-permute-start.10 = (bf16[32,1664]{1,0:T(8,128)(2,1)S(1)}, bf16[32,1664]{1,0:T(8,128)(2,1)S(1)}, u32[]{:S(2)}, u32[]{:S(2)}) collective-permute-start(bf16[32,1664]{1,0:T(8,128)(2,1)S(1)} %get-tuple-element.111), channel_id=1, source_target_pairs={{0,4},{4,8},{8,12},{12,0},{16,20},{20,24},{24,28},{28,16},{32,36},... | collective-permute-start | bytes 319496 | tf_op jit(solution)/shard_map/ppermute | solution.py:634
  137.9 12.2 %collective-permute-start.13 = (bf16[32,1792]{1,0:T(8,128)(2,1)S(1)}, bf16[32,1792]{1,0:T(8,128)(2,1)S(1)}, u32[]{:S(2)}, u32[]{:S(2)}) collective-permute-start(bf16[32,1792]{1,0:T(8,128)(2,1)S(1)} %get-tuple-element.115), channel_id=1, source_target_pairs={{0,64},{4,68},{8,72},{12,76},{16,80},{20,84},{24,88},{28,92},{32,9... | collective-permute-start | bytes 344072 | tf_op jit(solution)/shard_map/ppermute | solution.py:634
  138.0 12.1 %collective-permute-start.15 = (bf16[32,1792]{1,0:T(8,128)(2,1)S(1)}, bf16[32,1792]{1,0:T(8,128)(2,1)S(1)}, u32[]{:S(2)}, u32[]{:S(2)}) collective-permute-start(bf16[32,1792]{1,0:T(8,128)(2,1)S(1)} %get-tuple-element.117), channel_id=1, source_target_pairs={{0,192},{4,196},{8,200},{12,204},{16,208},{20,212},{24,216},{28,22... | collective-permute-start | bytes 344072 | tf_op jit(solution)/shard_map/ppermute | solution.py:634
  140.1 6.2 %collective-permute-start.11 = (bf16[32,1664]{1,0:T(8,128)(2,1)S(1)}, bf16[32,1664]{1,0:T(8,128)(2,1)S(1)}, u32[]{:S(2)}, u32[]{:S(2)}) collective-permute-start(bf16[32,1664]{1,0:T(8,128)(2,1)S(1)} %get-tuple-element.112), channel_id=1, source_target_pairs={{0,8},{4,12},{8,0},{12,4},{16,24},{20,28},{24,16},{28,20},{32,40},... | collective-permute-start | bytes 319496 | tf_op jit(solution)/shard_map/ppermute | solution.py:634
  143.4 4.7 %collective-permute-start.12 = (bf16[32,1664]{1,0:T(8,128)(2,1)S(1)}, bf16[32,1664]{1,0:T(8,128)(2,1)S(1)}, u32[]{:S(2)}, u32[]{:S(2)}) collective-permute-start(bf16[32,1664]{1,0:T(8,128)(2,1)S(1)} %get-tuple-element.113), channel_id=1, source_target_pairs={{0,12},{4,0},{8,4},{12,8},{16,28},{20,16},{24,20},{28,24},{32,44},... | collective-permute-start | bytes 319496 | tf_op jit(solution)/shard_map/ppermute | solution.py:634
  144.0 6.2 %collective-permute-start.14 = (bf16[32,1664]{1,0:T(8,128)(2,1)S(1)}, bf16[32,1664]{1,0:T(8,128)(2,1)S(1)}, u32[]{:S(2)}, u32[]{:S(2)}) collective-permute-start(bf16[32,1664]{1,0:T(8,128)(2,1)S(1)} %get-tuple-element.116), channel_id=1, source_target_pairs={{0,128},{4,132},{8,136},{12,140},{16,144},{20,148},{24,152},{28,15... | collective-permute-start | bytes 319496 | tf_op jit(solution)/shard_map/ppermute | solution.py:634
  150.2 13.0 %copy-start.5 = (f32[128,512]{1,0:T(8,128)S(1)}, f32[128,512]{1,0:T(8,128)}, u32[]{:S(2)}) copy-start(f32[128,512]{1,0:T(8,128)} %get-tuple-element.124.refs_5_) | copy-start | bytes 786436
  150.9 12.3 %collective-permute-start.16 = (bf16[16,1920]{1,0:T(8,128)(2,1)S(1)}, bf16[16,1920]{1,0:T(8,128)(2,1)S(1)}, u32[]{:S(2)}, u32[]{:S(2)}) collective-permute-start(bf16[16,1920]{1,0:T(8,128)(2,1)S(1)} %get-tuple-element.120), channel_id=1, source_target_pairs={{0,16},{4,20},{8,24},{12,28},{16,32},{20,36},{24,40},{28,44},{32,4... | collective-permute-start | bytes 184328 | tf_op jit(solution)/shard_map/ppermute | solution.py:634
  151.0 12.2 %collective-permute-start.18 = (bf16[16,1920]{1,0:T(8,128)(2,1)S(1)}, bf16[16,1920]{1,0:T(8,128)(2,1)S(1)}, u32[]{:S(2)}, u32[]{:S(2)}) collective-permute-start(bf16[16,1920]{1,0:T(8,128)(2,1)S(1)} %get-tuple-element.122), channel_id=1, source_target_pairs={{0,48},{4,52},{8,56},{12,60},{16,0},{20,4},{24,8},{28,12},{32,16},... | collective-permute-start | bytes 184328 | tf_op jit(solution)/shard_map/ppermute | solution.py:634
  155.1 8.1 %collective-permute-start.17 = (bf16[16,1664]{1,0:T(8,128)(2,1)S(1)}, bf16[16,1664]{1,0:T(8,128)(2,1)S(1)}, u32[]{:S(2)}, u32[]{:S(2)}) collective-permute-start(bf16[16,1664]{1,0:T(8,128)(2,1)S(1)} %get-tuple-element.121), channel_id=1, source_target_pairs={{0,32},{4,36},{8,40},{12,44},{16,48},{20,52},{24,56},{28,60},{32,0... | collective-permute-start | bytes 159752 | tf_op jit(solution)/shard_map/ppermute | solution.py:634

commit v12 on v8

--- a/solution.py
+++ b/solution.py
@@ -245,9 +245,10 @@
     inner = got.shape[1] - 16
     part = inner // SIDE
     totals = tails_of(got, inner)
+    blocks = []
     for place in range(4):
         block = chain(got, totals, place, jnp.zeros((part, state), f32), lambda at, value: None)
-        out[:, 16 * place : 16 * place + 16, :] = block.reshape(16, 16, state).astype(bf16)
+        blocks.append(block.reshape(16, 16, state))
     lanes = iota((16, state), 1)
     packed = jnp.zeros((16, state), f32)
     for frame in range(2):
@@ -257,7 +258,8 @@
         packed = pack_column(packed, column, lanes, frame)
     chosen = ones_where(iota((16, 16), 1) == iota((16, 16), 0) // SIDE)
     packed = mm(chosen, packed.astype(bf16))
-    out[:, 64:, :] = jnp.broadcast_to(packed.reshape(16, 1, state), (16, 8, state)).astype(bf16)
+    blocks.append(jnp.broadcast_to(packed.reshape(16, 1, state), (16, 8, state)))
+    out[...] = jnp.concatenate(blocks, axis=1).astype(bf16)
 
 
 def spread_kernel(got, entering, out):
@@ -543,8 +545,8 @@
     d_normal = d_normal + mm(d_step[...], step_proj[...])
     d_wide = norm_back(both[...], d_normal, gain[...])
     base[...] = d_wide[:rows] + mirror_wide(d_wide[rows:])
-    first = norm_back(low[8:, :], through[2 * rows : 2 * rows + 8], gain[...])
-    second = norm_back(mirror_exact(high[...])[8:, :], through[2 * rows + 8 :], gain[...])
+    first = norm_back(low[...].astype(f32)[8:], through[2 * rows : 2 * rows + 8], gain[...])
+    second = norm_back(mirror_exact(high[...]).astype(f32)[8:], through[2 * rows + 8 :], gain[...])
     at_start = (place[0] + place[1] + place[2]) == 0
     at_end = (place[0] + place[1] + place[2]) == 3 * (SIDE - 1)
     to_both[32:, :] = fold_rows(first * (1.0 - scalar_flag(at_start))).astype(bf16)

time: 165 us -> 165 us (level)
  no operation moved by 1% of the time
where the time goes in v12:
time: 165 us; the launch traced here: 164 us
  waiting for transfers between devices  46.3 us (28%)
  starting transfers between devices  45.9 us (28%)
  Pallas kernels  35 us (21%)
  blocking collectives  31.9 us (19%)
  local copies, waits for them, and re-layouts  3.06 us (2%)
    pallas_call x11, Pallas kernels, call(): pl.pallas_call(used, out_shape=[jax.ShapeDtypeStruct(shape, kind) for sha...  35 us
    all_to_all x2, blocking collectives, transpose_over(): return lax.all_to_all(parts, 'seq', 0, 0, axis_index_groups=groups)  31.9 us
    ppermute x9, waiting for transfers between devices, exchange(): lax.ppermute(parts[step], 'seq', axis_pairs(stride, step))  13.8 us
    all_to_all x2, waiting for transfers between devices, transpose_over(): return lax.all_to_all(parts, 'seq', 0, 0, axis_index_groups=groups)  13.6 us
    ppermute x1, starting transfers between devices, shards(): high = lax.ppermute(sequence[:16], 'seq', downward)  10.9 us
    ppermute x9, starting transfers between devices, exchange(): lax.ppermute(parts[step], 'seq', axis_pairs(stride, step))  10.8 us
    all_to_all x2, starting transfers between devices, transpose_over(): return lax.all_to_all(parts, 'seq', 0, 0, axis_index_groups=groups)  9.47 us
    ppermute x1, waiting for transfers between devices, shards(): low = lax.ppermute(sequence[rows - 16:], 'seq', upward)  8.8 us
  transfers between devices with their start and end apart: 21, of which 10 were waited for; matrix products, arithmetic and copies ran while one was open for 0% of the time, Pallas kernels for 8%

profile of v12, /device:TPU:6, one launch (start us, length us, event | category | flops | bytes accessed | tf_op | source)
XLA Modules:
  0.0 163.6 jit_solution(4212428968502631383)
XLA Ops:
  0.6 0.7 fusion
  1.4 10.9 %collective-permute-start.1 = (bf16[16,512]{1,0:T(8,128)(2,1)S(1)}, bf16[16,512]{1,0:T(8,128)(2,1)S(1)}, u32[]{:S(2)}, u32[]{:S(2)}) collective-permute-start(bf16[16,512]{1,0:T(8,128)(2,1)S(1)} %get-tuple-element.130), channel_id=1, source_target_pairs={{4,0},{8,4},{12,8},{16,12},{20,16},{24,20},{28,24},{32,28},{36,32}... | collective-permute-start | bytes 49160 | tf_op jit(solution)/shard_map/ppermute | solution.py:680
  12.3 1.9 %collective-permute-start = (bf16[16,512]{1,0:T(8,128)(2,1)S(1)}, bf16[16,512]{1,0:T(8,128)(2,1)S(1)}, u32[]{:S(2)}, u32[]{:S(2)}) collective-permute-start(bf16[16,512]{1,0:T(8,128)(2,1)S(1)} %get-tuple-element.131), channel_id=1, source_target_pairs={{0,4},{4,8},{8,12},{12,16},{16,20},{20,24},{24,28},{28,32},{32,36}... | collective-permute-start | bytes 49160 | tf_op jit(solution)/shard_map/ppermute | solution.py:679
  14.2 0.0 collective-permute-done.1.refs_3_.refs_10_
  14.2 8.8 %collective-permute-done.refs_2_.refs_9_ = bf16[16,512]{1,0:T(8,128)(2,1)S(1)} collective-permute-done((bf16[16,512]{1,0:T(8,128)(2,1)S(1)}, bf16[16,512]{1,0:T(8,128)(2,1)S(1)}, u32[]{:S(2)}, u32[]{:S(2)}) %collective-permute-start) | collective-permute-done | bytes 16416 | tf_op jit(solution)/shard_map/ppermute | solution.py:679
  23.0 0.0 copy-done.8
  23.0 0.6 copy-done.9
  23.6 7.0 %shard_map.138 = (bf16[4,1040,128]{2,1,0:T(8,128)(2,1)}, bf16[256,512]{1,0:T(8,128)(2,1)}, bf16[256,512]{1,0:T(8,128)(2,1)}, bf16[32,512]{1,0:T(8,128)(2,1)}, bf...) custom-call(bf16[128,512]{1,0:T(8,128)(2,1)} %refs_0_.1, ...), custom_call_target="tpu_custom_call" | custom-call | flops 1000000000 | bytes 3746944 | tf_op jit(solution)/shard_map/pallas_call | solution.py:28
  30.6 17.6 %all_to_all.20.refs_0_ = bf16[4,1040,128]{2,1,0:T(8,128)(2,1)S(1)} all-to-all(bf16[4,1040,128]{2,1,0:T(8,128)(2,1)} %get-tuple-element.68), channel_id=1, replica_groups={{0,4,8,12},{16,20,24,28},{32,36,40,44},{48,52,56,60},{64,68,72,76},{80,..., dimensions={0} | all-to-all | bytes 2129920 | tf_op jit(solution)/shard_map/all_to_all | solution.py:646
  48.3 0.4 shard_map.139
  48.6 14.2 %all_to_all.21.refs_0_ = bf16[16,72,128]{2,1,0:T(8,128)(2,1)S(1)} all-to-all(bf16[16,72,128]{2,1,0:T(8,128)(2,1)S(1)} %shard_map.139), channel_id=1, replica_groups={{0,16,32,48,64,80,96,112,128,144,160,176,192,208,224,240},{4,20,36,52,6..., dimensions={0} | all-to-all | bytes 589824 | tf_op jit(solution)/shard_map/all_to_all | solution.py:646
  62.9 1.6 shard_map.140
  64.5 5.8 %all-to-all-start.2 = ((bf16[16,64,128]{2,1,0:T(8,128)(2,1)}), bf16[16,64,128]{2,1,0:T(8,128)(2,1)S(1)}, u32[]{:S(2)}, u32[]{:S(2)}) async-start(bf16[16,64,128]{2,1,0:T(8,128)(2,1)} %shard_map.140), calls=%async_computation.2 | async-start | bytes 524288 | tf_op jit(solution)/shard_map/all_to_all | solution.py:646
  70.2 9.8 %all-to-all-done.2.refs_1_ = bf16[16,64,128]{2,1,0:T(8,128)(2,1)S(1)} async-done(((bf16[16,64,128]{2,1,0:T(8,128)(2,1)}), bf16[16,64,128]{2,1,0:T(8,128)(2,1)S(1)}, u32[]{:S(2)}, u32[]{:S(2)}) %all-to-all-start.2) | async-done | bytes 262176 | tf_op jit(solution)/shard_map/all_to_all | solution.py:646
  80.0 1.3 shard_map.141
  81.3 3.7 %all-to-all-start.3 = ((bf16[4,1024,128]{2,1,0:T(8,128)(2,1)}), bf16[4,1024,128]{2,1,0:T(8,128)(2,1)S(1)}, u32[]{:S(2)}, u32[]{:S(2)}) async-start(bf16[4,1024,128]{2,1,0:T(8,128)(2,1)} %shard_map.141), calls=%async_computation.3 | async-start | bytes 2097152 | tf_op jit(solution)/shard_map/all_to_all | solution.py:646
  85.0 0.7 pad_add_fusion.refs_0_
  85.7 6.2 %shard_map.142 = (bf16[256,1024]{1,0:T(8,128)(2,1)}, bf16[256,1024]{1,0:T(8,128)(2,1)}, bf16[256,1024]{1,0:T(8,128)(2,1)}, bf16[256,1024]{1,0:T(8,128)(2,1)}, bf...) custom-call(bf16[256,1280]{1,0:T(8,128)(2,1)} %get-tuple-element.69., ...), custom_call_target="tpu_custom_call" | custom-call | flops 8000000000 | bytes 2048064 | tf_op jit(solution)/shard_map/pallas_call | solution.py:28
  91.9 3.8 %all-to-all-done.3.refs_1_ = bf16[4,1024,128]{2,1,0:T(8,128)(2,1)S(1)} async-done(((bf16[4,1024,128]{2,1,0:T(8,128)(2,1)}), bf16[4,1024,128]{2,1,0:T(8,128)(2,1)S(1)}, u32[]{:S(2)}, u32[]{:S(2)}) %all-to-all-start.3) | async-done | bytes 1048608 | tf_op jit(solution)/shard_map/all_to_all | solution.py:646
  95.7 1.0 copy-done.7
  96.7 9.4 %shard_map.143 = (bf16[256,1024]{1,0:T(8,128)(2,1)}, bf16[256,1024]{1,0:T(8,128)(2,1)}, bf16[256,1280]{1,0:T(8,128)(2,1)}, f32[8,1280]{1,0:T(8,128)}, f32[8,1280...) custom-call(s32[3]{0:T(128)} %pad_add_fusion.refs_0_, ...), custom_call_target="tpu_custom_call" | custom-call | flops 1000000000 | bytes 6426764 | tf_op jit(solution)/shard_map/pallas_call | solution.py:28
  106.2 2.5 %collective-permute-start.2 = (bf16[128,1664]{1,0:T(8,128)(2,1)}, bf16[128,1664]{1,0:T(8,128)(2,1)S(1)}, u32[]{:S(2)}, u32[]{:S(2)}) collective-permute-start(bf16[128,1664]{1,0:T(8,128)(2,1)} %get-tuple-element.100), channel_id=1, source_target_pairs={{0,64},{4,68},{8,72},{12,76},{16,80},{20,84},{24,88},{28,92},{32,9... | collective-permute-start | bytes 1277960 | tf_op jit(solution)/shard_map/ppermute | solution.py:640
  108.6 0.0 collective-permute-start.3
  108.6 0.6 collective-permute-start.4
  109.2 2.7 %collective-permute-start.5 = (bf16[128,1664]{1,0:T(8,128)(2,1)}, bf16[128,1664]{1,0:T(8,128)(2,1)S(1)}, u32[]{:S(2)}, u32[]{:S(2)}) collective-permute-start(bf16[128,1664]{1,0:T(8,128)(2,1)} %get-tuple-element.105), channel_id=1, source_target_pairs={{0,12},{4,0},{8,4},{12,8},{16,28},{20,16},{24,20},{28,24},{32,44},... | collective-permute-start | bytes 1277960 | tf_op jit(solution)/shard_map/ppermute | solution.py:641
  111.9 6.4 %shard_map.144 = (bf16[128,512]{1,0:T(8,128)(2,1)}, f32[128,512]{1,0:T(8,128)}, bf16[64,128]{1,0:T(8,128)(2,1)}) custom-call(s32[3]{0:T(128)} %pad_add_fusion.refs_0_, bf16[256,512]{1,0:T(8,128)(2,1)} %get-tuple-element.67.refs_1_, f32[512]{0:T(512)} %refs_2_.1, bf16[256,1024]{1,0:T(8,128)(2,1)} %get-tuple-element.92.refs_3_, bf16[1024,512]{1,0:T(8,128)(2,1)} %refs_4_.3, ...), custom_call_target="tpu_custom_call" | custom-call | flops 8000000000 | bytes 5515276 | tf_op jit(solution)/shard_map/pallas_call | solution.py:28
  118.3 0.0 collective-permute-done.2.refs_1_.refs_2_
  118.3 0.0 collective-permute-done.3.refs_2_.refs_3_
  118.3 1.9 %collective-permute-done.4.refs_4_.refs_7_ = bf16[128,1664]{1,0:T(8,128)(2,1)S(1)} collective-permute-done((bf16[128,1664]{1,0:T(8,128)(2,1)}, bf16[128,1664]{1,0:T(8,128)(2,1)S(1)}, u32[]{:S(2)}, u32[]{:S(2)}) %collective-permute-start.4) | collective-permute-done | bytes 426016 | tf_op jit(solution)/shard_map/ppermute | solution.py:640
  120.2 0.0 collective-permute-done.5.refs_5_.refs_8_
  120.2 0.0 copy-done.3
  120.2 0.0 copy-start.6
  120.2 0.7 copy-done.6
  120.9 0.2 shard_map.145
  121.2 0.1 collective-permute-start.8
  121.2 3.6 %collective-permute-start.9 = (bf16[64,1792]{1,0:T(8,128)(2,1)S(1)}, bf16[64,1792]{1,0:T(8,128)(2,1)S(1)}, u32[]{:S(2)}, u32[]{:S(2)}) collective-permute-start(bf16[64,1792]{1,0:T(8,128)(2,1)S(1)} %get-tuple-element.111), channel_id=1, source_target_pairs={{0,12},{4,0},{8,4},{12,8},{16,28},{20,16},{24,20},{28,24},{32,44},... | collective-permute-start | bytes 688136 | tf_op jit(solution)/shard_map/ppermute | solution.py:641
  124.8 3.4 %collective-permute-start.6 = (bf16[64,1664]{1,0:T(8,128)(2,1)S(1)}, bf16[64,1664]{1,0:T(8,128)(2,1)S(1)}, u32[]{:S(2)}, u32[]{:S(2)}) collective-permute-start(bf16[64,1664]{1,0:T(8,128)(2,1)S(1)} %get-tuple-element.107), channel_id=1, source_target_pairs={{0,64},{4,68},{8,72},{12,76},{16,80},{20,84},{24,88},{28,92},{32,9... | collective-permute-start | bytes 638984 | tf_op jit(solution)/shard_map/ppermute | solution.py:640
  128.2 0.0 collective-permute-start.7
  128.2 3.4 %collective-permute-done.6.refs_4_ = bf16[64,1664]{1,0:T(8,128)(2,1)S(1)} collective-permute-done((bf16[64,1664]{1,0:T(8,128)(2,1)S(1)}, bf16[64,1664]{1,0:T(8,128)(2,1)S(1)}, u32[]{:S(2)}, u32[]{:S(2)}) %collective-permute-start.6) | collective-permute-done | bytes 213024 | tf_op jit(solution)/shard_map/ppermute | solution.py:640
  131.6 4.8 %collective-permute-done.7.refs_5_ = bf16[64,1664]{1,0:T(8,128)(2,1)S(1)} collective-permute-done((bf16[64,1664]{1,0:T(8,128)(2,1)S(1)}, bf16[64,1664]{1,0:T(8,128)(2,1)S(1)}, u32[]{:S(2)}, u32[]{:S(2)}) %collective-permute-start.7) | collective-permute-done | bytes 213024 | tf_op jit(solution)/shard_map/ppermute | solution.py:641
  136.4 0.0 collective-permute-done.8.refs_9_
  136.4 0.0 collective-permute-done.9.refs_10_
  136.5 1.1 shard_map.146
  137.5 0.1 collective-permute-start.10
  137.6 0.1 collective-permute-start.13
  137.7 2.0 %collective-permute-start.15 = (bf16[32,1792]{1,0:T(8,128)(2,1)S(1)}, bf16[32,1792]{1,0:T(8,128)(2,1)S(1)}, u32[]{:S(2)}, u32[]{:S(2)}) collective-permute-start(bf16[32,1792]{1,0:T(8,128)(2,1)S(1)} %get-tuple-element.119), channel_id=1, source_target_pairs={{0,192},{4,196},{8,200},{12,204},{16,208},{20,212},{24,216},{28,22... | collective-permute-start | bytes 344072 | tf_op jit(solution)/shard_map/ppermute | solution.py:635
  139.7 3.3 %collective-permute-start.11 = (bf16[32,1664]{1,0:T(8,128)(2,1)S(1)}, bf16[32,1664]{1,0:T(8,128)(2,1)S(1)}, u32[]{:S(2)}, u32[]{:S(2)}) collective-permute-start(bf16[32,1664]{1,0:T(8,128)(2,1)S(1)} %get-tuple-element.114), channel_id=1, source_target_pairs={{0,8},{4,12},{8,0},{12,4},{16,24},{20,28},{24,16},{28,20},{32,40},... | collective-permute-start | bytes 319496 | tf_op jit(solution)/shard_map/ppermute | solution.py:635
  143.0 0.6 collective-permute-start.12
  143.6 0.0 collective-permute-done.10.refs_2_
  143.6 0.0 collective-permute-start.14
  143.6 2.3 %collective-permute-done.11.refs_3_ = bf16[32,1664]{1,0:T(8,128)(2,1)S(1)} collective-permute-done((bf16[32,1664]{1,0:T(8,128)(2,1)S(1)}, bf16[32,1664]{1,0:T(8,128)(2,1)S(1)}, u32[]{:S(2)}, u32[]{:S(2)}) %collective-permute-start.11) | collective-permute-done | bytes 106528 | tf_op jit(solution)/shard_map/ppermute | solution.py:635
  145.9 1.8 %collective-permute-done.12.refs_4_ = bf16[32,1664]{1,0:T(8,128)(2,1)S(1)} collective-permute-done((bf16[32,1664]{1,0:T(8,128)(2,1)S(1)}, bf16[32,1664]{1,0:T(8,128)(2,1)S(1)}, u32[]{:S(2)}, u32[]{:S(2)}) %collective-permute-start.12) | collective-permute-done | bytes 106528 | tf_op jit(solution)/shard_map/ppermute | solution.py:635
  147.7 2.1 %collective-permute-done.14.refs_7_ = bf16[32,1664]{1,0:T(8,128)(2,1)S(1)} collective-permute-done((bf16[32,1664]{1,0:T(8,128)(2,1)S(1)}, bf16[32,1664]{1,0:T(8,128)(2,1)S(1)}, u32[]{:S(2)}, u32[]{:S(2)}) %collective-permute-start.14) | collective-permute-done | bytes 106528 | tf_op jit(solution)/shard_map/ppermute | solution.py:635
  149.9 0.0 collective-permute-done.13.refs_6_
  149.9 0.0 collective-permute-done.15.refs_8_
  149.9 0.7 shard_map.147
  150.6 0.1 collective-permute-start.16
  150.7 4.1 %collective-permute-start.18 = (bf16[16,1920]{1,0:T(8,128)(2,1)S(1)}, bf16[16,1920]{1,0:T(8,128)(2,1)S(1)}, u32[]{:S(2)}, u32[]{:S(2)}) collective-permute-start(bf16[16,1920]{1,0:T(8,128)(2,1)S(1)} %get-tuple-element.124), channel_id=1, source_target_pairs={{0,48},{4,52},{8,56},{12,60},{16,0},{20,4},{24,8},{28,12},{32,16},... | collective-permute-start | bytes 184328 | tf_op jit(solution)/shard_map/ppermute | solution.py:635
  154.8 0.5 collective-permute-start.17
  155.3 7.6 %collective-permute-done.17.refs_2_ = bf16[16,1664]{1,0:T(8,128)(2,1)S(1)} collective-permute-done((bf16[16,1664]{1,0:T(8,128)(2,1)S(1)}, bf16[16,1664]{1,0:T(8,128)(2,1)S(1)}, u32[]{:S(2)}, u32[]{:S(2)}) %collective-permute-start.17) | collective-permute-done | bytes 53280 | tf_op jit(solution)/shard_map/ppermute | solution.py:635
  162.9 0.0 collective-permute-done.16.refs_1_
  162.9 0.0 collective-permute-done.18.refs_3_
  162.9 0.0 copy-done.5
  162.9 0.7 shard_map.148
  (13 shorter events, 0.0 us)
Async XLA Ops:
  1.4 12.9 %collective-permute-start.1 = (bf16[16,512]{1,0:T(8,128)(2,1)S(1)}, bf16[16,512]{1,0:T(8,128)(2,1)S(1)}, u32[]{:S(2)}, u32[]{:S(2)}) collective-permute-start(bf16[16,512]{1,0:T(8,128)(2,1)S(1)} %get-tuple-element.130), channel_id=1, source_target_pairs={{4,0},{8,4},{12,8},{16,12},{20,16},{24,20},{28,24},{32,28},{36,32}... | collective-permute-start | bytes 49160 | tf_op jit(solution)/shard_map/ppermute | solution.py:680
  12.3 10.8 %collective-permute-start = (bf16[16,512]{1,0:T(8,128)(2,1)S(1)}, bf16[16,512]{1,0:T(8,128)(2,1)S(1)}, u32[]{:S(2)}, u32[]{:S(2)}) collective-permute-start(bf16[16,512]{1,0:T(8,128)(2,1)S(1)} %get-tuple-element.131), channel_id=1, source_target_pairs={{0,4},{4,8},{8,12},{12,16},{16,20},{20,24},{24,28},{28,32},{32,36}... | collective-permute-start | bytes 49160 | tf_op jit(solution)/shard_map/ppermute | solution.py:679
  14.2 8.8 %copy-start.8 = (bf16[16,512]{1,0:T(8,128)(2,1)}, bf16[16,512]{1,0:T(8,128)(2,1)S(1)}, u32[]{:S(2)}) copy-start(bf16[16,512]{1,0:T(8,128)(2,1)S(1)} %collective-permute-done.1.refs_3_.refs_10_) | copy-start | bytes 49156
  23.0 0.6 copy-start.9
  64.5 15.5 %all-to-all-start.2 = ((bf16[16,64,128]{2,1,0:T(8,128)(2,1)}), bf16[16,64,128]{2,1,0:T(8,128)(2,1)S(1)}, u32[]{:S(2)}, u32[]{:S(2)}) async-start(bf16[16,64,128]{2,1,0:T(8,128)(2,1)} %shard_map.140), calls=%async_computation.2 | async-start | bytes 524288 | tf_op jit(solution)/shard_map/all_to_all | solution.py:646
  81.3 14.4 %all-to-all-start.3 = ((bf16[4,1024,128]{2,1,0:T(8,128)(2,1)}), bf16[4,1024,128]{2,1,0:T(8,128)(2,1)S(1)}, u32[]{:S(2)}, u32[]{:S(2)}) async-start(bf16[4,1024,128]{2,1,0:T(8,128)(2,1)} %shard_map.141), calls=%async_computation.3 | async-start | bytes 2097152 | tf_op jit(solution)/shard_map/all_to_all | solution.py:646
  95.7 1.0 copy-start.7
  106.2 12.1 %collective-permute-start.2 = (bf16[128,1664]{1,0:T(8,128)(2,1)}, bf16[128,1664]{1,0:T(8,128)(2,1)S(1)}, u32[]{:S(2)}, u32[]{:S(2)}) collective-permute-start(bf16[128,1664]{1,0:T(8,128)(2,1)} %get-tuple-element.100), channel_id=1, source_target_pairs={{0,64},{4,68},{8,72},{12,76},{16,80},{20,84},{24,88},{28,92},{32,9... | collective-permute-start | bytes 1277960 | tf_op jit(solution)/shard_map/ppermute | solution.py:640
  108.6 9.7 %collective-permute-start.3 = (bf16[128,1664]{1,0:T(8,128)(2,1)}, bf16[128,1664]{1,0:T(8,128)(2,1)S(1)}, u32[]{:S(2)}, u32[]{:S(2)}) collective-permute-start(bf16[128,1664]{1,0:T(8,128)(2,1)} %get-tuple-element.101), channel_id=1, source_target_pairs={{0,192},{4,196},{8,200},{12,204},{16,208},{20,212},{24,216},{28,22... | collective-permute-start | bytes 1277960 | tf_op jit(solution)/shard_map/ppermute | solution.py:641
  108.6 11.6 %collective-permute-start.4 = (bf16[128,1664]{1,0:T(8,128)(2,1)}, bf16[128,1664]{1,0:T(8,128)(2,1)S(1)}, u32[]{:S(2)}, u32[]{:S(2)}) collective-permute-start(bf16[128,1664]{1,0:T(8,128)(2,1)} %get-tuple-element.104), channel_id=1, source_target_pairs={{0,4},{4,8},{8,12},{12,0},{16,20},{20,24},{24,28},{28,16},{32,36},... | collective-permute-start | bytes 1277960 | tf_op jit(solution)/shard_map/ppermute | solution.py:640
  109.2 11.0 %collective-permute-start.5 = (bf16[128,1664]{1,0:T(8,128)(2,1)}, bf16[128,1664]{1,0:T(8,128)(2,1)S(1)}, u32[]{:S(2)}, u32[]{:S(2)}) collective-permute-start(bf16[128,1664]{1,0:T(8,128)(2,1)} %get-tuple-element.105), channel_id=1, source_target_pairs={{0,12},{4,0},{8,4},{12,8},{16,28},{20,16},{24,20},{28,24},{32,44},... | collective-permute-start | bytes 1277960 | tf_op jit(solution)/shard_map/ppermute | solution.py:641
  111.9 8.3 %copy-start.3 = (bf16[128,1664]{1,0:T(8,128)(2,1)S(1)}, bf16[128,1664]{1,0:T(8,128)(2,1)}, u32[]{:S(2)}) copy-start(bf16[128,1664]{1,0:T(8,128)(2,1)} %get-tuple-element.102.refs_0_) | copy-start | bytes 1277956
  111.9 8.3 %copy-start.4 = (bf16[128,1664]{1,0:T(8,128)(2,1)S(1)}, bf16[128,1664]{1,0:T(8,128)(2,1)}, u32[]{:S(2)}) copy-start(bf16[128,1664]{1,0:T(8,128)(2,1)} %get-tuple-element.103.refs_3_) | copy-start | bytes 1277956
  120.2 0.7 copy-start.6
  120.9 15.5 %copy-start = (s32[3]{0:T(128)S(1)}, s32[3]{0:T(128)}, u32[]{:S(2)}) copy-start(s32[3]{0:T(128)} %pad_add_fusion.refs_0_) | copy-start | bytes 40
  120.9 15.5 %copy-start.1 = (bf16[128,1664]{1,0:T(8,128)(2,1)S(1)}, bf16[128,1664]{1,0:T(8,128)(2,1)}, u32[]{:S(2)}) copy-start(bf16[128,1664]{1,0:T(8,128)(2,1)} %get-tuple-element.99.refs_1_) | copy-start | bytes 1277956
  120.9 15.5 %copy-start.2 = (bf16[128,1664]{1,0:T(8,128)(2,1)S(1)}, bf16[128,1664]{1,0:T(8,128)(2,1)}, u32[]{:S(2)}) copy-start(bf16[128,1664]{1,0:T(8,128)(2,1)} %get-tuple-element.109.refs_6_) | copy-start | bytes 1277956
  121.2 15.3 %collective-permute-start.8 = (bf16[64,1792]{1,0:T(8,128)(2,1)S(1)}, bf16[64,1792]{1,0:T(8,128)(2,1)S(1)}, u32[]{:S(2)}, u32[]{:S(2)}) collective-permute-start(bf16[64,1792]{1,0:T(8,128)(2,1)S(1)} %get-tuple-element.110), channel_id=1, source_target_pairs={{0,4},{4,8},{8,12},{12,0},{16,20},{20,24},{24,28},{28,16},{32,36},... | collective-permute-start | bytes 688136 | tf_op jit(solution)/shard_map/ppermute | solution.py:640
  121.2 15.2 %collective-permute-start.9 = (bf16[64,1792]{1,0:T(8,128)(2,1)S(1)}, bf16[64,1792]{1,0:T(8,128)(2,1)S(1)}, u32[]{:S(2)}, u32[]{:S(2)}) collective-permute-start(bf16[64,1792]{1,0:T(8,128)(2,1)S(1)} %get-tuple-element.111), channel_id=1, source_target_pairs={{0,12},{4,0},{8,4},{12,8},{16,28},{20,16},{24,20},{28,24},{32,44},... | collective-permute-start | bytes 688136 | tf_op jit(solution)/shard_map/ppermute | solution.py:641
  124.8 6.8 %collective-permute-start.6 = (bf16[64,1664]{1,0:T(8,128)(2,1)S(1)}, bf16[64,1664]{1,0:T(8,128)(2,1)S(1)}, u32[]{:S(2)}, u32[]{:S(2)}) collective-permute-start(bf16[64,1664]{1,0:T(8,128)(2,1)S(1)} %get-tuple-element.107), channel_id=1, source_target_pairs={{0,64},{4,68},{8,72},{12,76},{16,80},{20,84},{24,88},{28,92},{32,9... | collective-permute-start | bytes 638984 | tf_op jit(solution)/shard_map/ppermute | solution.py:640
  128.2 8.2 %collective-permute-start.7 = (bf16[64,1664]{1,0:T(8,128)(2,1)S(1)}, bf16[64,1664]{1,0:T(8,128)(2,1)S(1)}, u32[]{:S(2)}, u32[]{:S(2)}) collective-permute-start(bf16[64,1664]{1,0:T(8,128)(2,1)S(1)} %get-tuple-element.108), channel_id=1, source_target_pairs={{0,192},{4,196},{8,200},{12,204},{16,208},{20,212},{24,216},{28,22... | collective-permute-start | bytes 638984 | tf_op jit(solution)/shard_map/ppermute | solution.py:641
  137.5 6.1 %collective-permute-start.10 = (bf16[32,1664]{1,0:T(8,128)(2,1)S(1)}, bf16[32,1664]{1,0:T(8,128)(2,1)S(1)}, u32[]{:S(2)}, u32[]{:S(2)}) collective-permute-start(bf16[32,1664]{1,0:T(8,128)(2,1)S(1)} %get-tuple-element.113), channel_id=1, source_target_pairs={{0,4},{4,8},{8,12},{12,0},{16,20},{20,24},{24,28},{28,16},{32,36},... | collective-permute-start | bytes 319496 | tf_op jit(solution)/shard_map/ppermute | solution.py:635
  137.6 12.2 %collective-permute-start.13 = (bf16[32,1792]{1,0:T(8,128)(2,1)S(1)}, bf16[32,1792]{1,0:T(8,128)(2,1)S(1)}, u32[]{:S(2)}, u32[]{:S(2)}) collective-permute-start(bf16[32,1792]{1,0:T(8,128)(2,1)S(1)} %get-tuple-element.117), channel_id=1, source_target_pairs={{0,64},{4,68},{8,72},{12,76},{16,80},{20,84},{24,88},{28,92},{32,9... | collective-permute-start | bytes 344072 | tf_op jit(solution)/shard_map/ppermute | solution.py:635
  137.7 12.1 %collective-permute-start.15 = (bf16[32,1792]{1,0:T(8,128)(2,1)S(1)}, bf16[32,1792]{1,0:T(8,128)(2,1)S(1)}, u32[]{:S(2)}, u32[]{:S(2)}) collective-permute-start(bf16[32,1792]{1,0:T(8,128)(2,1)S(1)} %get-tuple-element.119), channel_id=1, source_target_pairs={{0,192},{4,196},{8,200},{12,204},{16,208},{20,212},{24,216},{28,22... | collective-permute-start | bytes 344072 | tf_op jit(solution)/shard_map/ppermute | solution.py:635
  139.7 6.2 %collective-permute-start.11 = (bf16[32,1664]{1,0:T(8,128)(2,1)S(1)}, bf16[32,1664]{1,0:T(8,128)(2,1)S(1)}, u32[]{:S(2)}, u32[]{:S(2)}) collective-permute-start(bf16[32,1664]{1,0:T(8,128)(2,1)S(1)} %get-tuple-element.114), channel_id=1, source_target_pairs={{0,8},{4,12},{8,0},{12,4},{16,24},{20,28},{24,16},{28,20},{32,40},... | collective-permute-start | bytes 319496 | tf_op jit(solution)/shard_map/ppermute | solution.py:635
  143.0 4.7 %collective-permute-start.12 = (bf16[32,1664]{1,0:T(8,128)(2,1)S(1)}, bf16[32,1664]{1,0:T(8,128)(2,1)S(1)}, u32[]{:S(2)}, u32[]{:S(2)}) collective-permute-start(bf16[32,1664]{1,0:T(8,128)(2,1)S(1)} %get-tuple-element.115), channel_id=1, source_target_pairs={{0,12},{4,0},{8,4},{12,8},{16,28},{20,16},{24,20},{28,24},{32,44},... | collective-permute-start | bytes 319496 | tf_op jit(solution)/shard_map/ppermute | solution.py:635
  143.6 6.2 %collective-permute-start.14 = (bf16[32,1664]{1,0:T(8,128)(2,1)S(1)}, bf16[32,1664]{1,0:T(8,128)(2,1)S(1)}, u32[]{:S(2)}, u32[]{:S(2)}) collective-permute-start(bf16[32,1664]{1,0:T(8,128)(2,1)S(1)} %get-tuple-element.118), channel_id=1, source_target_pairs={{0,128},{4,132},{8,136},{12,140},{16,144},{20,148},{24,152},{28,15... | collective-permute-start | bytes 319496 | tf_op jit(solution)/shard_map/ppermute | solution.py:635
  149.9 13.0 %copy-start.5 = (f32[128,512]{1,0:T(8,128)S(1)}, f32[128,512]{1,0:T(8,128)}, u32[]{:S(2)}) copy-start(f32[128,512]{1,0:T(8,128)} %get-tuple-element.126.refs_5_) | copy-start | bytes 786436
  150.6 12.3 %collective-permute-start.16 = (bf16[16,1920]{1,0:T(8,128)(2,1)S(1)}, bf16[16,1920]{1,0:T(8,128)(2,1)S(1)}, u32[]{:S(2)}, u32[]{:S(2)}) collective-permute-start(bf16[16,1920]{1,0:T(8,128)(2,1)S(1)} %get-tuple-element.122), channel_id=1, source_target_pairs={{0,16},{4,20},{8,24},{12,28},{16,32},{20,36},{24,40},{28,44},{32,4... | collective-permute-start | bytes 184328 | tf_op jit(solution)/shard_map/ppermute | solution.py:635
  150.7 12.2 %collective-permute-start.18 = (bf16[16,1920]{1,0:T(8,128)(2,1)S(1)}, bf16[16,1920]{1,0:T(8,128)(2,1)S(1)}, u32[]{:S(2)}, u32[]{:S(2)}) collective-permute-start(bf16[16,1920]{1,0:T(8,128)(2,1)S(1)} %get-tuple-element.124), channel_id=1, source_target_pairs={{0,48},{4,52},{8,56},{12,60},{16,0},{20,4},{24,8},{28,12},{32,16},... | collective-permute-start | bytes 184328 | tf_op jit(solution)/shard_map/ppermute | solution.py:635
  154.8 8.1 %collective-permute-start.17 = (bf16[16,1664]{1,0:T(8,128)(2,1)S(1)}, bf16[16,1664]{1,0:T(8,128)(2,1)S(1)}, u32[]{:S(2)}, u32[]{:S(2)}) collective-permute-start(bf16[16,1664]{1,0:T(8,128)(2,1)S(1)} %get-tuple-element.123), channel_id=1, source_target_pairs={{0,32},{4,36},{8,40},{12,44},{16,48},{20,52},{24,56},{28,60},{32,0... | collective-permute-start | bytes 159752 | tf_op jit(solution)/shard_map/ppermute | solution.py:635
